TPU v7x, 32 devices: a whole 2x2x4 slice. The times are simulated.
32 devices in a mesh: dp: 4 (over z), fsdp: 8 (over y, x, core).
Axes of the slice: x: 2, y: 2, z: 4, core: 2. Of those that a mesh axis runs over, the one named last changes fastest.
Arguments:
- latents: bfloat16 [2, 32, 256, 384], P(None, ('dp', 'fsdp')), may hold values from -6 to 6
- condition: bfloat16 [2, 32, 384], P(None, ('dp', 'fsdp')), may hold values from -6 to 6
- cotangent: bfloat16 [2, 32, 256, 384], P(None, ('dp', 'fsdp')), may hold values from -6 to 6
- counts: int32 [2, 32], P(None, ('dp', 'fsdp')), may hold values from 0 to 1, as said below
- ada_weight: bfloat16 [384, 2304], P('fsdp'), may hold values from -0.3125 to 0.3125
- ada_bias: bfloat16 [2304], P('fsdp'), may hold values from -4 to 4
- qkv_weight: bfloat16 [384, 1152], P('fsdp'), may hold values from -0.4375 to 0.4375
- qv_bias: bfloat16 [768], P('fsdp'), may hold values from -4 to 4
- proj_weight: bfloat16 [384, 384], P('fsdp'), may hold values from -0.875 to 0.875
- proj_bias: bfloat16 [384], P('fsdp'), may hold values from -4 to 4
- fc1_weight: bfloat16 [384, 1536], P('fsdp'), may hold values from -0.3125 to 0.3125
- fc1_bias: bfloat16 [1536], P('fsdp'), may hold values from -4 to 4
- fc2_weight: bfloat16 [1536, 384], P('fsdp'), may hold values from -0.15625 to 0.15625
- fc2_bias: bfloat16 [384], P('fsdp'), may hold values from -4 to 4
Outputs:
- block_out: bfloat16 [2, 32, 256, 384], P(None, ('dp', 'fsdp'))
- latents_grad: bfloat16 [2, 32, 256, 384], P(None, ('dp', 'fsdp'))
- condition_grad: bfloat16 [2, 32, 384], P(None, ('dp', 'fsdp'))
- ada_weight_grad: float32 [384, 2304], P('fsdp')
- ada_bias_grad: float32 [2304], P('fsdp')
- qkv_weight_grad: float32 [384, 1152], P('fsdp')
- qv_bias_grad: float32 [768], P('fsdp')
- proj_weight_grad: float32 [384, 384], P('fsdp')
- proj_bias_grad: float32 [384], P('fsdp')
- fc1_weight_grad: float32 [384, 1536], P('fsdp')
- fc1_bias_grad: float32 [1536], P('fsdp')
- fc2_weight_grad: float32 [1536, 384], P('fsdp')
- fc2_bias_grad: float32 [384], P('fsdp')
Inputs may be any that keep to these rules, and one draw needn't show every extreme that they name: `counts`: the live latents of a device in a micro-batch are its first slots; a device may have none; in every micro-batch some device has all 1 slots live.
All inputs are finite; a program needn't handle non-finite values.
Results may differ from a plain program's by a relative error of at most 0.019.
The roundings to bfloat16 on the way count: a program that leaves them out, or rounds other values in their place, can miss the bound.
Values may be sent and summed in bfloat16 or wider, within the bound.
No kernel may reach another device: no remote copies, remote signals or barrier semaphores. Data moves between devices by JAX's collectives and lax.ppermute only.
A program may use at most 64 MiB of HBM per device.

v0:
```python
import jax
import jax.numpy as jnp
from jax import lax
from jax.sharding import PartitionSpec as P

HEADS = 6


EPSILON = 1e-06


def normalize(inputs):
    center = inputs - jnp.mean(inputs, axis=-1, keepdims=True)
    spread = jnp.mean(center * center, axis=-1, keepdims=True)
    inv_root = lax.rsqrt(spread + EPSILON)
    return (center * inv_root, inv_root)


def norm_back(grad_norm, normed, inv_root):
    first_mean = jnp.mean(grad_norm, axis=-1, keepdims=True)
    second_mean = jnp.mean(grad_norm * normed, axis=-1, keepdims=True)
    return inv_root * (grad_norm - first_mean - normed * second_mean)


def gelu_tanh(values):
    return jax.nn.gelu(values, approximate=True)


def forward_pass(weights, latent_block, cond_block, live_slots):
    (
        ada_weight,
        ada_bias,
        qkv_weight,
        qv_bias,
        proj_weight,
        proj_bias,
        fc1_weight,
        fc1_bias,
        fc2_weight,
        fc2_bias,
    ) = weights
    latent_count, length, model_width = latent_block.shape
    head_size = model_width // HEADS
    row_count = latent_count * length
    inputs = latent_block.astype(jnp.float32)
    cond_act = jax.nn.silu(cond_block.astype(jnp.float32)).astype(jnp.bfloat16)
    modulation = jnp.dot(
        cond_act, ada_weight, preferred_element_type=jnp.float32
    ) + ada_bias.astype(jnp.float32)
    shift_attn, scale_attn, gate_attn, shift_mlp, scale_mlp, gate_mlp = jnp.split(
        modulation[:, None, :], 6, axis=-1
    )
    first_norm, first_rstd = normalize(inputs)
    attn_in = (first_norm * (1.0 + scale_attn) + shift_attn).astype(jnp.bfloat16)
    full_bias = jnp.concatenate(
        [
            qv_bias[:model_width].astype(jnp.float32),
            jnp.zeros((model_width,), jnp.float32),
            qv_bias[model_width:].astype(jnp.float32),
        ]
    )
    projected = jnp.dot(
        attn_in.reshape(row_count, model_width), qkv_weight, preferred_element_type=jnp.float32
    )
    projected = (projected + full_bias).astype(jnp.bfloat16)
    queries, key_rows, value_rows = [
        section.reshape(latent_count, length, HEADS, head_size)
        for section in jnp.split(projected, 3, axis=-1)
    ]
    scale_factor = head_size ** (-0.5)
    scores = (
        jnp.einsum("lqhd,lkhd->lhqk", queries, key_rows, preferred_element_type=jnp.float32)
        * scale_factor
    )
    row_top = jnp.max(scores, axis=-1, keepdims=True)
    exponent = jnp.exp(scores - row_top)
    row_total = jnp.sum(exponent, axis=-1, keepdims=True)
    probabilities = exponent / row_total
    log_total = row_top + jnp.log(row_total)
    mixed = jnp.einsum(
        "lhqk,lkhd->lqhd",
        probabilities.astype(jnp.bfloat16),
        value_rows,
        preferred_element_type=jnp.float32,
    )
    mixed = mixed.astype(jnp.bfloat16).reshape(row_count, model_width)
    attn_out = jnp.dot(mixed, proj_weight, preferred_element_type=jnp.float32) + proj_bias.astype(
        jnp.float32
    )
    attn_out = attn_out.reshape(latent_count, length, model_width)
    middle = inputs + gate_attn * attn_out
    second_norm, second_rstd = normalize(middle)
    mlp_in = (second_norm * (1.0 + scale_mlp) + shift_mlp).astype(jnp.bfloat16)
    hidden_pre = jnp.dot(
        mlp_in.reshape(row_count, model_width), fc1_weight, preferred_element_type=jnp.float32
    )
    hidden_pre = hidden_pre + fc1_bias.astype(jnp.float32)
    hidden_act = gelu_tanh(hidden_pre).astype(jnp.bfloat16)
    mlp_out = jnp.dot(hidden_act, fc2_weight, preferred_element_type=jnp.float32) + fc2_bias.astype(
        jnp.float32
    )
    mlp_out = mlp_out.reshape(latent_count, length, model_width)
    result = ((middle + gate_mlp * mlp_out) * live_slots[:, None, None]).astype(jnp.bfloat16)
    kept_state = (
        cond_block,
        cond_act,
        modulation,
        first_norm,
        first_rstd,
        attn_in,
        queries,
        key_rows,
        value_rows,
        log_total,
        mixed,
        attn_out,
        second_norm,
        second_rstd,
        mlp_in,
        hidden_pre,
        hidden_act,
        mlp_out,
    )
    return (kept_state, result)


def backward_pass(weights, kept_state, upstream_block, live_slots):
    (
        ada_weight,
        ada_bias,
        qkv_weight,
        qv_bias,
        proj_weight,
        proj_bias,
        fc1_weight,
        fc1_bias,
        fc2_weight,
        fc2_bias,
    ) = weights
    (
        cond_block,
        cond_act,
        modulation,
        first_norm,
        first_rstd,
        attn_in,
        queries,
        key_rows,
        value_rows,
        log_total,
        mixed,
        attn_out,
        second_norm,
        second_rstd,
        mlp_in,
        hidden_pre,
        hidden_act,
        mlp_out,
    ) = kept_state
    latent_count, length, model_width = upstream_block.shape
    head_size = model_width // HEADS
    row_count = latent_count * length
    scale_factor = head_size ** (-0.5)
    shift_attn, scale_attn, gate_attn, shift_mlp, scale_mlp, gate_mlp = jnp.split(
        modulation[:, None, :], 6, axis=-1
    )
    upstream = upstream_block.astype(jnp.float32) * live_slots[:, None, None]
    grad_gate_mlp = jnp.sum(upstream * mlp_out, axis=1)
    grad_mlp_out = (gate_mlp * upstream).astype(jnp.bfloat16).reshape(row_count, model_width)
    grad_fc2 = jnp.dot(hidden_act.T, grad_mlp_out, preferred_element_type=jnp.float32)
    grad_fc2_bias = jnp.sum(grad_mlp_out.astype(jnp.float32), axis=0)
    grad_act = jnp.dot(grad_mlp_out, fc2_weight.T, preferred_element_type=jnp.float32)
    grad_pre = jax.vjp(gelu_tanh, hidden_pre)[1](grad_act)[0].astype(jnp.bfloat16)
    grad_fc1 = jnp.dot(
        mlp_in.reshape(row_count, model_width).T, grad_pre, preferred_element_type=jnp.float32
    )
    grad_fc1_bias = jnp.sum(grad_pre.astype(jnp.float32), axis=0)
    grad_mlp_in = jnp.dot(grad_pre, fc1_weight.T, preferred_element_type=jnp.float32)
    grad_mlp_in = grad_mlp_in.reshape(latent_count, length, model_width)
    grad_shift_mlp = jnp.sum(grad_mlp_in, axis=1)
    grad_scale_mlp = jnp.sum(grad_mlp_in * second_norm, axis=1)
    grad_middle = upstream + norm_back(grad_mlp_in * (1.0 + scale_mlp), second_norm, second_rstd)
    grad_gate_attn = jnp.sum(grad_middle * attn_out, axis=1)
    grad_attn_out = (gate_attn * grad_middle).astype(jnp.bfloat16).reshape(row_count, model_width)
    grad_proj = jnp.dot(mixed.T, grad_attn_out, preferred_element_type=jnp.float32)
    grad_proj_bias = jnp.sum(grad_attn_out.astype(jnp.float32), axis=0)
    grad_mixed = jnp.dot(grad_attn_out, proj_weight.T, preferred_element_type=jnp.float32)
    grad_mixed = grad_mixed.astype(jnp.bfloat16).reshape(latent_count, length, HEADS, head_size)
    scores = (
        jnp.einsum("lqhd,lkhd->lhqk", queries, key_rows, preferred_element_type=jnp.float32)
        * scale_factor
    )
    probabilities = jnp.exp(scores - log_total)
    grad_probs = jnp.einsum(
        "lqhd,lkhd->lhqk", grad_mixed, value_rows, preferred_element_type=jnp.float32
    )
    grad_values = jnp.einsum(
        "lhqk,lqhd->lkhd",
        probabilities.astype(jnp.bfloat16),
        grad_mixed,
        preferred_element_type=jnp.float32,
    )
    row_inner = jnp.sum(probabilities * grad_probs, axis=-1, keepdims=True)
    grad_scores = (probabilities * (grad_probs - row_inner)).astype(jnp.bfloat16)
    grad_queries = (
        jnp.einsum("lhqk,lkhd->lqhd", grad_scores, key_rows, preferred_element_type=jnp.float32)
        * scale_factor
    )
    grad_keys = (
        jnp.einsum("lhqk,lqhd->lkhd", grad_scores, queries, preferred_element_type=jnp.float32)
        * scale_factor
    )
    grad_projected = jnp.concatenate(
        [
            grad_queries.reshape(row_count, model_width),
            grad_keys.reshape(row_count, model_width),
            grad_values.reshape(row_count, model_width),
        ],
        axis=-1,
    ).astype(jnp.bfloat16)
    grad_qkv = jnp.dot(
        attn_in.reshape(row_count, model_width).T,
        grad_projected,
        preferred_element_type=jnp.float32,
    )
    column_sums = jnp.sum(grad_projected.astype(jnp.float32), axis=0)
    grad_qv_bias = jnp.concatenate([column_sums[:model_width], column_sums[2 * model_width :]])
    grad_attn_in = jnp.dot(grad_projected, qkv_weight.T, preferred_element_type=jnp.float32)
    grad_attn_in = grad_attn_in.reshape(latent_count, length, model_width)
    grad_shift_attn = jnp.sum(grad_attn_in, axis=1)
    grad_scale_attn = jnp.sum(grad_attn_in * first_norm, axis=1)
    grad_inputs = grad_middle + norm_back(grad_attn_in * (1.0 + scale_attn), first_norm, first_rstd)
    grad_modulation = jnp.concatenate(
        [
            grad_shift_attn,
            grad_scale_attn,
            grad_gate_attn,
            grad_shift_mlp,
            grad_scale_mlp,
            grad_gate_mlp,
        ],
        axis=-1,
    ).astype(jnp.bfloat16)
    grad_ada = jnp.dot(cond_act.T, grad_modulation, preferred_element_type=jnp.float32)
    grad_ada_bias = jnp.sum(grad_modulation.astype(jnp.float32), axis=0)
    grad_cond_act = jnp.dot(grad_modulation, ada_weight.T, preferred_element_type=jnp.float32)
    grad_cond = jax.vjp(jax.nn.silu, cond_block.astype(jnp.float32))[1](grad_cond_act)[0]
    weight_grads = (
        grad_ada,
        grad_ada_bias,
        grad_qkv,
        grad_qv_bias,
        grad_proj,
        grad_proj_bias,
        grad_fc1,
        grad_fc1_bias,
        grad_fc2,
        grad_fc2_bias,
    )
    return (weight_grads, grad_inputs.astype(jnp.bfloat16), grad_cond.astype(jnp.bfloat16))


def shards(
    latents,
    condition,
    cotangent,
    counts,
    ada_weight,
    ada_bias,
    qkv_weight,
    qv_bias,
    proj_weight,
    proj_bias,
    fc1_weight,
    fc1_bias,
    fc2_weight,
    fc2_bias,
):
    micro_count = latents.shape[0]
    slot_count = latents.shape[1]
    full_grads = None
    owned_grads = None
    outputs = []
    input_grads = []
    cond_grads = []
    for micro_index in range(micro_count):
        forward_weights = (
            lax.all_gather(ada_weight, "fsdp", axis=0, tiled=True),
            lax.all_gather(ada_bias, "fsdp", axis=0, tiled=True),
            lax.all_gather(qkv_weight, "fsdp", axis=0, tiled=True),
            lax.all_gather(qv_bias, "fsdp", axis=0, tiled=True),
            lax.all_gather(proj_weight, "fsdp", axis=0, tiled=True),
            lax.all_gather(proj_bias, "fsdp", axis=0, tiled=True),
            lax.all_gather(fc1_weight, "fsdp", axis=0, tiled=True),
            lax.all_gather(fc1_bias, "fsdp", axis=0, tiled=True),
            lax.all_gather(fc2_weight, "fsdp", axis=0, tiled=True),
            lax.all_gather(fc2_bias, "fsdp", axis=0, tiled=True),
        )
        live_slots = (jnp.arange(slot_count, dtype=jnp.int32) < counts[micro_index, 0]).astype(
            jnp.float32
        )
        kept_state, result = forward_pass(
            forward_weights, latents[micro_index], condition[micro_index], live_slots
        )
        backward_weights = (
            lax.all_gather(ada_weight, "fsdp", axis=0, tiled=True),
            lax.all_gather(ada_bias, "fsdp", axis=0, tiled=True),
            lax.all_gather(qkv_weight, "fsdp", axis=0, tiled=True),
            lax.all_gather(qv_bias, "fsdp", axis=0, tiled=True),
            lax.all_gather(proj_weight, "fsdp", axis=0, tiled=True),
            lax.all_gather(proj_bias, "fsdp", axis=0, tiled=True),
            lax.all_gather(fc1_weight, "fsdp", axis=0, tiled=True),
            lax.all_gather(fc1_bias, "fsdp", axis=0, tiled=True),
            lax.all_gather(fc2_weight, "fsdp", axis=0, tiled=True),
            lax.all_gather(fc2_bias, "fsdp", axis=0, tiled=True),
        )
        weight_grads, grad_inputs, grad_cond = backward_pass(
            backward_weights, kept_state, cotangent[micro_index], live_slots
        )
        if full_grads is None:
            full_grads = tuple(weight_grads)
        else:
            full_grads = tuple((summed + fresh for summed, fresh in zip(full_grads, weight_grads)))
        outputs.append(result)
        input_grads.append(grad_inputs)
        cond_grads.append(grad_cond)
    owned_grads = (
        lax.psum_scatter(
            full_grads[0].astype(jnp.bfloat16), "fsdp", scatter_dimension=0, tiled=True
        ).astype(jnp.float32),
        lax.psum_scatter(
            full_grads[1].astype(jnp.bfloat16), "fsdp", scatter_dimension=0, tiled=True
        ).astype(jnp.float32),
        lax.psum_scatter(
            full_grads[2].astype(jnp.bfloat16), "fsdp", scatter_dimension=0, tiled=True
        ).astype(jnp.float32),
        lax.psum_scatter(
            full_grads[3].astype(jnp.bfloat16), "fsdp", scatter_dimension=0, tiled=True
        ).astype(jnp.float32),
        lax.psum_scatter(
            full_grads[4].astype(jnp.bfloat16), "fsdp", scatter_dimension=0, tiled=True
        ).astype(jnp.float32),
        lax.psum_scatter(
            full_grads[5].astype(jnp.bfloat16), "fsdp", scatter_dimension=0, tiled=True
        ).astype(jnp.float32),
        lax.psum_scatter(
            full_grads[6].astype(jnp.bfloat16), "fsdp", scatter_dimension=0, tiled=True
        ).astype(jnp.float32),
        lax.psum_scatter(
            full_grads[7].astype(jnp.bfloat16), "fsdp", scatter_dimension=0, tiled=True
        ).astype(jnp.float32),
        lax.psum_scatter(
            full_grads[8].astype(jnp.bfloat16), "fsdp", scatter_dimension=0, tiled=True
        ).astype(jnp.float32),
        lax.psum_scatter(
            full_grads[9].astype(jnp.bfloat16), "fsdp", scatter_dimension=0, tiled=True
        ).astype(jnp.float32),
    )
    replicated = (
        lax.psum(owned_grads[0].astype(jnp.bfloat16), "dp").astype(jnp.float32),
        lax.psum(owned_grads[1].astype(jnp.bfloat16), "dp").astype(jnp.float32),
        lax.psum(owned_grads[2].astype(jnp.bfloat16), "dp").astype(jnp.float32),
        lax.psum(owned_grads[3].astype(jnp.bfloat16), "dp").astype(jnp.float32),
        lax.psum(owned_grads[4].astype(jnp.bfloat16), "dp").astype(jnp.float32),
        lax.psum(owned_grads[5].astype(jnp.bfloat16), "dp").astype(jnp.float32),
        lax.psum(owned_grads[6].astype(jnp.bfloat16), "dp").astype(jnp.float32),
        lax.psum(owned_grads[7].astype(jnp.bfloat16), "dp").astype(jnp.float32),
        lax.psum(owned_grads[8].astype(jnp.bfloat16), "dp").astype(jnp.float32),
        lax.psum(owned_grads[9].astype(jnp.bfloat16), "dp").astype(jnp.float32),
    )
    return (
        jnp.stack(outputs),
        jnp.stack(input_grads),
        jnp.stack(cond_grads),
        replicated[0],
        replicated[1],
        replicated[2],
        replicated[3],
        replicated[4],
        replicated[5],
        replicated[6],
        replicated[7],
        replicated[8],
        replicated[9],
    )


def solution(mesh):
    in_specs = (
        P(None, ("dp", "fsdp"), None, None),
        P(None, ("dp", "fsdp"), None),
        P(None, ("dp", "fsdp"), None, None),
        P(None, ("dp", "fsdp")),
        P("fsdp", None),
        P("fsdp"),
        P("fsdp", None),
        P("fsdp"),
        P("fsdp", None),
        P("fsdp"),
        P("fsdp", None),
        P("fsdp"),
        P("fsdp", None),
        P("fsdp"),
    )
    out_specs = (
        P(None, ("dp", "fsdp"), None, None),
        P(None, ("dp", "fsdp"), None, None),
        P(None, ("dp", "fsdp"), None),
        P("fsdp", None),
        P("fsdp"),
        P("fsdp", None),
        P("fsdp"),
        P("fsdp", None),
        P("fsdp"),
        P("fsdp", None),
        P("fsdp"),
        P("fsdp", None),
        P("fsdp"),
    )
    return jax.shard_map(shards, mesh=mesh, in_specs=in_specs, out_specs=out_specs, check_vma=False)
```

profile of v0, /device:TPU:0, one launch (start us, length us, event | category | flops | bytes accessed | tf_op | source)
XLA Modules:
  0.0 374.8 jit_solution(8547051336335403966)
XLA Ops:
  7.2 0.7 all-gather.4.cloned.1.call-update
  8.0 0.7 all-gather.6.cloned.1.call-update
  8.7 0.7 all-gather.8.cloned.1.call-update
  9.5 1.3 fusion.116
  13.4 1.3 fusion.117
  16.0 1.2 convert_reduce_fusion.5
  17.2 1.3 fusion.64
  18.5 0.8 convert_reduce_fusion.11
  21.0 0.8 dynamic-update-slice.2
  21.9 0.8 dynamic-update-slice.4
  22.7 0.8 dynamic-update-slice.1
  23.6 0.8 dynamic-update-slice.3
  24.4 0.9 dynamic-update-slice
  25.3 25.7 %all-reduce.11 = (bf16[768]{0:T(1024)(128)(2,1)S(1)}, bf16[2304]{0:T(1024)(128)(2,1)S(1)}, bf16[384]{0:T(512)(128)(2,1)S(1)}, bf16[384]{0:T(512)(128)(2,1)S(1)}, bf16[1536]{0:T(1024)(128)(2,1)S(1)}) all-reduce(bf16[768]{0:T(1024)(128)(2,1)S(1)} %dynamic-update-slice.1, ...), channel_id=1, replica_groups=mesh['dp'=4,'fsdp'=8] {'fsdp'}, use_global_device_ids=true, to_apply=%add.1 | all-reduce | flops 5376 | bytes 21504
  52.2 10.9 %all_gather.24 = bf16[384,384]{1,0:T(8,128)(2,1)} all-gather(bf16[48,384]{1,0:T(8,128)(2,1)} %param.22), channel_id=1, replica_groups=mesh['dp'=4,'fsdp'=8] {'fsdp'}, dimensions={0}, use_global_device_ids=true | all-gather | bytes 331776 | tf_op jit(solution)/shard_map/all_gather | solution.py:292
  63.2 9.9 %all_gather.22 = bf16[384,1152]{1,0:T(8,128)(2,1)S(1)} all-gather(bf16[48,1152]{1,0:T(8,128)(2,1)S(1)} %copy-done.50), channel_id=1, replica_groups=mesh['dp'=4,'fsdp'=8] {'fsdp'}, dimensions={0}, use_global_device_ids=true | all-gather | bytes 995328 | tf_op jit(solution)/shard_map/all_gather | solution.py:290
  73.2 2.2 convolution_reduce_fusion
  75.9 0.6 slice_reduce_fusion.5
  76.6 0.6 slice_reduce_fusion.1
  78.4 0.8 copy.73
  79.2 0.8 copy.72
  80.1 0.8 copy.71
  86.0 1.1 fusion.108
  89.2 3.1 convolution_add_fusion.6
  92.4 3.9 %convert_reduce_fusion.1 = (f32[1536]{0:T(1024)}, bf16[256,1536]{1,0:T(8,128)(2,1)S(1)}) fusion(f32[256,1536]{1,0:T(8,128)} %convolution_add_fusion.6, bf16[1536,384]{1,0:T(8,128)(2,1)} %all-gather.8.cloned.1.call-done, f32[]{:T(128)} %bitcast.12, f32[384]{0:T(512)} %get-tuple-element.40, bf16[2,1,256,384]{3,2,1,0:T(8,128)(2,1)} %param.16), kind=kOutput, calls=%fused_computation.32 | convolution fusion | flops 311032320 | bytes 3744256 | tf_op jit(solution)/shard_map/dot_general | solution.py:172
  96.5 1.2 multiply_reduce_fusion.4
  97.7 0.6 convolution_add_fusion.5
  99.0 0.7 convolution_add_fusion.8
  100.1 0.8 copy-done.25
  101.0 2.4 convert_reduce_fusion.6
  103.4 0.7 copy-done.41
  104.1 1.0 convolution_convert_fusion.1
  105.1 1.7 copy.75
  106.8 2.1 convolution_convert_fusion.3
  109.4 0.6 multiply_convert_fusion.1
  110.9 0.9 copy-done.27
  111.9 2.0 convert_reduce_fusion
  113.9 1.2 multiply_reduce_fusion.2
  115.1 0.8 convert_reduce_fusion.8
  120.0 1.5 fusion.2
  121.7 2.3 fusion.76
  124.0 2.0 fusion.1
  126.1 1.7 fusion.98
  127.8 2.8 fusion.61
  131.9 1.7 fusion
  134.5 2.4 multiply_reduce_fusion.5
  139.1 1.7 add_convert_fusion
  144.7 0.8 convert_reduce_fusion.3
  146.1 1.0 fusion.21
  148.7 8.5 %reduce-scatter.8.cloned.1.call-done = bf16[48,1152]{1,0:T(8,128)(2,1)} async-done(((bf16[384,1152]{1,0:T(8,128)(2,1)}), bf16[48,1152]{1,0:T(8,128)(2,1)}) %reduce-scatter.8.cloned.1.call-update) | async-done | bytes 110608 | tf_op jit(solution)/shard_map/reduce_scatter | solution.py:334
  157.1 40.2 %reduce-scatter.14.cloned.1.call-done = bf16[192,384]{1,0:T(8,128)(2,1)} async-done(((bf16[1536,384]{1,0:T(8,128)(2,1)}), bf16[192,384]{1,0:T(8,128)(2,1)}) %reduce-scatter.14.cloned.1.call-update) | async-done | bytes 147472 | tf_op jit(solution)/shard_map/reduce_scatter | solution.py:352
  197.3 39.9 %reduce-scatter.12.cloned.1.call-done = bf16[48,1536]{1,0:T(8,128)(2,1)} async-done(((bf16[384,1536]{1,0:T(8,128)(2,1)}), bf16[48,1536]{1,0:T(8,128)(2,1)}) %reduce-scatter.12.cloned.1.call-update) | async-done | bytes 147472 | tf_op jit(solution)/shard_map/reduce_scatter | solution.py:346
  237.2 43.1 %reduce-scatter.6.cloned.1.call-done = bf16[48,2304]{1,0:T(8,128)(2,1)} async-done(((bf16[384,2304]{1,0:T(8,128)(2,1)}), bf16[48,2304]{1,0:T(8,128)(2,1)}) %reduce-scatter.6.cloned.1.call-update) | async-done | bytes 221200 | tf_op jit(solution)/shard_map/reduce_scatter | solution.py:328
  280.4 23.1 %all-reduce.10 = (bf16[2304]{0:T(1024)(128)(2,1)S(1)}, bf16[768]{0:T(1024)(128)(2,1)S(1)}, bf16[384]{0:T(512)(128)(2,1)S(1)}, bf16[1536]{0:T(1024)(128)(2,1)S(1)}, bf16[384]{0:T(512)(128)(2,1)S(1)}) all-reduce(bf16[2304]{0:T(1024)(128)(2,1)S(1)} %add_convert_fusion.3, ...), channel_id=3, replica_groups=mesh['dp'=4,'fsdp'=8] {'fsdp'}, use_global_device_ids=true, to_apply=%region_36.37.clone | all-reduce | flops 5376 | bytes 21504
  304.5 0.8 pad_maximum_fusion.2
  305.3 0.8 pad_maximum_fusion.3
  306.1 11.1 %reduce-scatter.10.cloned.1.call-done = bf16[48,384]{1,0:T(8,128)(2,1)} async-done(((bf16[384,384]{1,0:T(8,128)(2,1)}), bf16[48,384]{1,0:T(8,128)(2,1)}) %reduce-scatter.10.cloned.1.call-update) | async-done | bytes 36880 | tf_op jit(solution)/shard_map/reduce_scatter | solution.py:340
  317.2 20.5 %all-reduce.12 = (bf16[288]{0:T(512)(128)(2,1)S(1)}, bf16[96]{0:T(256)(128)(2,1)S(1)}, bf16[48,384]{1,0:T(8,128)(2,1)S(1)}, bf16[48]{0:T(256)(128)(2,1)S(1)}, bf...) all-reduce(bf16[288]{0:T(512)(128)(2,1)S(1)} %dynamic-slice.6, ...), channel_id=1, replica_groups=mesh['dp'=4,'fsdp'=8] {'dp'}, use_global_device_ids=true, to_apply=%region_37.38 | all-reduce | flops 19104 | bytes 76416 | tf_op jit(solution)/shard_map/psum | solution.py:361
  340.4 0.6 convert_element_type.457
  341.0 20.6 %all-reduce.16.cloned.1.call-done = (bf16[48,2304]{1,0:T(8,128)(2,1)}, bf16[48,1152]{1,0:T(8,128)(2,1)}, bf16[48,1536]{1,0:T(8,128)(2,1)}, bf16[192,384]{1,0:T(8,128)(2,1)}) async-done(((bf16[48,2304]{1,0:T(8,128)(2,1)}, bf16[48,1152]{1,0:T(8,128)(2,1)}, bf16[48,1536]{1,0:T(8,128)(2,1)}, bf16[192,384]{1,0:T(8,128)(2,1)}), (bf16[48,2304]{1,0:T(8,128)(2,1)}, bf16[48,1152]{1,0:T(8,128)(2,1)}, ...) | async-done | bytes 626704 | tf_op jit(solution)/shard_map/psum | solution.py:360
  361.6 1.7 convert_element_type.447
  363.4 1.6 convert_element_type.451
  365.0 1.6 convert_element_type.463
  366.6 1.6 convert_element_type.469
  (367 shorter events, 29.5 us)
Async XLA Ops:
  7.2 56.0 %copy-start.50 = (bf16[48,1152]{1,0:T(8,128)(2,1)S(1)}, bf16[48,1152]{1,0:T(8,128)(2,1)}, u32[]{:S(2)}) copy-start(bf16[48,1152]{1,0:T(8,128)(2,1)} %param.20) | copy-start | bytes 331780
  7.2 66.0 %all-gather.4.cloned.1.call-start = ((), (), s32[]{:S(2)}) async-start(), calls=%async_computation.5 | async-start | bytes 1990656 | tf_op jit(solution)/shard_map/all_gather | solution.py:288
  7.9 81.3 %all-gather.6.cloned.1.call-start = ((), (), s32[]{:S(2)}) async-start(), calls=%async_computation.6 | async-start | bytes 1327104 | tf_op jit(solution)/shard_map/all_gather | solution.py:294
  8.7 83.7 %all-gather.8.cloned.1.call-start = ((), (), s32[]{:S(2)}) async-start(), calls=%async_computation.7 | async-start | bytes 1327104 | tf_op jit(solution)/shard_map/all_gather | solution.py:296
  9.4 147.7 %reduce-scatter.8.cloned.1.call-start = ((), (), s32[]{:S(2)}) async-start(), calls=%async_computation.9 | async-start | bytes 995328 | tf_op jit(solution)/shard_map/reduce_scatter | solution.py:334
  17.2 63.7 %copy-start.80 = (f32[256]{0:T(256)}, f32[256]{0:T(256)S(1)}, u32[]{:S(2)}) copy-start(f32[256]{0:T(256)S(1)} %broadcast_multiply_fusion.11) | copy-start | bytes 3076
  17.2 60.0 %copy-start.82 = (f32[256]{0:T(256)}, f32[256]{0:T(256)S(1)}, u32[]{:S(2)}) copy-start(f32[256]{0:T(256)S(1)} %broadcast_multiply_fusion.9) | copy-start | bytes 3076
  18.5 62.4 %copy-start.90 = (f32[256]{0:T(256)}, f32[256]{0:T(256)S(1)}, u32[]{:S(2)}) copy-start(f32[256]{0:T(256)S(1)} %add_rsqrt_fusion.3) | copy-start | bytes 3076
  18.5 58.7 %copy-start.92 = (f32[256]{0:T(256)}, f32[256]{0:T(256)S(1)}, u32[]{:S(2)}) copy-start(f32[256]{0:T(256)S(1)} %add_rsqrt_fusion.1) | copy-start | bytes 3076
  73.1 7.8 %copy-start.30 = (bf16[384,1152]{1,0:T(8,128)(2,1)}, bf16[384,1152]{1,0:T(8,128)(2,1)S(1)}, u32[]{:S(2)}) copy-start(bf16[384,1152]{1,0:T(8,128)(2,1)S(1)} %all_gather.22) | copy-start | bytes 2654212
  73.2 2.4 copy-start
  73.2 4.6 %copy-start.2 = (bf16[2,1,256,384]{3,2,1,0:T(8,128)(2,1)S(1)}, bf16[2,1,256,384]{3,2,1,0:T(8,128)(2,1)}, u32[]{:S(2)}) copy-start(bf16[2,1,256,384]{3,2,1,0:T(8,128)(2,1)} %param.14) | copy-start | bytes 1179652
  76.6 4.3 %copy-start.78 = (f32[384]{0:T(512)}, f32[384]{0:T(512)S(1)}, u32[]{:S(2)}) copy-start(f32[384]{0:T(512)S(1)} %get-tuple-element.44) | copy-start | bytes 4612
  76.6 4.3 %copy-start.103 = (f32[384]{0:T(512)}, f32[384]{0:T(512)S(1)}, u32[]{:S(2)}) copy-start(f32[384]{0:T(512)S(1)} %get-tuple-element.43) | copy-start | bytes 4612
  77.2 8.8 %copy-start.76 = (f32[384]{0:T(512)}, f32[384]{0:T(512)S(1)}, u32[]{:S(2)}) copy-start(f32[384]{0:T(512)S(1)} %get-tuple-element.51) | copy-start | bytes 4612
  83.1 2.8 copy-start.39
  85.1 2.1 copy-start.33
  85.9 2.1 copy-start.13
  87.1 2.1 copy-start.60
  92.4 4.0 %copy-start.9 = (f32[256,384]{1,0:T(8,128)S(1)}, f32[256,384]{1,0:T(8,128)}, u32[]{:S(2)}) copy-start(f32[256,384]{1,0:T(8,128)} %copy-done.8) | copy-start | bytes 1179652
  92.4 4.0 %copy-start.11 = (bf16[384,1536]{1,0:T(8,128)(2,1)S(1)}, bf16[384,1536]{1,0:T(8,128)(2,1)}, u32[]{:S(2)}) copy-start(bf16[384,1536]{1,0:T(8,128)(2,1)} %all-gather.6.cloned.1.call-done) | copy-start | bytes 3538948
  92.4 4.0 %copy-start.74 = (f32[384]{0:T(512)S(1)}, f32[384]{0:T(512)}, u32[]{:S(2)}) copy-start(f32[384]{0:T(512)} %get-tuple-element.42) | copy-start | bytes 4612
  92.4 4.0 %copy-start.88 = (f32[256]{0:T(256)S(1)}, f32[256]{0:T(256)}, u32[]{:S(2)}) copy-start(f32[256]{0:T(256)} %copy-done.87) | copy-start | bytes 3076
  92.4 4.0 %copy-start.94 = (f32[256]{0:T(256)S(1)}, f32[256]{0:T(256)}, u32[]{:S(2)}) copy-start(f32[256]{0:T(256)} %add_rsqrt_fusion.2) | copy-start | bytes 3076
  101.0 3.1 copy-start.6
  106.8 2.1 copy-start.24
  106.8 2.1 copy-start.38
  111.9 2.0 copy-start.58
  111.9 2.0 copy-start.62
  111.9 2.0 copy-start.85
  113.9 2.1 copy-start.31
  113.9 2.0 copy-start.7
  121.6 75.8 %reduce-scatter.14.cloned.1.call-start = ((), (), s32[]{:S(2)}) async-start(), calls=%async_computation.12 | async-start | bytes 1327104 | tf_op jit(solution)/shard_map/reduce_scatter | solution.py:352
  121.6 2.3 copy-start.28
  126.0 111.2 %reduce-scatter.12.cloned.1.call-start = ((), (), s32[]{:S(2)}) async-start(), calls=%async_computation.11 | async-start | bytes 1327104 | tf_op jit(solution)/shard_map/reduce_scatter | solution.py:346
  127.8 2.9 copy-start.47
  127.8 2.9 copy-start.10
  127.8 2.9 copy-start.44
  127.8 2.9 copy-start.73
  127.8 2.9 copy-start.75
  127.8 2.9 copy-start.89
  127.8 2.9 copy-start.95
  131.9 2.5 copy-start.14
  131.9 2.5 copy-start.29
  133.6 146.8 %reduce-scatter.6.cloned.1.call-start = ((), (), s32[]{:S(2)}) async-start(), calls=%async_computation.8 | async-start | bytes 1990656 | tf_op jit(solution)/shard_map/reduce_scatter | solution.py:328
  134.4 2.7 copy-start.117
  134.4 2.9 copy-start.116
  134.4 3.1 copy-start.118
  134.4 3.9 %copy-start.120 = (bf16[384]{0:T(512)(128)(2,1)S(1)}, bf16[384]{0:T(512)(128)(2,1)}, u32[]{:S(2)}) copy-start(bf16[384]{0:T(512)(128)(2,1)} %get-tuple-element.35) | copy-start | bytes 2308
  134.5 4.2 %copy-start.119 = (bf16[384]{0:T(512)(128)(2,1)S(1)}, bf16[384]{0:T(512)(128)(2,1)}, u32[]{:S(2)}) copy-start(bf16[384]{0:T(512)(128)(2,1)} %get-tuple-element.17) | copy-start | bytes 2308
  134.5 4.4 %copy-start.115 = (bf16[384]{0:T(512)(128)(2,1)S(1)}, bf16[384]{0:T(512)(128)(2,1)}, u32[]{:S(2)}) copy-start(bf16[384]{0:T(512)(128)(2,1)} %get-tuple-element.28) | copy-start | bytes 2308
  134.5 4.6 %copy-start.97 = (f32[384]{0:T(512)S(1)}, f32[384]{0:T(512)}, u32[]{:S(2)}) copy-start(f32[384]{0:T(512)} %get-tuple-element.80) | copy-start | bytes 4612
  134.5 4.6 %copy-start.98 = (f32[384]{0:T(512)S(1)}, f32[384]{0:T(512)}, u32[]{:S(2)}) copy-start(f32[384]{0:T(512)} %get-tuple-element.82) | copy-start | bytes 4612
  140.8 5.1 %copy-start.40 = (bf16[6,64,256]{2,1,0:T(8,128)(2,1)S(1)}, bf16[6,64,256]{2,1,0:T(8,128)(2,1)}, u32[]{:S(2)}) copy-start(bf16[6,64,256]{2,1,0:T(8,128)(2,1)} %copy-done.39) | copy-start | bytes 589828
  140.8 5.1 %copy-start.42 = (bf16[256,384]{1,0:T(8,128)(2,1)S(1)}, bf16[256,384]{1,0:T(8,128)(2,1)}, u32[]{:S(2)}) copy-start(bf16[256,384]{1,0:T(8,128)(2,1)} %copy-done.41) | copy-start | bytes 589828
  140.8 5.4 %copy-start.34 = (bf16[6,64,256]{2,1,0:T(8,128)(2,1)S(1)}, bf16[6,64,256]{2,1,0:T(8,128)(2,1)}, u32[]{:S(2)}) copy-start(bf16[6,64,256]{2,1,0:T(8,128)(2,1)} %copy-done.33) | copy-start | bytes 589828
  140.8 176.4 %reduce-scatter.10.cloned.1.call-start = ((), (), s32[]{:S(2)}) async-start(), calls=%async_computation.10 | async-start | bytes 331776 | tf_op jit(solution)/shard_map/reduce_scatter | solution.py:340
  147.1 214.5 %all-reduce.16.cloned.1.call-start = ((), (), s32[]{:S(2)}) async-start(), calls=%async_computation.13 | async-start | bytes 1253376 | tf_op jit(solution)/shard_map/psum | solution.py:360
  147.9 155.7 %copy-start.68 = (f32[384]{0:T(512)S(1)}, f32[384]{0:T(512)}, u32[]{:S(2)}) copy-start(f32[384]{0:T(512)} %copy-done.67) | copy-start | bytes 4612
  147.9 155.7 %copy-start.70 = (f32[384]{0:T(512)S(1)}, f32[384]{0:T(512)}, u32[]{:S(2)}) copy-start(f32[384]{0:T(512)} %copy-done.69) | copy-start | bytes 4612
  147.9 156.6 %copy-start.48 = (bf16[1,1,256,384]{3,2,1,0:T(8,128)(2,1)S(1)}, bf16[1,1,256,384]{3,2,1,0:T(8,128)(2,1)}, u32[]{:S(2)}) copy-start(bf16[1,1,256,384]{3,2,1,0:T(8,128)(2,1)} %get-tuple-element.94) | copy-start | bytes 589828
  147.9 156.6 %copy-start.49 = (bf16[1,1,256,384]{3,2,1,0:T(8,128)(2,1)S(1)}, bf16[1,1,256,384]{3,2,1,0:T(8,128)(2,1)}, u32[]{:S(2)}) copy-start(bf16[1,1,256,384]{3,2,1,0:T(8,128)(2,1)} %get-tuple-element.98) | copy-start | bytes 589828
  148.0 157.4 %copy-start.45 = (bf16[1,1,256,384]{3,2,1,0:T(8,128)(2,1)S(1)}, bf16[1,1,256,384]{3,2,1,0:T(8,128)(2,1)}, u32[]{:S(2)}) copy-start(bf16[1,1,256,384]{3,2,1,0:T(8,128)(2,1)} %get-tuple-element.100) | copy-start | bytes 589828
  148.0 157.3 %copy-start.46 = (bf16[1,1,256,384]{3,2,1,0:T(8,128)(2,1)S(1)}, bf16[1,1,256,384]{3,2,1,0:T(8,128)(2,1)}, u32[]{:S(2)}) copy-start(bf16[1,1,256,384]{3,2,1,0:T(8,128)(2,1)} %get-tuple-element.101) | copy-start | bytes 589828
  (68 other events, 85.0 us)
Sparse Core Ops, SparseCore 0:
  9.9 29.3 all-gather.3
  41.2 24.4 all-gather.5
  67.6 24.0 all-gather.7
  121.7 35.3 reduce-scatter.7
  160.5 36.7 reduce-scatter.13
  200.4 36.7 reduce-scatter.11
  241.0 39.3 reduce-scatter.5
  284.3 32.8 reduce-scatter.9
  320.0 41.6 all-reduce.15
where the time goes:
time: 376 us; the launch traced here: 375 us
  waiting for transfers between devices  166 us (44%)
  blocking collectives  90.2 us (24%)
  matrix products  43.5 us (12%)
  other arithmetic  28.1 us (7%)
  local copies, waits for them, and re-layouts  24.9 us (7%)
  between operations  21.9 us (6%)
    unnamed x2, blocking collectives  48.8 us
    reduce_scatter x1, waiting for transfers between devices, shards(): lax.psum_scatter(full_grads[0].astype(jnp.bfloat16), 'fsdp', scatter_dime...  43.1 us
    reduce_scatter x1, waiting for transfers between devices, shards(): lax.psum_scatter(full_grads[8].astype(jnp.bfloat16), 'fsdp', scatter_dime...  40.2 us
    reduce_scatter x1, waiting for transfers between devices, shards(): lax.psum_scatter(full_grads[6].astype(jnp.bfloat16), 'fsdp', scatter_dime...  39.9 us
    psum x1, waiting for transfers between devices, shards(): lax.psum(owned_grads[0].astype(jnp.bfloat16), 'dp').astype(jnp.float32)  20.6 us
    psum x1, blocking collectives, shards(): lax.psum(owned_grads[1].astype(jnp.bfloat16), 'dp').astype(jnp.float32)  20.5 us
    unnamed x272, local copies, waits for them, and re-layouts  17 us
    reduce_scatter x1, waiting for transfers between devices, shards(): lax.psum_scatter(full_grads[4].astype(jnp.bfloat16), 'fsdp', scatter_dime...  11.1 us
  transfers between devices with their start and end apart: 9, of which 6 were waited for; matrix products, arithmetic and copies ran while one was open for 15% of the time, Pallas kernels for 0%

commit v1 on v0

v1 whole, which is shorter than its diff:
```python
import functools

import jax
import jax.numpy as jnp
from jax import lax
from jax.experimental import pallas as pl
from jax.experimental.pallas import tpu as pltpu
from jax.sharding import PartitionSpec as P

HEADS = 6
EPSILON = 1e-06
BF = jnp.bfloat16
F32 = jnp.float32
SQRT_2_PI = 0.7978845608028654
CUBIC = 0.044715
MOD_ROWS = 16
VMEM_BYTES = 56 * 1024 * 1024


def dot(a, b):
    return lax.dot_general(a, b, (((1,), (0,)), ((), ())), preferred_element_type=F32)


def dot_nt(a, b):
    return lax.dot_general(a, b, (((1,), (1,)), ((), ())), preferred_element_type=F32)


def dot_tn(a, b):
    return lax.dot_general(a, b, (((0,), (0,)), ((), ())), preferred_element_type=F32)


def normalize(inputs):
    center = inputs - jnp.mean(inputs, axis=-1, keepdims=True)
    spread = jnp.mean(center * center, axis=-1, keepdims=True)
    inv_root = lax.rsqrt(spread + EPSILON)
    return center * inv_root, inv_root


def norm_back(grad_norm, normed, inv_root):
    first_mean = jnp.mean(grad_norm, axis=-1, keepdims=True)
    second_mean = jnp.mean(grad_norm * normed, axis=-1, keepdims=True)
    return inv_root * (grad_norm - first_mean - normed * second_mean)


def silu(v):
    return v / (1.0 + jnp.exp(-v))


def call(body, outs, ins, scratch=(), smem=(), flops=1 << 24, moved=1 << 20):
    specs = [
        pl.BlockSpec(memory_space=pltpu.SMEM if i in smem else pltpu.VMEM) for i in range(len(ins))
    ]
    return pl.pallas_call(
        body,
        out_shape=[jax.ShapeDtypeStruct(shape, kind) for shape, kind in outs],
        in_specs=specs,
        out_specs=[pl.BlockSpec(memory_space=pltpu.VMEM)] * len(outs),
        scratch_shapes=list(scratch),
        compiler_params=pltpu.CompilerParams(vmem_limit_bytes=VMEM_BYTES),
        cost_estimate=pl.CostEstimate(flops=flops, bytes_accessed=moved, transcendentals=0),
    )(*ins)


class Plan:
    def __init__(self, latents, ada_weight, fc1_weight, fsdp, dp):
        self.fsdp, self.dp = fsdp, dp
        self.mb, self.slots, self.seq, self.d = latents.shape
        self.group = self.mb * self.slots
        self.tokens = self.group * self.seq
        self.ff = fc1_weight.shape[1]
        self.ffb = self.ff // self.d
        own = ada_weight.shape[0]
        power = fsdp >= 2 and fsdp & (fsdp - 1) == 0 and dp & (dp - 1) == 0 and dp >= 2
        self.direct = power and own % 16 == 0 and (own * 4) % (16 * dp) == 0 and self.group == 2
        self.shards = fsdp if self.direct else 1
        self.rows = own if self.direct else self.d
        self.peers = [2 * m for m in range(fsdp // 2)]


def shard_of(plan, k):
    if not plan.direct:
        return 0
    return lax.axis_index("fsdp") ^ k


def pack_body(plan, ada, qkv, proj, fc1, bias, first, second, rows_s):
    d, r = plan.d, plan.rows
    me = lax.axis_index("fsdp") if plan.direct else 0
    blocks = [qkv[:, j * d : (j + 1) * d] for j in range(3)]
    blocks += [ada[:, j * d : (j + 1) * d] for j in range(2)]
    for j, block in enumerate(blocks):
        first[j * r : (j + 1) * r, :] = block
    blocks = [fc1[:, j * d : (j + 1) * d] for j in range(plan.ffb)]
    blocks += [ada[:, j * d : (j + 1) * d] for j in range(2, 6)]
    blocks += [proj[...]]
    for j, block in enumerate(blocks):
        second[j * r : (j + 1) * r, :] = block
    rows_s[...] = jnp.zeros_like(rows_s)
    at = 0
    for row, count in ((0, 6), (1, 2), (2, 1), (3, plan.ffb), (4, 1)):
        wide = bias[:, : count * d]
        if plan.direct:
            wide = pltpu.roll(wide, me * (count * d // plan.fsdp), 1)
        for j in range(count):
            rows_s[at + j : at + j + 1, :] = wide[row : row + 1, j * d : (j + 1) * d]
        at += count
    first[5 * r : 5 * r + 16, :] = rows_s[...].astype(BF)


def place(plan, shards, block, target, column):
    d, r = plan.d, plan.rows
    for k, shard in enumerate(shards):
        at = pl.multiple_of(shard_of(plan, k) * r, 16)
        target[pl.ds(at, r), column * d : (column + 1) * d] = shard[block * r : (block + 1) * r, :]


def emit(plan, grads, blocks, send, keep, rows):
    r = plan.rows
    for name, xor in ((keep, 0),) if send is None else ((send, 1), (keep, 0)):
        for m in range(len(plan.peers) if plan.direct else 1):
            owner = shard_of(plan, 2 * m + xor)
            for at, ref, column, stride, offset in blocks:
                start = pl.multiple_of(owner * (stride * r) + offset * r, 16)
                name[m * rows + at * r : m * rows + (at + 1) * r, :] = ref[
                    pl.ds(start, r), column * plan.d : (column + 1) * plan.d
                ]


def attn_forward(plan, *refs):
    s = plan.shards
    x, cond = refs[:2]
    shards = refs[2 : 2 + s]
    projected, mixed, attn_in, modulation, bias, qkv, ada = refs[2 + s : 9 + s]
    d, length = plan.d, plan.seq
    for j in range(3):
        place(plan, shards, j, qkv, j)
    for j in range(2):
        place(plan, shards, 3 + j, ada, j)
    total = shards[0][5 * plan.rows : 5 * plan.rows + 16, :].astype(F32)
    for shard in shards[1:]:
        total = total + shard[5 * plan.rows : 5 * plan.rows + 16, :].astype(F32)
    bias[...] = total
    cond_act = silu(cond[...].astype(F32)).astype(BF)
    mod = dot(cond_act, ada[...])
    for j in range(2):
        modulation[:, j * d : (j + 1) * d] = mod[:, j * d : (j + 1) * d] + bias[j : j + 1, :]
    left = lax.broadcasted_iota(jnp.int32, (1, 128), 1) < 64

    def latent(g, carry):
        at = pl.ds(pl.multiple_of(g * length, length), length)
        shift = modulation[pl.ds(g, 1), 0:d]
        scale = modulation[pl.ds(g, 1), d : 2 * d]
        normed, _ = normalize(x[at, :].astype(F32))
        rounded = (normed * (1.0 + scale) + shift).astype(BF)
        attn_in[at, :] = rounded
        for j in range(3):
            piece = dot(rounded, qkv[:, j * d : (j + 1) * d])
            if j != 1:
                piece = piece + bias[6 + j // 2 : 7 + j // 2, :]
            projected[at, j * d : (j + 1) * d] = piece.astype(BF)
        for pair in range(HEADS // 2):
            lanes = slice(pair * 128, (pair + 1) * 128)
            q = projected[at, lanes] * jnp.asarray(0.125, BF)
            k = projected[at, d + pair * 128 : d + (pair + 1) * 128]
            v = projected[at, 2 * d + pair * 128 : 2 * d + (pair + 1) * 128]
            halves = []
            for side in (left, ~left):
                scores = dot_nt(jnp.where(side, q, jnp.zeros_like(q)), k)
                exponent = jnp.exp(scores - jnp.max(scores, axis=-1, keepdims=True))
                probs = exponent * (1.0 / jnp.sum(exponent, axis=-1, keepdims=True))
                halves.append(dot(probs.astype(BF), v))
            mixed[at, lanes] = jnp.where(left, halves[0], halves[1]).astype(BF)
        return carry

    lax.fori_loop(0, plan.group, latent, 0)


def mlp_first(plan, *refs):
    s = plan.shards
    counts, x, cond, cot, mixed, bias = refs[:6]
    shards = refs[6 : 6 + s]
    outs = refs[6 + s :]
    (send, outs) = (outs[0], outs[1:]) if plan.direct else (None, outs)
    keep, act, gelu_back, mlp_in, grad_out, middle, attn_out, modulation, fc1, ada, proj = outs[:11]
    grad_fc2 = outs[11]
    d, length, ffb = plan.d, plan.seq, plan.ffb
    for j in range(ffb):
        place(plan, shards, j, fc1, j)
    for j in range(4):
        place(plan, shards, ffb + j, ada, j)
    place(plan, shards, ffb + 4, proj, 0)
    cond_act = silu(cond[...].astype(F32)).astype(BF)
    mod = dot(cond_act, ada[...])
    for j in range(4):
        modulation[:, j * d : (j + 1) * d] = mod[:, j * d : (j + 1) * d] + bias[2 + j : 3 + j, :]

    def latent(g, carry):
        at = pl.ds(pl.multiple_of(g * length, length), length)
        gate_attn, shift, scale, gate = [
            modulation[pl.ds(g, 1), j * d : (j + 1) * d] for j in range(4)
        ]
        live = jnp.where(g % plan.slots < counts[g // plan.slots, 0], 1.0, 0.0).astype(F32)
        out = dot(mixed[at, :], proj[...]) + bias[8:9, :]
        attn_out[at, :] = out
        mid = x[at, :].astype(F32) + gate_attn * out
        middle[at, :] = mid
        normed, _ = normalize(mid)
        mlp_in[at, :] = (normed * (1.0 + scale) + shift).astype(BF)
        grad_out[at, :] = ((gate * live) * cot[at, :].astype(F32)).astype(BF)
        return carry

    lax.fori_loop(0, plan.group, latent, 0)
    step = 256
    for c in range(plan.ff // step):
        cols = slice(c * step, (c + 1) * step)
        row, lane = divmod(c * step, d)
        pieces = []
        start, rest = c * step, step
        while rest:
            row, lane = divmod(start, d)
            width = min(rest, d - lane)
            pieces.append(bias[9 + row : 10 + row, lane : lane + width])
            start, rest = start + width, rest - width
        shift = pieces[0] if len(pieces) == 1 else jnp.concatenate(pieces, axis=1)
        pre = dot(mlp_in[...], fc1[:, cols]) + shift
        square = pre * pre
        bend = jnp.tanh(pre * (SQRT_2_PI + (SQRT_2_PI * CUBIC) * square))
        half = 0.5 + 0.5 * bend
        value = (pre * half).astype(BF)
        act[:, cols] = value
        slope = (0.5 * SQRT_2_PI) + (1.5 * SQRT_2_PI * CUBIC) * square
        gelu_back[:, cols] = half + pre * (1.0 - bend * bend) * slope
        grad_fc2[cols, :] = dot_tn(value, grad_out[...]).astype(BF)
    emit(plan, None, [(j, grad_fc2, 0, 4, j) for j in range(ffb)], send, keep, ffb * plan.rows)


def mlp_second(plan, *refs):
    s = plan.shards
    grad_out, gelu_back, mlp_in = refs[:3]
    shards = refs[3 : 3 + s]
    outs = refs[3 + s :]
    (send, outs) = (outs[0], outs[1:]) if plan.direct else (None, outs)
    keep, grad_pre, fc2 = outs[:3]
    turned, grad_fc1 = outs[3:]
    r4 = plan.rows * plan.ffb
    for k, shard in enumerate(shards):
        fc2[pl.ds(pl.multiple_of(shard_of(plan, k) * r4, 16), r4), :] = shard[...]
    turned[...] = mlp_in[...].T
    step = 256
    for c in range(plan.ff // step):
        cols = slice(c * step, (c + 1) * step)
        grad = (dot_nt(grad_out[...], fc2[cols, :]) * gelu_back[:, cols]).astype(BF)
        grad_pre[:, cols] = grad
        grad_fc1[:, cols] = dot(turned[...], grad).astype(BF)
    emit(plan, None, [(j, grad_fc1, j, 1, 0) for j in range(plan.ffb)], send, keep, r4)


def mlp_back(plan, *refs):
    (counts, cot, act, fc2, grad_pre, fc1, middle, attn_out, modulation, bias, mixed, proj,
     grad_out) = refs[:13]
    block_out, grad_mixed, grad_middle, grad_proj, misc, grad_mod = refs[13:19]
    d, length = plan.d, plan.seq
    grad_gates = refs[19]
    misc[...] = jnp.zeros_like(misc)
    sums = jnp.sum(grad_pre[...].astype(F32), axis=0, keepdims=True)
    for j in range(plan.ffb):
        misc[3 + j : 4 + j, :] = sums[:, j * d : (j + 1) * d]
    misc[3 + plan.ffb : 4 + plan.ffb, :] = jnp.sum(
        grad_out[...].astype(F32), axis=0, keepdims=True
    )

    def latent(g, carry):
        at = pl.ds(pl.multiple_of(g * length, length), length)
        gate_attn, _, scale, gate = [modulation[pl.ds(g, 1), j * d : (j + 1) * d] for j in range(4)]
        live = jnp.where(g % plan.slots < counts[g // plan.slots, 0], 1.0, 0.0).astype(F32)
        upstream = cot[at, :].astype(F32) * live
        mid = middle[at, :]
        mlp_out = dot(act[at, :], fc2[...]) + bias[9 + plan.ffb : 10 + plan.ffb, :]
        block_out[at, :] = (live * (mid + gate * mlp_out)).astype(BF)
        normed, rstd = normalize(mid)
        grad_in = dot_nt(grad_pre[at, :], fc1[...])
        grad_mid = upstream + norm_back(grad_in * (1.0 + scale), normed, rstd)
        grad_middle[at, :] = grad_mid
        rounded = (gate_attn * grad_mid).astype(BF)
        grad_gates[at, :] = rounded
        grad_mixed[at, :] = dot_nt(rounded, proj[...]).astype(BF)
        pieces = [grad_mid * attn_out[at, :], grad_in, grad_in * normed, upstream * mlp_out]
        for j, piece in enumerate(pieces):
            grad_mod[pl.ds(g, 1), j * d : (j + 1) * d] = jnp.sum(piece, axis=0, keepdims=True)
        return carry

    lax.fori_loop(0, plan.group, latent, 0)
    misc[2:3, :] = jnp.sum(grad_gates[...].astype(F32), axis=0, keepdims=True)
    grad_proj[...] = dot_tn(mixed[...], grad_gates[...]).astype(BF)


def attn_back(plan, *refs):
    (x, cond, projected, grad_mixed, grad_middle, attn_in, qkv, modulation, grad_proj, misc,
     grad_mod) = refs[:11]
    outs = refs[11:]
    (send, outs) = (outs[0], outs[1:]) if plan.direct else (None, outs)
    keep, latents_grad, mods = outs[:3]
    grad_proj_in, grad_qkv, rows_s, misc_s, cond_s = outs[3:]
    d, length, r = plan.d, plan.seq, plan.rows
    left = lax.broadcasted_iota(jnp.int32, (1, 128), 1) < 64
    misc_s[...] = misc[...]
    rows_s[...] = jnp.zeros_like(rows_s)
    cond_s[...] = silu(cond[...].astype(F32))

    def latent(g, carry):
        at = pl.ds(pl.multiple_of(g * length, length), length)
        scale = modulation[pl.ds(g, 1), d : 2 * d]
        for pair in range(HEADS // 2):
            lanes = slice(pair * 128, (pair + 1) * 128)
            q = projected[at, lanes] * jnp.asarray(0.125, BF)
            k = projected[at, d + pair * 128 : d + (pair + 1) * 128]
            v = projected[at, 2 * d + pair * 128 : 2 * d + (pair + 1) * 128]
            gm = grad_mixed[at, lanes]
            grads_q, grads_k, grads_v = [], [], []
            for side in (left, ~left):
                scores = dot_nt(jnp.where(side, q, jnp.zeros_like(q)), k)
                exponent = jnp.exp(scores - jnp.max(scores, axis=-1, keepdims=True))
                probs = exponent * (1.0 / jnp.sum(exponent, axis=-1, keepdims=True))
                grad_probs = dot_nt(jnp.where(side, gm, jnp.zeros_like(gm)), v)
                inner = jnp.sum(probs * grad_probs, axis=-1, keepdims=True)
                grad_scores = (probs * (grad_probs - inner)).astype(BF)
                grads_q.append(dot(grad_scores, k))
                grads_k.append(dot_tn(grad_scores, q))
                grads_v.append(dot_tn(probs.astype(BF), gm))
            for j, (pieces, factor) in enumerate(((grads_q, 0.125), (grads_k, 1.0), (grads_v, 1.0))):
                merged = jnp.where(left, pieces[0], pieces[1]) * factor
                grad_proj_in[at, j * d + pair * 128 : j * d + (pair + 1) * 128] = merged.astype(BF)
        normed, rstd = normalize(x[at, :].astype(F32))
        grad_in = dot_nt(grad_proj_in[at, :], qkv[...])
        grad = grad_middle[at, :] + norm_back(grad_in * (1.0 + scale), normed, rstd)
        latents_grad[at, :] = grad.astype(BF)
        base = g * 7
        pieces = [cond_s[pl.ds(g, 1), :], jnp.sum(grad_in, axis=0, keepdims=True)]
        pieces += [jnp.sum(grad_in * normed, axis=0, keepdims=True)]
        pieces += [grad_mod[pl.ds(g, 1), j * d : (j + 1) * d] for j in range(4)]
        for j, piece in enumerate(pieces):
            rows_s[pl.ds(base + j, 1), :] = piece
        return carry

    lax.fori_loop(0, plan.group, latent, 0)
    mods[...] = rows_s[...].astype(BF)
    turned = attn_in[...].T
    for j in range(3):
        cols = slice(j * d, (j + 1) * d)
        grad_qkv[:, cols] = dot(turned, grad_proj_in[:, cols]).astype(BF)
        if j != 1:
            misc_s[j // 2 : j // 2 + 1, :] = jnp.sum(
                grad_proj_in[:, cols].astype(F32), axis=0, keepdims=True
            )
    blocks = [(j, grad_qkv, j, 1, 0) for j in range(3)] + [(3, grad_proj, 0, 1, 0)]
    rows = 4 * r + 16
    emit(plan, None, blocks, send, keep, rows)
    low = misc_s[...].astype(BF)
    for name in (keep,) if send is None else (send, keep):
        for m in range(len(plan.peers) if plan.direct else 1):
            name[m * rows + 4 * r : (m + 1) * rows, :] = low


def cond_back(plan, cond, mods, first, second, grad):
    d = plan.d
    rows = mods[...].astype(F32)
    total = None
    kept = []
    for g in range(plan.group):
        total = jnp.zeros((1, d), F32)
        for j in range(6):
            weight = first[:, j * d : (j + 1) * d] if j < 2 else second[:, (j - 2) * d : (j - 1) * d]
            line = jnp.broadcast_to(rows[g * 7 + 1 + j : g * 7 + 2 + j, :], (8, d)).astype(BF)
            total = total + dot_nt(line, weight)[0:1, :]
        kept.append(total)
    for g in range(plan.group):
        v = cond[g : g + 1, :].astype(F32)
        gate = 1.0 / (1.0 + jnp.exp(-v))
        grad[g : g + 1, :] = (kept[g] * (gate * (1.0 + v * (1.0 - gate)))).astype(BF)


def add_siblings(peers, rows, *refs):
    keep, received, own = refs[:3]
    outs = refs[3:]
    for m in range(peers):
        at = slice(m * rows, (m + 1) * rows)
        total = keep[at, :].astype(F32) + received[at, :].astype(F32)
        if m == 0:
            own[...] = total
        else:
            outs[m - 1][...] = total.astype(BF)


def add_chips(count, dp, quarter, own, *refs):
    received, mine, outs = refs[:count], refs[count], refs[count + 1 : count + dp]
    total_s = refs[count + dp]
    total = own[...]
    for piece in received:
        total = total + piece[...].astype(F32)
    total_s[...] = total
    me = lax.axis_index("dp")
    for j in range(dp):
        part = total_s[pl.ds(pl.multiple_of((me ^ j) * quarter, 16), quarter), :]
        if j == 0:
            mine[...] = part
        else:
            outs[j - 1][...] = part.astype(BF)


def add_groups(dp, *refs):
    total = refs[0][...]
    for piece in refs[1:dp]:
        total = total + piece[...].astype(F32)
    refs[dp][...] = total.astype(BF)


def gather_groups(dp, quarter, layout, *refs):
    pieces, outs, rows_s = refs[:dp], refs[dp:-1], refs[-1]
    me = lax.axis_index("dp")
    for j, piece in enumerate(pieces):
        rows_s[pl.ds(pl.multiple_of((me ^ j) * quarter, 16), quarter), :] = piece[...].astype(F32)
    d = rows_s.shape[1]
    at = 0
    for out, (blocks, rows) in zip(outs, layout):
        for j in range(blocks):
            out[:, j * d : (j + 1) * d] = rows_s[at : at + rows, :]
            at += rows


def last_sibling(peers, rows, *refs):
    keep, received, mods, mods_in, own = refs[:5]
    outs = refs[5:]
    for m in range(peers):
        at = slice(m * rows, (m + 1) * rows)
        total = keep[at, :].astype(F32) + received[at, :].astype(F32)
        if m == 0:
            own[0:rows, :] = total
            own[rows : rows + MOD_ROWS, :] = mods[...].astype(F32)
            own[rows + MOD_ROWS : rows + 2 * MOD_ROWS, :] = mods_in[...].astype(F32)
        else:
            outs[m - 1][0:rows, :] = total.astype(BF)
            outs[m - 1][rows : rows + MOD_ROWS, :] = mods[...]
            outs[m - 1][rows + MOD_ROWS : rows + 2 * MOD_ROWS, :] = mods_in[...]


def last_chips(count, dp, quarter, rows, own, *refs):
    received, mine, outs = refs[:count], refs[count], refs[count + 1 : count + dp]
    total_s, tail_s = refs[count + dp :]
    total = own[0 : rows, :]
    for piece in received:
        total = total + piece[0:rows, :].astype(F32)
    total_s[...] = total[: rows - 16]
    tail_s[0:16, :] = total[rows - 16 :].astype(BF)
    tail_s[16 : 16 + 2 * MOD_ROWS, :] = own[rows:, :].astype(BF)
    for i, piece in enumerate(received):
        at = 16 + (i + 1) * 2 * MOD_ROWS
        tail_s[at : at + 2 * MOD_ROWS, :] = piece[rows:, :]
    me = lax.axis_index("dp")
    for j in range(dp):
        part = total_s[pl.ds(pl.multiple_of((me ^ j) * quarter, 16), quarter), :]
        name = mine if j == 0 else outs[j - 1]
        name[0:quarter, :] = part.astype(name.dtype)
        name[quarter:, :] = tail_s[...].astype(name.dtype)


def last_groups(dp, quarter, *refs):
    pieces, low = refs[:dp], refs[dp]
    total = pieces[0][0:quarter, :]
    for piece in pieces[1:]:
        total = total + piece[0:quarter, :].astype(F32)
    low[...] = total.astype(BF)


def ada_grads(plan, quarter, *refs):
    dp, d, r = plan.dp, plan.d, plan.rows
    pieces = refs[:dp]
    ada, ada_bias, qv, proj, fc1, fc2 = refs[dp : dp + 6]
    rows_s, turned_s = refs[dp + 6 :]
    each = plan.fsdp * MOD_ROWS
    total = pieces[0][quarter : quarter + 16, :].astype(F32)
    for piece in pieces[1:]:
        total = total + piece[quarter : quarter + 16, :].astype(F32)
    for j, piece in enumerate(pieces):
        rows_s[j * each : (j + 1) * each, :] = piece[quarter + 16 :, :].astype(BF)
    count = dp * each
    row = lax.broadcasted_iota(jnp.int32, (count, count), 0)
    column = lax.broadcasted_iota(jnp.int32, (count, count), 1)
    slot = row % MOD_ROWS
    source = row - slot + jnp.where(slot >= 7, 7, 0)
    pick = ((column == source) & (slot < 14)).astype(BF)
    turned_s[...] = dot(pick, rows_s[...]).T
    me = lax.axis_index("fsdp")
    mine = turned_s[pl.ds(pl.multiple_of(me * r, 16), r), :].astype(BF)
    lane = lax.broadcasted_iota(jnp.int32, (1, count), 1) % MOD_ROWS
    tall = lax.broadcasted_iota(jnp.int32, (count, 1), 0) % MOD_ROWS
    values = rows_s[...]
    sums = []
    for j in range(6):
        here = (lane == 1 + j) | (lane == 8 + j)
        ada[:, j * d : (j + 1) * d] = dot(jnp.where(here, mine, jnp.zeros_like(mine)), values)
        there = (tall == 1 + j) | (tall == 8 + j)
        sums.append(
            jnp.sum(jnp.where(there, values.astype(F32), 0.0), axis=0, keepdims=True)
        )
    lists = [
        (ada_bias, sums),
        (qv, [total[0:1], total[1:2]]),
        (proj, [total[2:3]]),
        (fc1, [total[3 + j : 4 + j] for j in range(plan.ffb)]),
        (fc2, [total[3 + plan.ffb : 4 + plan.ffb]]),
    ]
    for out, lines in lists:
        wide = lines[0] if len(lines) == 1 else jnp.concatenate(lines, axis=1)
        width = wide.shape[1]
        own = width // plan.fsdp
        wide = jnp.broadcast_to(wide, (8, width))
        wide = pltpu.roll(wide, lax.rem(width - me * own, width), 1)
        out[...] = wide[0:1, :own]


def swap(plan, value, k, axis="fsdp"):
    size = plan.fsdp if axis == "fsdp" else plan.dp
    return lax.ppermute(value, axis, [(i, i ^ k) for i in range(size)])


def gather_shards(plan, value):
    if not plan.direct:
        return [value]
    chips = [value] + [swap(plan, value, k) for k in plan.peers[1:]]
    cores = [swap(plan, shard, 1) for shard in chips]
    return [shard for pair in zip(chips, cores) for shard in pair]


def reduce_chunk(plan, send, keep, layout):
    d, dp, peers = plan.d, plan.dp, len(plan.peers)
    rows = keep.shape[0] // peers
    quarter = rows // dp
    received = swap(plan, send, 1)
    own, *pieces = call(
        functools.partial(add_siblings, peers, rows),
        [((rows, d), F32)] + [((rows, d), BF)] * (peers - 1),
        [keep, received],
    )
    pieces = [swap(plan, piece, k) for piece, k in zip(pieces, plan.peers[1:])]
    mine, *quarters = call(
        functools.partial(add_chips, peers - 1, dp, quarter),
        [((quarter, d), F32)] + [((quarter, d), BF)] * (dp - 1),
        [own] + pieces,
        [pltpu.VMEM((rows, d), F32)],
    )
    quarters = [swap(plan, part, j + 1, "dp") for j, part in enumerate(quarters)]
    (low,) = call(functools.partial(add_groups, dp), [((quarter, d), BF)], [mine] + quarters)
    parts = [low] + [swap(plan, low, j, "dp") for j in range(1, dp)]
    return call(
        functools.partial(gather_groups, dp, quarter, layout),
        [((height, blocks * d), F32) for blocks, height in layout],
        parts,
        [pltpu.VMEM((rows, d), F32)],
    )


def reduce_last(plan, send, keep, mods):
    d, dp, peers, r = plan.d, plan.dp, len(plan.peers), plan.rows
    rows = keep.shape[0] // peers
    quarter = (rows - 16) // dp
    received, mods_in = swap(plan, send, 1), swap(plan, mods, 1)
    long = rows + 2 * MOD_ROWS
    own, *pieces = call(
        functools.partial(last_sibling, peers, rows),
        [((long, d), F32)] + [((long, d), BF)] * (peers - 1),
        [keep, received, mods, mods_in],
    )
    pieces = [swap(plan, piece, k) for piece, k in zip(pieces, plan.peers[1:])]
    tail = 16 + plan.fsdp * MOD_ROWS
    mine, *quarters = call(
        functools.partial(last_chips, peers - 1, dp, quarter, rows),
        [((quarter + tail, d), F32)] + [((quarter + tail, d), BF)] * (dp - 1),
        [own] + pieces,
        [pltpu.VMEM((rows - 16, d), F32), pltpu.VMEM((tail, d), BF)],
    )
    quarters = [swap(plan, part, j + 1, "dp") for j, part in enumerate(quarters)]
    (low,) = call(functools.partial(last_groups, dp, quarter), [((quarter, d), BF)], [mine] + quarters)
    parts = [low] + [swap(plan, low, j, "dp") for j in range(1, dp)]
    widths = [6, 2, 1, plan.ffb, 1]
    ada, *biases = call(
        functools.partial(ada_grads, plan, quarter),
        [((r, 6 * d), F32)] + [((1, w * d // plan.fsdp), F32) for w in widths],
        [mine] + quarters,
        [
            pltpu.VMEM((dp * plan.fsdp * MOD_ROWS, d), BF),
            pltpu.VMEM((d, dp * plan.fsdp * MOD_ROWS), F32),
        ],
    )
    qkv, proj = call(
        functools.partial(gather_groups, dp, quarter, ((3, r), (1, r))),
        [((r, 3 * d), F32), ((r, d), F32)],
        parts,
        [pltpu.VMEM((rows - 16, d), F32)],
    )
    return qkv, proj, ada, [bias.reshape(-1) for bias in biases]


def reduce_whole(plan, fc2_rows, fc1_rows, last, mods):
    d, ffb = plan.d, plan.ffb

    def unpack(rows, blocks):
        return rows.reshape(blocks, d, d).transpose(1, 0, 2).reshape(d, blocks * d)

    mods = mods[: 7 * plan.group].reshape(plan.group, 7, d)
    cond_act, grad_mod = mods[:, 0], mods[:, 1:].reshape(plan.group, 6 * d)
    ada = jnp.dot(cond_act.T, grad_mod, preferred_element_type=F32)
    misc = last[4 * d : 4 * d + 16]
    grads = (
        ada,
        jnp.sum(grad_mod.astype(F32), axis=0),
        unpack(last[: 3 * d], 3),
        misc[0:2].reshape(-1),
        last[3 * d : 4 * d],
        misc[2],
        unpack(fc1_rows, ffb),
        misc[3 : 3 + ffb].reshape(-1),
        fc2_rows,
        misc[3 + ffb],
    )
    owned = [
        lax.psum_scatter(grad.astype(BF), "fsdp", scatter_dimension=0, tiled=True) for grad in grads
    ]
    return [lax.psum(grad, "dp").astype(F32) for grad in owned]


def shards(
    fsdp,
    dp,
    latents,
    condition,
    cotangent,
    counts,
    ada_weight,
    ada_bias,
    qkv_weight,
    qv_bias,
    proj_weight,
    proj_bias,
    fc1_weight,
    fc1_bias,
    fc2_weight,
    fc2_bias,
):
    plan = Plan(latents, ada_weight, fc1_weight, fsdp, dp)
    d, n, group, ff, r = plan.d, plan.tokens, plan.group, plan.ff, plan.rows
    x = latents.reshape(n, d)
    cot = cotangent.reshape(n, d)
    cond = condition.reshape(group, d)
    biases = [ada_bias, qv_bias, proj_bias, fc1_bias, fc2_bias]
    weights = [ada_weight, qkv_weight, proj_weight, fc1_weight]
    third = fc2_weight
    if not plan.direct:
        def whole(v):
            return lax.all_gather(v, "fsdp", axis=0, tiled=True)

        biases, weights, third = [whole(v) for v in biases], [whole(v) for v in weights], whole(third)
    rows = [jnp.pad(bias.astype(F32), (0, 6 * d - bias.shape[0])) for bias in biases]
    rows = jnp.stack(rows + [jnp.zeros_like(rows[0])] * 3)
    first, second = call(
        functools.partial(pack_body, plan),
        [((5 * r + 16, d), BF), (((plan.ffb + 5) * r, d), BF)],
        weights + [rows],
        [pltpu.VMEM((16, d), F32)],
    )
    first, second, third = [gather_shards(plan, v) for v in (first, second, third)]

    projected, mixed, attn_in, mod_first, bias, qkv, ada_first = call(
        functools.partial(attn_forward, plan),
        [
            ((n, 3 * d), BF),
            ((n, d), BF),
            ((n, d), BF),
            ((group, 2 * d), F32),
            ((16, d), F32),
            ((d, 3 * d), BF),
            ((d, 2 * d), BF),
        ],
        [x, cond] + first,
        flops=1 << 30,
        moved=1 << 24,
    )
    halves = len(plan.peers) if plan.direct else 1
    sides = 2 if plan.direct else 1
    outs = call(
        functools.partial(mlp_first, plan),
        [((halves * plan.ffb * r, d), BF)] * sides
        + [
            ((n, ff), BF),
            ((n, ff), F32),
            ((n, d), BF),
            ((n, d), BF),
            ((n, d), F32),
            ((n, d), F32),
            ((group, 4 * d), F32),
            ((d, ff), BF),
            ((d, 4 * d), BF),
            ((d, d), BF),
        ],
        [counts, x, cond, cot, mixed, bias] + second,
        [pltpu.VMEM((ff, d), BF)],
        smem=(0,),
        flops=1 << 30,
        moved=1 << 24,
    )
    fc2_chunk = outs[:sides]
    act, gelu_back, mlp_in, grad_out, middle, attn_out, mod_second, fc1, ada_second, proj = outs[sides:]
    outs = call(
        functools.partial(mlp_second, plan),
        [((halves * plan.ffb * r, d), BF)] * sides + [((n, ff), BF), ((ff, d), BF)],
        [grad_out, gelu_back, mlp_in] + third,
        [pltpu.VMEM((d, n), BF), pltpu.VMEM((d, ff), BF)],
        flops=1 << 30,
        moved=1 << 24,
    )
    fc1_chunk = outs[:sides]
    grad_pre, fc2 = outs[sides:]
    block_out, grad_mixed, grad_middle, grad_proj, misc, grad_mod = call(
        functools.partial(mlp_back, plan),
        [
            ((n, d), BF),
            ((n, d), BF),
            ((n, d), F32),
            ((d, d), BF),
            ((16, d), F32),
            ((group, 4 * d), F32),
        ],
        [counts, cot, act, fc2, grad_pre, fc1, middle, attn_out, mod_second, bias, mixed, proj, grad_out],
        [pltpu.VMEM((n, d), BF)],
        smem=(0,),
        flops=1 << 30,
        moved=1 << 24,
    )
    outs = call(
        functools.partial(attn_back, plan),
        [((halves * (4 * r + 16), d), BF)] * sides + [((n, d), BF), ((MOD_ROWS, d), BF)],
        [x, cond, projected, grad_mixed, grad_middle, attn_in, qkv, mod_first, grad_proj, misc, grad_mod],
        [
            pltpu.VMEM((n, 3 * d), BF),
            pltpu.VMEM((d, 3 * d), BF),
            pltpu.VMEM((MOD_ROWS, d), F32),
            pltpu.VMEM((16, d), F32),
            pltpu.VMEM((group, d), F32),
        ],
        flops=1 << 30,
        moved=1 << 24,
    )
    last_chunk = outs[:sides]
    latents_grad, mods = outs[sides:]
    (cond_grad,) = call(
        functools.partial(cond_back, plan), [((group, d), BF)], [cond, mods, ada_first, ada_second]
    )
    if plan.direct:
        (fc2_grad,) = reduce_chunk(plan, *fc2_chunk, ((1, plan.ffb * r),))
        (fc1_grad,) = reduce_chunk(plan, *fc1_chunk, ((plan.ffb, r),))
        qkv_grad, proj_grad, ada_grad, bias_grads = reduce_last(plan, *last_chunk, mods)
        weight_grads = [ada_grad, qkv_grad, proj_grad, fc1_grad, fc2_grad]
        grads = [grad for pair in zip(weight_grads, bias_grads) for grad in pair]
    else:
        grads = reduce_whole(plan, fc2_chunk[0], fc1_chunk[0], last_chunk[0], mods)
    return (
        block_out.reshape(latents.shape),
        latents_grad.reshape(latents.shape),
        cond_grad.reshape(condition.shape),
        *grads,
    )


def solution(mesh):
    tokens = P(None, ("dp", "fsdp"), None, None)
    per_latent = P(None, ("dp", "fsdp"), None)
    weight, bias = P("fsdp", None), P("fsdp")
    in_specs = (tokens, per_latent, tokens, P(None, ("dp", "fsdp"))) + (weight, bias) * 5
    out_specs = (tokens, tokens, per_latent) + (weight, bias) * 5
    body = functools.partial(shards, mesh.shape["fsdp"], mesh.shape["dp"])
    return jax.shard_map(body, mesh=mesh, in_specs=in_specs, out_specs=out_specs, check_vma=False)
```

time: 376 us -> 182 us (0.48)
  waiting for transfers between devices: 166 us -> 35.2 us
  blocking collectives: 90.2 us -> 0 us
  Pallas kernels: 0 us -> 74 us
  starting transfers between devices: 0.62 us -> 56.6 us
  matrix products: 43.5 us -> 0 us
  other arithmetic: 28.1 us -> 4.59 us
  between operations: 21.9 us -> 1.03 us
  local copies, waits for them, and re-layouts: 24.9 us -> 9.7 us
    reduce_scatter x5 -> x0, waiting for transfers between devices: 143 us -> none  [the longest x1 43.1 us: shards(): lax.psum_scatter(full_grads[0].astype(jnp.bfloat16), 'fsdp', scatter_dime...]
    pallas_call x0 -> x20, Pallas kernels: none -> 74 us  [call(): pl.pallas_call(body, out_shape=[jax.ShapeDtypeStruct(shape, kind) for sha...]
    ppermute x0 -> x52, starting transfers between devices: none -> 56.6 us  [swap(): return lax.ppermute(value, axis, [(i, i ^ k) for i in range(size)])]
    unnamed x2 -> x0, blocking collectives: 48.8 us -> none
    dot_general x40 -> x0, matrix products: 43.5 us -> none  [the longest x2 5.95 us: backward_pass(): jnp.dot(grad_mlp_out, fc2_weight.T, preferred_element_type=jnp.float32)]
    ppermute x0 -> x52, waiting for transfers between devices: none -> 35.2 us  [swap(): return lax.ppermute(value, axis, [(i, i ^ k) for i in range(size)])]
    all_gather x2 -> x0, blocking collectives: 20.9 us -> none  [the longest x1 10.9 us: shards(): lax.all_gather(proj_weight, 'fsdp', axis=0, tiled=True)]
    psum x1 -> x0, waiting for transfers between devices: 20.6 us -> none  [shards(): lax.psum(owned_grads[0].astype(jnp.bfloat16), 'dp').astype(jnp.float32)]
  transfers between devices with their start and end apart: 9 -> 52, of which waited for: 6 -> 12; matrix products, arithmetic and copies ran while one was open for 15% -> 4% of each run, Pallas kernels for 0% -> 25%
where the time goes in v1:
time: 182 us; the launch traced here: 181 us
  Pallas kernels  74 us (41%)
  starting transfers between devices  56.6 us (31%)
  waiting for transfers between devices  35.2 us (19%)
  local copies, waits for them, and re-layouts  9.7 us (5%)
  other arithmetic  4.59 us (3%)
    pallas_call x20, Pallas kernels, call(): pl.pallas_call(body, out_shape=[jax.ShapeDtypeStruct(shape, kind) for sha...  74 us
    ppermute x52, starting transfers between devices, swap(): return lax.ppermute(value, axis, [(i, i ^ k) for i in range(size)])  56.6 us
    ppermute x52, waiting for transfers between devices, swap(): return lax.ppermute(value, axis, [(i, i ^ k) for i in range(size)])  35.2 us
    unnamed x111, local copies, waits for them, and re-layouts  8.91 us
  transfers between devices with their start and end apart: 52, of which 12 were waited for; matrix products, arithmetic and copies ran while one was open for 4% of the time, Pallas kernels for 25%

profile of v1, /device:TPU:0, one launch (start us, length us, event | category | flops | bytes accessed | tf_op | source)
XLA Modules:
  0.0 181.1 jit_solution(14238524241331913475)
XLA Ops:
  0.6 3.0 %collective-permute-start.17 = (bf16[192,384]{1,0:T(8,128)(2,1)}, bf16[192,384]{1,0:T(8,128)(2,1)S(1)}, u32[]{:S(2)}, u32[]{:S(2)}) collective-permute-start(bf16[192,384]{1,0:T(8,128)(2,1)} %refs_3_.1), channel_id=1, source_target_pairs={{0,4},{1,5},{2,6},{3,7},{4,0},{5,1},{6,2},{7,3},{8,12},{9,13},{10,... | collective-permute-start | bytes 442376 | tf_op jit(solution)/shard_map/ppermute | solution.py:523
  3.7 1.5 collective-permute-start.15
  5.2 0.7 pad_convert_fusion.4
  7.2 0.7 pad_convert_fusion.1
  8.6 0.7 stack.47.bias
  9.4 2.0 %shard_map.237 = (bf16[256,384]{1,0:T(8,128)(2,1)}, bf16[432,384]{1,0:T(8,128)(2,1)}) custom-call(bf16[48,2304]{1,0:T(8,128)(2,1)} %ada.1, bf16[48,1152]{1,0:T(8,128)(2,1)} %qkv.1, bf16[48,384]{1,0:T(8,128)(2,1)} %proj.1, bf16[48,1536]{1,0:T(8,128)(2,1)} %fc1.1, f32[8,2304]{1,0:T(8,128)} %stack.47.bias), custom_call_target="tpu_custom_call" | custom-call | flops 16777216 | bytes 1048576 | tf_op jit(solution)/shard_map/pallas_call | solution.py:53
  11.4 2.9 %collective-permute-start.5 = (bf16[256,384]{1,0:T(8,128)(2,1)}, bf16[256,384]{1,0:T(8,128)(2,1)S(1)}, u32[]{:S(2)}, u32[]{:S(2)}) collective-permute-start(bf16[256,384]{1,0:T(8,128)(2,1)} %get-tuple-element.80.refs_2_), channel_id=1, source_target_pairs={{0,6},{1,7},{2,4},{3,5},{4,2},{5,3},{6,0},{7,1},{8,14},{9,15},{10,... | collective-permute-start | bytes 589832 | tf_op jit(solution)/shard_map/ppermute | solution.py:523
  14.9 2.9 %collective-permute-start.12 = (bf16[432,384]{1,0:T(8,128)(2,1)}, bf16[432,384]{1,0:T(8,128)(2,1)S(1)}, u32[]{:S(2)}, u32[]{:S(2)}) collective-permute-start(bf16[432,384]{1,0:T(8,128)(2,1)} %get-tuple-element.83.refs_6_), channel_id=1, source_target_pairs={{0,6},{1,7},{2,4},{3,5},{4,2},{5,3},{6,0},{7,1},{8,14},{9,15},{10,... | collective-permute-start | bytes 995336 | tf_op jit(solution)/shard_map/ppermute | solution.py:523
  18.3 1.9 %collective-permute-done.5.refs_8_ = bf16[256,384]{1,0:T(8,128)(2,1)S(1)} collective-permute-done((bf16[256,384]{1,0:T(8,128)(2,1)}, bf16[256,384]{1,0:T(8,128)(2,1)S(1)}, u32[]{:S(2)}, u32[]{:S(2)}) %collective-permute-start.5) | collective-permute-done | bytes 196640 | tf_op jit(solution)/shard_map/ppermute | solution.py:523
  20.2 9.4 %collective-permute-done.3.refs_6_ = bf16[256,384]{1,0:T(8,128)(2,1)S(1)} collective-permute-done((bf16[256,384]{1,0:T(8,128)(2,1)}, bf16[256,384]{1,0:T(8,128)(2,1)S(1)}, u32[]{:S(2)}, u32[]{:S(2)}) %collective-permute-start.3) | collective-permute-done | bytes 196640 | tf_op jit(solution)/shard_map/ppermute | solution.py:523
  30.4 1.0 collective-permute-done.12.refs_12_
  31.4 5.6 %collective-permute-done.10.refs_10_ = bf16[432,384]{1,0:T(8,128)(2,1)S(1)} collective-permute-done((bf16[432,384]{1,0:T(8,128)(2,1)}, bf16[432,384]{1,0:T(8,128)(2,1)S(1)}, u32[]{:S(2)}, u32[]{:S(2)}) %collective-permute-start.10) | collective-permute-done | bytes 331808 | tf_op jit(solution)/shard_map/ppermute | solution.py:523
  37.8 0.7 copy-done.52
  38.7 1.3 copy.28.refs_0_
  41.1 6.4 %shard_map.238 = (bf16[512,1152]{1,0:T(8,128)(2,1)}, bf16[512,384]{1,0:T(8,128)(2,1)}, bf16[512,384]{1,0:T(8,128)(2,1)}, f32[2,768]{1,0:T(2,128)}, f32[16,384]{1...) custom-call(bf16[512,384]{1,0:T(8,128)(2,1)} %bitcast.16, bf16[2,384]{1,0:T(2,128)(2,1)} %bitcast.19, ...), custom_call_target="tpu_custom_call" | custom-call | flops 1073741824 | bytes 16777216 | tf_op jit(solution)/shard_map/pallas_call | solution.py:53
  47.6 0.7 copy-done.47
  48.3 9.8 %shard_map.239 = (bf16[768,384]{1,0:T(8,128)(2,1)}, bf16[768,384]{1,0:T(8,128)(2,1)}, bf16[512,1536]{1,0:T(8,128)(2,1)}, f32[512,1536]{1,0:T(8,128)}, bf16[512,3...) custom-call(s32[2,1]{1,0:T(2,128)} %copy.28.refs_0_, ...), custom_call_target="tpu_custom_call" | custom-call | flops 1073741824 | bytes 16777216 | tf_op jit(solution)/shard_map/pallas_call | solution.py:53
  58.9 7.6 %shard_map.240 = (bf16[768,384]{1,0:T(8,128)(2,1)}, bf16[768,384]{1,0:T(8,128)(2,1)}, bf16[512,1536]{1,0:T(8,128)(2,1)}, bf16[1536,384]{1,0:T(8,128)(2,1)}) custom-call(bf16[512,384]{1,0:T(8,128)(2,1)} %get-tuple-element.85.refs_0_.refs_12_, f32[512,1536]{1,0:T(8,128)} %get-tuple-element.86.refs_1_, bf16[512,384]{1,0:T(8,128)(2,1)} %get-tuple-element.87.refs_2_, ...), custom_call_target="tpu_custom_call" | custom-call | flops 1073741824 | bytes 16777216 | tf_op jit(solution)/shard_map/pallas_call | solution.py:53
  66.5 7.5 %shard_map.241 = (bf16[512,384]{1,0:T(8,128)(2,1)}, bf16[512,384]{1,0:T(8,128)(2,1)}, f32[512,384]{1,0:T(8,128)}, bf16[384,384]{1,0:T(8,128)(2,1)}, f32[16,384]{1,0:T(8,128)}, /*index=5*/f32[2,1536]{1,0:T(2,128)}) custom-call(s32[2,1]{1,0:T(2,128)} %copy.28.refs_0_, bf16[512,384]{1,0:T(8,128)(2,1)} %bitcast.15, bf16[512,1536]{1,0:T(8,128)(2,1)} %get-tuple-element.84.refs_2_, ...), custom_call_target="tpu_custom_call" | custom-call | flops 1073741824 | bytes 16777216 | tf_op jit(solution)/shard_map/pallas_call | solution.py:53
  74.0 12.4 %shard_map.242 = (bf16[832,384]{1,0:T(8,128)(2,1)}, bf16[832,384]{1,0:T(8,128)(2,1)}, bf16[512,384]{1,0:T(8,128)(2,1)}, bf16[16,384]{1,0:T(8,128)(2,1)}) custom-call(bf16[512,384]{1,0:T(8,128)(2,1)} %bitcast.18, bf16[2,384]{1,0:T(2,128)(2,1)} %bitcast.21, bf16[512,1152]{1,0:T(8,128)(2,1)} %get-tuple-element.96.refs_2_, ...), custom_call_target="tpu_custom_call" | custom-call | flops 1073741824 | bytes 16777216 | tf_op jit(solution)/shard_map/pallas_call | solution.py:53
  87.2 2.2 %collective-permute-done.42.refs_1_ = bf16[768,384]{1,0:T(8,128)(2,1)S(1)} collective-permute-done((bf16[768,384]{1,0:T(8,128)(2,1)S(1)}, bf16[768,384]{1,0:T(8,128)(2,1)S(1)}, u32[]{:S(2)}, u32[]{:S(2)}) %collective-permute-start.42) | collective-permute-done | bytes 589856 | tf_op jit(solution)/shard_map/ppermute | solution.py:523
  89.4 0.8 copy-done.2
  90.2 2.1 %shard_map.253 = (f32[192,384]{1,0:T(8,128)}, bf16[192,384]{1,0:T(8,128)(2,1)}, bf16[192,384]{1,0:T(8,128)(2,1)}, bf16[192,384]{1,0:T(8,128)(2,1)}) custom-call(bf16[768,384]{1,0:T(8,128)(2,1)} %get-tuple-element.136.refs_0_, bf16[768,384]{1,0:T(8,128)(2,1)} %copy-done.2), custom_call_target="tpu_custom_call" | custom-call | flops 16777216 | bytes 1048576 | tf_op jit(solution)/shard_map/pallas_call | solution.py:53
  92.3 1.7 collective-permute-start.43
  94.0 1.2 collective-permute-done.22.refs_3_
  96.0 2.2 %shard_map.244 = (f32[240,384]{1,0:T(8,128)}, bf16[240,384]{1,0:T(8,128)(2,1)}, bf16[240,384]{1,0:T(8,128)(2,1)}, bf16[240,384]{1,0:T(8,128)(2,1)}) custom-call(bf16[832,384]{1,0:T(8,128)(2,1)} %get-tuple-element.109.refs_0_, bf16[832,384]{1,0:T(8,128)(2,1)} %copy-done, bf16[16,384]{1,0:T(8,128)(2,1)} %get-tuple-element.106.mods.refs_2_, ...), custom_call_target="tpu_custom_call" | custom-call | flops 16777216 | bytes 1048576 | tf_op jit(solution)/shard_map/pallas_call | solution.py:53
  98.6 1.7 collective-permute-start.44
  100.3 1.4 collective-permute-start.45
  101.7 0.7 collective-permute-start.24
  102.4 1.2 collective-permute-start.25
  103.6 2.1 %shard_map.249 = (f32[192,384]{1,0:T(8,128)}, bf16[192,384]{1,0:T(8,128)(2,1)}, bf16[192,384]{1,0:T(8,128)(2,1)}, bf16[192,384]{1,0:T(8,128)(2,1)}) custom-call(bf16[768,384]{1,0:T(8,128)(2,1)} %get-tuple-element.125.refs_0_, bf16[768,384]{1,0:T(8,128)(2,1)} %copy-done.1), custom_call_target="tpu_custom_call" | custom-call | flops 16777216 | bytes 1048576 | tf_op jit(solution)/shard_map/pallas_call | solution.py:53
  105.7 7.9 %collective-permute-start.33 = (bf16[192,384]{1,0:T(8,128)(2,1)}, bf16[192,384]{1,0:T(8,128)(2,1)S(1)}, u32[]{:S(2)}, u32[]{:S(2)}) collective-permute-start(bf16[192,384]{1,0:T(8,128)(2,1)} %get-tuple-element.128), channel_id=1, source_target_pairs={{0,2},{1,3},{2,0},{3,1},{4,6},{5,7},{6,4},{7,5},{8,10},{9,11},{10,... | collective-permute-start | bytes 442376 | tf_op jit(solution)/shard_map/ppermute | solution.py:523
  113.8 1.5 collective-permute-start.35
  115.3 1.9 %shard_map.254 = (f32[48,384]{1,0:T(8,128)}, bf16[48,384]{1,0:T(8,128)(2,1)}, bf16[48,384]{1,0:T(8,128)(2,1)}, bf16[48,384]{1,0:T(8,128)(2,1)}) custom-call(f32[192,384]{1,0:T(8,128)} %get-tuple-element.138.own, bf16[192,384]{1,0:T(8,128)(2,1)} %copy-done.17, bf16[192,384]{1,0:T(8,128)(2,1)} %copy-done.20, bf16[192,384]{1,0:T(8,128)(2,1)} %copy-done.21), custom_call_target="tpu_custom_call" | custom-call | flops 16777216 | bytes 1048576 | tf_op jit(solution)/shard_map/pallas_call | solution.py:53
  117.7 1.7 collective-permute-start.46
  119.4 0.7 copy-done.8
  120.0 2.2 %shard_map.245 = (f32[192,384]{1,0:T(8,128)}, bf16[192,384]{1,0:T(8,128)(2,1)}, bf16[192,384]{1,0:T(8,128)(2,1)}, bf16[192,384]{1,0:T(8,128)(2,1)}) custom-call(f32[240,384]{1,0:T(8,128)} %get-tuple-element.111.own, bf16[240,384]{1,0:T(8,128)(2,1)} %copy-done.6, bf16[240,384]{1,0:T(8,128)(2,1)} %copy-done.7, bf16[240,384]{1,0:T(8,128)(2,1)} %copy-done.8), custom_call_target="tpu_custom_call" | custom-call | flops 16777216 | bytes 1048576 | tf_op jit(solution)/shard_map/pallas_call | solution.py:53
  122.6 2.7 %collective-permute-start.27 = (bf16[192,384]{1,0:T(8,128)(2,1)}, bf16[192,384]{1,0:T(8,128)(2,1)S(1)}, u32[]{:S(2)}, u32[]{:S(2)}) collective-permute-start(bf16[192,384]{1,0:T(8,128)(2,1)} %get-tuple-element.117), channel_id=1, source_target_pairs={{0,16},{8,24},{16,0},{24,8},{1,17},{9,25},{17,1},{25,9},{2,18},{10... | collective-permute-start | bytes 442376 | tf_op jit(solution)/shard_map/ppermute | solution.py:523
  125.3 1.3 collective-permute-start.28
  126.6 1.7 collective-permute-start.47
  128.4 1.0 collective-permute-start.48
  129.3 1.9 %shard_map.250 = (f32[48,384]{1,0:T(8,128)}, bf16[48,384]{1,0:T(8,128)(2,1)}, bf16[48,384]{1,0:T(8,128)(2,1)}, bf16[48,384]{1,0:T(8,128)(2,1)}) custom-call(f32[192,384]{1,0:T(8,128)} %get-tuple-element.127.own, bf16[192,384]{1,0:T(8,128)(2,1)} %copy-done.16, bf16[192,384]{1,0:T(8,128)(2,1)} %copy-done.18, bf16[192,384]{1,0:T(8,128)(2,1)} %copy-done.19), custom_call_target="tpu_custom_call" | custom-call | flops 16777216 | bytes 1048576 | tf_op jit(solution)/shard_map/pallas_call | solution.py:53
  131.2 9.5 %collective-permute-done.47.refs_2_ = bf16[48,384]{1,0:T(8,128)(2,1)S(1)} collective-permute-done((bf16[48,384]{1,0:T(8,128)(2,1)}, bf16[48,384]{1,0:T(8,128)(2,1)S(1)}, u32[]{:S(2)}, u32[]{:S(2)}) %collective-permute-start.47) | collective-permute-done | bytes 36896 | tf_op jit(solution)/shard_map/ppermute | solution.py:523
  140.7 3.2 %collective-permute-start.37 = (bf16[48,384]{1,0:T(8,128)(2,1)}, bf16[48,384]{1,0:T(8,128)(2,1)S(1)}, u32[]{:S(2)}, u32[]{:S(2)}) collective-permute-start(bf16[48,384]{1,0:T(8,128)(2,1)} %get-tuple-element.133), channel_id=1, source_target_pairs={{0,16},{8,24},{16,0},{24,8},{1,17},{9,25},{17,1},{25,9},{2,18},{10... | collective-permute-start | bytes 110600 | tf_op jit(solution)/shard_map/ppermute | solution.py:523
  144.0 0.9 collective-permute-done.36.refs_1_
  144.9 2.7 %collective-permute-start.38 = (bf16[48,384]{1,0:T(8,128)(2,1)}, bf16[48,384]{1,0:T(8,128)(2,1)S(1)}, u32[]{:S(2)}, u32[]{:S(2)}) collective-permute-start(bf16[48,384]{1,0:T(8,128)(2,1)} %get-tuple-element.134), channel_id=1, source_target_pairs={{0,24},{8,16},{16,8},{24,0},{1,25},{9,17},{17,9},{25,1},{2,26},{10... | collective-permute-start | bytes 110600 | tf_op jit(solution)/shard_map/ppermute | solution.py:523
  147.6 1.5 shard_map.255.refs_0_
  149.1 1.1 collective-permute-start.51
  150.3 1.1 collective-permute-done.38.refs_3_
  152.0 1.5 shard_map.251.refs_0_
  153.5 1.6 collective-permute-done.51.refs_3_
  155.1 0.7 collective-permute-start.49
  155.8 1.5 collective-permute-start.41
  157.3 1.3 collective-permute-start.40
  158.6 1.6 collective-permute-start.39
  160.2 1.8 shard_map.247.refs_0_
  162.0 1.5 collective-permute-start.31
  164.1 2.3 %collective-permute-start.29 = (bf16[48,384]{1,0:T(8,128)(2,1)}, bf16[48,384]{1,0:T(8,128)(2,1)S(1)}, u32[]{:S(2)}, u32[]{:S(2)}) collective-permute-start(bf16[48,384]{1,0:T(8,128)(2,1)} %shard_map.247.refs_0_), channel_id=1, source_target_pairs={{0,8},{8,0},{16,24},{24,16},{1,9},{9,1},{17,25},{25,17},{2,10},{10... | collective-permute-start | bytes 110600 | tf_op jit(solution)/shard_map/ppermute | solution.py:523
  166.4 3.2 %shard_map.243 = bf16[2,384]{1,0:T(2,128)(2,1)} custom-call(bf16[2,384]{1,0:T(2,128)(2,1)} %bitcast.22, bf16[16,384]{1,0:T(8,128)(2,1)} %get-tuple-element.106.mods.refs_2_, bf16[384,768]{1,0:T(8,128)(2,1)} %get-tuple-element.107.first, bf16[384,1536]{1,0:T(8,128)(2,1)} %get-tuple-element.108.second), custom_call_target="tpu_custom_call" | custom-call | flops 16777216 | bytes 1048576 | tf_op jit(solution)/shard_map/pallas_call | solution.py:53
  169.6 1.6 shard_map.256
  172.4 1.6 shard_map.252
  174.0 3.1 %shard_map.246 = (f32[48,2304]{1,0:T(8,128)}, f32[1,288]{1,0:T(1,128)}, f32[1,96]{1,0:T(1,128)}, f32[1,48]{1,0:T(1,128)}, f32[1,192]{1,0:T(1,128)}, /*index=5*/f32[1,48]{1,0:T(1,128)}) custom-call(f32[192,384]{1,0:T(8,128)} %get-tuple-element.115.refs_0_, bf16[192,384]{1,0:T(8,128)(2,1)} %copy-done.3, bf16[192,384]{1,0:T(8,128)(2,1)} %copy-done.4, ...), custom_call_target="tpu_custom_call" | custom-call | flops 16777216 | bytes 1048576 | tf_op jit(solution)/shard_map/pallas_call | solution.py:53
  177.0 1.3 reduce
  179.6 1.6 shard_map.248
  (185 shorter events, 13.7 us)
Async XLA Ops:
  0.6 14.1 %collective-permute-start.17 = (bf16[192,384]{1,0:T(8,128)(2,1)}, bf16[192,384]{1,0:T(8,128)(2,1)S(1)}, u32[]{:S(2)}, u32[]{:S(2)}) collective-permute-start(bf16[192,384]{1,0:T(8,128)(2,1)} %refs_3_.1), channel_id=1, source_target_pairs={{0,4},{1,5},{2,6},{3,7},{4,0},{5,1},{6,2},{7,3},{8,12},{9,13},{10,... | collective-permute-start | bytes 442376 | tf_op jit(solution)/shard_map/ppermute | solution.py:523
  3.7 11.2 %collective-permute-start.15 = (bf16[192,384]{1,0:T(8,128)(2,1)}, bf16[192,384]{1,0:T(8,128)(2,1)S(1)}, u32[]{:S(2)}, u32[]{:S(2)}) collective-permute-start(bf16[192,384]{1,0:T(8,128)(2,1)} %refs_3_.1), channel_id=1, source_target_pairs={{0,2},{1,3},{2,0},{3,1},{4,6},{5,7},{6,4},{7,5},{8,10},{9,11},{10,... | collective-permute-start | bytes 442376 | tf_op jit(solution)/shard_map/ppermute | solution.py:523
  5.2 12.6 %collective-permute-start.19 = (bf16[192,384]{1,0:T(8,128)(2,1)}, bf16[192,384]{1,0:T(8,128)(2,1)S(1)}, u32[]{:S(2)}, u32[]{:S(2)}) collective-permute-start(bf16[192,384]{1,0:T(8,128)(2,1)} %refs_3_.1), channel_id=1, source_target_pairs={{0,6},{1,7},{2,4},{3,5},{4,2},{5,3},{6,0},{7,1},{8,14},{9,15},{10,... | collective-permute-start | bytes 442376 | tf_op jit(solution)/shard_map/ppermute | solution.py:523
  11.4 8.8 %collective-permute-start.5 = (bf16[256,384]{1,0:T(8,128)(2,1)}, bf16[256,384]{1,0:T(8,128)(2,1)S(1)}, u32[]{:S(2)}, u32[]{:S(2)}) collective-permute-start(bf16[256,384]{1,0:T(8,128)(2,1)} %get-tuple-element.80.refs_2_), channel_id=1, source_target_pairs={{0,6},{1,7},{2,4},{3,5},{4,2},{5,3},{6,0},{7,1},{8,14},{9,15},{10,... | collective-permute-start | bytes 589832 | tf_op jit(solution)/shard_map/ppermute | solution.py:523
  14.3 15.3 %collective-permute-start.3 = (bf16[256,384]{1,0:T(8,128)(2,1)}, bf16[256,384]{1,0:T(8,128)(2,1)S(1)}, u32[]{:S(2)}, u32[]{:S(2)}) collective-permute-start(bf16[256,384]{1,0:T(8,128)(2,1)} %get-tuple-element.80.refs_2_), channel_id=1, source_target_pairs={{0,4},{1,5},{2,6},{3,7},{4,0},{5,1},{6,2},{7,3},{8,12},{9,13},{10,... | collective-permute-start | bytes 589832 | tf_op jit(solution)/shard_map/ppermute | solution.py:523
  14.8 32.7 %copy-start.9 = (bf16[192,384]{1,0:T(8,128)(2,1)}, bf16[192,384]{1,0:T(8,128)(2,1)S(1)}, u32[]{:S(2)}) copy-start(bf16[192,384]{1,0:T(8,128)(2,1)S(1)} %collective-permute-done.17.refs_7_) | copy-start | bytes 442372
  14.8 15.1 %collective-permute-start.1 = (bf16[256,384]{1,0:T(8,128)(2,1)}, bf16[256,384]{1,0:T(8,128)(2,1)S(1)}, u32[]{:S(2)}, u32[]{:S(2)}) collective-permute-start(bf16[256,384]{1,0:T(8,128)(2,1)} %get-tuple-element.80.refs_2_), channel_id=1, source_target_pairs={{0,2},{1,3},{2,0},{3,1},{4,6},{5,7},{6,4},{7,5},{8,10},{9,11},{10,... | collective-permute-start | bytes 589832 | tf_op jit(solution)/shard_map/ppermute | solution.py:523
  14.9 32.6 %copy-start.10 = (bf16[192,384]{1,0:T(8,128)(2,1)}, bf16[192,384]{1,0:T(8,128)(2,1)S(1)}, u32[]{:S(2)}) copy-start(bf16[192,384]{1,0:T(8,128)(2,1)S(1)} %collective-permute-done.15.refs_5_) | copy-start | bytes 442372
  14.9 16.5 %collective-permute-start.12 = (bf16[432,384]{1,0:T(8,128)(2,1)}, bf16[432,384]{1,0:T(8,128)(2,1)S(1)}, u32[]{:S(2)}, u32[]{:S(2)}) collective-permute-start(bf16[432,384]{1,0:T(8,128)(2,1)} %get-tuple-element.83.refs_6_), channel_id=1, source_target_pairs={{0,6},{1,7},{2,4},{3,5},{4,2},{5,3},{6,0},{7,1},{8,14},{9,15},{10,... | collective-permute-start | bytes 995336 | tf_op jit(solution)/shard_map/ppermute | solution.py:523
  17.8 29.7 %copy-start.11 = (bf16[192,384]{1,0:T(8,128)(2,1)}, bf16[192,384]{1,0:T(8,128)(2,1)S(1)}, u32[]{:S(2)}) copy-start(bf16[192,384]{1,0:T(8,128)(2,1)S(1)} %collective-permute-done.19.refs_9_) | copy-start | bytes 442372
  17.8 19.2 %collective-permute-start.10 = (bf16[432,384]{1,0:T(8,128)(2,1)}, bf16[432,384]{1,0:T(8,128)(2,1)S(1)}, u32[]{:S(2)}, u32[]{:S(2)}) collective-permute-start(bf16[432,384]{1,0:T(8,128)(2,1)} %get-tuple-element.83.refs_6_), channel_id=1, source_target_pairs={{0,4},{1,5},{2,6},{3,7},{4,0},{5,1},{6,2},{7,3},{8,12},{9,13},{10,... | collective-permute-start | bytes 995336 | tf_op jit(solution)/shard_map/ppermute | solution.py:523
  20.2 20.9 %copy-start.48 = (bf16[256,384]{1,0:T(8,128)(2,1)}, bf16[256,384]{1,0:T(8,128)(2,1)S(1)}, u32[]{:S(2)}) copy-start(bf16[256,384]{1,0:T(8,128)(2,1)S(1)} %collective-permute-done.5.refs_8_) | copy-start | bytes 589828
  20.2 9.7 %collective-permute-start = (bf16[256,384]{1,0:T(8,128)(2,1)}, bf16[256,384]{1,0:T(8,128)(2,1)S(1)}, u32[]{:S(2)}, u32[]{:S(2)}) collective-permute-start(bf16[256,384]{1,0:T(8,128)(2,1)} %get-tuple-element.80.refs_2_), channel_id=1, source_target_pairs={{0,1},{1,0},{2,3},{3,2},{4,5},{5,4},{6,7},{7,6},{8,9},{9,8},{10,11... | collective-permute-start | bytes 589832 | tf_op jit(solution)/shard_map/ppermute | solution.py:523
  29.6 11.5 %copy-start.49 = (bf16[256,384]{1,0:T(8,128)(2,1)}, bf16[256,384]{1,0:T(8,128)(2,1)S(1)}, u32[]{:S(2)}) copy-start(bf16[256,384]{1,0:T(8,128)(2,1)S(1)} %collective-permute-done.3.refs_6_) | copy-start | bytes 589828
  29.6 7.6 %collective-permute-start.8 = (bf16[432,384]{1,0:T(8,128)(2,1)}, bf16[432,384]{1,0:T(8,128)(2,1)S(1)}, u32[]{:S(2)}, u32[]{:S(2)}) collective-permute-start(bf16[432,384]{1,0:T(8,128)(2,1)} %get-tuple-element.83.refs_6_), channel_id=1, source_target_pairs={{0,2},{1,3},{2,0},{3,1},{4,6},{5,7},{6,4},{7,5},{8,10},{9,11},{10,... | collective-permute-start | bytes 995336 | tf_op jit(solution)/shard_map/ppermute | solution.py:523
  29.9 11.2 %copy-start.50 = (bf16[256,384]{1,0:T(8,128)(2,1)}, bf16[256,384]{1,0:T(8,128)(2,1)S(1)}, u32[]{:S(2)}) copy-start(bf16[256,384]{1,0:T(8,128)(2,1)S(1)} %collective-permute-done.1.refs_4_) | copy-start | bytes 589828
  29.9 7.6 %collective-permute-start.7 = (bf16[432,384]{1,0:T(8,128)(2,1)}, bf16[432,384]{1,0:T(8,128)(2,1)S(1)}, u32[]{:S(2)}, u32[]{:S(2)}) collective-permute-start(bf16[432,384]{1,0:T(8,128)(2,1)} %get-tuple-element.83.refs_6_), channel_id=1, source_target_pairs={{0,1},{1,0},{2,3},{3,2},{4,5},{5,4},{6,7},{7,6},{8,9},{9,8},{10,11... | collective-permute-start | bytes 995336 | tf_op jit(solution)/shard_map/ppermute | solution.py:523
  29.9 7.9 %collective-permute-start.6 = (bf16[256,384]{1,0:T(8,128)(2,1)S(1)}, bf16[256,384]{1,0:T(8,128)(2,1)S(1)}, u32[]{:S(2)}, u32[]{:S(2)}) collective-permute-start(bf16[256,384]{1,0:T(8,128)(2,1)S(1)} %collective-permute-done.5.refs_8_), channel_id=1, source_target_pairs={{0,1},{1,0},{2,3},{3,2},{4,5},{5,4},{6,7},{7,6},{8,9},{9,8},{10,11... | collective-permute-start | bytes 589832 | tf_op jit(solution)/shard_map/ppermute | solution.py:523
  31.4 16.1 %copy-start.41 = (bf16[432,384]{1,0:T(8,128)(2,1)}, bf16[432,384]{1,0:T(8,128)(2,1)S(1)}, u32[]{:S(2)}) copy-start(bf16[432,384]{1,0:T(8,128)(2,1)S(1)} %collective-permute-done.12.refs_12_) | copy-start | bytes 995332
  31.4 9.2 %collective-permute-start.13 = (bf16[432,384]{1,0:T(8,128)(2,1)S(1)}, bf16[432,384]{1,0:T(8,128)(2,1)S(1)}, u32[]{:S(2)}, u32[]{:S(2)}) collective-permute-start(bf16[432,384]{1,0:T(8,128)(2,1)S(1)} %collective-permute-done.12.refs_12_), channel_id=1, source_target_pairs={{0,1},{1,0},{2,3},{3,2},{4,5},{5,4},{6,7},{7,6},{8,9},{9,8},{10,11... | collective-permute-start | bytes 995336 | tf_op jit(solution)/shard_map/ppermute | solution.py:523
  37.0 3.8 %collective-permute-start.11 = (bf16[432,384]{1,0:T(8,128)(2,1)S(1)}, bf16[432,384]{1,0:T(8,128)(2,1)S(1)}, u32[]{:S(2)}, u32[]{:S(2)}) collective-permute-start(bf16[432,384]{1,0:T(8,128)(2,1)S(1)} %collective-permute-done.10.refs_10_), channel_id=1, source_target_pairs={{0,1},{1,0},{2,3},{3,2},{4,5},{5,4},{6,7},{7,6},{8,9},{9,8},{10,11... | collective-permute-start | bytes 995336 | tf_op jit(solution)/shard_map/ppermute | solution.py:523
  37.3 10.3 %collective-permute-start.9 = (bf16[432,384]{1,0:T(8,128)(2,1)S(1)}, bf16[432,384]{1,0:T(8,128)(2,1)S(1)}, u32[]{:S(2)}, u32[]{:S(2)}) collective-permute-start(bf16[432,384]{1,0:T(8,128)(2,1)S(1)} %collective-permute-done.8.refs_8_), channel_id=1, source_target_pairs={{0,1},{1,0},{2,3},{3,2},{4,5},{5,4},{6,7},{7,6},{8,9},{9,8},{10,11... | collective-permute-start | bytes 995336 | tf_op jit(solution)/shard_map/ppermute | solution.py:523
  37.5 2.5 %collective-permute-start.4 = (bf16[256,384]{1,0:T(8,128)(2,1)S(1)}, bf16[256,384]{1,0:T(8,128)(2,1)}, u32[]{:S(2)}, u32[]{:S(2)}) collective-permute-start(bf16[256,384]{1,0:T(8,128)(2,1)S(1)} %collective-permute-done.3.refs_6_), channel_id=1, source_target_pairs={{0,1},{1,0},{2,3},{3,2},{4,5},{5,4},{6,7},{7,6},{8,9},{9,8},{10,11... | collective-permute-start | bytes 589832 | tf_op jit(solution)/shard_map/ppermute | solution.py:523
  38.5 1.8 %collective-permute-start.2 = (bf16[256,384]{1,0:T(8,128)(2,1)S(1)}, bf16[256,384]{1,0:T(8,128)(2,1)}, u32[]{:S(2)}, u32[]{:S(2)}) collective-permute-start(bf16[256,384]{1,0:T(8,128)(2,1)S(1)} %collective-permute-done.1.refs_4_), channel_id=1, source_target_pairs={{0,1},{1,0},{2,3},{3,2},{4,5},{5,4},{6,7},{7,6},{8,9},{9,8},{10,11... | collective-permute-start | bytes 589832 | tf_op jit(solution)/shard_map/ppermute | solution.py:523
  40.0 18.1 %collective-permute-start.14 = (bf16[192,384]{1,0:T(8,128)(2,1)}, bf16[192,384]{1,0:T(8,128)(2,1)S(1)}, u32[]{:S(2)}, u32[]{:S(2)}) collective-permute-start(bf16[192,384]{1,0:T(8,128)(2,1)} %refs_3_.1), channel_id=1, source_target_pairs={{0,1},{1,0},{2,3},{3,2},{4,5},{5,4},{6,7},{7,6},{8,9},{9,8},{10,11... | collective-permute-start | bytes 442376 | tf_op jit(solution)/shard_map/ppermute | solution.py:523
  40.3 17.9 %collective-permute-start.18 = (bf16[192,384]{1,0:T(8,128)(2,1)S(1)}, bf16[192,384]{1,0:T(8,128)(2,1)S(1)}, u32[]{:S(2)}, u32[]{:S(2)}) collective-permute-start(bf16[192,384]{1,0:T(8,128)(2,1)S(1)} %collective-permute-done.17.refs_7_), channel_id=1, source_target_pairs={{0,1},{1,0},{2,3},{3,2},{4,5},{5,4},{6,7},{7,6},{8,9},{9,8},{10,11... | collective-permute-start | bytes 442376 | tf_op jit(solution)/shard_map/ppermute | solution.py:523
  40.6 17.6 %collective-permute-start.16 = (bf16[192,384]{1,0:T(8,128)(2,1)S(1)}, bf16[192,384]{1,0:T(8,128)(2,1)S(1)}, u32[]{:S(2)}, u32[]{:S(2)}) collective-permute-start(bf16[192,384]{1,0:T(8,128)(2,1)S(1)} %collective-permute-done.15.refs_5_), channel_id=1, source_target_pairs={{0,1},{1,0},{2,3},{3,2},{4,5},{5,4},{6,7},{7,6},{8,9},{9,8},{10,11... | collective-permute-start | bytes 442376 | tf_op jit(solution)/shard_map/ppermute | solution.py:523
  40.8 17.4 %collective-permute-start.20 = (bf16[192,384]{1,0:T(8,128)(2,1)S(1)}, bf16[192,384]{1,0:T(8,128)(2,1)S(1)}, u32[]{:S(2)}, u32[]{:S(2)}) collective-permute-start(bf16[192,384]{1,0:T(8,128)(2,1)S(1)} %collective-permute-done.19.refs_9_), channel_id=1, source_target_pairs={{0,1},{1,0},{2,3},{3,2},{4,5},{5,4},{6,7},{7,6},{8,9},{9,8},{10,11... | collective-permute-start | bytes 442376 | tf_op jit(solution)/shard_map/ppermute | solution.py:523
  74.0 12.7 %copy-start.40 = (bf16[768,384]{1,0:T(8,128)(2,1)S(1)}, bf16[768,384]{1,0:T(8,128)(2,1)}, u32[]{:S(2)}) copy-start(bf16[768,384]{1,0:T(8,128)(2,1)} %get-tuple-element.137) | copy-start | bytes 1769476
  74.0 13.0 %copy-start.39 = (bf16[768,384]{1,0:T(8,128)(2,1)S(1)}, bf16[768,384]{1,0:T(8,128)(2,1)}, u32[]{:S(2)}) copy-start(bf16[768,384]{1,0:T(8,128)(2,1)} %get-tuple-element.126) | copy-start | bytes 1769476
  86.4 8.8 %collective-permute-start.21 = (bf16[832,384]{1,0:T(8,128)(2,1)}, bf16[832,384]{1,0:T(8,128)(2,1)S(1)}, u32[]{:S(2)}, u32[]{:S(2)}) collective-permute-start(bf16[832,384]{1,0:T(8,128)(2,1)} %get-tuple-element.110), channel_id=1, source_target_pairs={{0,1},{1,0},{2,3},{3,2},{4,5},{5,4},{6,7},{7,6},{8,9},{9,8},{10,11... | collective-permute-start | bytes 1916936 | tf_op jit(solution)/shard_map/ppermute | solution.py:523
  86.7 2.7 %collective-permute-start.42 = (bf16[768,384]{1,0:T(8,128)(2,1)S(1)}, bf16[768,384]{1,0:T(8,128)(2,1)S(1)}, u32[]{:S(2)}, u32[]{:S(2)}) collective-permute-start(bf16[768,384]{1,0:T(8,128)(2,1)S(1)} %copy-done.40), channel_id=1, source_target_pairs={{0,1},{1,0},{2,3},{3,2},{4,5},{5,4},{6,7},{7,6},{8,9},{9,8},{10,11... | collective-permute-start | bytes 1769480 | tf_op jit(solution)/shard_map/ppermute | solution.py:523
  87.0 14.7 %collective-permute-start.32 = (bf16[768,384]{1,0:T(8,128)(2,1)S(1)}, bf16[768,384]{1,0:T(8,128)(2,1)S(1)}, u32[]{:S(2)}, u32[]{:S(2)}) collective-permute-start(bf16[768,384]{1,0:T(8,128)(2,1)S(1)} %copy-done.39), channel_id=1, source_target_pairs={{0,1},{1,0},{2,3},{3,2},{4,5},{5,4},{6,7},{7,6},{8,9},{9,8},{10,11... | collective-permute-start | bytes 1769480 | tf_op jit(solution)/shard_map/ppermute | solution.py:523
  92.3 10.1 %collective-permute-start.43 = (bf16[192,384]{1,0:T(8,128)(2,1)}, bf16[192,384]{1,0:T(8,128)(2,1)S(1)}, u32[]{:S(2)}, u32[]{:S(2)}) collective-permute-start(bf16[192,384]{1,0:T(8,128)(2,1)} %get-tuple-element.139), channel_id=1, source_target_pairs={{0,2},{1,3},{2,0},{3,1},{4,6},{5,7},{6,4},{7,5},{8,10},{9,11},{10,... | collective-permute-start | bytes 442376 | tf_op jit(solution)/shard_map/ppermute | solution.py:523
  94.0 1.2 collective-permute-start.22
  98.2 15.6 %collective-permute-start.23 = (bf16[240,384]{1,0:T(8,128)(2,1)}, bf16[240,384]{1,0:T(8,128)(2,1)S(1)}, u32[]{:S(2)}, u32[]{:S(2)}) collective-permute-start(bf16[240,384]{1,0:T(8,128)(2,1)} %get-tuple-element.112), channel_id=1, source_target_pairs={{0,2},{1,3},{2,0},{3,1},{4,6},{5,7},{6,4},{7,5},{8,10},{9,11},{10,... | collective-permute-start | bytes 552968 | tf_op jit(solution)/shard_map/ppermute | solution.py:523
  98.6 7.1 %collective-permute-start.44 = (bf16[192,384]{1,0:T(8,128)(2,1)S(1)}, bf16[192,384]{1,0:T(8,128)(2,1)S(1)}, u32[]{:S(2)}, u32[]{:S(2)}) collective-permute-start(bf16[192,384]{1,0:T(8,128)(2,1)S(1)} %copy-done.54), channel_id=1, source_target_pairs={{0,4},{1,5},{2,6},{3,7},{4,0},{5,1},{6,2},{7,3},{8,12},{9,13},{10,... | collective-permute-start | bytes 442376 | tf_op jit(solution)/shard_map/ppermute | solution.py:523
  100.3 13.3 %collective-permute-start.45 = (bf16[192,384]{1,0:T(8,128)(2,1)S(1)}, bf16[192,384]{1,0:T(8,128)(2,1)S(1)}, u32[]{:S(2)}, u32[]{:S(2)}) collective-permute-start(bf16[192,384]{1,0:T(8,128)(2,1)S(1)} %copy-done.53), channel_id=1, source_target_pairs={{0,6},{1,7},{2,4},{3,5},{4,2},{5,3},{6,0},{7,1},{8,14},{9,15},{10,... | collective-permute-start | bytes 442376 | tf_op jit(solution)/shard_map/ppermute | solution.py:523
  101.7 16.0 %collective-permute-start.24 = (bf16[240,384]{1,0:T(8,128)(2,1)}, bf16[240,384]{1,0:T(8,128)(2,1)S(1)}, u32[]{:S(2)}, u32[]{:S(2)}) collective-permute-start(bf16[240,384]{1,0:T(8,128)(2,1)} %get-tuple-element.113), channel_id=1, source_target_pairs={{0,4},{1,5},{2,6},{3,7},{4,0},{5,1},{6,2},{7,3},{8,12},{9,13},{10,... | collective-permute-start | bytes 552968 | tf_op jit(solution)/shard_map/ppermute | solution.py:523
  102.4 12.9 %copy-start.17 = (bf16[192,384]{1,0:T(8,128)(2,1)}, bf16[192,384]{1,0:T(8,128)(2,1)S(1)}, u32[]{:S(2)}) copy-start(bf16[192,384]{1,0:T(8,128)(2,1)S(1)} %collective-permute-done.43.refs_0_) | copy-start | bytes 442372
  102.4 16.9 %collective-permute-start.25 = (bf16[240,384]{1,0:T(8,128)(2,1)}, bf16[240,384]{1,0:T(8,128)(2,1)S(1)}, u32[]{:S(2)}, u32[]{:S(2)}) collective-permute-start(bf16[240,384]{1,0:T(8,128)(2,1)} %get-tuple-element.114), channel_id=1, source_target_pairs={{0,6},{1,7},{2,4},{3,5},{4,2},{5,3},{6,0},{7,1},{8,14},{9,15},{10,... | collective-permute-start | bytes 552968 | tf_op jit(solution)/shard_map/ppermute | solution.py:523
  105.7 16.9 %collective-permute-start.33 = (bf16[192,384]{1,0:T(8,128)(2,1)}, bf16[192,384]{1,0:T(8,128)(2,1)S(1)}, u32[]{:S(2)}, u32[]{:S(2)}) collective-permute-start(bf16[192,384]{1,0:T(8,128)(2,1)} %get-tuple-element.128), channel_id=1, source_target_pairs={{0,2},{1,3},{2,0},{3,1},{4,6},{5,7},{6,4},{7,5},{8,10},{9,11},{10,... | collective-permute-start | bytes 442376 | tf_op jit(solution)/shard_map/ppermute | solution.py:523
  113.6 11.7 %collective-permute-start.34 = (bf16[192,384]{1,0:T(8,128)(2,1)}, bf16[192,384]{1,0:T(8,128)(2,1)S(1)}, u32[]{:S(2)}, u32[]{:S(2)}) collective-permute-start(bf16[192,384]{1,0:T(8,128)(2,1)} %get-tuple-element.129), channel_id=1, source_target_pairs={{0,4},{1,5},{2,6},{3,7},{4,0},{5,1},{6,2},{7,3},{8,12},{9,13},{10,... | collective-permute-start | bytes 442376 | tf_op jit(solution)/shard_map/ppermute | solution.py:523
  113.8 12.8 %collective-permute-start.35 = (bf16[192,384]{1,0:T(8,128)(2,1)}, bf16[192,384]{1,0:T(8,128)(2,1)S(1)}, u32[]{:S(2)}, u32[]{:S(2)}) collective-permute-start(bf16[192,384]{1,0:T(8,128)(2,1)} %get-tuple-element.130), channel_id=1, source_target_pairs={{0,6},{1,7},{2,4},{3,5},{4,2},{5,3},{6,0},{7,1},{8,14},{9,15},{10,... | collective-permute-start | bytes 442376 | tf_op jit(solution)/shard_map/ppermute | solution.py:523
  117.7 10.6 %collective-permute-start.46 = (bf16[48,384]{1,0:T(8,128)(2,1)}, bf16[48,384]{1,0:T(8,128)(2,1)S(1)}, u32[]{:S(2)}, u32[]{:S(2)}) collective-permute-start(bf16[48,384]{1,0:T(8,128)(2,1)} %get-tuple-element.143), channel_id=1, source_target_pairs={{0,8},{8,0},{16,24},{24,16},{1,9},{9,1},{17,25},{25,17},{2,10},{10... | collective-permute-start | bytes 110600 | tf_op jit(solution)/shard_map/ppermute | solution.py:523
  122.2 33.5 %collective-permute-start.26 = (bf16[192,384]{1,0:T(8,128)(2,1)}, bf16[192,384]{1,0:T(8,128)(2,1)S(1)}, u32[]{:S(2)}, u32[]{:S(2)}) collective-permute-start(bf16[192,384]{1,0:T(8,128)(2,1)} %get-tuple-element.116), channel_id=1, source_target_pairs={{0,8},{8,0},{16,24},{24,16},{1,9},{9,1},{17,25},{25,17},{2,10},{10... | collective-permute-start | bytes 442376 | tf_op jit(solution)/shard_map/ppermute | solution.py:523
  122.6 34.7 %collective-permute-start.27 = (bf16[192,384]{1,0:T(8,128)(2,1)}, bf16[192,384]{1,0:T(8,128)(2,1)S(1)}, u32[]{:S(2)}, u32[]{:S(2)}) collective-permute-start(bf16[192,384]{1,0:T(8,128)(2,1)} %get-tuple-element.117), channel_id=1, source_target_pairs={{0,16},{8,24},{16,0},{24,8},{1,17},{9,25},{17,1},{25,9},{2,18},{10... | collective-permute-start | bytes 442376 | tf_op jit(solution)/shard_map/ppermute | solution.py:523
  125.3 33.3 %collective-permute-start.28 = (bf16[192,384]{1,0:T(8,128)(2,1)}, bf16[192,384]{1,0:T(8,128)(2,1)S(1)}, u32[]{:S(2)}, u32[]{:S(2)}) collective-permute-start(bf16[192,384]{1,0:T(8,128)(2,1)} %get-tuple-element.118), channel_id=1, source_target_pairs={{0,24},{8,16},{16,8},{24,0},{1,25},{9,17},{17,9},{25,1},{2,26},{10... | collective-permute-start | bytes 442376 | tf_op jit(solution)/shard_map/ppermute | solution.py:523
  126.6 14.1 %collective-permute-start.47 = (bf16[48,384]{1,0:T(8,128)(2,1)}, bf16[48,384]{1,0:T(8,128)(2,1)S(1)}, u32[]{:S(2)}, u32[]{:S(2)}) collective-permute-start(bf16[48,384]{1,0:T(8,128)(2,1)} %get-tuple-element.144), channel_id=1, source_target_pairs={{0,16},{8,24},{16,0},{24,8},{1,17},{9,25},{17,1},{25,9},{2,18},{10... | collective-permute-start | bytes 110600 | tf_op jit(solution)/shard_map/ppermute | solution.py:523
  128.3 19.2 %copy-start.29 = (bf16[48,384]{1,0:T(8,128)(2,1)}, bf16[48,384]{1,0:T(8,128)(2,1)S(1)}, u32[]{:S(2)}) copy-start(bf16[48,384]{1,0:T(8,128)(2,1)S(1)} %collective-permute-done.46.refs_1_) | copy-start | bytes 110596
  128.4 12.4 %collective-permute-start.48 = (bf16[48,384]{1,0:T(8,128)(2,1)}, bf16[48,384]{1,0:T(8,128)(2,1)S(1)}, u32[]{:S(2)}, u32[]{:S(2)}) collective-permute-start(bf16[48,384]{1,0:T(8,128)(2,1)} %get-tuple-element.145), channel_id=1, source_target_pairs={{0,24},{8,16},{16,8},{24,0},{1,25},{9,17},{17,9},{25,1},{2,26},{10... | collective-permute-start | bytes 110600 | tf_op jit(solution)/shard_map/ppermute | solution.py:523
  140.7 4.2 %collective-permute-start.36 = (bf16[48,384]{1,0:T(8,128)(2,1)}, bf16[48,384]{1,0:T(8,128)(2,1)S(1)}, u32[]{:S(2)}, u32[]{:S(2)}) collective-permute-start(bf16[48,384]{1,0:T(8,128)(2,1)} %get-tuple-element.132), channel_id=1, source_target_pairs={{0,8},{8,0},{16,24},{24,16},{1,9},{9,1},{17,25},{25,17},{2,10},{10... | collective-permute-start | bytes 110600 | tf_op jit(solution)/shard_map/ppermute | solution.py:523
  140.7 8.4 %collective-permute-start.37 = (bf16[48,384]{1,0:T(8,128)(2,1)}, bf16[48,384]{1,0:T(8,128)(2,1)S(1)}, u32[]{:S(2)}, u32[]{:S(2)}) collective-permute-start(bf16[48,384]{1,0:T(8,128)(2,1)} %get-tuple-element.133), channel_id=1, source_target_pairs={{0,16},{8,24},{16,0},{24,8},{1,17},{9,25},{17,1},{25,9},{2,18},{10... | collective-permute-start | bytes 110600 | tf_op jit(solution)/shard_map/ppermute | solution.py:523
  144.9 6.5 %collective-permute-start.38 = (bf16[48,384]{1,0:T(8,128)(2,1)}, bf16[48,384]{1,0:T(8,128)(2,1)S(1)}, u32[]{:S(2)}, u32[]{:S(2)}) collective-permute-start(bf16[48,384]{1,0:T(8,128)(2,1)} %get-tuple-element.134), channel_id=1, source_target_pairs={{0,24},{8,16},{16,8},{24,0},{1,25},{9,17},{17,9},{25,1},{2,26},{10... | collective-permute-start | bytes 110600 | tf_op jit(solution)/shard_map/ppermute | solution.py:523
  149.1 6.0 %collective-permute-start.51 = (bf16[48,384]{1,0:T(8,128)(2,1)}, bf16[48,384]{1,0:T(8,128)(2,1)S(1)}, u32[]{:S(2)}, u32[]{:S(2)}) collective-permute-start(bf16[48,384]{1,0:T(8,128)(2,1)} %shard_map.255.refs_0_), channel_id=1, source_target_pairs={{0,24},{8,16},{16,8},{24,0},{1,25},{9,17},{17,9},{25,1},{2,26},{10... | collective-permute-start | bytes 110600 | tf_op jit(solution)/shard_map/ppermute | solution.py:523
  151.4 10.6 %collective-permute-start.50 = (bf16[48,384]{1,0:T(8,128)(2,1)}, bf16[48,384]{1,0:T(8,128)(2,1)S(1)}, u32[]{:S(2)}, u32[]{:S(2)}) collective-permute-start(bf16[48,384]{1,0:T(8,128)(2,1)} %shard_map.255.refs_0_), channel_id=1, source_target_pairs={{0,16},{8,24},{16,0},{24,8},{1,17},{9,25},{17,1},{25,9},{2,18},{10... | collective-permute-start | bytes 110600 | tf_op jit(solution)/shard_map/ppermute | solution.py:523
  155.1 14.4 %copy-start.23 = (bf16[48,384]{1,0:T(8,128)(2,1)}, bf16[48,384]{1,0:T(8,128)(2,1)S(1)}, u32[]{:S(2)}) copy-start(bf16[48,384]{1,0:T(8,128)(2,1)S(1)} %collective-permute-done.51.refs_3_) | copy-start | bytes 110596
  155.1 8.4 %collective-permute-start.49 = (bf16[48,384]{1,0:T(8,128)(2,1)}, bf16[48,384]{1,0:T(8,128)(2,1)S(1)}, u32[]{:S(2)}, u32[]{:S(2)}) collective-permute-start(bf16[48,384]{1,0:T(8,128)(2,1)} %shard_map.255.refs_0_), channel_id=1, source_target_pairs={{0,8},{8,0},{16,24},{24,16},{1,9},{9,1},{17,25},{25,17},{2,10},{10... | collective-permute-start | bytes 110600 | tf_op jit(solution)/shard_map/ppermute | solution.py:523
  155.8 8.3 %collective-permute-start.41 = (bf16[48,384]{1,0:T(8,128)(2,1)}, bf16[48,384]{1,0:T(8,128)(2,1)S(1)}, u32[]{:S(2)}, u32[]{:S(2)}) collective-permute-start(bf16[48,384]{1,0:T(8,128)(2,1)} %shard_map.251.refs_0_), channel_id=1, source_target_pairs={{0,24},{8,16},{16,8},{24,0},{1,25},{9,17},{17,9},{25,1},{2,26},{10... | collective-permute-start | bytes 110600 | tf_op jit(solution)/shard_map/ppermute | solution.py:523
  157.3 13.8 %collective-permute-start.40 = (bf16[48,384]{1,0:T(8,128)(2,1)}, bf16[48,384]{1,0:T(8,128)(2,1)S(1)}, u32[]{:S(2)}, u32[]{:S(2)}) collective-permute-start(bf16[48,384]{1,0:T(8,128)(2,1)} %shard_map.251.refs_0_), channel_id=1, source_target_pairs={{0,16},{8,24},{16,0},{24,8},{1,17},{9,25},{17,1},{25,9},{2,18},{10... | collective-permute-start | bytes 110600 | tf_op jit(solution)/shard_map/ppermute | solution.py:523
  158.6 12.5 %collective-permute-start.39 = (bf16[48,384]{1,0:T(8,128)(2,1)}, bf16[48,384]{1,0:T(8,128)(2,1)S(1)}, u32[]{:S(2)}, u32[]{:S(2)}) collective-permute-start(bf16[48,384]{1,0:T(8,128)(2,1)} %shard_map.251.refs_0_), channel_id=1, source_target_pairs={{0,8},{8,0},{16,24},{24,16},{1,9},{9,1},{17,25},{25,17},{2,10},{10... | collective-permute-start | bytes 110600 | tf_op jit(solution)/shard_map/ppermute | solution.py:523
  162.0 16.4 %collective-permute-start.31 = (bf16[48,384]{1,0:T(8,128)(2,1)}, bf16[48,384]{1,0:T(8,128)(2,1)S(1)}, u32[]{:S(2)}, u32[]{:S(2)}) collective-permute-start(bf16[48,384]{1,0:T(8,128)(2,1)} %shard_map.247.refs_0_), channel_id=1, source_target_pairs={{0,24},{8,16},{16,8},{24,0},{1,25},{9,17},{17,9},{25,1},{2,26},{10... | collective-permute-start | bytes 110600 | tf_op jit(solution)/shard_map/ppermute | solution.py:523
  163.5 14.8 %collective-permute-start.30 = (bf16[48,384]{1,0:T(8,128)(2,1)}, bf16[48,384]{1,0:T(8,128)(2,1)S(1)}, u32[]{:S(2)}, u32[]{:S(2)}) collective-permute-start(bf16[48,384]{1,0:T(8,128)(2,1)} %shard_map.247.refs_0_), channel_id=1, source_target_pairs={{0,16},{8,24},{16,0},{24,8},{1,17},{9,25},{17,1},{25,9},{2,18},{10... | collective-permute-start | bytes 110600 | tf_op jit(solution)/shard_map/ppermute | solution.py:523
  164.1 14.2 %collective-permute-start.29 = (bf16[48,384]{1,0:T(8,128)(2,1)}, bf16[48,384]{1,0:T(8,128)(2,1)S(1)}, u32[]{:S(2)}, u32[]{:S(2)}) collective-permute-start(bf16[48,384]{1,0:T(8,128)(2,1)} %shard_map.247.refs_0_), channel_id=1, source_target_pairs={{0,8},{8,0},{16,24},{24,16},{1,9},{9,1},{17,25},{25,17},{2,10},{10... | collective-permute-start | bytes 110600 | tf_op jit(solution)/shard_map/ppermute | solution.py:523
  (43 other events, 174.3 us)

commit v2 on v1

--- a/solution.py
+++ b/solution.py
@@ -1,4 +1,5 @@
 import functools
+import math
 
 import jax
 import jax.numpy as jnp
@@ -13,8 +14,9 @@
 F32 = jnp.float32
 SQRT_2_PI = 0.7978845608028654
 CUBIC = 0.044715
+MARGIN = 0.25
+PACK_LIMIT = 56 * 1024 * 1024
 MOD_ROWS = 16
-VMEM_BYTES = 56 * 1024 * 1024
 
 
 def dot(a, b):
@@ -46,18 +48,32 @@
     return v / (1.0 + jnp.exp(-v))
 
 
-def call(body, outs, ins, scratch=(), smem=(), flops=1 << 24, moved=1 << 20):
+def call(body, outs, ins, scratch=(), smem=(), far=(), far_outs=(), room=2, micros=0.2, limit=0):
     specs = [
-        pl.BlockSpec(memory_space=pltpu.SMEM if i in smem else pltpu.VMEM) for i in range(len(ins))
+        pl.BlockSpec(
+            memory_space=pltpu.SMEM if i in smem else pltpu.HBM if i in far else pltpu.VMEM
+        )
+        for i in range(len(ins))
     ]
+    def size(shape, kind):
+        width = -(-shape[-1] // 128) * 128
+        return math.prod(shape[:-1]) * width * jnp.dtype(kind).itemsize
+
+    held = sum(size(v.shape, v.dtype) for v in scratch if len(v.shape) > 1)
+    held += MARGIN * (sum(size(v.shape, v.dtype) for v in ins) + sum(size(*out) for out in outs))
     return pl.pallas_call(
         body,
         out_shape=[jax.ShapeDtypeStruct(shape, kind) for shape, kind in outs],
         in_specs=specs,
-        out_specs=[pl.BlockSpec(memory_space=pltpu.VMEM)] * len(outs),
+        out_specs=[
+            pl.BlockSpec(memory_space=pltpu.HBM if i in far_outs else pltpu.VMEM)
+            for i in range(len(outs))
+        ],
         scratch_shapes=list(scratch),
-        compiler_params=pltpu.CompilerParams(vmem_limit_bytes=VMEM_BYTES),
-        cost_estimate=pl.CostEstimate(flops=flops, bytes_accessed=moved, transcendentals=0),
+        compiler_params=pltpu.CompilerParams(vmem_limit_bytes=limit or int(held) + room * 1024 * 1024),
+        cost_estimate=pl.CostEstimate(
+            flops=0, bytes_accessed=int(micros * 3.69e6), transcendentals=0
+        ),
     )(*ins)
 
 
@@ -75,6 +91,8 @@
         self.shards = fsdp if self.direct else 1
         self.rows = own if self.direct else self.d
         self.peers = [2 * m for m in range(fsdp // 2)]
+        self.sides = 2 if self.direct else 1
+        self.bias_rows = [6, 2, 1, self.ffb, 1]
 
 
 def shard_of(plan, k):
@@ -83,28 +101,62 @@
     return lax.axis_index("fsdp") ^ k
 
 
-def pack_body(plan, ada, qkv, proj, fc1, bias, first, second, rows_s):
+def pack_weights(plan, ada, qkv, proj, fc1, fc2, biases, first, second, rows_s, sems):
     d, r = plan.d, plan.rows
-    me = lax.axis_index("fsdp") if plan.direct else 0
-    blocks = [qkv[:, j * d : (j + 1) * d] for j in range(3)]
-    blocks += [ada[:, j * d : (j + 1) * d] for j in range(2)]
-    for j, block in enumerate(blocks):
-        first[j * r : (j + 1) * r, :] = block
-    blocks = [fc1[:, j * d : (j + 1) * d] for j in range(plan.ffb)]
-    blocks += [ada[:, j * d : (j + 1) * d] for j in range(2, 6)]
-    blocks += [proj[...]]
-    for j, block in enumerate(blocks):
-        second[j * r : (j + 1) * r, :] = block
+
+    def cut(ref, start, stop):
+        return [ref.at[:, pl.ds(j * d, d)] for j in range(start, stop)]
+
+    copies = []
+    for packed, blocks in (
+        (first, cut(qkv, 0, 3) + cut(ada, 0, 2)),
+        (second, cut(fc1, 0, plan.ffb) + cut(ada, 2, 6) + [proj, fc2]),
+    ):
+        at = 0
+        for block in blocks:
+            target = packed.at[pl.ds(at, block.shape[0]), :]
+            copies.append(pltpu.make_async_copy(block, target, sems.at[len(copies)]))
+            at += block.shape[0]
+    for copy in copies:
+        copy.start()
     rows_s[...] = jnp.zeros_like(rows_s)
-    at = 0
-    for row, count in ((0, 6), (1, 2), (2, 1), (3, plan.ffb), (4, 1)):
-        wide = bias[:, : count * d]
+    line = jnp.broadcast_to(biases[...], (8, biases.shape[1]))
+    at, start = 0, 0
+    for count in plan.bias_rows:
+        width = max(count * d, line.shape[1])
+        wide = line
+        if width > line.shape[1]:
+            wide = jnp.concatenate([line, jnp.zeros((8, width - line.shape[1]), F32)], axis=1)
         if plan.direct:
-            wide = pltpu.roll(wide, me * (count * d // plan.fsdp), 1)
+            own = count * d // plan.fsdp
+            me = lax.axis_index("fsdp")
+            wide = pltpu.roll(wide, lax.rem(me * own + (width - start), width), 1)
+            lane = lax.broadcasted_iota(jnp.int32, (8, width), 1)
+            wide = jnp.where((lane >= me * own) & (lane < (me + 1) * own), wide, 0.0)
+            start += own
+        else:
+            wide = line[:, start : start + count * d]
+            start += count * d
         for j in range(count):
-            rows_s[at + j : at + j + 1, :] = wide[row : row + 1, j * d : (j + 1) * d]
+            rows_s[at + j : at + j + 1, :] = wide[0:1, j * d : (j + 1) * d]
         at += count
     first[5 * r : 5 * r + 16, :] = rows_s[...].astype(BF)
+    for copy in copies:
+        copy.wait()
+
+
+def join(count, gate, *refs):
+    del gate
+    out = refs[count]
+    rows = refs[0].shape[0]
+    for m, shard in enumerate(refs[:count]):
+        out[m * rows : (m + 1) * rows, :] = shard[...]
+
+
+def views(plan, joined):
+    count = plan.shards // len(joined)
+    rows = joined[0].shape[0] // count
+    return [ref.at[pl.ds(m * rows, rows), :] for m in range(count) for ref in joined]
 
 
 def place(plan, shards, block, target, column):
@@ -130,15 +182,21 @@
     s = plan.shards
     x, cond = refs[:2]
     shards = refs[2 : 2 + s]
-    projected, mixed, attn_in, modulation, bias, qkv, ada = refs[2 + s : 9 + s]
-    d, length = plan.d, plan.seq
+    projected, mixed, modulation, bias, qkv_out, ada_out, qkv, ada, sems = refs[2 + s :]
+    d, length, r = plan.d, plan.seq, plan.rows
     for j in range(3):
         place(plan, shards, j, qkv, j)
     for j in range(2):
         place(plan, shards, 3 + j, ada, j)
-    total = shards[0][5 * plan.rows : 5 * plan.rows + 16, :].astype(F32)
+    copies = [
+        pltpu.make_async_copy(qkv, qkv_out, sems.at[0]),
+        pltpu.make_async_copy(ada, ada_out, sems.at[1]),
+    ]
+    for copy in copies:
+        copy.start()
+    total = shards[0][5 * r : 5 * r + 16, :].astype(F32)
     for shard in shards[1:]:
-        total = total + shard[5 * plan.rows : 5 * plan.rows + 16, :].astype(F32)
+        total = total + shard[5 * r : 5 * r + 16, :].astype(F32)
     bias[...] = total
     cond_act = silu(cond[...].astype(F32)).astype(BF)
     mod = dot(cond_act, ada[...])
@@ -152,7 +210,6 @@
         scale = modulation[pl.ds(g, 1), d : 2 * d]
         normed, _ = normalize(x[at, :].astype(F32))
         rounded = (normed * (1.0 + scale) + shift).astype(BF)
-        attn_in[at, :] = rounded
         for j in range(3):
             piece = dot(rounded, qkv[:, j * d : (j + 1) * d])
             if j != 1:
@@ -173,22 +230,28 @@
         return carry
 
     lax.fori_loop(0, plan.group, latent, 0)
+    for copy in copies:
+        copy.wait()
 
 
 def mlp_first(plan, *refs):
-    s = plan.shards
+    s = plan.sides
     counts, x, cond, cot, mixed, bias = refs[:6]
-    shards = refs[6 : 6 + s]
-    outs = refs[6 + s :]
-    (send, outs) = (outs[0], outs[1:]) if plan.direct else (None, outs)
-    keep, act, gelu_back, mlp_in, grad_out, middle, attn_out, modulation, fc1, ada, proj = outs[:11]
-    grad_fc2 = outs[11]
+    shards = views(plan, refs[6 : 6 + s])
+    (act, gelu_back, mlp_in, grad_out, middle, attn_out, modulation, fc1, ada_out, proj, grad_fc2,
+     fc2, ada, sems) = refs[6 + s :]
     d, length, ffb = plan.d, plan.seq, plan.ffb
     for j in range(ffb):
         place(plan, shards, j, fc1, j)
     for j in range(4):
         place(plan, shards, ffb + j, ada, j)
+    copy = pltpu.make_async_copy(ada, ada_out, sems.at[0])
+    copy.start()
     place(plan, shards, ffb + 4, proj, 0)
+    r, r4 = plan.rows, plan.rows * ffb
+    for k, shard in enumerate(shards):
+        at = pl.multiple_of(shard_of(plan, k) * r4, 16)
+        fc2[pl.ds(at, r4), :] = shard[(ffb + 5) * r : (ffb + 5) * r + r4, :]
     cond_act = silu(cond[...].astype(F32)).astype(BF)
     mod = dot(cond_act, ada[...])
     for j in range(4):
@@ -231,20 +294,15 @@
         slope = (0.5 * SQRT_2_PI) + (1.5 * SQRT_2_PI * CUBIC) * square
         gelu_back[:, cols] = half + pre * (1.0 - bend * bend) * slope
         grad_fc2[cols, :] = dot_tn(value, grad_out[...]).astype(BF)
-    emit(plan, None, [(j, grad_fc2, 0, 4, j) for j in range(ffb)], send, keep, ffb * plan.rows)
+    copy.wait()
 
 
 def mlp_second(plan, *refs):
-    s = plan.shards
-    grad_out, gelu_back, mlp_in = refs[:3]
-    shards = refs[3 : 3 + s]
-    outs = refs[3 + s :]
+    grad_out, gelu_back, mlp_in, grad_fc2, fc2 = refs[:5]
+    outs = refs[5:]
     (send, outs) = (outs[0], outs[1:]) if plan.direct else (None, outs)
-    keep, grad_pre, fc2 = outs[:3]
-    turned, grad_fc1 = outs[3:]
+    keep, grad_pre, turned, grad_fc1 = outs
     r4 = plan.rows * plan.ffb
-    for k, shard in enumerate(shards):
-        fc2[pl.ds(pl.multiple_of(shard_of(plan, k) * r4, 16), r4), :] = shard[...]
     turned[...] = mlp_in[...].T
     step = 256
     for c in range(plan.ff // step):
@@ -252,15 +310,30 @@
         grad = (dot_nt(grad_out[...], fc2[cols, :]) * gelu_back[:, cols]).astype(BF)
         grad_pre[:, cols] = grad
         grad_fc1[:, cols] = dot(turned[...], grad).astype(BF)
-    emit(plan, None, [(j, grad_fc1, j, 1, 0) for j in range(plan.ffb)], send, keep, r4)
-
-
-def mlp_back(plan, *refs):
-    (counts, cot, act, fc2, grad_pre, fc1, middle, attn_out, modulation, bias, mixed, proj,
-     grad_out) = refs[:13]
-    block_out, grad_mixed, grad_middle, grad_proj, misc, grad_mod = refs[13:19]
+    blocks = [(j, grad_fc1, j, 1, 0) for j in range(plan.ffb)]
+    blocks += [(plan.ffb + j, grad_fc2, 0, plan.ffb, j) for j in range(plan.ffb)]
+    emit(plan, None, blocks, send, keep, 2 * r4)
+
+
+def mlp_close(plan, counts, cot, act, fc2, middle, modulation, bias, block_out, grad_gate):
     d, length = plan.d, plan.seq
-    grad_gates = refs[19]
+
+    def latent(g, carry):
+        at = pl.ds(pl.multiple_of(g * length, length), length)
+        gate = modulation[pl.ds(g, 1), 3 * d : 4 * d]
+        live = jnp.where(g % plan.slots < counts[g // plan.slots, 0], 1.0, 0.0).astype(F32)
+        mlp_out = dot(act[at, :], fc2[...]) + bias[9 + plan.ffb : 10 + plan.ffb, :]
+        block_out[at, :] = (live * (middle[at, :] + gate * mlp_out)).astype(BF)
+        upstream = cot[at, :].astype(F32) * live
+        grad_gate[pl.ds(g, 1), :] = jnp.sum(upstream * mlp_out, axis=0, keepdims=True)
+        return carry
+
+    lax.fori_loop(0, plan.group, latent, 0)
+
+
+def mlp_back(plan, counts, cot, grad_pre, fc1, middle, attn_out, modulation, mixed, proj, grad_out,
+             grad_mixed, grad_middle, grad_proj, misc, grad_mod, grad_gates):
+    d, length = plan.d, plan.seq
     misc[...] = jnp.zeros_like(misc)
     sums = jnp.sum(grad_pre[...].astype(F32), axis=0, keepdims=True)
     for j in range(plan.ffb):
@@ -271,20 +344,17 @@
 
     def latent(g, carry):
         at = pl.ds(pl.multiple_of(g * length, length), length)
-        gate_attn, _, scale, gate = [modulation[pl.ds(g, 1), j * d : (j + 1) * d] for j in range(4)]
+        gate_attn, _, scale = [modulation[pl.ds(g, 1), j * d : (j + 1) * d] for j in range(3)]
         live = jnp.where(g % plan.slots < counts[g // plan.slots, 0], 1.0, 0.0).astype(F32)
         upstream = cot[at, :].astype(F32) * live
-        mid = middle[at, :]
-        mlp_out = dot(act[at, :], fc2[...]) + bias[9 + plan.ffb : 10 + plan.ffb, :]
-        block_out[at, :] = (live * (mid + gate * mlp_out)).astype(BF)
-        normed, rstd = normalize(mid)
+        normed, rstd = normalize(middle[at, :])
         grad_in = dot_nt(grad_pre[at, :], fc1[...])
         grad_mid = upstream + norm_back(grad_in * (1.0 + scale), normed, rstd)
         grad_middle[at, :] = grad_mid
         rounded = (gate_attn * grad_mid).astype(BF)
         grad_gates[at, :] = rounded
         grad_mixed[at, :] = dot_nt(rounded, proj[...]).astype(BF)
-        pieces = [grad_mid * attn_out[at, :], grad_in, grad_in * normed, upstream * mlp_out]
+        pieces = [grad_mid * attn_out[at, :], grad_in, grad_in * normed]
         for j, piece in enumerate(pieces):
             grad_mod[pl.ds(g, 1), j * d : (j + 1) * d] = jnp.sum(piece, axis=0, keepdims=True)
         return carry
@@ -294,50 +364,64 @@
     grad_proj[...] = dot_tn(mixed[...], grad_gates[...]).astype(BF)
 
 
-def attn_back(plan, *refs):
-    (x, cond, projected, grad_mixed, grad_middle, attn_in, qkv, modulation, grad_proj, misc,
-     grad_mod) = refs[:11]
-    outs = refs[11:]
+def attn_core_back(plan, at, projected, grad_mixed, out, where):
+    d = plan.d
+    left = lax.broadcasted_iota(jnp.int32, (1, 128), 1) < 64
+    for pair in range(HEADS // 2):
+        lanes = slice(pair * 128, (pair + 1) * 128)
+        q = projected[at, lanes] * jnp.asarray(0.125, BF)
+        k = projected[at, d + pair * 128 : d + (pair + 1) * 128]
+        v = projected[at, 2 * d + pair * 128 : 2 * d + (pair + 1) * 128]
+        gm = grad_mixed[at, lanes]
+        grads_q, grads_k, grads_v = [], [], []
+        for side in (left, ~left):
+            scores = dot_nt(jnp.where(side, q, jnp.zeros_like(q)), k)
+            exponent = jnp.exp(scores - jnp.max(scores, axis=-1, keepdims=True))
+            probs = exponent * (1.0 / jnp.sum(exponent, axis=-1, keepdims=True))
+            grad_probs = dot_nt(jnp.where(side, gm, jnp.zeros_like(gm)), v)
+            inner = jnp.sum(probs * grad_probs, axis=-1, keepdims=True)
+            grad_scores = (probs * (grad_probs - inner)).astype(BF)
+            grads_q.append(dot(grad_scores, k))
+            grads_k.append(dot_tn(grad_scores, q))
+            grads_v.append(dot_tn(probs.astype(BF), gm))
+        for j, (pieces, factor) in enumerate(((grads_q, 0.125), (grads_k, 1.0), (grads_v, 1.0))):
+            merged = jnp.where(left, pieces[0], pieces[1]) * factor
+            out[where, j * d + pair * 128 : j * d + (pair + 1) * 128] = merged.astype(BF)
+
+
+def attn_back(plan, g, projected, grad_mixed, out):
+    at = slice(g * plan.seq, (g + 1) * plan.seq)
+    attn_core_back(plan, at, projected, grad_mixed, out, slice(0, plan.seq))
+
+
+def attn_close(plan, *refs):
+    (x, cond, grad_middle, qkv, modulation, grad_proj, misc, grad_mod,
+     grad_gate) = refs[:9]
+    parts, outs = refs[9 : 9 + plan.group], refs[9 + plan.group :]
     (send, outs) = (outs[0], outs[1:]) if plan.direct else (None, outs)
     keep, latents_grad, mods = outs[:3]
-    grad_proj_in, grad_qkv, rows_s, misc_s, cond_s = outs[3:]
+    grad_proj_in, grad_qkv, rows_s, misc_s, cond_s, attn_in = outs[3:]
     d, length, r = plan.d, plan.seq, plan.rows
-    left = lax.broadcasted_iota(jnp.int32, (1, 128), 1) < 64
     misc_s[...] = misc[...]
     rows_s[...] = jnp.zeros_like(rows_s)
     cond_s[...] = silu(cond[...].astype(F32))
+    for g, part in enumerate(parts):
+        grad_proj_in[g * length : (g + 1) * length, :] = part[...]
 
     def latent(g, carry):
         at = pl.ds(pl.multiple_of(g * length, length), length)
+        shift = modulation[pl.ds(g, 1), 0:d]
         scale = modulation[pl.ds(g, 1), d : 2 * d]
-        for pair in range(HEADS // 2):
-            lanes = slice(pair * 128, (pair + 1) * 128)
-            q = projected[at, lanes] * jnp.asarray(0.125, BF)
-            k = projected[at, d + pair * 128 : d + (pair + 1) * 128]
-            v = projected[at, 2 * d + pair * 128 : 2 * d + (pair + 1) * 128]
-            gm = grad_mixed[at, lanes]
-            grads_q, grads_k, grads_v = [], [], []
-            for side in (left, ~left):
-                scores = dot_nt(jnp.where(side, q, jnp.zeros_like(q)), k)
-                exponent = jnp.exp(scores - jnp.max(scores, axis=-1, keepdims=True))
-                probs = exponent * (1.0 / jnp.sum(exponent, axis=-1, keepdims=True))
-                grad_probs = dot_nt(jnp.where(side, gm, jnp.zeros_like(gm)), v)
-                inner = jnp.sum(probs * grad_probs, axis=-1, keepdims=True)
-                grad_scores = (probs * (grad_probs - inner)).astype(BF)
-                grads_q.append(dot(grad_scores, k))
-                grads_k.append(dot_tn(grad_scores, q))
-                grads_v.append(dot_tn(probs.astype(BF), gm))
-            for j, (pieces, factor) in enumerate(((grads_q, 0.125), (grads_k, 1.0), (grads_v, 1.0))):
-                merged = jnp.where(left, pieces[0], pieces[1]) * factor
-                grad_proj_in[at, j * d + pair * 128 : j * d + (pair + 1) * 128] = merged.astype(BF)
         normed, rstd = normalize(x[at, :].astype(F32))
+        attn_in[at, :] = (normed * (1.0 + scale) + shift).astype(BF)
         grad_in = dot_nt(grad_proj_in[at, :], qkv[...])
         grad = grad_middle[at, :] + norm_back(grad_in * (1.0 + scale), normed, rstd)
         latents_grad[at, :] = grad.astype(BF)
         base = g * 7
         pieces = [cond_s[pl.ds(g, 1), :], jnp.sum(grad_in, axis=0, keepdims=True)]
         pieces += [jnp.sum(grad_in * normed, axis=0, keepdims=True)]
-        pieces += [grad_mod[pl.ds(g, 1), j * d : (j + 1) * d] for j in range(4)]
+        pieces += [grad_mod[pl.ds(g, 1), j * d : (j + 1) * d] for j in range(3)]
+        pieces += [grad_gate[pl.ds(g, 1), :]]
         for j, piece in enumerate(pieces):
             rows_s[pl.ds(base + j, 1), :] = piece
         return carry
@@ -427,34 +511,30 @@
             at += rows
 
 
-def last_sibling(peers, rows, *refs):
-    keep, received, mods, mods_in, own = refs[:5]
-    outs = refs[5:]
+def last_sibling(peers, rows, keep, received, mods, own, *outs):
     for m in range(peers):
         at = slice(m * rows, (m + 1) * rows)
         total = keep[at, :].astype(F32) + received[at, :].astype(F32)
         if m == 0:
             own[0:rows, :] = total
             own[rows : rows + MOD_ROWS, :] = mods[...].astype(F32)
-            own[rows + MOD_ROWS : rows + 2 * MOD_ROWS, :] = mods_in[...].astype(F32)
         else:
             outs[m - 1][0:rows, :] = total.astype(BF)
             outs[m - 1][rows : rows + MOD_ROWS, :] = mods[...]
-            outs[m - 1][rows + MOD_ROWS : rows + 2 * MOD_ROWS, :] = mods_in[...]
 
 
 def last_chips(count, dp, quarter, rows, own, *refs):
     received, mine, outs = refs[:count], refs[count], refs[count + 1 : count + dp]
     total_s, tail_s = refs[count + dp :]
-    total = own[0 : rows, :]
+    total = own[0:rows, :]
     for piece in received:
         total = total + piece[0:rows, :].astype(F32)
     total_s[...] = total[: rows - 16]
     tail_s[0:16, :] = total[rows - 16 :].astype(BF)
-    tail_s[16 : 16 + 2 * MOD_ROWS, :] = own[rows:, :].astype(BF)
+    tail_s[16 : 16 + MOD_ROWS, :] = own[rows:, :].astype(BF)
     for i, piece in enumerate(received):
-        at = 16 + (i + 1) * 2 * MOD_ROWS
-        tail_s[at : at + 2 * MOD_ROWS, :] = piece[rows:, :]
+        at = 16 + (i + 1) * MOD_ROWS
+        tail_s[at : at + MOD_ROWS, :] = piece[rows:, :]
     me = lax.axis_index("dp")
     for j in range(dp):
         part = total_s[pl.ds(pl.multiple_of((me ^ j) * quarter, 16), quarter), :]
@@ -464,25 +544,28 @@
 
 
 def last_groups(dp, quarter, *refs):
-    pieces, low = refs[:dp], refs[dp]
+    pieces, low, mods = refs[:dp], refs[dp], refs[dp + 1]
     total = pieces[0][0:quarter, :]
     for piece in pieces[1:]:
         total = total + piece[0:quarter, :].astype(F32)
     low[...] = total.astype(BF)
+    each = pieces[0].shape[0] - quarter - 16
+    for j, piece in enumerate(pieces):
+        mods[j * each : (j + 1) * each, :] = piece[quarter + 16 :, :].astype(BF)
 
 
 def ada_grads(plan, quarter, *refs):
     dp, d, r = plan.dp, plan.d, plan.rows
-    pieces = refs[:dp]
-    ada, ada_bias, qv, proj, fc1, fc2 = refs[dp : dp + 6]
-    rows_s, turned_s = refs[dp + 6 :]
-    each = plan.fsdp * MOD_ROWS
+    pieces, mods = refs[:dp], refs[dp : dp + 2]
+    ada, ada_bias, qv, proj, fc1, fc2 = refs[dp + 2 : dp + 8]
+    rows_s, turned_s = refs[dp + 8 :]
+    each = dp * plan.fsdp * MOD_ROWS // 2
     total = pieces[0][quarter : quarter + 16, :].astype(F32)
     for piece in pieces[1:]:
         total = total + piece[quarter : quarter + 16, :].astype(F32)
-    for j, piece in enumerate(pieces):
-        rows_s[j * each : (j + 1) * each, :] = piece[quarter + 16 :, :].astype(BF)
-    count = dp * each
+    for j, rows in enumerate(mods):
+        rows_s[j * each : (j + 1) * each, :] = rows[...]
+    count = 2 * each
     row = lax.broadcasted_iota(jnp.int32, (count, count), 0)
     column = lax.broadcasted_iota(jnp.int32, (count, count), 1)
     slot = row % MOD_ROWS
@@ -523,39 +606,73 @@
     return lax.ppermute(value, axis, [(i, i ^ k) for i in range(size)])
 
 
-def gather_shards(plan, value):
+def behind(values, *gates):
+    gates = [gate for gate in gates if gate is not None]
+    return list(lax.optimization_barrier((tuple(values), tuple(gates)))[0])
+
+
+def gather_chips(plan, value):
     if not plan.direct:
         return [value]
-    chips = [value] + [swap(plan, value, k) for k in plan.peers[1:]]
+    return [value] + [swap(plan, value, k) for k in plan.peers[1:]]
+
+
+def gather_joined(plan, chips, gate):
+    if not plan.direct:
+        return chips
+    rows, d = chips[0].shape
+    (mine,) = call(
+        functools.partial(join, len(chips)),
+        [((len(chips) * rows, d), BF)],
+        [gate] + chips,
+        micros=0.4,
+    )
+    return [mine, swap(plan, mine, 1)]
+
+
+def gather_cores(plan, chips):
+    if not plan.direct:
+        return chips
     cores = [swap(plan, shard, 1) for shard in chips]
     return [shard for pair in zip(chips, cores) for shard in pair]
 
 
-def reduce_chunk(plan, send, keep, layout):
-    d, dp, peers = plan.d, plan.dp, len(plan.peers)
+def chunk_siblings(plan, send, keep, gate):
+    d, peers = plan.d, len(plan.peers)
     rows = keep.shape[0] // peers
-    quarter = rows // dp
     received = swap(plan, send, 1)
+    keep, received = behind([keep, received], gate)
     own, *pieces = call(
         functools.partial(add_siblings, peers, rows),
         [((rows, d), F32)] + [((rows, d), BF)] * (peers - 1),
         [keep, received],
     )
-    pieces = [swap(plan, piece, k) for piece, k in zip(pieces, plan.peers[1:])]
+    return own, [swap(plan, piece, k) for piece, k in zip(pieces, plan.peers[1:])]
+
+
+def chunk_chips(plan, own, pieces):
+    d, dp = plan.d, plan.dp
+    rows = own.shape[0]
+    quarter = rows // dp
     mine, *quarters = call(
-        functools.partial(add_chips, peers - 1, dp, quarter),
+        functools.partial(add_chips, len(pieces), dp, quarter),
         [((quarter, d), F32)] + [((quarter, d), BF)] * (dp - 1),
         [own] + pieces,
         [pltpu.VMEM((rows, d), F32)],
     )
-    quarters = [swap(plan, part, j + 1, "dp") for j, part in enumerate(quarters)]
+    return mine, [swap(plan, part, j + 1, "dp") for j, part in enumerate(quarters)]
+
+
+def chunk_groups(plan, mine, quarters, layout):
+    d, dp = plan.d, plan.dp
+    quarter = mine.shape[0]
     (low,) = call(functools.partial(add_groups, dp), [((quarter, d), BF)], [mine] + quarters)
     parts = [low] + [swap(plan, low, j, "dp") for j in range(1, dp)]
     return call(
         functools.partial(gather_groups, dp, quarter, layout),
         [((height, blocks * d), F32) for blocks, height in layout],
         parts,
-        [pltpu.VMEM((rows, d), F32)],
+        [pltpu.VMEM((quarter * dp, d), F32)],
     )
 
 
@@ -563,15 +680,15 @@
     d, dp, peers, r = plan.d, plan.dp, len(plan.peers), plan.rows
     rows = keep.shape[0] // peers
     quarter = (rows - 16) // dp
-    received, mods_in = swap(plan, send, 1), swap(plan, mods, 1)
-    long = rows + 2 * MOD_ROWS
+    received = swap(plan, send, 1)
+    long = rows + MOD_ROWS
     own, *pieces = call(
         functools.partial(last_sibling, peers, rows),
         [((long, d), F32)] + [((long, d), BF)] * (peers - 1),
-        [keep, received, mods, mods_in],
+        [keep, received, mods],
     )
     pieces = [swap(plan, piece, k) for piece, k in zip(pieces, plan.peers[1:])]
-    tail = 16 + plan.fsdp * MOD_ROWS
+    tail = 16 + peers * MOD_ROWS
     mine, *quarters = call(
         functools.partial(last_chips, peers - 1, dp, quarter, rows),
         [((quarter + tail, d), F32)] + [((quarter + tail, d), BF)] * (dp - 1),
@@ -579,17 +696,20 @@
         [pltpu.VMEM((rows - 16, d), F32), pltpu.VMEM((tail, d), BF)],
     )
     quarters = [swap(plan, part, j + 1, "dp") for j, part in enumerate(quarters)]
-    (low,) = call(functools.partial(last_groups, dp, quarter), [((quarter, d), BF)], [mine] + quarters)
+    half = dp * peers * MOD_ROWS
+    low, mods = call(
+        functools.partial(last_groups, dp, quarter),
+        [((quarter, d), BF), ((half, d), BF)],
+        [mine] + quarters,
+    )
     parts = [low] + [swap(plan, low, j, "dp") for j in range(1, dp)]
-    widths = [6, 2, 1, plan.ffb, 1]
+    widths = plan.bias_rows
     ada, *biases = call(
         functools.partial(ada_grads, plan, quarter),
         [((r, 6 * d), F32)] + [((1, w * d // plan.fsdp), F32) for w in widths],
-        [mine] + quarters,
-        [
-            pltpu.VMEM((dp * plan.fsdp * MOD_ROWS, d), BF),
-            pltpu.VMEM((d, dp * plan.fsdp * MOD_ROWS), F32),
-        ],
+        [mine] + quarters + [mods, swap(plan, mods, 1)],
+        [pltpu.VMEM((2 * half, d), BF), pltpu.VMEM((d, 2 * half), F32)],
+        micros=2,
     )
     qkv, proj = call(
         functools.partial(gather_groups, dp, quarter, ((3, r), (1, r))),
@@ -600,8 +720,9 @@
     return qkv, proj, ada, [bias.reshape(-1) for bias in biases]
 
 
-def reduce_whole(plan, fc2_rows, fc1_rows, last, mods):
+def reduce_whole(plan, mlp, last, mods):
     d, ffb = plan.d, plan.ffb
+    fc1_rows, fc2_rows = mlp[: ffb * d], mlp[ffb * d :]
 
     def unpack(rows, blocks):
         return rows.reshape(blocks, d, d).transpose(1, 0, 2).reshape(d, blocks * d)
@@ -659,21 +780,28 @@
             return lax.all_gather(v, "fsdp", axis=0, tiled=True)
 
         biases, weights, third = [whole(v) for v in biases], [whole(v) for v in weights], whole(third)
-    rows = [jnp.pad(bias.astype(F32), (0, 6 * d - bias.shape[0])) for bias in biases]
-    rows = jnp.stack(rows + [jnp.zeros_like(rows[0])] * 3)
+    lengths = [bias.shape[0] for bias in biases]
+    width = -(-sum(lengths) // 128) * 128
+    line = sum(
+        jnp.pad(bias.astype(F32), (sum(lengths[:i]), width - sum(lengths[: i + 1])))
+        for i, bias in enumerate(biases)
+    )
     first, second = call(
-        functools.partial(pack_body, plan),
-        [((5 * r + 16, d), BF), (((plan.ffb + 5) * r, d), BF)],
-        weights + [rows],
-        [pltpu.VMEM((16, d), F32)],
-    )
-    first, second, third = [gather_shards(plan, v) for v in (first, second, third)]
-
-    projected, mixed, attn_in, mod_first, bias, qkv, ada_first = call(
+        functools.partial(pack_weights, plan),
+        [((5 * r + 16, d), BF), (((2 * plan.ffb + 5) * r, d), BF)],
+        weights + [third, line[None, :]],
+        [pltpu.VMEM((16, d), F32), pltpu.SemaphoreType.DMA((plan.ffb + 11,))],
+        far=(0, 1, 2, 3, 4),
+        limit=PACK_LIMIT,
+        micros=1.0,
+    )
+    first = gather_cores(plan, gather_chips(plan, first))
+    second = gather_chips(plan, second)
+
+    projected, mixed, mod_first, bias, qkv, ada_first = call(
         functools.partial(attn_forward, plan),
         [
             ((n, 3 * d), BF),
-            ((n, d), BF),
             ((n, d), BF),
             ((group, 2 * d), F32),
             ((16, d), F32),
@@ -681,15 +809,22 @@
             ((d, 2 * d), BF),
         ],
         [x, cond] + first,
-        flops=1 << 30,
-        moved=1 << 24,
-    )
+        [
+            pltpu.VMEM((d, 3 * d), BF),
+            pltpu.VMEM((d, 2 * d), BF),
+            pltpu.SemaphoreType.DMA((2,)),
+        ],
+        far_outs=(4, 5),
+        room=8,
+        micros=4,
+    )
+    second = gather_joined(plan, second, mod_first)
     halves = len(plan.peers) if plan.direct else 1
-    sides = 2 if plan.direct else 1
-    outs = call(
+    sides = plan.sides
+    (act, gelu_back, mlp_in, grad_out, middle, attn_out, mod_second, fc1, ada_second, proj,
+     grad_fc2, fc2) = call(
         functools.partial(mlp_first, plan),
-        [((halves * plan.ffb * r, d), BF)] * sides
-        + [
+        [
             ((n, ff), BF),
             ((n, ff), F32),
             ((n, d), BF),
@@ -700,68 +835,93 @@
             ((d, ff), BF),
             ((d, 4 * d), BF),
             ((d, d), BF),
+            ((ff, d), BF),
+            ((ff, d), BF),
         ],
         [counts, x, cond, cot, mixed, bias] + second,
-        [pltpu.VMEM((ff, d), BF)],
+        [pltpu.VMEM((d, 4 * d), BF), pltpu.SemaphoreType.DMA((1,))],
         smem=(0,),
-        flops=1 << 30,
-        moved=1 << 24,
-    )
-    fc2_chunk = outs[:sides]
-    act, gelu_back, mlp_in, grad_out, middle, attn_out, mod_second, fc1, ada_second, proj = outs[sides:]
+        far_outs=(8,),
+        room=8,
+        micros=6,
+    )
     outs = call(
         functools.partial(mlp_second, plan),
-        [((halves * plan.ffb * r, d), BF)] * sides + [((n, ff), BF), ((ff, d), BF)],
-        [grad_out, gelu_back, mlp_in] + third,
+        [((halves * 2 * plan.ffb * r, d), BF)] * sides + [((n, ff), BF)],
+        [grad_out, gelu_back, mlp_in, grad_fc2, fc2],
         [pltpu.VMEM((d, n), BF), pltpu.VMEM((d, ff), BF)],
-        flops=1 << 30,
-        moved=1 << 24,
-    )
-    fc1_chunk = outs[:sides]
-    grad_pre, fc2 = outs[sides:]
-    block_out, grad_mixed, grad_middle, grad_proj, misc, grad_mod = call(
+        room=8,
+        micros=4,
+    )
+    mlp_chunk = outs[:sides]
+    (grad_pre,) = outs[sides:]
+    block_out, grad_gate = call(
+        functools.partial(mlp_close, plan),
+        [((n, d), BF), ((group, d), F32)],
+        [counts, cot, act, fc2, middle, mod_second, bias],
+        smem=(0,),
+        room=8,
+        micros=1.5,
+    )
+    if plan.direct:
+        mlp_own, mlp_pieces = chunk_siblings(plan, *mlp_chunk, grad_gate)
+        (grad_pre,) = behind([grad_pre], mlp_own)
+    grad_mixed, grad_middle, grad_proj, misc, grad_mod = call(
         functools.partial(mlp_back, plan),
         [
-            ((n, d), BF),
             ((n, d), BF),
             ((n, d), F32),
             ((d, d), BF),
             ((16, d), F32),
-            ((group, 4 * d), F32),
+            ((group, 3 * d), F32),
         ],
-        [counts, cot, act, fc2, grad_pre, fc1, middle, attn_out, mod_second, bias, mixed, proj, grad_out],
+        [counts, cot, grad_pre, fc1, middle, attn_out, mod_second, mixed, proj, grad_out],
         [pltpu.VMEM((n, d), BF)],
         smem=(0,),
-        flops=1 << 30,
-        moved=1 << 24,
-    )
+        room=8,
+        micros=3,
+    )
+    parts = []
+    for g in range(group):
+        parts += call(
+            functools.partial(attn_back, plan, g),
+            [((plan.seq, 3 * d), BF)],
+            [projected, behind([grad_mixed], *parts)[0]],
+            room=8,
+            micros=3.3,
+        )
+    if plan.direct:
+        mlp_mine, mlp_quarters = chunk_chips(plan, mlp_own, mlp_pieces)
+        parts = behind(parts, *mlp_pieces)
     outs = call(
-        functools.partial(attn_back, plan),
+        functools.partial(attn_close, plan),
         [((halves * (4 * r + 16), d), BF)] * sides + [((n, d), BF), ((MOD_ROWS, d), BF)],
-        [x, cond, projected, grad_mixed, grad_middle, attn_in, qkv, mod_first, grad_proj, misc, grad_mod],
+        [x, cond, grad_middle, qkv, mod_first, grad_proj, misc, grad_mod, grad_gate] + parts,
         [
             pltpu.VMEM((n, 3 * d), BF),
             pltpu.VMEM((d, 3 * d), BF),
             pltpu.VMEM((MOD_ROWS, d), F32),
             pltpu.VMEM((16, d), F32),
             pltpu.VMEM((group, d), F32),
+            pltpu.VMEM((n, d), BF),
         ],
-        flops=1 << 30,
-        moved=1 << 24,
+        room=8,
+        micros=3,
     )
     last_chunk = outs[:sides]
     latents_grad, mods = outs[sides:]
     (cond_grad,) = call(
-        functools.partial(cond_back, plan), [((group, d), BF)], [cond, mods, ada_first, ada_second]
+        functools.partial(cond_back, plan), [((group, d), BF)], [cond, mods, ada_first, ada_second],
+        micros=2,
     )
     if plan.direct:
-        (fc2_grad,) = reduce_chunk(plan, *fc2_chunk, ((1, plan.ffb * r),))
-        (fc1_grad,) = reduce_chunk(plan, *fc1_chunk, ((plan.ffb, r),))
+        layout = ((plan.ffb, r), (1, plan.ffb * r))
+        fc1_grad, fc2_grad = chunk_groups(plan, mlp_mine, mlp_quarters, layout)
         qkv_grad, proj_grad, ada_grad, bias_grads = reduce_last(plan, *last_chunk, mods)
         weight_grads = [ada_grad, qkv_grad, proj_grad, fc1_grad, fc2_grad]
         grads = [grad for pair in zip(weight_grads, bias_grads) for grad in pair]
     else:
-        grads = reduce_whole(plan, fc2_chunk[0], fc1_chunk[0], last_chunk[0], mods)
+        grads = reduce_whole(plan, mlp_chunk[0], last_chunk[0], mods)
     return (
         block_out.reshape(latents.shape),
         latents_grad.reshape(latents.shape),

time: 182 us -> 133 us (0.73)
  Pallas kernels: 74 us -> 38.1 us
  starting transfers between devices: 56.6 us -> 37.4 us
  waiting for transfers between devices: 35.2 us -> 48.7 us
  local copies, waits for them, and re-layouts: 9.7 us -> 5.67 us
  other arithmetic: 4.59 us -> 1.42 us
    pallas_call x20, Pallas kernels: 74 us -> 38.1 us  [call(): pl.pallas_call(body, out_shape=[jax.ShapeDtypeStruct(shape, kind) for sha...]
    ppermute x52 -> x32, starting transfers between devices: 56.6 us -> 37.4 us  [swap(): return lax.ppermute(value, axis, [(i, i ^ k) for i in range(size)])]
    ppermute x52 -> x32, waiting for transfers between devices: 35.2 us -> 48.7 us  [swap(): return lax.ppermute(value, axis, [(i, i ^ k) for i in range(size)])]
    unnamed x111 -> x33, local copies, waits for them, and re-layouts: 8.91 us -> 5.09 us
    another operation x5 -> x0, other arithmetic: 3.31 us -> none  [shards(): rows = jnp.stack(rows + [jnp.zeros_like(rows[0])] * 3)]
  transfers between devices with their start and end apart: 52 -> 32, of which waited for: 12 -> 22; matrix products, arithmetic and copies ran while one was open for 4% -> 0% of each run, Pallas kernels for 25% -> 15%
where the time goes in v2:
time: 133 us; the launch traced here: 132 us
  waiting for transfers between devices  48.7 us (37%)
  Pallas kernels  38.1 us (29%)
  starting transfers between devices  37.4 us (28%)
  local copies, waits for them, and re-layouts  5.67 us (4%)
  other arithmetic  1.42 us (1%)
    ppermute x32, waiting for transfers between devices, swap(): return lax.ppermute(value, axis, [(i, i ^ k) for i in range(size)])  48.7 us
    pallas_call x20, Pallas kernels, call(): pl.pallas_call(body, out_shape=[jax.ShapeDtypeStruct(shape, kind) for sha...  38.1 us
    ppermute x32, starting transfers between devices, swap(): return lax.ppermute(value, axis, [(i, i ^ k) for i in range(size)])  37.4 us
    unnamed x33, local copies, waits for them, and re-layouts  5.09 us
  transfers between devices with their start and end apart: 32, of which 22 were waited for; matrix products, arithmetic and copies ran while one was open for 0% of the time, Pallas kernels for 15%

profile of v2, /device:TPU:0, one launch (start us, length us, event | category | flops | bytes accessed | tf_op | source)
XLA Modules:
  0.0 132.2 jit_solution(9308638474775821036)
XLA Ops:
  0.6 0.8 convert_add_fusion
  1.5 0.6 broadcast_in_dim.3.biases
  2.1 2.9 %shard_map.237 = (bf16[256,384]{1,0:T(8,128)(2,1)}, bf16[624,384]{1,0:T(8,128)(2,1)}) custom-call(bf16[48,2304]{1,0:T(8,128)(2,1)} %ada.1, bf16[48,1152]{1,0:T(8,128)(2,1)} %qkv.1, bf16[48,384]{1,0:T(8,128)(2,1)} %proj.1, bf16[48,1536]{1,0:T(8,128)(2,1)} %fc1.1, bf16[192,384]{1,0:T(8,128)(2,1)} %fc2.1, f32[1,768]{1,0:T(1,128)} %broadcast_in_dim.3.biases), custom_call_target="tpu_custom_call" | custom-call | bytes 3690000 | tf_op jit(solution)/shard_map/pallas_call | solution.py:64
  4.9 4.0 %collective-permute-start.5 = (bf16[256,384]{1,0:T(8,128)(2,1)}, bf16[256,384]{1,0:T(8,128)(2,1)S(1)}, u32[]{:S(2)}, u32[]{:S(2)}) collective-permute-start(bf16[256,384]{1,0:T(8,128)(2,1)} %get-tuple-element.81.refs_2_), channel_id=1, source_target_pairs={{0,6},{1,7},{2,4},{3,5},{4,2},{5,3},{6,0},{7,1},{8,14},{9,15},{10,... | collective-permute-start | bytes 589832 | tf_op jit(solution)/shard_map/ppermute | solution.py:606
  8.9 0.5 collective-permute-start.3
  9.6 2.8 %collective-permute-start.9 = (bf16[624,384]{1,0:T(8,128)(2,1)}, bf16[624,384]{1,0:T(8,128)(2,1)S(1)}, u32[]{:S(2)}, u32[]{:S(2)}) collective-permute-start(bf16[624,384]{1,0:T(8,128)(2,1)} %get-tuple-element.85.refs_0_), channel_id=1, source_target_pairs={{0,6},{1,7},{2,4},{3,5},{4,2},{5,3},{6,0},{7,1},{8,14},{9,15},{10,... | collective-permute-start | bytes 1437704 | tf_op jit(solution)/shard_map/ppermute | solution.py:606
  12.4 0.5 collective-permute-start.8
  12.9 2.0 %collective-permute-done.5.refs_8_ = bf16[256,384]{1,0:T(8,128)(2,1)S(1)} collective-permute-done((bf16[256,384]{1,0:T(8,128)(2,1)}, bf16[256,384]{1,0:T(8,128)(2,1)S(1)}, u32[]{:S(2)}, u32[]{:S(2)}) %collective-permute-start.5) | collective-permute-done | bytes 196640 | tf_op jit(solution)/shard_map/ppermute | solution.py:606
  14.9 2.0 %collective-permute-start.7 = (bf16[624,384]{1,0:T(8,128)(2,1)}, bf16[624,384]{1,0:T(8,128)(2,1)S(1)}, u32[]{:S(2)}, u32[]{:S(2)}) collective-permute-start(bf16[624,384]{1,0:T(8,128)(2,1)} %get-tuple-element.85.refs_0_), channel_id=1, source_target_pairs={{0,2},{1,3},{2,0},{3,1},{4,6},{5,7},{6,4},{7,5},{8,10},{9,11},{10,... | collective-permute-start | bytes 1437704 | tf_op jit(solution)/shard_map/ppermute | solution.py:606
  16.9 2.3 %collective-permute-done.3.refs_6_ = bf16[256,384]{1,0:T(8,128)(2,1)S(1)} collective-permute-done((bf16[256,384]{1,0:T(8,128)(2,1)}, bf16[256,384]{1,0:T(8,128)(2,1)S(1)}, u32[]{:S(2)}, u32[]{:S(2)}) %collective-permute-start.3) | collective-permute-done | bytes 196640 | tf_op jit(solution)/shard_map/ppermute | solution.py:606
  19.2 0.5 collective-permute-done.1.refs_4_
  19.7 1.1 collective-permute-done.refs_3_
  21.1 0.2 collective-permute-start.2
  21.3 0.9 collective-permute-done.4.refs_7_
  22.3 0.3 collective-permute-done.2.refs_5_
  22.6 1.0 copy-done.1
  23.6 0.9 copy-done.12
  24.5 0.7 copy-done.13
  25.2 4.0 %shard_map.238 = (bf16[512,1152]{1,0:T(8,128)(2,1)S(1)}, bf16[512,384]{1,0:T(8,128)(2,1)S(1)}, f32[2,768]{1,0:T(2,128)S(1)}, f32[16,384]{1,0:T(8,128)S(1)}, bf16...) custom-call(bf16[512,384]{1,0:T(8,128)(2,1)S(1)} %bitcast.17, bf16[2,384]{1,0:T(2,128)(2,1)S(1)} %bitcast.20, ...), custom_call_target="tpu_custom_call" | custom-call | bytes 14760000 | tf_op jit(solution)/shard_map/pallas_call | solution.py:64
  29.4 9.4 %collective-permute-done.8.refs_2_ = bf16[624,384]{1,0:T(8,128)(2,1)S(1)} collective-permute-done((bf16[624,384]{1,0:T(8,128)(2,1)}, bf16[624,384]{1,0:T(8,128)(2,1)S(1)}, u32[]{:S(2)}, u32[]{:S(2)}) %collective-permute-start.8) | collective-permute-done | bytes 479264 | tf_op jit(solution)/shard_map/ppermute | solution.py:606
  38.8 0.3 collective-permute-done.7.refs_1_
  39.4 0.4 copy-done.15
  39.9 3.6 %collective-permute-done.10.refs_7_ = bf16[2496,384]{1,0:T(8,128)(2,1)} collective-permute-done((bf16[2496,384]{1,0:T(8,128)(2,1)S(1)}, bf16[2496,384]{1,0:T(8,128)(2,1)}, u32[]{:S(2)}, u32[]{:S(2)}) %collective-permute-start.10) | collective-permute-done | bytes 1916960 | tf_op jit(solution)/shard_map/ppermute | solution.py:606
  43.4 1.0 copy-done.2
  44.4 1.0 copy-done.5
  45.4 6.5 %shard_map.240 = (bf16[512,1536]{1,0:T(8,128)(2,1)S(1)}, f32[512,1536]{1,0:T(8,128)S(1)}, bf16[512,384]{1,0:T(8,128)(2,1)S(1)}, bf16[512,384]{1,0:T(8,128)(2,1)S...) custom-call(s32[2,1]{1,0:T(2,128)S(1)} %copy.28.refs_0_.counts, ...), custom_call_target="tpu_custom_call" | custom-call | bytes 22140000 | tf_op jit(solution)/shard_map/pallas_call | solution.py:64
  51.9 3.3 %shard_map.242 = (bf16[1536,384]{1,0:T(8,128)(2,1)S(1)}, bf16[1536,384]{1,0:T(8,128)(2,1)S(1)}, bf16[512,1536]{1,0:T(8,128)(2,1)S(1)}) custom-call(bf16[512,384]{1,0:T(8,128)(2,1)S(1)} %get-tuple-element.91.refs_0_.grad_out, f32[512,1536]{1,0:T(8,128)S(1)} %get-tuple-element.92.refs_1_, bf16[512,384]{1,0:T(8,128)(2,1)S(1)} %get-tuple-element.93.refs_2_, ...), custom_call_target="tpu_custom_call" | custom-call | bytes 14760000 | tf_op jit(solution)/shard_map/pallas_call | solution.py:64
  55.4 2.5 %shard_map.241 = (bf16[512,384]{1,0:T(8,128)(2,1)}, f32[2,384]{1,0:T(2,128)S(1)}) custom-call(s32[2,1]{1,0:T(2,128)S(1)} %copy.28.refs_0_.counts, bf16[512,384]{1,0:T(8,128)(2,1)S(1)} %bitcast.15, bf16[512,1536]{1,0:T(8,128)(2,1)S(1)} %get-tuple-element.86.act, bf16[1536,384]{1,0:T(8,128)(2,1)S(1)} %get-tuple-element.87.fc2.refs_4_, ...), custom_call_target="tpu_custom_call" | custom-call | bytes 5535000 | tf_op jit(solution)/shard_map/pallas_call | solution.py:64
  58.2 0.3 shard_map.243
  58.5 1.6 %collective-permute-start.12 = (bf16[384,384]{1,0:T(8,128)(2,1)S(1)}, bf16[384,384]{1,0:T(8,128)(2,1)S(1)}, u32[]{:S(2)}, u32[]{:S(2)}) collective-permute-start(bf16[384,384]{1,0:T(8,128)(2,1)S(1)} %get-tuple-element.114), channel_id=1, source_target_pairs={{0,2},{1,3},{2,0},{3,1},{4,6},{5,7},{6,4},{7,5},{8,10},{9,11},{10,... | collective-permute-start | bytes 884744 | tf_op jit(solution)/shard_map/ppermute | solution.py:606
  60.0 0.6 collective-permute-start.13
  60.6 1.4 %collective-permute-start.14 = (bf16[384,384]{1,0:T(8,128)(2,1)S(1)}, bf16[384,384]{1,0:T(8,128)(2,1)S(1)}, u32[]{:S(2)}, u32[]{:S(2)}) collective-permute-start(bf16[384,384]{1,0:T(8,128)(2,1)S(1)} %get-tuple-element.116), channel_id=1, source_target_pairs={{0,6},{1,7},{2,4},{3,5},{4,2},{5,3},{6,0},{7,1},{8,14},{9,15},{10,... | collective-permute-start | bytes 884744 | tf_op jit(solution)/shard_map/ppermute | solution.py:606
  62.0 3.3 %shard_map.244 = (bf16[512,384]{1,0:T(8,128)(2,1)S(1)}, f32[512,384]{1,0:T(8,128)S(1)}, bf16[384,384]{1,0:T(8,128)(2,1)S(1)}, f32[16,384]{1,0:T(8,128)S(1)}, f32[2,1152]{1,0:T(2,128)S(1)}) custom-call(s32[2,1]{1,0:T(2,128)S(1)} %copy.28.refs_0_.counts, bf16[512,384]{1,0:T(8,128)(2,1)S(1)} %bitcast.16, bf16[512,1536]{1,0:T(8,128)(2,1)S(1)} %get-tuple-element.102.grad_pre, ...), custom_call_target="tpu_custom_call" | custom-call | bytes 11070000 | tf_op jit(solution)/shard_map/pallas_call | solution.py:64
  65.4 3.5 %shard_map.245.refs_9_ = bf16[256,1152]{1,0:T(8,128)(2,1)S(1)} custom-call(bf16[512,1152]{1,0:T(8,128)(2,1)S(1)} %get-tuple-element.111.projected, bf16[512,384]{1,0:T(8,128)(2,1)S(1)} %get-tuple-element.113.grad_mixed), custom_call_target="tpu_custom_call" | custom-call | bytes 12177000 | tf_op jit(solution)/shard_map/pallas_call | solution.py:64
  68.9 3.5 %shard_map.246.refs_10_ = bf16[256,1152]{1,0:T(8,128)(2,1)S(1)} custom-call(bf16[512,1152]{1,0:T(8,128)(2,1)S(1)} %get-tuple-element.111.projected, bf16[512,384]{1,0:T(8,128)(2,1)S(1)} %get-tuple-element.113.grad_mixed), custom_call_target="tpu_custom_call" | custom-call | bytes 12177000 | tf_op jit(solution)/shard_map/pallas_call | solution.py:64
  72.3 2.8 %collective-permute-done.13.refs_1_ = bf16[384,384]{1,0:T(8,128)(2,1)S(1)} collective-permute-done((bf16[384,384]{1,0:T(8,128)(2,1)S(1)}, bf16[384,384]{1,0:T(8,128)(2,1)S(1)}, u32[]{:S(2)}, u32[]{:S(2)}) %collective-permute-start.13) | collective-permute-done | bytes 294944 | tf_op jit(solution)/shard_map/ppermute | solution.py:606
  75.1 2.3 %shard_map.247 = (bf16[832,384]{1,0:T(8,128)(2,1)S(1)}, bf16[832,384]{1,0:T(8,128)(2,1)S(1)}, bf16[512,384]{1,0:T(8,128)(2,1)}, bf16[16,384]{1,0:T(8,128)(2,1)S(1)}) custom-call(bf16[512,384]{1,0:T(8,128)(2,1)S(1)} %bitcast.19, bf16[2,384]{1,0:T(2,128)(2,1)S(1)} %bitcast.22, f32[512,384]{1,0:T(8,128)S(1)} %get-tuple-element.106.refs_2_, ...), custom_call_target="tpu_custom_call" | custom-call | bytes 11070000 | tf_op jit(solution)/shard_map/pallas_call | solution.py:64
  77.6 2.1 %collective-permute-done.15.received = bf16[832,384]{1,0:T(8,128)(2,1)S(1)} collective-permute-done((bf16[832,384]{1,0:T(8,128)(2,1)S(1)}, bf16[832,384]{1,0:T(8,128)(2,1)S(1)}, u32[]{:S(2)}, u32[]{:S(2)}) %collective-permute-start.15) | collective-permute-done | bytes 639008 | tf_op jit(solution)/shard_map/ppermute | solution.py:606
  79.8 0.6 collective-permute-start.16
  80.4 1.4 %collective-permute-start.17 = (bf16[224,384]{1,0:T(8,128)(2,1)S(1)}, bf16[224,384]{1,0:T(8,128)(2,1)S(1)}, u32[]{:S(2)}, u32[]{:S(2)}) collective-permute-start(bf16[224,384]{1,0:T(8,128)(2,1)S(1)} %get-tuple-element.127), channel_id=1, source_target_pairs={{0,4},{1,5},{2,6},{3,7},{4,0},{5,1},{6,2},{7,3},{8,12},{9,13},{10,... | collective-permute-start | bytes 516104 | tf_op jit(solution)/shard_map/ppermute | solution.py:606
  81.8 1.6 %collective-permute-start.18 = (bf16[224,384]{1,0:T(8,128)(2,1)S(1)}, bf16[224,384]{1,0:T(8,128)(2,1)S(1)}, u32[]{:S(2)}, u32[]{:S(2)}) collective-permute-start(bf16[224,384]{1,0:T(8,128)(2,1)S(1)} %get-tuple-element.128), channel_id=1, source_target_pairs={{0,6},{1,7},{2,4},{3,5},{4,2},{5,3},{6,0},{7,1},{8,14},{9,15},{10,... | collective-permute-start | bytes 516104 | tf_op jit(solution)/shard_map/ppermute | solution.py:606
  83.3 3.7 %collective-permute-done.16.refs_0_ = bf16[224,384]{1,0:T(8,128)(2,1)S(1)} collective-permute-done((bf16[224,384]{1,0:T(8,128)(2,1)S(1)}, bf16[224,384]{1,0:T(8,128)(2,1)S(1)}, u32[]{:S(2)}, u32[]{:S(2)}) %collective-permute-start.16) | collective-permute-done | bytes 172064 | tf_op jit(solution)/shard_map/ppermute | solution.py:606
  87.1 3.1 %collective-permute-done.17.refs_1_ = bf16[224,384]{1,0:T(8,128)(2,1)S(1)} collective-permute-done((bf16[224,384]{1,0:T(8,128)(2,1)S(1)}, bf16[224,384]{1,0:T(8,128)(2,1)S(1)}, u32[]{:S(2)}, u32[]{:S(2)}) %collective-permute-start.17) | collective-permute-done | bytes 172064 | tf_op jit(solution)/shard_map/ppermute | solution.py:606
  90.3 2.2 %collective-permute-start.19 = (bf16[128,384]{1,0:T(8,128)(2,1)S(1)}, bf16[128,384]{1,0:T(8,128)(2,1)S(1)}, u32[]{:S(2)}, u32[]{:S(2)}) collective-permute-start(bf16[128,384]{1,0:T(8,128)(2,1)S(1)} %get-tuple-element.130), channel_id=1, source_target_pairs={{0,8},{8,0},{16,24},{24,16},{1,9},{9,1},{17,25},{25,17},{2,10},{10... | collective-permute-start | bytes 294920 | tf_op jit(solution)/shard_map/ppermute | solution.py:606
  92.6 2.6 %collective-permute-start.20 = (bf16[128,384]{1,0:T(8,128)(2,1)S(1)}, bf16[128,384]{1,0:T(8,128)(2,1)S(1)}, u32[]{:S(2)}, u32[]{:S(2)}) collective-permute-start(bf16[128,384]{1,0:T(8,128)(2,1)S(1)} %get-tuple-element.131), channel_id=1, source_target_pairs={{0,16},{8,24},{16,0},{24,8},{1,17},{9,25},{17,1},{25,9},{2,18},{10... | collective-permute-start | bytes 294920 | tf_op jit(solution)/shard_map/ppermute | solution.py:606
  95.2 7.3 %collective-permute-done.20.refs_2_ = bf16[128,384]{1,0:T(8,128)(2,1)S(1)} collective-permute-done((bf16[128,384]{1,0:T(8,128)(2,1)S(1)}, bf16[128,384]{1,0:T(8,128)(2,1)S(1)}, u32[]{:S(2)}, u32[]{:S(2)}) %collective-permute-start.20) | collective-permute-done | bytes 98336 | tf_op jit(solution)/shard_map/ppermute | solution.py:606
  102.6 0.2 shard_map.254
  102.8 1.7 %collective-permute-start.26 = (bf16[96,384]{1,0:T(8,128)(2,1)S(1)}, bf16[96,384]{1,0:T(8,128)(2,1)S(1)}, u32[]{:S(2)}, u32[]{:S(2)}) collective-permute-start(bf16[96,384]{1,0:T(8,128)(2,1)S(1)} %get-tuple-element.142), channel_id=1, source_target_pairs={{0,8},{8,0},{16,24},{24,16},{1,9},{9,1},{17,25},{25,17},{2,10},{10... | collective-permute-start | bytes 221192 | tf_op jit(solution)/shard_map/ppermute | solution.py:606
  104.5 1.4 %collective-permute-start.27 = (bf16[96,384]{1,0:T(8,128)(2,1)S(1)}, bf16[96,384]{1,0:T(8,128)(2,1)S(1)}, u32[]{:S(2)}, u32[]{:S(2)}) collective-permute-start(bf16[96,384]{1,0:T(8,128)(2,1)S(1)} %get-tuple-element.143), channel_id=1, source_target_pairs={{0,16},{8,24},{16,0},{24,8},{1,17},{9,25},{17,1},{25,9},{2,18},{10... | collective-permute-start | bytes 221192 | tf_op jit(solution)/shard_map/ppermute | solution.py:606
  105.9 1.3 %collective-permute-start.28 = (bf16[96,384]{1,0:T(8,128)(2,1)S(1)}, bf16[96,384]{1,0:T(8,128)(2,1)S(1)}, u32[]{:S(2)}, u32[]{:S(2)}) collective-permute-start(bf16[96,384]{1,0:T(8,128)(2,1)S(1)} %get-tuple-element.144), channel_id=1, source_target_pairs={{0,24},{8,16},{16,8},{24,0},{1,25},{9,17},{17,9},{25,1},{2,26},{10... | collective-permute-start | bytes 221192 | tf_op jit(solution)/shard_map/ppermute | solution.py:606
  107.3 0.3 collective-permute-done.26.refs_1_
  107.6 5.9 %collective-permute-done.27.refs_2_ = bf16[96,384]{1,0:T(8,128)(2,1)S(1)} collective-permute-done((bf16[96,384]{1,0:T(8,128)(2,1)S(1)}, bf16[96,384]{1,0:T(8,128)(2,1)S(1)}, u32[]{:S(2)}, u32[]{:S(2)}) %collective-permute-start.27) | collective-permute-done | bytes 73760 | tf_op jit(solution)/shard_map/ppermute | solution.py:606
  113.5 2.4 %collective-permute-start.31 = (bf16[96,384]{1,0:T(8,128)(2,1)S(1)}, bf16[96,384]{1,0:T(8,128)(2,1)S(1)}, u32[]{:S(2)}, u32[]{:S(2)}) collective-permute-start(bf16[96,384]{1,0:T(8,128)(2,1)S(1)} %shard_map.255.refs_0_), channel_id=1, source_target_pairs={{0,24},{8,16},{16,8},{24,0},{1,25},{9,17},{17,9},{25,1},{2,26},{10... | collective-permute-start | bytes 221192 | tf_op jit(solution)/shard_map/ppermute | solution.py:606
  115.8 0.8 collective-permute-start.30
  116.7 1.3 collective-permute-start.29
  117.9 2.3 %collective-permute-start.25 = (bf16[48,384]{1,0:T(8,128)(2,1)S(1)}, bf16[48,384]{1,0:T(8,128)(2,1)S(1)}, u32[]{:S(2)}, u32[]{:S(2)}) collective-permute-start(bf16[48,384]{1,0:T(8,128)(2,1)S(1)} %get-tuple-element.136.refs_0_), channel_id=1, source_target_pairs={{0,24},{8,16},{16,8},{24,0},{1,25},{9,17},{17,9},{25,1},{2,26},{10... | collective-permute-start | bytes 110600 | tf_op jit(solution)/shard_map/ppermute | solution.py:606
  120.4 3.5 %collective-permute-start.24 = (bf16[48,384]{1,0:T(8,128)(2,1)S(1)}, bf16[48,384]{1,0:T(8,128)(2,1)S(1)}, u32[]{:S(2)}, u32[]{:S(2)}) collective-permute-start(bf16[48,384]{1,0:T(8,128)(2,1)S(1)} %get-tuple-element.136.refs_0_), channel_id=1, source_target_pairs={{0,16},{8,24},{16,0},{24,8},{1,17},{9,25},{17,1},{25,9},{2,18},{10... | collective-permute-start | bytes 110600 | tf_op jit(solution)/shard_map/ppermute | solution.py:606
  123.9 1.0 collective-permute-done.30.refs_2_
  125.0 1.7 %shard_map.248 = bf16[2,384]{1,0:T(2,128)(2,1)} custom-call(bf16[2,384]{1,0:T(2,128)(2,1)S(1)} %bitcast.23, bf16[16,384]{1,0:T(8,128)(2,1)S(1)} %get-tuple-element.120.mods, bf16[384,768]{1,0:T(8,128)(2,1)S(1)} %copy-done.10, bf16[384,1536]{1,0:T(8,128)(2,1)S(1)} %get-tuple-element.122.second), custom_call_target="tpu_custom_call" | custom-call | bytes 7380000 | tf_op jit(solution)/shard_map/pallas_call | solution.py:64
  126.7 0.9 shard_map.256
  127.6 1.4 %collective-permute-done.23.refs_1_ = bf16[48,384]{1,0:T(8,128)(2,1)S(1)} collective-permute-done((bf16[48,384]{1,0:T(8,128)(2,1)S(1)}, bf16[48,384]{1,0:T(8,128)(2,1)S(1)}, u32[]{:S(2)}, u32[]{:S(2)}) %collective-permute-start.23) | collective-permute-done | bytes 36896 | tf_op jit(solution)/shard_map/ppermute | solution.py:606
  128.9 0.7 shard_map.253
  129.7 1.9 %shard_map.252 = (f32[48,2304]{1,0:T(8,128)}, f32[1,288]{1,0:T(1,128)S(1)}, f32[1,96]{1,0:T(1,128)}, f32[1,48]{1,0:T(1,128)}, f32[1,192]{1,0:T(1,128)}, /*index=5*/f32[1,48]{1,0:T(1,128)}) custom-call(f32[128,384]{1,0:T(8,128)S(1)} %get-tuple-element.129.refs_0_, bf16[128,384]{1,0:T(8,128)(2,1)S(1)} %collective-permute-done.19.refs_1_, ...), custom_call_target="tpu_custom_call" | custom-call | bytes 7380000 | tf_op jit(solution)/shard_map/pallas_call | solution.py:64
  131.6 0.6 reduce
  (56 shorter events, 2.1 us)
Async XLA Ops:
  4.9 9.9 %collective-permute-start.5 = (bf16[256,384]{1,0:T(8,128)(2,1)}, bf16[256,384]{1,0:T(8,128)(2,1)S(1)}, u32[]{:S(2)}, u32[]{:S(2)}) collective-permute-start(bf16[256,384]{1,0:T(8,128)(2,1)} %get-tuple-element.81.refs_2_), channel_id=1, source_target_pairs={{0,6},{1,7},{2,4},{3,5},{4,2},{5,3},{6,0},{7,1},{8,14},{9,15},{10,... | collective-permute-start | bytes 589832 | tf_op jit(solution)/shard_map/ppermute | solution.py:606
  8.9 10.3 %collective-permute-start.3 = (bf16[256,384]{1,0:T(8,128)(2,1)}, bf16[256,384]{1,0:T(8,128)(2,1)S(1)}, u32[]{:S(2)}, u32[]{:S(2)}) collective-permute-start(bf16[256,384]{1,0:T(8,128)(2,1)} %get-tuple-element.81.refs_2_), channel_id=1, source_target_pairs={{0,4},{1,5},{2,6},{3,7},{4,0},{5,1},{6,2},{7,3},{8,12},{9,13},{10,... | collective-permute-start | bytes 589832 | tf_op jit(solution)/shard_map/ppermute | solution.py:606
  9.4 10.3 %collective-permute-start.1 = (bf16[256,384]{1,0:T(8,128)(2,1)}, bf16[256,384]{1,0:T(8,128)(2,1)S(1)}, u32[]{:S(2)}, u32[]{:S(2)}) collective-permute-start(bf16[256,384]{1,0:T(8,128)(2,1)} %get-tuple-element.81.refs_2_), channel_id=1, source_target_pairs={{0,2},{1,3},{2,0},{3,1},{4,6},{5,7},{6,4},{7,5},{8,10},{9,11},{10,... | collective-permute-start | bytes 589832 | tf_op jit(solution)/shard_map/ppermute | solution.py:606
  9.6 19.9 %collective-permute-start.9 = (bf16[624,384]{1,0:T(8,128)(2,1)}, bf16[624,384]{1,0:T(8,128)(2,1)S(1)}, u32[]{:S(2)}, u32[]{:S(2)}) collective-permute-start(bf16[624,384]{1,0:T(8,128)(2,1)} %get-tuple-element.85.refs_0_), channel_id=1, source_target_pairs={{0,6},{1,7},{2,4},{3,5},{4,2},{5,3},{6,0},{7,1},{8,14},{9,15},{10,... | collective-permute-start | bytes 1437704 | tf_op jit(solution)/shard_map/ppermute | solution.py:606
  12.4 26.4 %collective-permute-start.8 = (bf16[624,384]{1,0:T(8,128)(2,1)}, bf16[624,384]{1,0:T(8,128)(2,1)S(1)}, u32[]{:S(2)}, u32[]{:S(2)}) collective-permute-start(bf16[624,384]{1,0:T(8,128)(2,1)} %get-tuple-element.85.refs_0_), channel_id=1, source_target_pairs={{0,4},{1,5},{2,6},{3,7},{4,0},{5,1},{6,2},{7,3},{8,12},{9,13},{10,... | collective-permute-start | bytes 1437704 | tf_op jit(solution)/shard_map/ppermute | solution.py:606
  14.9 24.2 %collective-permute-start.7 = (bf16[624,384]{1,0:T(8,128)(2,1)}, bf16[624,384]{1,0:T(8,128)(2,1)S(1)}, u32[]{:S(2)}, u32[]{:S(2)}) collective-permute-start(bf16[624,384]{1,0:T(8,128)(2,1)} %get-tuple-element.85.refs_0_), channel_id=1, source_target_pairs={{0,2},{1,3},{2,0},{3,1},{4,6},{5,7},{6,4},{7,5},{8,10},{9,11},{10,... | collective-permute-start | bytes 1437704 | tf_op jit(solution)/shard_map/ppermute | solution.py:606
  19.2 1.7 %collective-permute-start = (bf16[256,384]{1,0:T(8,128)(2,1)}, bf16[256,384]{1,0:T(8,128)(2,1)S(1)}, u32[]{:S(2)}, u32[]{:S(2)}) collective-permute-start(bf16[256,384]{1,0:T(8,128)(2,1)} %get-tuple-element.81.refs_2_), channel_id=1, source_target_pairs={{0,1},{1,0},{2,3},{3,2},{4,5},{5,4},{6,7},{7,6},{8,9},{9,8},{10,11... | collective-permute-start | bytes 589832 | tf_op jit(solution)/shard_map/ppermute | solution.py:606
  19.7 1.4 %collective-permute-start.6 = (bf16[256,384]{1,0:T(8,128)(2,1)S(1)}, bf16[256,384]{1,0:T(8,128)(2,1)S(1)}, u32[]{:S(2)}, u32[]{:S(2)}) collective-permute-start(bf16[256,384]{1,0:T(8,128)(2,1)S(1)} %collective-permute-done.5.refs_8_), channel_id=1, source_target_pairs={{0,1},{1,0},{2,3},{3,2},{4,5},{5,4},{6,7},{7,6},{8,9},{9,8},{10,11... | collective-permute-start | bytes 589832 | tf_op jit(solution)/shard_map/ppermute | solution.py:606
  20.8 1.4 %collective-permute-start.4 = (bf16[256,384]{1,0:T(8,128)(2,1)S(1)}, bf16[256,384]{1,0:T(8,128)(2,1)S(1)}, u32[]{:S(2)}, u32[]{:S(2)}) collective-permute-start(bf16[256,384]{1,0:T(8,128)(2,1)S(1)} %collective-permute-done.3.refs_6_), channel_id=1, source_target_pairs={{0,1},{1,0},{2,3},{3,2},{4,5},{5,4},{6,7},{7,6},{8,9},{9,8},{10,11... | collective-permute-start | bytes 589832 | tf_op jit(solution)/shard_map/ppermute | solution.py:606
  21.1 1.4 %collective-permute-start.2 = (bf16[256,384]{1,0:T(8,128)(2,1)S(1)}, bf16[256,384]{1,0:T(8,128)(2,1)S(1)}, u32[]{:S(2)}, u32[]{:S(2)}) collective-permute-start(bf16[256,384]{1,0:T(8,128)(2,1)S(1)} %collective-permute-done.1.refs_4_), channel_id=1, source_target_pairs={{0,1},{1,0},{2,3},{3,2},{4,5},{5,4},{6,7},{7,6},{8,9},{9,8},{10,11... | collective-permute-start | bytes 589832 | tf_op jit(solution)/shard_map/ppermute | solution.py:606
  22.6 1.0 copy-start.1
  23.6 0.9 copy-start.12
  24.5 0.7 copy-start.13
  25.2 13.9 %copy-start.11 = (bf16[624,384]{1,0:T(8,128)(2,1)S(1)}, bf16[624,384]{1,0:T(8,128)(2,1)}, u32[]{:S(2)}) copy-start(bf16[624,384]{1,0:T(8,128)(2,1)} %get-tuple-element.85.refs_0_) | copy-start | bytes 1437700
  29.2 10.1 %copy-start.4 = (bf16[512,384]{1,0:T(8,128)(2,1)}, bf16[512,384]{1,0:T(8,128)(2,1)S(1)}, u32[]{:S(2)}) copy-start(bf16[512,384]{1,0:T(8,128)(2,1)S(1)} %get-tuple-element.82.refs_4_.mixed) | copy-start | bytes 1179652
  29.2 10.1 %copy-start.7 = (bf16[384,1152]{1,0:T(8,128)(2,1)}, bf16[384,1152]{1,0:T(8,128)(2,1)S(1)}, u32[]{:S(2)}) copy-start(bf16[384,1152]{1,0:T(8,128)(2,1)S(1)} %get-tuple-element.107.refs_3_) | copy-start | bytes 2654212
  29.2 10.1 %copy-start.9 = (bf16[384,768]{1,0:T(8,128)(2,1)}, bf16[384,768]{1,0:T(8,128)(2,1)S(1)}, u32[]{:S(2)}) copy-start(bf16[384,768]{1,0:T(8,128)(2,1)S(1)} %get-tuple-element.121.first) | copy-start | bytes 1769476
  39.1 0.7 copy-start.15
  39.1 4.3 %copy-start = (bf16[2,1,256,384]{3,2,1,0:T(8,128)(2,1)S(1)}, bf16[2,1,256,384]{3,2,1,0:T(8,128)(2,1)}, u32[]{:S(2)}) copy-start(bf16[2,1,256,384]{3,2,1,0:T(8,128)(2,1)} %param.16) | copy-start | bytes 1179652
  39.1 4.3 %copy-start.14 = (bf16[2,1,384]{2,0,1:T(2,128)(2,1)S(1)}, bf16[2,1,384]{2,0,1:T(2,128)(2,1)}, u32[]{:S(2)}) copy-start(bf16[2,1,384]{2,0,1:T(2,128)(2,1)} %param.15) | copy-start | bytes 4612
  39.3 4.1 %collective-permute-start.10 = (bf16[2496,384]{1,0:T(8,128)(2,1)S(1)}, bf16[2496,384]{1,0:T(8,128)(2,1)}, u32[]{:S(2)}, u32[]{:S(2)}) collective-permute-start(bf16[2496,384]{1,0:T(8,128)(2,1)S(1)} %shard_map.239.refs_6_), channel_id=1, source_target_pairs={{0,1},{1,0},{2,3},{3,2},{4,5},{5,4},{6,7},{7,6},{8,9},{9,8},{10,11... | collective-permute-start | bytes 5750792 | tf_op jit(solution)/shard_map/ppermute | solution.py:606
  43.4 1.0 copy-start.2
  44.4 1.0 copy-start.5
  55.2 2.9 %collective-permute-start.11 = (bf16[1536,384]{1,0:T(8,128)(2,1)S(1)}, bf16[1536,384]{1,0:T(8,128)(2,1)S(1)}, u32[]{:S(2)}, u32[]{:S(2)}) collective-permute-start(bf16[1536,384]{1,0:T(8,128)(2,1)S(1)} %get-tuple-element.97), channel_id=1, source_target_pairs={{0,1},{1,0},{2,3},{3,2},{4,5},{5,4},{6,7},{7,6},{8,9},{9,8},{10,11... | collective-permute-start | bytes 3538952 | tf_op jit(solution)/shard_map/ppermute | solution.py:606
  58.1 3.9 %copy-start.6 = (bf16[512,384]{1,0:T(8,128)(2,1)S(1)}, bf16[512,384]{1,0:T(8,128)(2,1)}, u32[]{:S(2)}) copy-start(bf16[512,384]{1,0:T(8,128)(2,1)} %copy-done.4) | copy-start | bytes 1179652
  58.5 13.9 %collective-permute-start.12 = (bf16[384,384]{1,0:T(8,128)(2,1)S(1)}, bf16[384,384]{1,0:T(8,128)(2,1)S(1)}, u32[]{:S(2)}, u32[]{:S(2)}) collective-permute-start(bf16[384,384]{1,0:T(8,128)(2,1)S(1)} %get-tuple-element.114), channel_id=1, source_target_pairs={{0,2},{1,3},{2,0},{3,1},{4,6},{5,7},{6,4},{7,5},{8,10},{9,11},{10,... | collective-permute-start | bytes 884744 | tf_op jit(solution)/shard_map/ppermute | solution.py:606
  60.0 15.1 %collective-permute-start.13 = (bf16[384,384]{1,0:T(8,128)(2,1)S(1)}, bf16[384,384]{1,0:T(8,128)(2,1)S(1)}, u32[]{:S(2)}, u32[]{:S(2)}) collective-permute-start(bf16[384,384]{1,0:T(8,128)(2,1)S(1)} %get-tuple-element.115), channel_id=1, source_target_pairs={{0,4},{1,5},{2,6},{3,7},{4,0},{5,1},{6,2},{7,3},{8,12},{9,13},{10,... | collective-permute-start | bytes 884744 | tf_op jit(solution)/shard_map/ppermute | solution.py:606
  60.6 14.6 %collective-permute-start.14 = (bf16[384,384]{1,0:T(8,128)(2,1)S(1)}, bf16[384,384]{1,0:T(8,128)(2,1)S(1)}, u32[]{:S(2)}, u32[]{:S(2)}) collective-permute-start(bf16[384,384]{1,0:T(8,128)(2,1)S(1)} %get-tuple-element.116), channel_id=1, source_target_pairs={{0,6},{1,7},{2,4},{3,5},{4,2},{5,3},{6,0},{7,1},{8,14},{9,15},{10,... | collective-permute-start | bytes 884744 | tf_op jit(solution)/shard_map/ppermute | solution.py:606
  68.8 6.3 %copy-start.3 = (bf16[2,1,256,384]{3,2,1,0:T(8,128)(2,1)S(1)}, bf16[2,1,256,384]{3,2,1,0:T(8,128)(2,1)}, u32[]{:S(2)}) copy-start(bf16[2,1,256,384]{3,2,1,0:T(8,128)(2,1)} %param.14) | copy-start | bytes 1179652
  68.8 6.3 %copy-start.8 = (bf16[384,1152]{1,0:T(8,128)(2,1)S(1)}, bf16[384,1152]{1,0:T(8,128)(2,1)}, u32[]{:S(2)}) copy-start(bf16[384,1152]{1,0:T(8,128)(2,1)} %copy-done.7) | copy-start | bytes 2654212
  77.5 2.1 %collective-permute-start.15 = (bf16[832,384]{1,0:T(8,128)(2,1)S(1)}, bf16[832,384]{1,0:T(8,128)(2,1)S(1)}, u32[]{:S(2)}, u32[]{:S(2)}) collective-permute-start(bf16[832,384]{1,0:T(8,128)(2,1)S(1)} %get-tuple-element.124), channel_id=1, source_target_pairs={{0,1},{1,0},{2,3},{3,2},{4,5},{5,4},{6,7},{7,6},{8,9},{9,8},{10,11... | collective-permute-start | bytes 1916936 | tf_op jit(solution)/shard_map/ppermute | solution.py:606
  79.8 7.3 %collective-permute-start.16 = (bf16[224,384]{1,0:T(8,128)(2,1)S(1)}, bf16[224,384]{1,0:T(8,128)(2,1)S(1)}, u32[]{:S(2)}, u32[]{:S(2)}) collective-permute-start(bf16[224,384]{1,0:T(8,128)(2,1)S(1)} %get-tuple-element.126), channel_id=1, source_target_pairs={{0,2},{1,3},{2,0},{3,1},{4,6},{5,7},{6,4},{7,5},{8,10},{9,11},{10,... | collective-permute-start | bytes 516104 | tf_op jit(solution)/shard_map/ppermute | solution.py:606
  80.4 9.8 %collective-permute-start.17 = (bf16[224,384]{1,0:T(8,128)(2,1)S(1)}, bf16[224,384]{1,0:T(8,128)(2,1)S(1)}, u32[]{:S(2)}, u32[]{:S(2)}) collective-permute-start(bf16[224,384]{1,0:T(8,128)(2,1)S(1)} %get-tuple-element.127), channel_id=1, source_target_pairs={{0,4},{1,5},{2,6},{3,7},{4,0},{5,1},{6,2},{7,3},{8,12},{9,13},{10,... | collective-permute-start | bytes 516104 | tf_op jit(solution)/shard_map/ppermute | solution.py:606
  81.8 8.4 %collective-permute-start.18 = (bf16[224,384]{1,0:T(8,128)(2,1)S(1)}, bf16[224,384]{1,0:T(8,128)(2,1)S(1)}, u32[]{:S(2)}, u32[]{:S(2)}) collective-permute-start(bf16[224,384]{1,0:T(8,128)(2,1)S(1)} %get-tuple-element.128), channel_id=1, source_target_pairs={{0,6},{1,7},{2,4},{3,5},{4,2},{5,3},{6,0},{7,1},{8,14},{9,15},{10,... | collective-permute-start | bytes 516104 | tf_op jit(solution)/shard_map/ppermute | solution.py:606
  90.3 4.8 %collective-permute-start.19 = (bf16[128,384]{1,0:T(8,128)(2,1)S(1)}, bf16[128,384]{1,0:T(8,128)(2,1)S(1)}, u32[]{:S(2)}, u32[]{:S(2)}) collective-permute-start(bf16[128,384]{1,0:T(8,128)(2,1)S(1)} %get-tuple-element.130), channel_id=1, source_target_pairs={{0,8},{8,0},{16,24},{24,16},{1,9},{9,1},{17,25},{25,17},{2,10},{10... | collective-permute-start | bytes 294920 | tf_op jit(solution)/shard_map/ppermute | solution.py:606
  92.6 9.9 %collective-permute-start.20 = (bf16[128,384]{1,0:T(8,128)(2,1)S(1)}, bf16[128,384]{1,0:T(8,128)(2,1)S(1)}, u32[]{:S(2)}, u32[]{:S(2)}) collective-permute-start(bf16[128,384]{1,0:T(8,128)(2,1)S(1)} %get-tuple-element.131), channel_id=1, source_target_pairs={{0,16},{8,24},{16,0},{24,8},{1,17},{9,25},{17,1},{25,9},{2,18},{10... | collective-permute-start | bytes 294920 | tf_op jit(solution)/shard_map/ppermute | solution.py:606
  95.2 7.3 %collective-permute-start.21 = (bf16[128,384]{1,0:T(8,128)(2,1)S(1)}, bf16[128,384]{1,0:T(8,128)(2,1)S(1)}, u32[]{:S(2)}, u32[]{:S(2)}) collective-permute-start(bf16[128,384]{1,0:T(8,128)(2,1)S(1)} %get-tuple-element.132), channel_id=1, source_target_pairs={{0,24},{8,16},{16,8},{24,0},{1,25},{9,17},{17,9},{25,1},{2,26},{10... | collective-permute-start | bytes 294920 | tf_op jit(solution)/shard_map/ppermute | solution.py:606
  102.5 22.5 %copy-start.10 = (bf16[384,768]{1,0:T(8,128)(2,1)S(1)}, bf16[384,768]{1,0:T(8,128)(2,1)}, u32[]{:S(2)}) copy-start(bf16[384,768]{1,0:T(8,128)(2,1)} %copy-done.9) | copy-start | bytes 1769476
  102.5 27.2 %collective-permute-start.22 = (bf16[256,384]{1,0:T(8,128)(2,1)S(1)}, bf16[256,384]{1,0:T(8,128)(2,1)S(1)}, u32[]{:S(2)}, u32[]{:S(2)}) collective-permute-start(bf16[256,384]{1,0:T(8,128)(2,1)S(1)} %get-tuple-element.133.refs_4_), channel_id=1, source_target_pairs={{0,1},{1,0},{2,3},{3,2},{4,5},{5,4},{6,7},{7,6},{8,9},{9,8},{10,11... | collective-permute-start | bytes 589832 | tf_op jit(solution)/shard_map/ppermute | solution.py:606
  102.8 4.7 %collective-permute-start.26 = (bf16[96,384]{1,0:T(8,128)(2,1)S(1)}, bf16[96,384]{1,0:T(8,128)(2,1)S(1)}, u32[]{:S(2)}, u32[]{:S(2)}) collective-permute-start(bf16[96,384]{1,0:T(8,128)(2,1)S(1)} %get-tuple-element.142), channel_id=1, source_target_pairs={{0,8},{8,0},{16,24},{24,16},{1,9},{9,1},{17,25},{25,17},{2,10},{10... | collective-permute-start | bytes 221192 | tf_op jit(solution)/shard_map/ppermute | solution.py:606
  104.5 8.9 %collective-permute-start.27 = (bf16[96,384]{1,0:T(8,128)(2,1)S(1)}, bf16[96,384]{1,0:T(8,128)(2,1)S(1)}, u32[]{:S(2)}, u32[]{:S(2)}) collective-permute-start(bf16[96,384]{1,0:T(8,128)(2,1)S(1)} %get-tuple-element.143), channel_id=1, source_target_pairs={{0,16},{8,24},{16,0},{24,8},{1,17},{9,25},{17,1},{25,9},{2,18},{10... | collective-permute-start | bytes 221192 | tf_op jit(solution)/shard_map/ppermute | solution.py:606
  105.9 7.5 %collective-permute-start.28 = (bf16[96,384]{1,0:T(8,128)(2,1)S(1)}, bf16[96,384]{1,0:T(8,128)(2,1)S(1)}, u32[]{:S(2)}, u32[]{:S(2)}) collective-permute-start(bf16[96,384]{1,0:T(8,128)(2,1)S(1)} %get-tuple-element.144), channel_id=1, source_target_pairs={{0,24},{8,16},{16,8},{24,0},{1,25},{9,17},{17,9},{25,1},{2,26},{10... | collective-permute-start | bytes 221192 | tf_op jit(solution)/shard_map/ppermute | solution.py:606
  113.5 6.9 %collective-permute-start.31 = (bf16[96,384]{1,0:T(8,128)(2,1)S(1)}, bf16[96,384]{1,0:T(8,128)(2,1)S(1)}, u32[]{:S(2)}, u32[]{:S(2)}) collective-permute-start(bf16[96,384]{1,0:T(8,128)(2,1)S(1)} %shard_map.255.refs_0_), channel_id=1, source_target_pairs={{0,24},{8,16},{16,8},{24,0},{1,25},{9,17},{17,9},{25,1},{2,26},{10... | collective-permute-start | bytes 221192 | tf_op jit(solution)/shard_map/ppermute | solution.py:606
  115.8 9.1 %collective-permute-start.30 = (bf16[96,384]{1,0:T(8,128)(2,1)S(1)}, bf16[96,384]{1,0:T(8,128)(2,1)S(1)}, u32[]{:S(2)}, u32[]{:S(2)}) collective-permute-start(bf16[96,384]{1,0:T(8,128)(2,1)S(1)} %shard_map.255.refs_0_), channel_id=1, source_target_pairs={{0,16},{8,24},{16,0},{24,8},{1,17},{9,25},{17,1},{25,9},{2,18},{10... | collective-permute-start | bytes 221192 | tf_op jit(solution)/shard_map/ppermute | solution.py:606
  116.7 10.0 %collective-permute-start.29 = (bf16[96,384]{1,0:T(8,128)(2,1)S(1)}, bf16[96,384]{1,0:T(8,128)(2,1)S(1)}, u32[]{:S(2)}, u32[]{:S(2)}) collective-permute-start(bf16[96,384]{1,0:T(8,128)(2,1)S(1)} %shard_map.255.refs_0_), channel_id=1, source_target_pairs={{0,8},{8,0},{16,24},{24,16},{1,9},{9,1},{17,25},{25,17},{2,10},{10... | collective-permute-start | bytes 221192 | tf_op jit(solution)/shard_map/ppermute | solution.py:606
  117.9 9.6 %collective-permute-start.25 = (bf16[48,384]{1,0:T(8,128)(2,1)S(1)}, bf16[48,384]{1,0:T(8,128)(2,1)S(1)}, u32[]{:S(2)}, u32[]{:S(2)}) collective-permute-start(bf16[48,384]{1,0:T(8,128)(2,1)S(1)} %get-tuple-element.136.refs_0_), channel_id=1, source_target_pairs={{0,24},{8,16},{16,8},{24,0},{1,25},{9,17},{17,9},{25,1},{2,26},{10... | collective-permute-start | bytes 110600 | tf_op jit(solution)/shard_map/ppermute | solution.py:606
  120.4 7.2 %collective-permute-start.24 = (bf16[48,384]{1,0:T(8,128)(2,1)S(1)}, bf16[48,384]{1,0:T(8,128)(2,1)S(1)}, u32[]{:S(2)}, u32[]{:S(2)}) collective-permute-start(bf16[48,384]{1,0:T(8,128)(2,1)S(1)} %get-tuple-element.136.refs_0_), channel_id=1, source_target_pairs={{0,16},{8,24},{16,0},{24,8},{1,17},{9,25},{17,1},{25,9},{2,18},{10... | collective-permute-start | bytes 110600 | tf_op jit(solution)/shard_map/ppermute | solution.py:606
  125.0 4.0 %collective-permute-start.23 = (bf16[48,384]{1,0:T(8,128)(2,1)S(1)}, bf16[48,384]{1,0:T(8,128)(2,1)S(1)}, u32[]{:S(2)}, u32[]{:S(2)}) collective-permute-start(bf16[48,384]{1,0:T(8,128)(2,1)S(1)} %get-tuple-element.136.refs_0_), channel_id=1, source_target_pairs={{0,8},{8,0},{16,24},{24,16},{1,9},{9,1},{17,25},{25,17},{2,10},{10... | collective-permute-start | bytes 110600 | tf_op jit(solution)/shard_map/ppermute | solution.py:606

commit v3 on v2

--- a/solution.py
+++ b/solution.py
@@ -14,7 +14,7 @@
 F32 = jnp.float32
 SQRT_2_PI = 0.7978845608028654
 CUBIC = 0.044715
-MARGIN = 0.25
+MARGIN = 0.0
 PACK_LIMIT = 56 * 1024 * 1024
 MOD_ROWS = 16
 
@@ -61,7 +61,7 @@
 
     held = sum(size(v.shape, v.dtype) for v in scratch if len(v.shape) > 1)
     held += MARGIN * (sum(size(v.shape, v.dtype) for v in ins) + sum(size(*out) for out in outs))
-    return pl.pallas_call(
+    made = pl.pallas_call(
         body,
         out_shape=[jax.ShapeDtypeStruct(shape, kind) for shape, kind in outs],
         in_specs=specs,
@@ -75,6 +75,7 @@
             flops=0, bytes_accessed=int(micros * 3.69e6), transcendentals=0
         ),
     )(*ins)
+    return list(made)
 
 
 class Plan:
@@ -101,7 +102,9 @@
     return lax.axis_index("fsdp") ^ k
 
 
-def pack_weights(plan, ada, qkv, proj, fc1, fc2, biases, first, second, rows_s, sems):
+def pack_weights(
+    plan, ada, qkv, proj, fc1, fc2, biases, counts, first, second, live, rows_s, sems
+):
     d, r = plan.d, plan.rows
 
     def cut(ref, start, stop):
@@ -119,6 +122,9 @@
             at += block.shape[0]
     for copy in copies:
         copy.start()
+    for g in range(plan.group):
+        alive = jnp.where(g % plan.slots < counts[0, g // plan.slots], 1.0, 0.0).astype(F32)
+        live[g : g + 1, :] = jnp.full((1, 128), alive)
     rows_s[...] = jnp.zeros_like(rows_s)
     line = jnp.broadcast_to(biases[...], (8, biases.shape[1]))
     at, start = 0, 0
@@ -145,18 +151,22 @@
         copy.wait()
 
 
-def join(count, gate, *refs):
-    del gate
-    out = refs[count]
-    rows = refs[0].shape[0]
-    for m, shard in enumerate(refs[:count]):
-        out[m * rows : (m + 1) * rows, :] = shard[...]
+def join(*refs):
+    out, at = refs[-1], 0
+    for ref in refs[:-1]:
+        out[at : at + ref.shape[0], :] = ref[...]
+        at += ref.shape[0]
 
 
 def views(plan, joined):
-    count = plan.shards // len(joined)
-    rows = joined[0].shape[0] // count
-    return [ref.at[pl.ds(m * rows, rows), :] for m in range(count) for ref in joined]
+    if not plan.direct:
+        return joined
+    found = []
+    rows = sum(ref.shape[0] for ref in joined) // plan.shards
+    for mine, sibling in zip(joined[::2], joined[1::2]):
+        for m in range(mine.shape[0] // rows):
+            found += [ref.at[pl.ds(m * rows, rows), :] for ref in (mine, sibling)]
+    return found
 
 
 def place(plan, shards, block, target, column):
@@ -180,9 +190,12 @@
 
 def attn_forward(plan, *refs):
     s = plan.shards
-    x, cond = refs[:2]
-    shards = refs[2 : 2 + s]
-    projected, mixed, modulation, bias, qkv_out, ada_out, qkv, ada, sems = refs[2 + s :]
+    x, cond, cot = refs[:3]
+    shards = refs[3 : 3 + s]
+    (projected, mixed, modulation, bias, qkv_out, ada_out, x_out, cot_out, qkv, ada,
+     sems) = refs[3 + s :]
+    x_out[...] = x[...]
+    cot_out[...] = cot[...]
     d, length, r = plan.d, plan.seq, plan.rows
     for j in range(3):
         place(plan, shards, j, qkv, j)
@@ -234,26 +247,28 @@
         copy.wait()
 
 
-def mlp_first(plan, *refs):
-    s = plan.sides
-    counts, x, cond, cot, mixed, bias = refs[:6]
-    shards = views(plan, refs[6 : 6 + s])
-    (act, gelu_back, mlp_in, grad_out, middle, attn_out, modulation, fc1, ada_out, proj, grad_fc2,
-     fc2, ada, sems) = refs[6 + s :]
-    d, length, ffb = plan.d, plan.seq, plan.ffb
+def mlp_both(plan, *refs):
+    s = 4 if plan.direct else 1
+    lives, x, cot, mixed, bias, cond = refs[:6]
+    shards, refs = views(plan, refs[6 : 6 + s]), refs[6 + s :]
+    (send, refs) = (refs[0], refs[1:]) if plan.direct else (None, refs)
+    (keep, act, grad_pre, grad_out, middle, attn_out, modulation, fc1, fc2, mixed_out, cot_out,
+     proj, ada_out, mlp_in, turned, grad_fc1, grad_fc2, ada, sems) = refs
+    mixed_out[...] = mixed[...]
+    cot_out[...] = cot[...]
+    d, length, ffb, r = plan.d, plan.seq, plan.ffb, plan.rows
+    r4 = r * ffb
     for j in range(ffb):
         place(plan, shards, j, fc1, j)
+    for k, shard in enumerate(shards):
+        at = pl.multiple_of(shard_of(plan, k) * r4, 16)
+        fc2[pl.ds(at, r4), :] = shard[(ffb + 5) * r : (ffb + 5) * r + r4, :]
     for j in range(4):
         place(plan, shards, ffb + j, ada, j)
     copy = pltpu.make_async_copy(ada, ada_out, sems.at[0])
     copy.start()
     place(plan, shards, ffb + 4, proj, 0)
-    r, r4 = plan.rows, plan.rows * ffb
-    for k, shard in enumerate(shards):
-        at = pl.multiple_of(shard_of(plan, k) * r4, 16)
-        fc2[pl.ds(at, r4), :] = shard[(ffb + 5) * r : (ffb + 5) * r + r4, :]
-    cond_act = silu(cond[...].astype(F32)).astype(BF)
-    mod = dot(cond_act, ada[...])
+    mod = dot(silu(cond[...].astype(F32)).astype(BF), ada[...])
     for j in range(4):
         modulation[:, j * d : (j + 1) * d] = mod[:, j * d : (j + 1) * d] + bias[2 + j : 3 + j, :]
 
@@ -262,7 +277,7 @@
         gate_attn, shift, scale, gate = [
             modulation[pl.ds(g, 1), j * d : (j + 1) * d] for j in range(4)
         ]
-        live = jnp.where(g % plan.slots < counts[g // plan.slots, 0], 1.0, 0.0).astype(F32)
+        live = lives[pl.ds(g, 1), 0:1]
         out = dot(mixed[at, :], proj[...]) + bias[8:9, :]
         attn_out[at, :] = out
         mid = x[at, :].astype(F32) + gate_attn * out
@@ -273,10 +288,10 @@
         return carry
 
     lax.fori_loop(0, plan.group, latent, 0)
+    turned[...] = mlp_in[...].T
     step = 256
     for c in range(plan.ff // step):
         cols = slice(c * step, (c + 1) * step)
-        row, lane = divmod(c * step, d)
         pieces = []
         start, rest = c * step, step
         while rest:
@@ -292,36 +307,24 @@
         value = (pre * half).astype(BF)
         act[:, cols] = value
         slope = (0.5 * SQRT_2_PI) + (1.5 * SQRT_2_PI * CUBIC) * square
-        gelu_back[:, cols] = half + pre * (1.0 - bend * bend) * slope
+        gelu_back = half + pre * (1.0 - bend * bend) * slope
+        grad = (dot_nt(grad_out[...], fc2[cols, :]) * gelu_back).astype(BF)
+        grad_pre[:, cols] = grad
         grad_fc2[cols, :] = dot_tn(value, grad_out[...]).astype(BF)
+        grad_fc1[:, cols] = dot(turned[...], grad).astype(BF)
+    blocks = [(j, grad_fc1, j, 1, 0) for j in range(ffb)]
+    blocks += [(ffb + j, grad_fc2, 0, ffb, j) for j in range(ffb)]
+    emit(plan, None, blocks, send, keep, 2 * r4)
     copy.wait()
 
 
-def mlp_second(plan, *refs):
-    grad_out, gelu_back, mlp_in, grad_fc2, fc2 = refs[:5]
-    outs = refs[5:]
-    (send, outs) = (outs[0], outs[1:]) if plan.direct else (None, outs)
-    keep, grad_pre, turned, grad_fc1 = outs
-    r4 = plan.rows * plan.ffb
-    turned[...] = mlp_in[...].T
-    step = 256
-    for c in range(plan.ff // step):
-        cols = slice(c * step, (c + 1) * step)
-        grad = (dot_nt(grad_out[...], fc2[cols, :]) * gelu_back[:, cols]).astype(BF)
-        grad_pre[:, cols] = grad
-        grad_fc1[:, cols] = dot(turned[...], grad).astype(BF)
-    blocks = [(j, grad_fc1, j, 1, 0) for j in range(plan.ffb)]
-    blocks += [(plan.ffb + j, grad_fc2, 0, plan.ffb, j) for j in range(plan.ffb)]
-    emit(plan, None, blocks, send, keep, 2 * r4)
-
-
-def mlp_close(plan, counts, cot, act, fc2, middle, modulation, bias, block_out, grad_gate):
+def mlp_close(plan, lives, cot, act, fc2, middle, modulation, bias, block_out, grad_gate):
     d, length = plan.d, plan.seq
 
     def latent(g, carry):
         at = pl.ds(pl.multiple_of(g * length, length), length)
         gate = modulation[pl.ds(g, 1), 3 * d : 4 * d]
-        live = jnp.where(g % plan.slots < counts[g // plan.slots, 0], 1.0, 0.0).astype(F32)
+        live = lives[pl.ds(g, 1), 0:1]
         mlp_out = dot(act[at, :], fc2[...]) + bias[9 + plan.ffb : 10 + plan.ffb, :]
         block_out[at, :] = (live * (middle[at, :] + gate * mlp_out)).astype(BF)
         upstream = cot[at, :].astype(F32) * live
@@ -331,7 +334,7 @@
     lax.fori_loop(0, plan.group, latent, 0)
 
 
-def mlp_back(plan, counts, cot, grad_pre, fc1, middle, attn_out, modulation, mixed, proj, grad_out,
+def mlp_back(plan, lives, cot, grad_pre, fc1, middle, attn_out, modulation, mixed, proj, grad_out,
              grad_mixed, grad_middle, grad_proj, misc, grad_mod, grad_gates):
     d, length = plan.d, plan.seq
     misc[...] = jnp.zeros_like(misc)
@@ -345,7 +348,7 @@
     def latent(g, carry):
         at = pl.ds(pl.multiple_of(g * length, length), length)
         gate_attn, _, scale = [modulation[pl.ds(g, 1), j * d : (j + 1) * d] for j in range(3)]
-        live = jnp.where(g % plan.slots < counts[g // plan.slots, 0], 1.0, 0.0).astype(F32)
+        live = lives[pl.ds(g, 1), 0:1]
         upstream = cot[at, :].astype(F32) * live
         normed, rstd = normalize(middle[at, :])
         grad_in = dot_nt(grad_pre[at, :], fc1[...])
@@ -395,47 +398,48 @@
 
 
 def attn_close(plan, *refs):
-    (x, cond, grad_middle, qkv, modulation, grad_proj, misc, grad_mod,
-     grad_gate) = refs[:9]
-    parts, outs = refs[9 : 9 + plan.group], refs[9 + plan.group :]
-    (send, outs) = (outs[0], outs[1:]) if plan.direct else (None, outs)
-    keep, latents_grad, mods = outs[:3]
-    grad_proj_in, grad_qkv, rows_s, misc_s, cond_s, attn_in = outs[3:]
-    d, length, r = plan.d, plan.seq, plan.rows
-    misc_s[...] = misc[...]
+    (x, cond, grad_middle, qkv, modulation, grad_mod, grad_gate) = refs[:7]
+    parts, outs = refs[7 : 7 + plan.group], refs[7 + plan.group :]
+    latents_grad, mods, attn_in, rows_s, cond_s = outs
+    d, length = plan.d, plan.seq
     rows_s[...] = jnp.zeros_like(rows_s)
     cond_s[...] = silu(cond[...].astype(F32))
     for g, part in enumerate(parts):
-        grad_proj_in[g * length : (g + 1) * length, :] = part[...]
-
-    def latent(g, carry):
-        at = pl.ds(pl.multiple_of(g * length, length), length)
-        shift = modulation[pl.ds(g, 1), 0:d]
-        scale = modulation[pl.ds(g, 1), d : 2 * d]
+        at = slice(g * length, (g + 1) * length)
+        shift = modulation[g : g + 1, 0:d]
+        scale = modulation[g : g + 1, d : 2 * d]
         normed, rstd = normalize(x[at, :].astype(F32))
         attn_in[at, :] = (normed * (1.0 + scale) + shift).astype(BF)
-        grad_in = dot_nt(grad_proj_in[at, :], qkv[...])
+        grad_in = dot_nt(part[...], qkv[...])
         grad = grad_middle[at, :] + norm_back(grad_in * (1.0 + scale), normed, rstd)
         latents_grad[at, :] = grad.astype(BF)
-        base = g * 7
-        pieces = [cond_s[pl.ds(g, 1), :], jnp.sum(grad_in, axis=0, keepdims=True)]
+        pieces = [cond_s[g : g + 1, :], jnp.sum(grad_in, axis=0, keepdims=True)]
         pieces += [jnp.sum(grad_in * normed, axis=0, keepdims=True)]
-        pieces += [grad_mod[pl.ds(g, 1), j * d : (j + 1) * d] for j in range(3)]
-        pieces += [grad_gate[pl.ds(g, 1), :]]
+        pieces += [grad_mod[g : g + 1, j * d : (j + 1) * d] for j in range(3)]
+        pieces += [grad_gate[g : g + 1, :]]
         for j, piece in enumerate(pieces):
-            rows_s[pl.ds(base + j, 1), :] = piece
-        return carry
-
-    lax.fori_loop(0, plan.group, latent, 0)
+            rows_s[g * 7 + j : g * 7 + j + 1, :] = piece
     mods[...] = rows_s[...].astype(BF)
-    turned = attn_in[...].T
+
+
+def attn_grads(plan, *refs):
+    attn_in, grad_proj, misc = refs[:3]
+    parts, outs = refs[3 : 3 + plan.group], refs[3 + plan.group :]
+    (send, outs) = (outs[0], outs[1:]) if plan.direct else (None, outs)
+    keep, grad_qkv, misc_s, turned = outs
+    d, length, r = plan.d, plan.seq, plan.rows
+    misc_s[...] = misc[...]
+    turned[...] = attn_in[...].T
     for j in range(3):
         cols = slice(j * d, (j + 1) * d)
-        grad_qkv[:, cols] = dot(turned, grad_proj_in[:, cols]).astype(BF)
+        total, sums = 0.0, 0.0
+        for g, part in enumerate(parts):
+            piece = part[:, cols]
+            total = total + dot(turned[:, g * length : (g + 1) * length], piece)
+            sums = sums + jnp.sum(piece.astype(F32), axis=0, keepdims=True)
+        grad_qkv[:, cols] = total.astype(BF)
         if j != 1:
-            misc_s[j // 2 : j // 2 + 1, :] = jnp.sum(
-                grad_proj_in[:, cols].astype(F32), axis=0, keepdims=True
-            )
+            misc_s[j // 2 : j // 2 + 1, :] = sums
     blocks = [(j, grad_qkv, j, 1, 0) for j in range(3)] + [(3, grad_proj, 0, 1, 0)]
     rows = 4 * r + 16
     emit(plan, None, blocks, send, keep, rows)
@@ -476,8 +480,7 @@
 
 
 def add_chips(count, dp, quarter, own, *refs):
-    received, mine, outs = refs[:count], refs[count], refs[count + 1 : count + dp]
-    total_s = refs[count + dp]
+    received, (mine, sent, total_s) = refs[:count], refs[count:]
     total = own[...]
     for piece in received:
         total = total + piece[...].astype(F32)
@@ -485,30 +488,33 @@
     me = lax.axis_index("dp")
     for j in range(dp):
         part = total_s[pl.ds(pl.multiple_of((me ^ j) * quarter, 16), quarter), :]
-        if j == 0:
-            mine[...] = part
-        else:
-            outs[j - 1][...] = part.astype(BF)
-
-
-def add_groups(dp, *refs):
-    total = refs[0][...]
-    for piece in refs[1:dp]:
-        total = total + piece[...].astype(F32)
-    refs[dp][...] = total.astype(BF)
-
-
-def gather_groups(dp, quarter, layout, *refs):
-    pieces, outs, rows_s = refs[:dp], refs[dp:-1], refs[-1]
+        out = sent if j % 2 else mine
+        out[j // 2 * quarter : (j // 2 + 1) * quarter, :] = part.astype(out.dtype)
+
+
+def halve(quarter, held, received, mine, sent):
+    for j in range(held.shape[0] // quarter):
+        at = slice(j * quarter, (j + 1) * quarter)
+        out = sent if j % 2 else mine
+        total = held[at, :] + received[at, :].astype(F32)
+        out[j // 2 * quarter : (j // 2 + 1) * quarter, :] = total.astype(out.dtype)
+
+
+def gather_groups(dp, sizes, layouts, *refs):
+    pieces, outs, scratch = refs[:dp], refs[dp : -len(sizes)], refs[-len(sizes) :]
     me = lax.axis_index("dp")
-    for j, piece in enumerate(pieces):
-        rows_s[pl.ds(pl.multiple_of((me ^ j) * quarter, 16), quarter), :] = piece[...].astype(F32)
-    d = rows_s.shape[1]
-    at = 0
-    for out, (blocks, rows) in zip(outs, layout):
-        for j in range(blocks):
-            out[:, j * d : (j + 1) * d] = rows_s[at : at + rows, :]
-            at += rows
+    start, outs = 0, list(outs)
+    for quarter, layout, rows_s in zip(sizes, layouts, scratch):
+        for j, piece in enumerate(pieces):
+            at = pl.multiple_of((me ^ j) * quarter, 16)
+            rows_s[pl.ds(at, quarter), :] = piece[start : start + quarter, :].astype(F32)
+        start += quarter
+        d, at = rows_s.shape[1], 0
+        for blocks, rows in layout:
+            out = outs.pop(0)
+            for j in range(blocks):
+                out[:, j * d : (j + 1) * d] = rows_s[at : at + rows, :]
+                at += rows
 
 
 def last_sibling(peers, rows, keep, received, mods, own, *outs):
@@ -543,12 +549,15 @@
         name[quarter:, :] = tail_s[...].astype(name.dtype)
 
 
-def last_groups(dp, quarter, *refs):
-    pieces, low, mods = refs[:dp], refs[dp], refs[dp + 1]
-    total = pieces[0][0:quarter, :]
-    for piece in pieces[1:]:
-        total = total + piece[0:quarter, :].astype(F32)
-    low[...] = total.astype(BF)
+def add_groups(dp, sizes, *refs):
+    low, mods = refs[2 + dp :]
+    start = 0
+    for quarter, pieces in zip(sizes, (refs[:2], refs[2 : 2 + dp])):
+        total = pieces[0][0:quarter, :]
+        for piece in pieces[1:]:
+            total = total + piece[0:quarter, :].astype(F32)
+        low[start : start + quarter, :] = total.astype(BF)
+        start += quarter
     each = pieces[0].shape[0] - quarter - 16
     for j, piece in enumerate(pieces):
         mods[j * each : (j + 1) * each, :] = piece[quarter + 16 :, :].astype(BF)
@@ -617,17 +626,16 @@
     return [value] + [swap(plan, value, k) for k in plan.peers[1:]]
 
 
-def gather_joined(plan, chips, gate):
+def gather_joined(plan, chips):
     if not plan.direct:
         return chips
-    rows, d = chips[0].shape
-    (mine,) = call(
-        functools.partial(join, len(chips)),
-        [((len(chips) * rows, d), BF)],
-        [gate] + chips,
-        micros=0.4,
-    )
-    return [mine, swap(plan, mine, 1)]
+    joined = []
+    count = len(chips) // 2
+    for some in (chips[:count], chips[count:]):
+        shape = (sum(v.shape[0] for v in some), plan.d)
+        (mine,) = call(join, [(shape, BF)], some, micros=0.4)
+        joined += [mine, swap(plan, mine, 1)]
+    return joined
 
 
 def gather_cores(plan, chips):
@@ -653,34 +661,35 @@
 def chunk_chips(plan, own, pieces):
     d, dp = plan.d, plan.dp
     rows = own.shape[0]
-    quarter = rows // dp
-    mine, *quarters = call(
-        functools.partial(add_chips, len(pieces), dp, quarter),
-        [((quarter, d), F32)] + [((quarter, d), BF)] * (dp - 1),
+    mine, sent = call(
+        functools.partial(add_chips, len(pieces), dp, rows // dp),
+        [((rows // 2, d), F32), ((rows // 2, d), BF)],
         [own] + pieces,
         [pltpu.VMEM((rows, d), F32)],
     )
-    return mine, [swap(plan, part, j + 1, "dp") for j, part in enumerate(quarters)]
-
-
-def chunk_groups(plan, mine, quarters, layout):
-    d, dp = plan.d, plan.dp
-    quarter = mine.shape[0]
-    (low,) = call(functools.partial(add_groups, dp), [((quarter, d), BF)], [mine] + quarters)
-    parts = [low] + [swap(plan, low, j, "dp") for j in range(1, dp)]
-    return call(
-        functools.partial(gather_groups, dp, quarter, layout),
-        [((height, blocks * d), F32) for blocks, height in layout],
-        parts,
-        [pltpu.VMEM((quarter * dp, d), F32)],
-    )
-
-
-def reduce_last(plan, send, keep, mods):
+    return mine, swap(plan, sent, 1, "dp")
+
+
+def chunk_halves(plan, mine, received):
+    dp, step = plan.dp, 2
+    quarter = 2 * mine.shape[0] // dp
+    while mine.shape[0] > quarter:
+        shape = (mine.shape[0] // 2, plan.d)
+        mine, sent = call(
+            functools.partial(halve, quarter), [(shape, F32), (shape, BF)], [mine, received]
+        )
+        received, step = swap(plan, sent, step, "dp"), 2 * step
+    return mine, received
+
+
+def finish(plan, mlp_own, mlp_pieces, mlp_layout, send, keep, mods, cond_grad):
     d, dp, peers, r = plan.d, plan.dp, len(plan.peers), plan.rows
     rows = keep.shape[0] // peers
     quarter = (rows - 16) // dp
     received = swap(plan, send, 1)
+    mlp_mine, mlp_half = chunk_chips(plan, mlp_own, mlp_pieces)
+    received, keep = behind([received, keep], mlp_mine)
+    mlp_mine, mlp_half = chunk_halves(plan, mlp_mine, mlp_half)
     long = rows + MOD_ROWS
     own, *pieces = call(
         functools.partial(last_sibling, peers, rows),
@@ -688,6 +697,7 @@
         [keep, received, mods],
     )
     pieces = [swap(plan, piece, k) for piece, k in zip(pieces, plan.peers[1:])]
+    pieces = behind(pieces, cond_grad, mlp_half)
     tail = 16 + peers * MOD_ROWS
     mine, *quarters = call(
         functools.partial(last_chips, peers - 1, dp, quarter, rows),
@@ -697,27 +707,30 @@
     )
     quarters = [swap(plan, part, j + 1, "dp") for j, part in enumerate(quarters)]
     half = dp * peers * MOD_ROWS
+    sizes = (mlp_mine.shape[0], quarter)
     low, mods = call(
-        functools.partial(last_groups, dp, quarter),
-        [((quarter, d), BF), ((half, d), BF)],
-        [mine] + quarters,
-    )
-    parts = [low] + [swap(plan, low, j, "dp") for j in range(1, dp)]
-    widths = plan.bias_rows
+        functools.partial(add_groups, dp, sizes),
+        [((sum(sizes), d), BF), ((half, d), BF)],
+        [mlp_mine, mlp_half, mine] + quarters,
+    )
+    parts = [swap(plan, low, j, "dp") for j in range(1, dp)]
     ada, *biases = call(
         functools.partial(ada_grads, plan, quarter),
-        [((r, 6 * d), F32)] + [((1, w * d // plan.fsdp), F32) for w in widths],
+        [((r, 6 * d), F32)] + [((1, w * d // plan.fsdp), F32) for w in plan.bias_rows],
         [mine] + quarters + [mods, swap(plan, mods, 1)],
         [pltpu.VMEM((2 * half, d), BF), pltpu.VMEM((d, 2 * half), F32)],
         micros=2,
     )
-    qkv, proj = call(
-        functools.partial(gather_groups, dp, quarter, ((3, r), (1, r))),
-        [((r, 3 * d), F32), ((r, d), F32)],
-        parts,
-        [pltpu.VMEM((rows - 16, d), F32)],
-    )
-    return qkv, proj, ada, [bias.reshape(-1) for bias in biases]
+    biases = [bias.reshape(-1) for bias in biases]
+    parts = behind(parts, ada, *biases)
+    layouts = (mlp_layout, ((3, r), (1, r)))
+    fc1, fc2, qkv, proj = call(
+        functools.partial(gather_groups, dp, sizes, layouts),
+        [((height, blocks * d), F32) for layout in layouts for blocks, height in layout],
+        [low] + parts,
+        [pltpu.VMEM((size * dp, d), F32) for size in sizes],
+    )
+    return [ada, qkv, proj, fc1, fc2], biases
 
 
 def reduce_whole(plan, mlp, last, mods):
@@ -786,11 +799,12 @@
         jnp.pad(bias.astype(F32), (sum(lengths[:i]), width - sum(lengths[: i + 1])))
         for i, bias in enumerate(biases)
     )
-    first, second = call(
+    first, second, live = call(
         functools.partial(pack_weights, plan),
-        [((5 * r + 16, d), BF), (((2 * plan.ffb + 5) * r, d), BF)],
-        weights + [third, line[None, :]],
+        [((5 * r + 16, d), BF), (((2 * plan.ffb + 5) * r, d), BF), ((group, 128), F32)],
+        weights + [third, line[None, :], counts.T],
         [pltpu.VMEM((16, d), F32), pltpu.SemaphoreType.DMA((plan.ffb + 11,))],
+        smem=(6,),
         far=(0, 1, 2, 3, 4),
         limit=PACK_LIMIT,
         micros=1.0,
@@ -798,7 +812,7 @@
     first = gather_cores(plan, gather_chips(plan, first))
     second = gather_chips(plan, second)
 
-    projected, mixed, mod_first, bias, qkv, ada_first = call(
+    projected, mixed, mod_first, bias, qkv, ada_first, x_near, cot_near = call(
         functools.partial(attn_forward, plan),
         [
             ((n, 3 * d), BF),
@@ -807,60 +821,62 @@
             ((16, d), F32),
             ((d, 3 * d), BF),
             ((d, 2 * d), BF),
+            ((n, d), BF),
+            ((n, d), BF),
         ],
-        [x, cond] + first,
+        [x, cond, cot] + first,
         [
             pltpu.VMEM((d, 3 * d), BF),
             pltpu.VMEM((d, 2 * d), BF),
             pltpu.SemaphoreType.DMA((2,)),
         ],
         far_outs=(4, 5),
-        room=8,
+        room=5,
         micros=4,
     )
-    second = gather_joined(plan, second, mod_first)
+    if plan.direct:
+        second = second[:1] + [behind([v], mod_first)[0] for v in second[1:]]
+    shards = gather_joined(plan, second)
     halves = len(plan.peers) if plan.direct else 1
     sides = plan.sides
-    (act, gelu_back, mlp_in, grad_out, middle, attn_out, mod_second, fc1, ada_second, proj,
-     grad_fc2, fc2) = call(
-        functools.partial(mlp_first, plan),
-        [
+    outs = call(
+        functools.partial(mlp_both, plan),
+        [((halves * 2 * plan.ffb * r, d), BF)] * sides
+        + [
             ((n, ff), BF),
-            ((n, ff), F32),
-            ((n, d), BF),
+            ((n, ff), BF),
             ((n, d), BF),
             ((n, d), F32),
             ((n, d), F32),
             ((group, 4 * d), F32),
             ((d, ff), BF),
+            ((ff, d), BF),
+            ((n, d), BF),
+            ((n, d), BF),
+            ((d, d), BF),
             ((d, 4 * d), BF),
-            ((d, d), BF),
-            ((ff, d), BF),
-            ((ff, d), BF),
         ],
-        [counts, x, cond, cot, mixed, bias] + second,
-        [pltpu.VMEM((d, 4 * d), BF), pltpu.SemaphoreType.DMA((1,))],
-        smem=(0,),
-        far_outs=(8,),
-        room=8,
-        micros=6,
-    )
-    outs = call(
-        functools.partial(mlp_second, plan),
-        [((halves * 2 * plan.ffb * r, d), BF)] * sides + [((n, ff), BF)],
-        [grad_out, gelu_back, mlp_in, grad_fc2, fc2],
-        [pltpu.VMEM((d, n), BF), pltpu.VMEM((d, ff), BF)],
-        room=8,
-        micros=4,
+        [live, x_near, cot_near, mixed, bias, cond] + shards,
+        [
+            pltpu.VMEM((n, d), BF),
+            pltpu.VMEM((d, n), BF),
+            pltpu.VMEM((d, ff), BF),
+            pltpu.VMEM((ff, d), BF),
+            pltpu.VMEM((d, 4 * d), BF),
+            pltpu.SemaphoreType.DMA((1,)),
+        ],
+        far_outs=(sides + 11,),
+        room=5,
+        micros=10,
     )
     mlp_chunk = outs[:sides]
-    (grad_pre,) = outs[sides:]
+    (act, grad_pre, grad_out, middle, attn_out, mod_second, fc1, fc2, mixed, cot_near, proj,
+     ada_second) = outs[sides:]
     block_out, grad_gate = call(
         functools.partial(mlp_close, plan),
         [((n, d), BF), ((group, d), F32)],
-        [counts, cot, act, fc2, middle, mod_second, bias],
-        smem=(0,),
-        room=8,
+        [live, cot_near, act, fc2, middle, mod_second, bias],
+        room=5,
         micros=1.5,
     )
     if plan.direct:
@@ -875,10 +891,9 @@
             ((16, d), F32),
             ((group, 3 * d), F32),
         ],
-        [counts, cot, grad_pre, fc1, middle, attn_out, mod_second, mixed, proj, grad_out],
+        [live, cot_near, grad_pre, fc1, middle, attn_out, mod_second, mixed, proj, grad_out],
         [pltpu.VMEM((n, d), BF)],
-        smem=(0,),
-        room=8,
+        room=5,
         micros=3,
     )
     parts = []
@@ -887,38 +902,42 @@
             functools.partial(attn_back, plan, g),
             [((plan.seq, 3 * d), BF)],
             [projected, behind([grad_mixed], *parts)[0]],
-            room=8,
+            room=5,
             micros=3.3,
         )
+    latents_grad, mods, attn_in = call(
+        functools.partial(attn_close, plan),
+        [((n, d), BF), ((MOD_ROWS, d), BF), ((n, d), BF)],
+        [x, cond, grad_middle, qkv, mod_first, grad_mod, grad_gate] + parts,
+        [pltpu.VMEM((MOD_ROWS, d), F32), pltpu.VMEM((group, d), F32)],
+        room=5,
+        micros=2,
+    )
+    (cond_grad,) = call(
+        functools.partial(cond_back, plan),
+        [((group, d), BF)],
+        [cond, mods, ada_first, ada_second],
+        micros=2,
+    )
     if plan.direct:
-        mlp_mine, mlp_quarters = chunk_chips(plan, mlp_own, mlp_pieces)
         parts = behind(parts, *mlp_pieces)
-    outs = call(
-        functools.partial(attn_close, plan),
-        [((halves * (4 * r + 16), d), BF)] * sides + [((n, d), BF), ((MOD_ROWS, d), BF)],
-        [x, cond, grad_middle, qkv, mod_first, grad_proj, misc, grad_mod, grad_gate] + parts,
+    last_chunk = call(
+        functools.partial(attn_grads, plan),
+        [((halves * (4 * r + 16), d), BF)] * sides,
+        [attn_in, grad_proj, misc] + parts,
         [
-            pltpu.VMEM((n, 3 * d), BF),
             pltpu.VMEM((d, 3 * d), BF),
-            pltpu.VMEM((MOD_ROWS, d), F32),
             pltpu.VMEM((16, d), F32),
-            pltpu.VMEM((group, d), F32),
-            pltpu.VMEM((n, d), BF),
+            pltpu.VMEM((d, n), BF),
         ],
-        room=8,
-        micros=3,
-    )
-    last_chunk = outs[:sides]
-    latents_grad, mods = outs[sides:]
-    (cond_grad,) = call(
-        functools.partial(cond_back, plan), [((group, d), BF)], [cond, mods, ada_first, ada_second],
-        micros=2,
+        room=5,
+        micros=1.5,
     )
     if plan.direct:
         layout = ((plan.ffb, r), (1, plan.ffb * r))
-        fc1_grad, fc2_grad = chunk_groups(plan, mlp_mine, mlp_quarters, layout)
-        qkv_grad, proj_grad, ada_grad, bias_grads = reduce_last(plan, *last_chunk, mods)
-        weight_grads = [ada_grad, qkv_grad, proj_grad, fc1_grad, fc2_grad]
+        weight_grads, bias_grads = finish(
+            plan, mlp_own, mlp_pieces, layout, *last_chunk, mods, cond_grad
+        )
         grads = [grad for pair in zip(weight_grads, bias_grads) for grad in pair]
     else:
         grads = reduce_whole(plan, mlp_chunk[0], last_chunk[0], mods)

time: 133 us -> 111 us (0.83)
  waiting for transfers between devices: 48.7 us -> 38.7 us
  starting transfers between devices: 37.4 us -> 31.6 us
  Pallas kernels: 38.1 us -> 33.7 us
  local copies, waits for them, and re-layouts: 5.67 us -> 4.2 us
    ppermute x32 -> x29, waiting for transfers between devices: 48.7 us -> 38.7 us  [swap(): return lax.ppermute(value, axis, [(i, i ^ k) for i in range(size)])]
    ppermute x32 -> x29, starting transfers between devices: 37.4 us -> 31.6 us  [swap(): return lax.ppermute(value, axis, [(i, i ^ k) for i in range(size)])]
    pallas_call x20, Pallas kernels: 38.1 us -> 33.7 us  [call(): pl.pallas_call(body, out_shape=[jax.ShapeDtypeStruct(shape, kind) for sha...]
    unnamed x33 -> x16, local copies, waits for them, and re-layouts: 5.09 us -> 3.62 us
  transfers between devices with their start and end apart: 32 -> 29, of which waited for: 22 -> 21; matrix products, arithmetic and copies ran while one was open for 0% -> 1% of each run, Pallas kernels for 15% -> 20%
where the time goes in v3:
time: 111 us; the launch traced here: 110 us
  waiting for transfers between devices  38.7 us (35%)
  Pallas kernels  33.7 us (30%)
  starting transfers between devices  31.6 us (28%)
  local copies, waits for them, and re-layouts  4.2 us (4%)
  other arithmetic  1.42 us (1%)
    ppermute x29, waiting for transfers between devices, swap(): return lax.ppermute(value, axis, [(i, i ^ k) for i in range(size)])  38.7 us
    pallas_call x20, Pallas kernels, call(): pl.pallas_call(body, out_shape=[jax.ShapeDtypeStruct(shape, kind) for sha...  33.7 us
    ppermute x29, starting transfers between devices, swap(): return lax.ppermute(value, axis, [(i, i ^ k) for i in range(size)])  31.6 us
    unnamed x16, local copies, waits for them, and re-layouts  3.62 us
  transfers between devices with their start and end apart: 29, of which 21 were waited for; matrix products, arithmetic and copies ran while one was open for 1% of the time, Pallas kernels for 20%

profile of v3, /device:TPU:0, one launch (start us, length us, event | category | flops | bytes accessed | tf_op | source)
XLA Modules:
  0.0 110.4 jit_solution(14406423149525696805)
XLA Ops:
  0.6 0.8 convert_add_fusion
  1.5 0.6 broadcast_in_dim.3.biases
  2.1 3.0 %shard_map.237 = (bf16[256,384]{1,0:T(8,128)(2,1)}, bf16[624,384]{1,0:T(8,128)(2,1)}, f32[2,128]{1,0:T(2,128)}) custom-call(bf16[48,2304]{1,0:T(8,128)(2,1)} %ada.1, bf16[48,1152]{1,0:T(8,128)(2,1)} %qkv.1, bf16[48,384]{1,0:T(8,128)(2,1)} %proj.1, bf16[48,1536]{1,0:T(8,128)(2,1)} %fc1.1, bf16[192,384]{1,0:T(8,128)(2,1)} %fc2.1, ...), custom_call_target="tpu_custom_call" | custom-call | bytes 3690000 | tf_op jit(solution)/shard_map/pallas_call | solution.py:64
  5.1 4.0 %collective-permute-start.5 = (bf16[256,384]{1,0:T(8,128)(2,1)}, bf16[256,384]{1,0:T(8,128)(2,1)S(1)}, u32[]{:S(2)}, u32[]{:S(2)}) collective-permute-start(bf16[256,384]{1,0:T(8,128)(2,1)} %get-tuple-element.96.refs_3_), channel_id=1, source_target_pairs={{0,6},{1,7},{2,4},{3,5},{4,2},{5,3},{6,0},{7,1},{8,14},{9,15},{10,... | collective-permute-start | bytes 589832 | tf_op jit(solution)/shard_map/ppermute | solution.py:615
  9.0 0.5 collective-permute-start.3
  9.7 2.8 %collective-permute-start.10 = (bf16[624,384]{1,0:T(8,128)(2,1)}, bf16[624,384]{1,0:T(8,128)(2,1)S(1)}, u32[]{:S(2)}, u32[]{:S(2)}) collective-permute-start(bf16[624,384]{1,0:T(8,128)(2,1)} %get-tuple-element.101.refs_0_), channel_id=1, source_target_pairs={{0,6},{1,7},{2,4},{3,5},{4,2},{5,3},{6,0},{7,1},{8,14},{9,15},{10,... | collective-permute-start | bytes 1437704 | tf_op jit(solution)/shard_map/ppermute | solution.py:615
  12.5 0.5 collective-permute-start.9
  13.0 2.0 %collective-permute-done.5.refs_9_ = bf16[256,384]{1,0:T(8,128)(2,1)S(1)} collective-permute-done((bf16[256,384]{1,0:T(8,128)(2,1)}, bf16[256,384]{1,0:T(8,128)(2,1)S(1)}, u32[]{:S(2)}, u32[]{:S(2)}) %collective-permute-start.5) | collective-permute-done | bytes 196640 | tf_op jit(solution)/shard_map/ppermute | solution.py:615
  15.0 2.0 %collective-permute-start.7 = (bf16[624,384]{1,0:T(8,128)(2,1)}, bf16[624,384]{1,0:T(8,128)(2,1)S(1)}, u32[]{:S(2)}, u32[]{:S(2)}) collective-permute-start(bf16[624,384]{1,0:T(8,128)(2,1)} %get-tuple-element.101.refs_0_), channel_id=1, source_target_pairs={{0,2},{1,3},{2,0},{3,1},{4,6},{5,7},{6,4},{7,5},{8,10},{9,11},{10,... | collective-permute-start | bytes 1437704 | tf_op jit(solution)/shard_map/ppermute | solution.py:615
  17.0 2.3 %collective-permute-done.3.refs_7_ = bf16[256,384]{1,0:T(8,128)(2,1)S(1)} collective-permute-done((bf16[256,384]{1,0:T(8,128)(2,1)}, bf16[256,384]{1,0:T(8,128)(2,1)S(1)}, u32[]{:S(2)}, u32[]{:S(2)}) %collective-permute-start.3) | collective-permute-done | bytes 196640 | tf_op jit(solution)/shard_map/ppermute | solution.py:615
  19.3 0.5 collective-permute-done.1.refs_5_
  19.8 1.1 %collective-permute-done.refs_4_ = bf16[256,384]{1,0:T(8,128)(2,1)S(1)} collective-permute-done((bf16[256,384]{1,0:T(8,128)(2,1)}, bf16[256,384]{1,0:T(8,128)(2,1)S(1)}, u32[]{:S(2)}, u32[]{:S(2)}) %collective-permute-start) | collective-permute-done | bytes 196640 | tf_op jit(solution)/shard_map/ppermute | solution.py:615
  20.9 0.1 collective-permute-start.4
  21.1 0.2 collective-permute-done.6.refs_10_
  21.2 0.2 collective-permute-start.2
  21.4 0.9 collective-permute-done.4.refs_8_
  22.4 0.3 collective-permute-done.2.refs_6_
  22.7 1.0 copy-done
  23.7 1.0 copy-done.3
  24.7 0.9 copy-done.4
  25.6 0.7 copy-done.5
  26.3 4.1 %shard_map.238 = (bf16[512,1152]{1,0:T(8,128)(2,1)S(1)}, bf16[512,384]{1,0:T(8,128)(2,1)S(1)}, f32[2,768]{1,0:T(2,128)S(1)}, f32[16,384]{1,0:T(8,128)S(1)}, bf16...) custom-call(bf16[512,384]{1,0:T(8,128)(2,1)S(1)} %bitcast.15, ...), custom_call_target="tpu_custom_call" | custom-call | bytes 14760000 | tf_op jit(solution)/shard_map/pallas_call | solution.py:64
  30.4 8.4 %collective-permute-done.9.refs_0_ = bf16[624,384]{1,0:T(8,128)(2,1)S(1)} collective-permute-done((bf16[624,384]{1,0:T(8,128)(2,1)}, bf16[624,384]{1,0:T(8,128)(2,1)S(1)}, u32[]{:S(2)}, u32[]{:S(2)}) %collective-permute-start.9) | collective-permute-done | bytes 479264 | tf_op jit(solution)/shard_map/ppermute | solution.py:615
  38.9 0.3 collective-permute-done.7.refs_1_
  39.5 0.6 collective-permute-start.11
  40.1 1.9 %collective-permute-done.8.refs_7_ = bf16[1248,384]{1,0:T(8,128)(2,1)S(1)} collective-permute-done((bf16[1248,384]{1,0:T(8,128)(2,1)S(1)}, bf16[1248,384]{1,0:T(8,128)(2,1)S(1)}, u32[]{:S(2)}, u32[]{:S(2)}) %collective-permute-start.8) | collective-permute-done | bytes 958496 | tf_op jit(solution)/shard_map/ppermute | solution.py:615
  41.9 1.4 %collective-permute-done.11.refs_9_ = bf16[1248,384]{1,0:T(8,128)(2,1)S(1)} collective-permute-done((bf16[1248,384]{1,0:T(8,128)(2,1)S(1)}, bf16[1248,384]{1,0:T(8,128)(2,1)S(1)}, u32[]{:S(2)}, u32[]{:S(2)}) %collective-permute-start.11) | collective-permute-done | bytes 958496 | tf_op jit(solution)/shard_map/ppermute | solution.py:615
  43.3 6.4 %shard_map.241 = (bf16[1536,384]{1,0:T(8,128)(2,1)S(1)}, bf16[1536,384]{1,0:T(8,128)(2,1)S(1)}, bf16[512,1536]{1,0:T(8,128)(2,1)S(1)}, bf16[512,1536]{1,0:T(8,12...) custom-call(f32[2,128]{1,0:T(2,128)S(1)} %copy-done.7, ...), custom_call_target="tpu_custom_call" | custom-call | bytes 36900000 | tf_op jit(solution)/shard_map/pallas_call | solution.py:64
  49.7 0.2 collective-permute-start.12
  49.9 2.0 %shard_map.242 = (bf16[512,384]{1,0:T(8,128)(2,1)}, f32[2,384]{1,0:T(2,128)S(1)}) custom-call(f32[2,128]{1,0:T(2,128)S(1)} %copy-done.7, bf16[512,384]{1,0:T(8,128)(2,1)S(1)} %get-tuple-element.106.cot, bf16[512,1536]{1,0:T(8,128)(2,1)S(1)} %get-tuple-element.107.act, bf16[1536,384]{1,0:T(8,128)(2,1)S(1)} %get-tuple-element.108.fc2, ...), custom_call_target="tpu_custom_call" | custom-call | bytes 5535000 | tf_op jit(solution)/shard_map/pallas_call | solution.py:64
  51.9 0.7 collective-permute-done.12.refs_1_
  52.6 0.3 shard_map.243
  52.9 1.6 %collective-permute-start.13 = (bf16[384,384]{1,0:T(8,128)(2,1)S(1)}, bf16[384,384]{1,0:T(8,128)(2,1)S(1)}, u32[]{:S(2)}, u32[]{:S(2)}) collective-permute-start(bf16[384,384]{1,0:T(8,128)(2,1)S(1)} %get-tuple-element.138), channel_id=1, source_target_pairs={{0,2},{1,3},{2,0},{3,1},{4,6},{5,7},{6,4},{7,5},{8,10},{9,11},{10,... | collective-permute-start | bytes 884744 | tf_op jit(solution)/shard_map/ppermute | solution.py:615
  54.5 0.6 collective-permute-start.14
  55.0 1.4 %collective-permute-start.15 = (bf16[384,384]{1,0:T(8,128)(2,1)S(1)}, bf16[384,384]{1,0:T(8,128)(2,1)S(1)}, u32[]{:S(2)}, u32[]{:S(2)}) collective-permute-start(bf16[384,384]{1,0:T(8,128)(2,1)S(1)} %get-tuple-element.140), channel_id=1, source_target_pairs={{0,6},{1,7},{2,4},{3,5},{4,2},{5,3},{6,0},{7,1},{8,14},{9,15},{10,... | collective-permute-start | bytes 884744 | tf_op jit(solution)/shard_map/ppermute | solution.py:615
  56.5 2.8 %shard_map.244 = (bf16[512,384]{1,0:T(8,128)(2,1)S(1)}, f32[512,384]{1,0:T(8,128)S(1)}, bf16[384,384]{1,0:T(8,128)(2,1)S(1)}, f32[16,384]{1,0:T(8,128)S(1)}, f32[2,1152]{1,0:T(2,128)S(1)}) custom-call(f32[2,128]{1,0:T(2,128)S(1)} %copy-done.7, bf16[512,384]{1,0:T(8,128)(2,1)S(1)} %get-tuple-element.106.cot, ...), custom_call_target="tpu_custom_call" | custom-call | bytes 11070000 | tf_op jit(solution)/shard_map/pallas_call | solution.py:64
  59.3 3.5 %shard_map.245.refs_7_.refs_3_ = bf16[256,1152]{1,0:T(8,128)(2,1)S(1)} custom-call(bf16[512,1152]{1,0:T(8,128)(2,1)S(1)} %get-tuple-element.128.projected, bf16[512,384]{1,0:T(8,128)(2,1)S(1)} %get-tuple-element.130.grad_mixed), custom_call_target="tpu_custom_call" | custom-call | bytes 12177000 | tf_op jit(solution)/shard_map/pallas_call | solution.py:64
  62.8 3.5 %shard_map.246.refs_8_.refs_4_ = bf16[256,1152]{1,0:T(8,128)(2,1)S(1)} custom-call(bf16[512,1152]{1,0:T(8,128)(2,1)S(1)} %get-tuple-element.128.projected, bf16[512,384]{1,0:T(8,128)(2,1)S(1)} %get-tuple-element.130.grad_mixed), custom_call_target="tpu_custom_call" | custom-call | bytes 12177000 | tf_op jit(solution)/shard_map/pallas_call | solution.py:64
  66.2 1.9 %shard_map.247 = (bf16[512,384]{1,0:T(8,128)(2,1)}, bf16[16,384]{1,0:T(8,128)(2,1)S(1)}, bf16[512,384]{1,0:T(8,128)(2,1)S(1)}) custom-call(bf16[512,384]{1,0:T(8,128)(2,1)S(1)} %bitcast.16, bf16[2,384]{1,0:T(2,128)(2,1)S(1)} %bitcast.20, f32[512,384]{1,0:T(8,128)S(1)} %get-tuple-element.125.refs_2_, bf16[384,1152]{1,0:T(8,128)(2,1)S(1)} %get-tuple-element.126.refs_3_, ...), custom_call_target="tpu_custom_call" | custom-call | bytes 7380000 | tf_op jit(solution)/shard_map/pallas_call | solution.py:64
  68.1 1.4 %collective-permute-done.14.refs_1_ = bf16[384,384]{1,0:T(8,128)(2,1)S(1)} collective-permute-done((bf16[384,384]{1,0:T(8,128)(2,1)S(1)}, bf16[384,384]{1,0:T(8,128)(2,1)S(1)}, u32[]{:S(2)}, u32[]{:S(2)}) %collective-permute-start.14) | collective-permute-done | bytes 294944 | tf_op jit(solution)/shard_map/ppermute | solution.py:615
  69.5 0.9 shard_map.249
  70.5 0.2 shard_map.250
  70.8 1.6 %collective-permute-start.20 = (bf16[192,384]{1,0:T(8,128)(2,1)S(1)}, bf16[192,384]{1,0:T(8,128)(2,1)S(1)}, u32[]{:S(2)}, u32[]{:S(2)}) collective-permute-start(bf16[192,384]{1,0:T(8,128)(2,1)S(1)} %get-tuple-element.152), channel_id=1, source_target_pairs={{0,8},{8,0},{16,24},{24,16},{1,9},{9,1},{17,25},{25,17},{2,10},{10... | collective-permute-start | bytes 442376 | tf_op jit(solution)/shard_map/ppermute | solution.py:615
  72.4 0.2 collective-permute-done.16.received
  72.6 0.1 shard_map.251
  72.7 1.2 %collective-permute-start.17 = (bf16[224,384]{1,0:T(8,128)(2,1)S(1)}, bf16[224,384]{1,0:T(8,128)(2,1)S(1)}, u32[]{:S(2)}, u32[]{:S(2)}) collective-permute-start(bf16[224,384]{1,0:T(8,128)(2,1)S(1)} %get-tuple-element.149), channel_id=1, source_target_pairs={{0,2},{1,3},{2,0},{3,1},{4,6},{5,7},{6,4},{7,5},{8,10},{9,11},{10,... | collective-permute-start | bytes 516104 | tf_op jit(solution)/shard_map/ppermute | solution.py:615
  74.0 0.8 collective-permute-start.18
  74.7 1.6 %collective-permute-start.19 = (bf16[224,384]{1,0:T(8,128)(2,1)S(1)}, bf16[224,384]{1,0:T(8,128)(2,1)S(1)}, u32[]{:S(2)}, u32[]{:S(2)}) collective-permute-start(bf16[224,384]{1,0:T(8,128)(2,1)S(1)} %get-tuple-element.151), channel_id=1, source_target_pairs={{0,6},{1,7},{2,4},{3,5},{4,2},{5,3},{6,0},{7,1},{8,14},{9,15},{10,... | collective-permute-start | bytes 516104 | tf_op jit(solution)/shard_map/ppermute | solution.py:615
  76.3 0.8 collective-permute-done.20.received
  77.1 2.7 %collective-permute-start.21 = (bf16[96,384]{1,0:T(8,128)(2,1)S(1)}, bf16[96,384]{1,0:T(8,128)(2,1)S(1)}, u32[]{:S(2)}, u32[]{:S(2)}) collective-permute-start(bf16[96,384]{1,0:T(8,128)(2,1)S(1)} %get-tuple-element.153), channel_id=1, source_target_pairs={{0,16},{8,24},{16,0},{24,8},{1,17},{9,25},{17,1},{25,9},{2,18},{10... | collective-permute-start | bytes 221192 | tf_op jit(solution)/shard_map/ppermute | solution.py:615
  79.8 1.7 %shard_map.248 = bf16[2,384]{1,0:T(2,128)(2,1)} custom-call(bf16[2,384]{1,0:T(2,128)(2,1)S(1)} %bitcast.21, bf16[16,384]{1,0:T(8,128)(2,1)S(1)} %get-tuple-element.132.mods, bf16[384,768]{1,0:T(8,128)(2,1)S(1)} %get-tuple-element.133.first, bf16[384,1536]{1,0:T(8,128)(2,1)S(1)} %get-tuple-element.134.second), custom_call_target="tpu_custom_call" | custom-call | bytes 7380000 | tf_op jit(solution)/shard_map/pallas_call | solution.py:64
  81.5 2.3 %collective-permute-done.21.refs_1_ = bf16[96,384]{1,0:T(8,128)(2,1)S(1)} collective-permute-done((bf16[96,384]{1,0:T(8,128)(2,1)S(1)}, bf16[96,384]{1,0:T(8,128)(2,1)S(1)}, u32[]{:S(2)}, u32[]{:S(2)}) %collective-permute-start.21) | collective-permute-done | bytes 73760 | tf_op jit(solution)/shard_map/ppermute | solution.py:615
  84.0 1.7 %collective-permute-start.22 = (bf16[128,384]{1,0:T(8,128)(2,1)S(1)}, bf16[128,384]{1,0:T(8,128)(2,1)S(1)}, u32[]{:S(2)}, u32[]{:S(2)}) collective-permute-start(bf16[128,384]{1,0:T(8,128)(2,1)S(1)} %get-tuple-element.158), channel_id=1, source_target_pairs={{0,8},{8,0},{16,24},{24,16},{1,9},{9,1},{17,25},{25,17},{2,10},{10... | collective-permute-start | bytes 294920 | tf_op jit(solution)/shard_map/ppermute | solution.py:615
  85.7 2.6 %collective-permute-start.23 = (bf16[128,384]{1,0:T(8,128)(2,1)S(1)}, bf16[128,384]{1,0:T(8,128)(2,1)S(1)}, u32[]{:S(2)}, u32[]{:S(2)}) collective-permute-start(bf16[128,384]{1,0:T(8,128)(2,1)S(1)} %get-tuple-element.159), channel_id=1, source_target_pairs={{0,16},{8,24},{16,0},{24,8},{1,17},{9,25},{17,1},{25,9},{2,18},{10... | collective-permute-start | bytes 294920 | tf_op jit(solution)/shard_map/ppermute | solution.py:615
  88.5 1.2 %collective-permute-done.22.refs_3_.refs_1_ = bf16[128,384]{1,0:T(8,128)(2,1)S(1)} collective-permute-done((bf16[128,384]{1,0:T(8,128)(2,1)S(1)}, bf16[128,384]{1,0:T(8,128)(2,1)S(1)}, u32[]{:S(2)}, u32[]{:S(2)}) %collective-permute-start.22) | collective-permute-done | bytes 98336 | tf_op jit(solution)/shard_map/ppermute | solution.py:615
  89.7 6.0 %collective-permute-done.23.refs_4_.refs_2_ = bf16[128,384]{1,0:T(8,128)(2,1)S(1)} collective-permute-done((bf16[128,384]{1,0:T(8,128)(2,1)S(1)}, bf16[128,384]{1,0:T(8,128)(2,1)S(1)}, u32[]{:S(2)}, u32[]{:S(2)}) %collective-permute-start.23) | collective-permute-done | bytes 98336 | tf_op jit(solution)/shard_map/ppermute | solution.py:615
  95.8 2.5 %collective-permute-start.28 = (bf16[144,384]{1,0:T(8,128)(2,1)S(1)}, bf16[144,384]{1,0:T(8,128)(2,1)S(1)}, u32[]{:S(2)}, u32[]{:S(2)}) collective-permute-start(bf16[144,384]{1,0:T(8,128)(2,1)S(1)} %get-tuple-element.165.refs_0_), channel_id=1, source_target_pairs={{0,24},{8,16},{16,8},{24,0},{1,25},{9,17},{17,9},{25,1},{2,26},{10... | collective-permute-start | bytes 331784 | tf_op jit(solution)/shard_map/ppermute | solution.py:615
  98.3 0.6 collective-permute-start.27
  98.9 1.3 %collective-permute-start.26 = (bf16[144,384]{1,0:T(8,128)(2,1)S(1)}, bf16[144,384]{1,0:T(8,128)(2,1)S(1)}, u32[]{:S(2)}, u32[]{:S(2)}) collective-permute-start(bf16[144,384]{1,0:T(8,128)(2,1)S(1)} %get-tuple-element.165.refs_0_), channel_id=1, source_target_pairs={{0,8},{8,0},{16,24},{24,16},{1,9},{9,1},{17,25},{25,17},{2,10},{10... | collective-permute-start | bytes 331784 | tf_op jit(solution)/shard_map/ppermute | solution.py:615
  100.2 1.9 %shard_map.255 = (f32[48,2304]{1,0:T(8,128)}, f32[1,288]{1,0:T(1,128)S(1)}, f32[1,96]{1,0:T(1,128)}, f32[1,48]{1,0:T(1,128)}, f32[1,192]{1,0:T(1,128)}, /*index=5*/f32[1,48]{1,0:T(1,128)}) custom-call(f32[128,384]{1,0:T(8,128)S(1)} %get-tuple-element.157.refs_2_.refs_0_, bf16[128,384]{1,0:T(8,128)(2,1)S(1)} %collective-permute-done.22.refs_3_.refs_1_, ...), custom_call_target="tpu_custom_call" | custom-call | bytes 7380000 | tf_op jit(solution)/shard_map/pallas_call | solution.py:64
  102.2 0.6 reduce
  102.7 0.8 collective-permute-done.28.refs_3_
  103.6 5.8 %collective-permute-done.27.refs_2_ = bf16[144,384]{1,0:T(8,128)(2,1)S(1)} collective-permute-done((bf16[144,384]{1,0:T(8,128)(2,1)S(1)}, bf16[144,384]{1,0:T(8,128)(2,1)S(1)}, u32[]{:S(2)}, u32[]{:S(2)}) %collective-permute-start.27) | collective-permute-done | bytes 110624 | tf_op jit(solution)/shard_map/ppermute | solution.py:615
  109.4 1.0 shard_map.256
  (33 shorter events, 1.0 us)
Async XLA Ops:
  5.1 9.9 %collective-permute-start.5 = (bf16[256,384]{1,0:T(8,128)(2,1)}, bf16[256,384]{1,0:T(8,128)(2,1)S(1)}, u32[]{:S(2)}, u32[]{:S(2)}) collective-permute-start(bf16[256,384]{1,0:T(8,128)(2,1)} %get-tuple-element.96.refs_3_), channel_id=1, source_target_pairs={{0,6},{1,7},{2,4},{3,5},{4,2},{5,3},{6,0},{7,1},{8,14},{9,15},{10,... | collective-permute-start | bytes 589832 | tf_op jit(solution)/shard_map/ppermute | solution.py:615
  9.0 10.3 %collective-permute-start.3 = (bf16[256,384]{1,0:T(8,128)(2,1)}, bf16[256,384]{1,0:T(8,128)(2,1)S(1)}, u32[]{:S(2)}, u32[]{:S(2)}) collective-permute-start(bf16[256,384]{1,0:T(8,128)(2,1)} %get-tuple-element.96.refs_3_), channel_id=1, source_target_pairs={{0,4},{1,5},{2,6},{3,7},{4,0},{5,1},{6,2},{7,3},{8,12},{9,13},{10,... | collective-permute-start | bytes 589832 | tf_op jit(solution)/shard_map/ppermute | solution.py:615
  9.5 10.3 %collective-permute-start.1 = (bf16[256,384]{1,0:T(8,128)(2,1)}, bf16[256,384]{1,0:T(8,128)(2,1)S(1)}, u32[]{:S(2)}, u32[]{:S(2)}) collective-permute-start(bf16[256,384]{1,0:T(8,128)(2,1)} %get-tuple-element.96.refs_3_), channel_id=1, source_target_pairs={{0,2},{1,3},{2,0},{3,1},{4,6},{5,7},{6,4},{7,5},{8,10},{9,11},{10,... | collective-permute-start | bytes 589832 | tf_op jit(solution)/shard_map/ppermute | solution.py:615
  9.7 20.8 %collective-permute-start.10 = (bf16[624,384]{1,0:T(8,128)(2,1)}, bf16[624,384]{1,0:T(8,128)(2,1)S(1)}, u32[]{:S(2)}, u32[]{:S(2)}) collective-permute-start(bf16[624,384]{1,0:T(8,128)(2,1)} %get-tuple-element.101.refs_0_), channel_id=1, source_target_pairs={{0,6},{1,7},{2,4},{3,5},{4,2},{5,3},{6,0},{7,1},{8,14},{9,15},{10,... | collective-permute-start | bytes 1437704 | tf_op jit(solution)/shard_map/ppermute | solution.py:615
  12.5 26.4 %collective-permute-start.9 = (bf16[624,384]{1,0:T(8,128)(2,1)}, bf16[624,384]{1,0:T(8,128)(2,1)S(1)}, u32[]{:S(2)}, u32[]{:S(2)}) collective-permute-start(bf16[624,384]{1,0:T(8,128)(2,1)} %get-tuple-element.101.refs_0_), channel_id=1, source_target_pairs={{0,4},{1,5},{2,6},{3,7},{4,0},{5,1},{6,2},{7,3},{8,12},{9,13},{10,... | collective-permute-start | bytes 1437704 | tf_op jit(solution)/shard_map/ppermute | solution.py:615
  15.0 24.2 %collective-permute-start.7 = (bf16[624,384]{1,0:T(8,128)(2,1)}, bf16[624,384]{1,0:T(8,128)(2,1)S(1)}, u32[]{:S(2)}, u32[]{:S(2)}) collective-permute-start(bf16[624,384]{1,0:T(8,128)(2,1)} %get-tuple-element.101.refs_0_), channel_id=1, source_target_pairs={{0,2},{1,3},{2,0},{3,1},{4,6},{5,7},{6,4},{7,5},{8,10},{9,11},{10,... | collective-permute-start | bytes 1437704 | tf_op jit(solution)/shard_map/ppermute | solution.py:615
  19.3 1.7 %collective-permute-start = (bf16[256,384]{1,0:T(8,128)(2,1)}, bf16[256,384]{1,0:T(8,128)(2,1)S(1)}, u32[]{:S(2)}, u32[]{:S(2)}) collective-permute-start(bf16[256,384]{1,0:T(8,128)(2,1)} %get-tuple-element.96.refs_3_), channel_id=1, source_target_pairs={{0,1},{1,0},{2,3},{3,2},{4,5},{5,4},{6,7},{7,6},{8,9},{9,8},{10,11... | collective-permute-start | bytes 589832 | tf_op jit(solution)/shard_map/ppermute | solution.py:615
  19.8 1.4 %collective-permute-start.6 = (bf16[256,384]{1,0:T(8,128)(2,1)S(1)}, bf16[256,384]{1,0:T(8,128)(2,1)S(1)}, u32[]{:S(2)}, u32[]{:S(2)}) collective-permute-start(bf16[256,384]{1,0:T(8,128)(2,1)S(1)} %collective-permute-done.5.refs_9_), channel_id=1, source_target_pairs={{0,1},{1,0},{2,3},{3,2},{4,5},{5,4},{6,7},{7,6},{8,9},{9,8},{10,11... | collective-permute-start | bytes 589832 | tf_op jit(solution)/shard_map/ppermute | solution.py:615
  20.9 1.4 %collective-permute-start.4 = (bf16[256,384]{1,0:T(8,128)(2,1)S(1)}, bf16[256,384]{1,0:T(8,128)(2,1)S(1)}, u32[]{:S(2)}, u32[]{:S(2)}) collective-permute-start(bf16[256,384]{1,0:T(8,128)(2,1)S(1)} %collective-permute-done.3.refs_7_), channel_id=1, source_target_pairs={{0,1},{1,0},{2,3},{3,2},{4,5},{5,4},{6,7},{7,6},{8,9},{9,8},{10,11... | collective-permute-start | bytes 589832 | tf_op jit(solution)/shard_map/ppermute | solution.py:615
  21.2 1.4 %collective-permute-start.2 = (bf16[256,384]{1,0:T(8,128)(2,1)S(1)}, bf16[256,384]{1,0:T(8,128)(2,1)S(1)}, u32[]{:S(2)}, u32[]{:S(2)}) collective-permute-start(bf16[256,384]{1,0:T(8,128)(2,1)S(1)} %collective-permute-done.1.refs_5_), channel_id=1, source_target_pairs={{0,1},{1,0},{2,3},{3,2},{4,5},{5,4},{6,7},{7,6},{8,9},{9,8},{10,11... | collective-permute-start | bytes 589832 | tf_op jit(solution)/shard_map/ppermute | solution.py:615
  22.7 1.0 copy-start
  23.7 1.0 copy-start.3
  24.7 0.9 copy-start.4
  25.6 0.7 copy-start.5
  26.3 13.0 %copy-start.2 = (bf16[624,384]{1,0:T(8,128)(2,1)S(1)}, bf16[624,384]{1,0:T(8,128)(2,1)}, u32[]{:S(2)}) copy-start(bf16[624,384]{1,0:T(8,128)(2,1)} %get-tuple-element.101.refs_0_) | copy-start | bytes 1437700
  39.3 4.0 %copy-start.6 = (bf16[2,1,384]{2,0,1:T(2,128)(2,1)S(1)}, bf16[2,1,384]{2,0,1:T(2,128)(2,1)}, u32[]{:S(2)}) copy-start(bf16[2,1,384]{2,0,1:T(2,128)(2,1)} %param.15) | copy-start | bytes 4612
  39.3 4.0 %copy-start.7 = (f32[2,128]{1,0:T(2,128)S(1)}, f32[2,128]{1,0:T(2,128)}, u32[]{:S(2)}) copy-start(f32[2,128]{1,0:T(2,128)} %get-tuple-element.95.refs_0_.lives) | copy-start | bytes 3076
  39.3 2.6 %collective-permute-start.8 = (bf16[1248,384]{1,0:T(8,128)(2,1)S(1)}, bf16[1248,384]{1,0:T(8,128)(2,1)S(1)}, u32[]{:S(2)}, u32[]{:S(2)}) collective-permute-start(bf16[1248,384]{1,0:T(8,128)(2,1)S(1)} %shard_map.239.refs_6_), channel_id=1, source_target_pairs={{0,1},{1,0},{2,3},{3,2},{4,5},{5,4},{6,7},{7,6},{8,9},{9,8},{10,11... | collective-permute-start | bytes 2875400 | tf_op jit(solution)/shard_map/ppermute | solution.py:615
  39.5 3.8 %collective-permute-start.11 = (bf16[1248,384]{1,0:T(8,128)(2,1)S(1)}, bf16[1248,384]{1,0:T(8,128)(2,1)S(1)}, u32[]{:S(2)}, u32[]{:S(2)}) collective-permute-start(bf16[1248,384]{1,0:T(8,128)(2,1)S(1)} %shard_map.240.refs_8_), channel_id=1, source_target_pairs={{0,1},{1,0},{2,3},{3,2},{4,5},{5,4},{6,7},{7,6},{8,9},{9,8},{10,11... | collective-permute-start | bytes 2875400 | tf_op jit(solution)/shard_map/ppermute | solution.py:615
  49.7 2.9 %collective-permute-start.12 = (bf16[1536,384]{1,0:T(8,128)(2,1)S(1)}, bf16[1536,384]{1,0:T(8,128)(2,1)S(1)}, u32[]{:S(2)}, u32[]{:S(2)}) collective-permute-start(bf16[1536,384]{1,0:T(8,128)(2,1)S(1)} %get-tuple-element.114), channel_id=1, source_target_pairs={{0,1},{1,0},{2,3},{3,2},{4,5},{5,4},{6,7},{7,6},{8,9},{9,8},{10,11... | collective-permute-start | bytes 3538952 | tf_op jit(solution)/shard_map/ppermute | solution.py:615
  52.9 15.2 %collective-permute-start.13 = (bf16[384,384]{1,0:T(8,128)(2,1)S(1)}, bf16[384,384]{1,0:T(8,128)(2,1)S(1)}, u32[]{:S(2)}, u32[]{:S(2)}) collective-permute-start(bf16[384,384]{1,0:T(8,128)(2,1)S(1)} %get-tuple-element.138), channel_id=1, source_target_pairs={{0,2},{1,3},{2,0},{3,1},{4,6},{5,7},{6,4},{7,5},{8,10},{9,11},{10,... | collective-permute-start | bytes 884744 | tf_op jit(solution)/shard_map/ppermute | solution.py:615
  54.5 15.1 %collective-permute-start.14 = (bf16[384,384]{1,0:T(8,128)(2,1)S(1)}, bf16[384,384]{1,0:T(8,128)(2,1)S(1)}, u32[]{:S(2)}, u32[]{:S(2)}) collective-permute-start(bf16[384,384]{1,0:T(8,128)(2,1)S(1)} %get-tuple-element.139), channel_id=1, source_target_pairs={{0,4},{1,5},{2,6},{3,7},{4,0},{5,1},{6,2},{7,3},{8,12},{9,13},{10,... | collective-permute-start | bytes 884744 | tf_op jit(solution)/shard_map/ppermute | solution.py:615
  55.0 14.5 %collective-permute-start.15 = (bf16[384,384]{1,0:T(8,128)(2,1)S(1)}, bf16[384,384]{1,0:T(8,128)(2,1)S(1)}, u32[]{:S(2)}, u32[]{:S(2)}) collective-permute-start(bf16[384,384]{1,0:T(8,128)(2,1)S(1)} %get-tuple-element.140), channel_id=1, source_target_pairs={{0,6},{1,7},{2,4},{3,5},{4,2},{5,3},{6,0},{7,1},{8,14},{9,15},{10,... | collective-permute-start | bytes 884744 | tf_op jit(solution)/shard_map/ppermute | solution.py:615
  62.7 3.5 %copy-start.1 = (bf16[2,1,256,384]{3,2,1,0:T(8,128)(2,1)S(1)}, bf16[2,1,256,384]{3,2,1,0:T(8,128)(2,1)}, u32[]{:S(2)}) copy-start(bf16[2,1,256,384]{3,2,1,0:T(8,128)(2,1)} %param.14) | copy-start | bytes 1179652
  70.4 2.1 %collective-permute-start.16 = (bf16[832,384]{1,0:T(8,128)(2,1)S(1)}, bf16[832,384]{1,0:T(8,128)(2,1)S(1)}, u32[]{:S(2)}, u32[]{:S(2)}) collective-permute-start(bf16[832,384]{1,0:T(8,128)(2,1)S(1)} %get-tuple-element.143), channel_id=1, source_target_pairs={{0,1},{1,0},{2,3},{3,2},{4,5},{5,4},{6,7},{7,6},{8,9},{9,8},{10,11... | collective-permute-start | bytes 1916936 | tf_op jit(solution)/shard_map/ppermute | solution.py:615
  70.8 6.3 %collective-permute-start.20 = (bf16[192,384]{1,0:T(8,128)(2,1)S(1)}, bf16[192,384]{1,0:T(8,128)(2,1)S(1)}, u32[]{:S(2)}, u32[]{:S(2)}) collective-permute-start(bf16[192,384]{1,0:T(8,128)(2,1)S(1)} %get-tuple-element.152), channel_id=1, source_target_pairs={{0,8},{8,0},{16,24},{24,16},{1,9},{9,1},{17,25},{25,17},{2,10},{10... | collective-permute-start | bytes 442376 | tf_op jit(solution)/shard_map/ppermute | solution.py:615
  72.7 11.0 %collective-permute-start.17 = (bf16[224,384]{1,0:T(8,128)(2,1)S(1)}, bf16[224,384]{1,0:T(8,128)(2,1)S(1)}, u32[]{:S(2)}, u32[]{:S(2)}) collective-permute-start(bf16[224,384]{1,0:T(8,128)(2,1)S(1)} %get-tuple-element.149), channel_id=1, source_target_pairs={{0,2},{1,3},{2,0},{3,1},{4,6},{5,7},{6,4},{7,5},{8,10},{9,11},{10,... | collective-permute-start | bytes 516104 | tf_op jit(solution)/shard_map/ppermute | solution.py:615
  74.0 9.8 %collective-permute-start.18 = (bf16[224,384]{1,0:T(8,128)(2,1)S(1)}, bf16[224,384]{1,0:T(8,128)(2,1)S(1)}, u32[]{:S(2)}, u32[]{:S(2)}) collective-permute-start(bf16[224,384]{1,0:T(8,128)(2,1)S(1)} %get-tuple-element.150), channel_id=1, source_target_pairs={{0,4},{1,5},{2,6},{3,7},{4,0},{5,1},{6,2},{7,3},{8,12},{9,13},{10,... | collective-permute-start | bytes 516104 | tf_op jit(solution)/shard_map/ppermute | solution.py:615
  74.7 9.1 %collective-permute-start.19 = (bf16[224,384]{1,0:T(8,128)(2,1)S(1)}, bf16[224,384]{1,0:T(8,128)(2,1)S(1)}, u32[]{:S(2)}, u32[]{:S(2)}) collective-permute-start(bf16[224,384]{1,0:T(8,128)(2,1)S(1)} %get-tuple-element.151), channel_id=1, source_target_pairs={{0,6},{1,7},{2,4},{3,5},{4,2},{5,3},{6,0},{7,1},{8,14},{9,15},{10,... | collective-permute-start | bytes 516104 | tf_op jit(solution)/shard_map/ppermute | solution.py:615
  77.1 6.7 %collective-permute-start.21 = (bf16[96,384]{1,0:T(8,128)(2,1)S(1)}, bf16[96,384]{1,0:T(8,128)(2,1)S(1)}, u32[]{:S(2)}, u32[]{:S(2)}) collective-permute-start(bf16[96,384]{1,0:T(8,128)(2,1)S(1)} %get-tuple-element.153), channel_id=1, source_target_pairs={{0,16},{8,24},{16,0},{24,8},{1,17},{9,25},{17,1},{25,9},{2,18},{10... | collective-permute-start | bytes 221192 | tf_op jit(solution)/shard_map/ppermute | solution.py:615
  84.0 5.7 %collective-permute-start.22 = (bf16[128,384]{1,0:T(8,128)(2,1)S(1)}, bf16[128,384]{1,0:T(8,128)(2,1)S(1)}, u32[]{:S(2)}, u32[]{:S(2)}) collective-permute-start(bf16[128,384]{1,0:T(8,128)(2,1)S(1)} %get-tuple-element.158), channel_id=1, source_target_pairs={{0,8},{8,0},{16,24},{24,16},{1,9},{9,1},{17,25},{25,17},{2,10},{10... | collective-permute-start | bytes 294920 | tf_op jit(solution)/shard_map/ppermute | solution.py:615
  85.7 9.9 %collective-permute-start.23 = (bf16[128,384]{1,0:T(8,128)(2,1)S(1)}, bf16[128,384]{1,0:T(8,128)(2,1)S(1)}, u32[]{:S(2)}, u32[]{:S(2)}) collective-permute-start(bf16[128,384]{1,0:T(8,128)(2,1)S(1)} %get-tuple-element.159), channel_id=1, source_target_pairs={{0,16},{8,24},{16,0},{24,8},{1,17},{9,25},{17,1},{25,9},{2,18},{10... | collective-permute-start | bytes 294920 | tf_op jit(solution)/shard_map/ppermute | solution.py:615
  88.3 7.3 %collective-permute-start.24 = (bf16[128,384]{1,0:T(8,128)(2,1)S(1)}, bf16[128,384]{1,0:T(8,128)(2,1)S(1)}, u32[]{:S(2)}, u32[]{:S(2)}) collective-permute-start(bf16[128,384]{1,0:T(8,128)(2,1)S(1)} %get-tuple-element.160), channel_id=1, source_target_pairs={{0,24},{8,16},{16,8},{24,0},{1,25},{9,17},{17,9},{25,1},{2,26},{10... | collective-permute-start | bytes 294920 | tf_op jit(solution)/shard_map/ppermute | solution.py:615
  95.7 4.5 %collective-permute-start.25 = (bf16[256,384]{1,0:T(8,128)(2,1)S(1)}, bf16[256,384]{1,0:T(8,128)(2,1)S(1)}, u32[]{:S(2)}, u32[]{:S(2)}) collective-permute-start(bf16[256,384]{1,0:T(8,128)(2,1)S(1)} %get-tuple-element.162.refs_4_), channel_id=1, source_target_pairs={{0,1},{1,0},{2,3},{3,2},{4,5},{5,4},{6,7},{7,6},{8,9},{9,8},{10,11... | collective-permute-start | bytes 589832 | tf_op jit(solution)/shard_map/ppermute | solution.py:615
  95.8 7.8 %collective-permute-start.28 = (bf16[144,384]{1,0:T(8,128)(2,1)S(1)}, bf16[144,384]{1,0:T(8,128)(2,1)S(1)}, u32[]{:S(2)}, u32[]{:S(2)}) collective-permute-start(bf16[144,384]{1,0:T(8,128)(2,1)S(1)} %get-tuple-element.165.refs_0_), channel_id=1, source_target_pairs={{0,24},{8,16},{16,8},{24,0},{1,25},{9,17},{17,9},{25,1},{2,26},{10... | collective-permute-start | bytes 331784 | tf_op jit(solution)/shard_map/ppermute | solution.py:615
  98.3 11.1 %collective-permute-start.27 = (bf16[144,384]{1,0:T(8,128)(2,1)S(1)}, bf16[144,384]{1,0:T(8,128)(2,1)S(1)}, u32[]{:S(2)}, u32[]{:S(2)}) collective-permute-start(bf16[144,384]{1,0:T(8,128)(2,1)S(1)} %get-tuple-element.165.refs_0_), channel_id=1, source_target_pairs={{0,16},{8,24},{16,0},{24,8},{1,17},{9,25},{17,1},{25,9},{2,18},{10... | collective-permute-start | bytes 331784 | tf_op jit(solution)/shard_map/ppermute | solution.py:615
  98.9 10.5 %collective-permute-start.26 = (bf16[144,384]{1,0:T(8,128)(2,1)S(1)}, bf16[144,384]{1,0:T(8,128)(2,1)S(1)}, u32[]{:S(2)}, u32[]{:S(2)}) collective-permute-start(bf16[144,384]{1,0:T(8,128)(2,1)S(1)} %get-tuple-element.165.refs_0_), channel_id=1, source_target_pairs={{0,8},{8,0},{16,24},{24,16},{1,9},{9,1},{17,25},{25,17},{2,10},{10... | collective-permute-start | bytes 331784 | tf_op jit(solution)/shard_map/ppermute | solution.py:615

commit v4 on v3

--- a/solution.py
+++ b/solution.py
@@ -16,6 +16,7 @@
 CUBIC = 0.044715
 MARGIN = 0.0
 PACK_LIMIT = 56 * 1024 * 1024
+MOD_USED = 14
 MOD_ROWS = 16
 
 
@@ -500,16 +501,19 @@
         out[j // 2 * quarter : (j // 2 + 1) * quarter, :] = total.astype(out.dtype)
 
 
-def gather_groups(dp, sizes, layouts, *refs):
-    pieces, outs, scratch = refs[:dp], refs[dp : -len(sizes)], refs[-len(sizes) :]
+def gather_groups(dp, orders, layouts, *refs):
+    count = sum(len(order) for order in orders)
+    arrays, outs, scratch = list(refs[:count]), list(refs[count : -len(orders)]), refs[-len(orders) :]
     me = lax.axis_index("dp")
-    start, outs = 0, list(outs)
-    for quarter, layout, rows_s in zip(sizes, layouts, scratch):
-        for j, piece in enumerate(pieces):
-            at = pl.multiple_of((me ^ j) * quarter, 16)
-            rows_s[pl.ds(at, quarter), :] = piece[start : start + quarter, :].astype(F32)
-        start += quarter
-        d, at = rows_s.shape[1], 0
+    for order, layout, rows_s in zip(orders, layouts, scratch):
+        quarter, d = rows_s.shape[0] // dp, rows_s.shape[1]
+        for some in order:
+            array = arrays.pop(0)
+            for i, j in enumerate(some):
+                at = pl.multiple_of((me ^ j) * quarter, 16)
+                piece = array[i * quarter : (i + 1) * quarter, :]
+                rows_s[pl.ds(at, quarter), :] = piece.astype(F32)
+        at = 0
         for blocks, rows in layout:
             out = outs.pop(0)
             for j in range(blocks):
@@ -532,15 +536,16 @@
 def last_chips(count, dp, quarter, rows, own, *refs):
     received, mine, outs = refs[:count], refs[count], refs[count + 1 : count + dp]
     total_s, tail_s = refs[count + dp :]
+    tail_s[...] = jnp.zeros_like(tail_s)
     total = own[0:rows, :]
     for piece in received:
         total = total + piece[0:rows, :].astype(F32)
     total_s[...] = total[: rows - 16]
-    tail_s[0:16, :] = total[rows - 16 :].astype(BF)
-    tail_s[16 : 16 + MOD_ROWS, :] = own[rows:, :].astype(BF)
-    for i, piece in enumerate(received):
-        at = 16 + (i + 1) * MOD_ROWS
-        tail_s[at : at + MOD_ROWS, :] = piece[rows:, :]
+    for i, piece in enumerate((own,) + received):
+        lines = piece[rows:, :].astype(F32)
+        tail_s[i * MOD_USED : (i + 1) * MOD_USED, :] = lines[0:MOD_USED]
+    end = (count + 1) * MOD_USED
+    tail_s[end : end + 8, :] = total[rows - 16 : rows - 8]
     me = lax.axis_index("dp")
     for j in range(dp):
         part = total_s[pl.ds(pl.multiple_of((me ^ j) * quarter, 16), quarter), :]
@@ -549,18 +554,19 @@
         name[quarter:, :] = tail_s[...].astype(name.dtype)
 
 
-def add_groups(dp, sizes, *refs):
-    low, mods = refs[2 + dp :]
-    start = 0
-    for quarter, pieces in zip(sizes, (refs[:2], refs[2 : 2 + dp])):
-        total = pieces[0][0:quarter, :]
-        for piece in pieces[1:]:
-            total = total + piece[0:quarter, :].astype(F32)
-        low[start : start + quarter, :] = total.astype(BF)
-        start += quarter
-    each = pieces[0].shape[0] - quarter - 16
+def add_two(first, second, out):
+    out[...] = (first[...] + second[...].astype(F32)).astype(BF)
+
+
+def add_groups(dp, quarter, *refs):
+    pieces, (low, mods) = refs[:dp], refs[dp:]
+    total = pieces[0][0:quarter, :]
+    for piece in pieces[1:]:
+        total = total + piece[0:quarter, :].astype(F32)
+    low[...] = total.astype(BF)
+    each = pieces[0].shape[0] - quarter
     for j, piece in enumerate(pieces):
-        mods[j * each : (j + 1) * each, :] = piece[quarter + 16 :, :].astype(BF)
+        mods[j * each : (j + 1) * each, :] = piece[quarter:, :].astype(BF)
 
 
 def ada_grads(plan, quarter, *refs):
@@ -568,29 +574,30 @@
     pieces, mods = refs[:dp], refs[dp : dp + 2]
     ada, ada_bias, qv, proj, fc1, fc2 = refs[dp + 2 : dp + 8]
     rows_s, turned_s = refs[dp + 8 :]
-    each = dp * plan.fsdp * MOD_ROWS // 2
-    total = pieces[0][quarter : quarter + 16, :].astype(F32)
+    block = pieces[0].shape[0] - quarter
+    used = len(plan.peers) * MOD_USED
+    each = dp * block
+    total = pieces[0][quarter + used : quarter + used + 8, :].astype(F32)
     for piece in pieces[1:]:
-        total = total + piece[quarter : quarter + 16, :].astype(F32)
+        total = total + piece[quarter:, :].astype(F32)[used : used + 8]
     for j, rows in enumerate(mods):
         rows_s[j * each : (j + 1) * each, :] = rows[...]
     count = 2 * each
     row = lax.broadcasted_iota(jnp.int32, (count, count), 0)
     column = lax.broadcasted_iota(jnp.int32, (count, count), 1)
-    slot = row % MOD_ROWS
-    source = row - slot + jnp.where(slot >= 7, 7, 0)
-    pick = ((column == source) & (slot < 14)).astype(BF)
+    slot = row % block
+    pick = ((column == row - slot % 7) & (slot < used)).astype(BF)
     turned_s[...] = dot(pick, rows_s[...]).T
     me = lax.axis_index("fsdp")
     mine = turned_s[pl.ds(pl.multiple_of(me * r, 16), r), :].astype(BF)
-    lane = lax.broadcasted_iota(jnp.int32, (1, count), 1) % MOD_ROWS
-    tall = lax.broadcasted_iota(jnp.int32, (count, 1), 0) % MOD_ROWS
+    lane = lax.broadcasted_iota(jnp.int32, (1, count), 1) % block
+    tall = lax.broadcasted_iota(jnp.int32, (count, 1), 0) % block
     values = rows_s[...]
     sums = []
     for j in range(6):
-        here = (lane == 1 + j) | (lane == 8 + j)
+        here = (lane % 7 == 1 + j) & (lane < used)
         ada[:, j * d : (j + 1) * d] = dot(jnp.where(here, mine, jnp.zeros_like(mine)), values)
-        there = (tall == 1 + j) | (tall == 8 + j)
+        there = (tall % 7 == 1 + j) & (tall < used)
         sums.append(
             jnp.sum(jnp.where(there, values.astype(F32), 0.0), axis=0, keepdims=True)
         )
@@ -626,12 +633,13 @@
     return [value] + [swap(plan, value, k) for k in plan.peers[1:]]
 
 
-def gather_joined(plan, chips):
+def gather_joined(plan, gate, chips):
     if not plan.direct:
         return chips
     joined = []
     count = len(chips) // 2
     for some in (chips[:count], chips[count:]):
+        some = [behind([v], gate, *joined[:1])[0] for v in some]
         shape = (sum(v.shape[0] for v in some), plan.d)
         (mine,) = call(join, [(shape, BF)], some, micros=0.4)
         joined += [mine, swap(plan, mine, 1)]
@@ -698,22 +706,29 @@
     )
     pieces = [swap(plan, piece, k) for piece, k in zip(pieces, plan.peers[1:])]
     pieces = behind(pieces, cond_grad, mlp_half)
-    tail = 16 + peers * MOD_ROWS
+    tail = -(-(peers * MOD_USED + 8) // 16) * 16
     mine, *quarters = call(
         functools.partial(last_chips, peers - 1, dp, quarter, rows),
         [((quarter + tail, d), F32)] + [((quarter + tail, d), BF)] * (dp - 1),
         [own] + pieces,
-        [pltpu.VMEM((rows - 16, d), F32), pltpu.VMEM((tail, d), BF)],
+        [pltpu.VMEM((rows - 16, d), F32), pltpu.VMEM((tail, d), F32)],
     )
     quarters = [swap(plan, part, j + 1, "dp") for j, part in enumerate(quarters)]
-    half = dp * peers * MOD_ROWS
-    sizes = (mlp_mine.shape[0], quarter)
+    mlp_mine, mlp_half = behind([mlp_mine, mlp_half], mine)
+    (held,) = call(add_two, [(mlp_mine.shape, BF)], [mlp_mine, mlp_half])
+    order, step = [0], dp // 2
+    while step > 1:
+        found = [held, swap(plan, held, step, "dp")]
+        order, step = order + [j ^ step for j in order], step // 2
+        (held,) = call(join, [((2 * held.shape[0], d), BF)], found)
+    half = dp * tail
     low, mods = call(
-        functools.partial(add_groups, dp, sizes),
-        [((sum(sizes), d), BF), ((half, d), BF)],
-        [mlp_mine, mlp_half, mine] + quarters,
-    )
-    parts = [swap(plan, low, j, "dp") for j in range(1, dp)]
+        functools.partial(add_groups, dp, quarter),
+        [((quarter, d), BF), ((half, d), BF)],
+        [mine] + quarters,
+    )
+    parts = [swap(plan, low, j, "dp") for j in range(1, dp)] + [swap(plan, held, 1, "dp")]
+    orders = ((order, [j ^ 1 for j in order]), [[j] for j in range(dp)])
     ada, *biases = call(
         functools.partial(ada_grads, plan, quarter),
         [((r, 6 * d), F32)] + [((1, w * d // plan.fsdp), F32) for w in plan.bias_rows],
@@ -722,13 +737,13 @@
         micros=2,
     )
     biases = [bias.reshape(-1) for bias in biases]
-    parts = behind(parts, ada, *biases)
+    *parts, other = behind(parts, ada, *biases)
     layouts = (mlp_layout, ((3, r), (1, r)))
     fc1, fc2, qkv, proj = call(
-        functools.partial(gather_groups, dp, sizes, layouts),
+        functools.partial(gather_groups, dp, orders, layouts),
         [((height, blocks * d), F32) for layout in layouts for blocks, height in layout],
-        [low] + parts,
-        [pltpu.VMEM((size * dp, d), F32) for size in sizes],
+        [held, other, low] + parts,
+        [pltpu.VMEM((size, d), F32) for size in (held.shape[0] * 2, quarter * dp)],
     )
     return [ada, qkv, proj, fc1, fc2], biases
 
@@ -794,7 +809,7 @@
 
         biases, weights, third = [whole(v) for v in biases], [whole(v) for v in weights], whole(third)
     lengths = [bias.shape[0] for bias in biases]
-    width = -(-sum(lengths) // 128) * 128
+    width = -(-sum(lengths) // 1024) * 1024
     line = sum(
         jnp.pad(bias.astype(F32), (sum(lengths[:i]), width - sum(lengths[: i + 1])))
         for i, bias in enumerate(biases)
@@ -802,7 +817,7 @@
     first, second, live = call(
         functools.partial(pack_weights, plan),
         [((5 * r + 16, d), BF), (((2 * plan.ffb + 5) * r, d), BF), ((group, 128), F32)],
-        weights + [third, line[None, :], counts.T],
+        weights + [third, line.reshape(1, -1), counts.T],
         [pltpu.VMEM((16, d), F32), pltpu.SemaphoreType.DMA((plan.ffb + 11,))],
         smem=(6,),
         far=(0, 1, 2, 3, 4),
@@ -834,9 +849,7 @@
         room=5,
         micros=4,
     )
-    if plan.direct:
-        second = second[:1] + [behind([v], mod_first)[0] for v in second[1:]]
-    shards = gather_joined(plan, second)
+    shards = gather_joined(plan, mod_first, second)
     halves = len(plan.peers) if plan.direct else 1
     sides = plan.sides
     outs = call(

time: 111 us -> 108 us (0.973)
  waiting for transfers between devices: 38.7 us -> 34.5 us
  starting transfers between devices: 31.6 us -> 33.4 us
    ppermute x29 -> x31, waiting for transfers between devices: 38.7 us -> 34.5 us  [swap(): return lax.ppermute(value, axis, [(i, i ^ k) for i in range(size)])]
    ppermute x29 -> x31, starting transfers between devices: 31.6 us -> 33.4 us  [swap(): return lax.ppermute(value, axis, [(i, i ^ k) for i in range(size)])]
    pallas_call x20 -> x22, Pallas kernels: 33.7 us -> 33.6 us  [call(): pl.pallas_call(body, out_shape=[jax.ShapeDtypeStruct(shape, kind) for sha...]
  transfers between devices with their start and end apart: 29 -> 31, of which waited for: 21 -> 20; matrix products, arithmetic and copies ran while one was open for 1% -> 1% of each run, Pallas kernels for 20% -> 20%
where the time goes in v4:
time: 108 us
  waiting for transfers between devices  34.5 us (32%)
  Pallas kernels  33.6 us (31%)
  starting transfers between devices  33.4 us (31%)
  local copies, waits for them, and re-layouts  3.62 us (3%)
  other arithmetic  2.01 us (2%)
    ppermute x31, waiting for transfers between devices, swap(): return lax.ppermute(value, axis, [(i, i ^ k) for i in range(size)])  34.5 us
    pallas_call x22, Pallas kernels, call(): pl.pallas_call(body, out_shape=[jax.ShapeDtypeStruct(shape, kind) for sha...  33.6 us
    ppermute x31, starting transfers between devices, swap(): return lax.ppermute(value, axis, [(i, i ^ k) for i in range(size)])  33.4 us
    unnamed x16, local copies, waits for them, and re-layouts  3.62 us
  transfers between devices with their start and end apart: 31, of which 20 were waited for; matrix products, arithmetic and copies ran while one was open for 1% of the time, Pallas kernels for 20%

profile of v4, /device:TPU:0, one launch (start us, length us, event | category | flops | bytes accessed | tf_op | source)
XLA Modules:
  0.0 108.0 jit_solution(7315507187161357148)
XLA Ops:
  0.6 1.4 %convert_add_fusion = f32[1024]{0:T(1024)} fusion(bf16[48]{0:T(256)(128)(2,1)} %param.27, bf16[192]{0:T(256)(128)(2,1)} %param.25, bf16[48]{0:T(256)(128)(2,1)} %param.23, bf16[96]{0:T(256)(128)(2,1)} %param.21, bf16[288]{0:T(512)(128)(2,1)} %param.19), kind=kLoop, calls=%fused_computation | loop fusion | flops 9216 | bytes 5440 | tf_op jit(solution)/shard_map/add | solution.py:813
  2.1 3.0 %shard_map.237 = (bf16[256,384]{1,0:T(8,128)(2,1)}, bf16[624,384]{1,0:T(8,128)(2,1)}, f32[2,128]{1,0:T(2,128)}) custom-call(bf16[48,2304]{1,0:T(8,128)(2,1)} %ada.1, bf16[48,1152]{1,0:T(8,128)(2,1)} %qkv.1, bf16[48,384]{1,0:T(8,128)(2,1)} %proj.1, bf16[48,1536]{1,0:T(8,128)(2,1)} %fc1.1, bf16[192,384]{1,0:T(8,128)(2,1)} %fc2.1, f32[1,1024]{1,0:T(1,128)} %bitcast.23, ...), custom_call_target="tpu_custom_call" | custom-call | bytes 3690000 | tf_op jit(solution)/shard_map/pallas_call | solution.py:65
  5.0 4.0 %collective-permute-start.5 = (bf16[256,384]{1,0:T(8,128)(2,1)}, bf16[256,384]{1,0:T(8,128)(2,1)S(1)}, u32[]{:S(2)}, u32[]{:S(2)}) collective-permute-start(bf16[256,384]{1,0:T(8,128)(2,1)} %get-tuple-element.100.refs_3_), channel_id=1, source_target_pairs={{0,6},{1,7},{2,4},{3,5},{4,2},{5,3},{6,0},{7,1},{8,14},{9,15},{10,... | collective-permute-start | bytes 589832 | tf_op jit(solution)/shard_map/ppermute | solution.py:622
  9.0 0.5 collective-permute-start.3
  9.7 1.9 %collective-permute-start.7 = (bf16[624,384]{1,0:T(8,128)(2,1)}, bf16[624,384]{1,0:T(8,128)(2,1)S(1)}, u32[]{:S(2)}, u32[]{:S(2)}) collective-permute-start(bf16[624,384]{1,0:T(8,128)(2,1)} %get-tuple-element.107.refs_0_), channel_id=1, source_target_pairs={{0,2},{1,3},{2,0},{3,1},{4,6},{5,7},{6,4},{7,5},{8,10},{9,11},{10,... | collective-permute-start | bytes 1437704 | tf_op jit(solution)/shard_map/ppermute | solution.py:622
  11.5 1.5 %collective-permute-start.10 = (bf16[624,384]{1,0:T(8,128)(2,1)}, bf16[624,384]{1,0:T(8,128)(2,1)S(1)}, u32[]{:S(2)}, u32[]{:S(2)}) collective-permute-start(bf16[624,384]{1,0:T(8,128)(2,1)} %get-tuple-element.107.refs_0_), channel_id=1, source_target_pairs={{0,6},{1,7},{2,4},{3,5},{4,2},{5,3},{6,0},{7,1},{8,14},{9,15},{10,... | collective-permute-start | bytes 1437704 | tf_op jit(solution)/shard_map/ppermute | solution.py:622
  13.0 2.0 %collective-permute-done.5.refs_9_ = bf16[256,384]{1,0:T(8,128)(2,1)S(1)} collective-permute-done((bf16[256,384]{1,0:T(8,128)(2,1)}, bf16[256,384]{1,0:T(8,128)(2,1)S(1)}, u32[]{:S(2)}, u32[]{:S(2)}) %collective-permute-start.5) | collective-permute-done | bytes 196640 | tf_op jit(solution)/shard_map/ppermute | solution.py:622
  15.0 2.0 %collective-permute-start.9 = (bf16[624,384]{1,0:T(8,128)(2,1)}, bf16[624,384]{1,0:T(8,128)(2,1)S(1)}, u32[]{:S(2)}, u32[]{:S(2)}) collective-permute-start(bf16[624,384]{1,0:T(8,128)(2,1)} %get-tuple-element.107.refs_0_), channel_id=1, source_target_pairs={{0,4},{1,5},{2,6},{3,7},{4,0},{5,1},{6,2},{7,3},{8,12},{9,13},{10,... | collective-permute-start | bytes 1437704 | tf_op jit(solution)/shard_map/ppermute | solution.py:622
  17.0 1.4 %collective-permute-done.3.refs_7_ = bf16[256,384]{1,0:T(8,128)(2,1)S(1)} collective-permute-done((bf16[256,384]{1,0:T(8,128)(2,1)}, bf16[256,384]{1,0:T(8,128)(2,1)S(1)}, u32[]{:S(2)}, u32[]{:S(2)}) %collective-permute-start.3) | collective-permute-done | bytes 196640 | tf_op jit(solution)/shard_map/ppermute | solution.py:622
  18.4 1.3 %collective-permute-done.1.refs_5_ = bf16[256,384]{1,0:T(8,128)(2,1)S(1)} collective-permute-done((bf16[256,384]{1,0:T(8,128)(2,1)}, bf16[256,384]{1,0:T(8,128)(2,1)S(1)}, u32[]{:S(2)}, u32[]{:S(2)}) %collective-permute-start.1) | collective-permute-done | bytes 196640 | tf_op jit(solution)/shard_map/ppermute | solution.py:622
  19.8 0.3 collective-permute-done.refs_4_
  20.1 0.2 collective-permute-start.4
  20.3 0.9 collective-permute-done.6.refs_10_
  21.2 0.1 collective-permute-start.2
  21.4 0.2 collective-permute-done.4.refs_8_
  21.5 1.1 %collective-permute-done.2.refs_6_ = bf16[256,384]{1,0:T(8,128)(2,1)S(1)} collective-permute-done((bf16[256,384]{1,0:T(8,128)(2,1)S(1)}, bf16[256,384]{1,0:T(8,128)(2,1)S(1)}, u32[]{:S(2)}, u32[]{:S(2)}) %collective-permute-start.2) | collective-permute-done | bytes 196640 | tf_op jit(solution)/shard_map/ppermute | solution.py:622
  22.7 1.0 copy-done
  23.7 1.0 copy-done.3
  24.7 0.9 copy-done.4
  25.6 0.7 copy-done.5
  26.3 4.1 %shard_map.238 = (bf16[512,1152]{1,0:T(8,128)(2,1)S(1)}, bf16[512,384]{1,0:T(8,128)(2,1)S(1)}, f32[2,768]{1,0:T(2,128)S(1)}, f32[16,384]{1,0:T(8,128)S(1)}, bf16...) custom-call(bf16[512,384]{1,0:T(8,128)(2,1)S(1)} %bitcast.16, ...), custom_call_target="tpu_custom_call" | custom-call | bytes 14760000 | tf_op jit(solution)/shard_map/pallas_call | solution.py:65
  30.5 8.4 %collective-permute-done.10.refs_1_ = bf16[624,384]{1,0:T(8,128)(2,1)S(1)} collective-permute-done((bf16[624,384]{1,0:T(8,128)(2,1)}, bf16[624,384]{1,0:T(8,128)(2,1)S(1)}, u32[]{:S(2)}, u32[]{:S(2)}) %collective-permute-start.10) | collective-permute-done | bytes 479264 | tf_op jit(solution)/shard_map/ppermute | solution.py:622
  39.1 0.5 collective-permute-start.8
  39.6 2.0 %collective-permute-done.11.refs_9_ = bf16[1248,384]{1,0:T(8,128)(2,1)S(1)} collective-permute-done((bf16[1248,384]{1,0:T(8,128)(2,1)S(1)}, bf16[1248,384]{1,0:T(8,128)(2,1)S(1)}, u32[]{:S(2)}, u32[]{:S(2)}) %collective-permute-start.11) | collective-permute-done | bytes 958496 | tf_op jit(solution)/shard_map/ppermute | solution.py:622
  41.6 1.4 %collective-permute-done.8.refs_7_ = bf16[1248,384]{1,0:T(8,128)(2,1)S(1)} collective-permute-done((bf16[1248,384]{1,0:T(8,128)(2,1)S(1)}, bf16[1248,384]{1,0:T(8,128)(2,1)S(1)}, u32[]{:S(2)}, u32[]{:S(2)}) %collective-permute-start.8) | collective-permute-done | bytes 958496 | tf_op jit(solution)/shard_map/ppermute | solution.py:622
  43.0 6.4 %shard_map.241 = (bf16[1536,384]{1,0:T(8,128)(2,1)S(1)}, bf16[1536,384]{1,0:T(8,128)(2,1)S(1)}, bf16[512,1536]{1,0:T(8,128)(2,1)S(1)}, bf16[512,1536]{1,0:T(8,12...) custom-call(f32[2,128]{1,0:T(2,128)S(1)} %copy-done.7, ...), custom_call_target="tpu_custom_call" | custom-call | bytes 36900000 | tf_op jit(solution)/shard_map/pallas_call | solution.py:65
  49.3 0.2 collective-permute-start.12
  49.6 2.0 %shard_map.242 = (bf16[512,384]{1,0:T(8,128)(2,1)}, f32[2,384]{1,0:T(2,128)S(1)}) custom-call(f32[2,128]{1,0:T(2,128)S(1)} %copy-done.7, bf16[512,384]{1,0:T(8,128)(2,1)S(1)} %get-tuple-element.111.cot, bf16[512,1536]{1,0:T(8,128)(2,1)S(1)} %get-tuple-element.112.act, bf16[1536,384]{1,0:T(8,128)(2,1)S(1)} %get-tuple-element.113.fc2, ...), custom_call_target="tpu_custom_call" | custom-call | bytes 5535000 | tf_op jit(solution)/shard_map/pallas_call | solution.py:65
  51.6 0.7 collective-permute-done.12.refs_1_
  52.3 0.3 shard_map.243
  52.6 1.8 %collective-permute-start.13 = (bf16[384,384]{1,0:T(8,128)(2,1)S(1)}, bf16[384,384]{1,0:T(8,128)(2,1)S(1)}, u32[]{:S(2)}, u32[]{:S(2)}) collective-permute-start(bf16[384,384]{1,0:T(8,128)(2,1)S(1)} %get-tuple-element.143), channel_id=1, source_target_pairs={{0,2},{1,3},{2,0},{3,1},{4,6},{5,7},{6,4},{7,5},{8,10},{9,11},{10,... | collective-permute-start | bytes 884744 | tf_op jit(solution)/shard_map/ppermute | solution.py:622
  54.3 1.5 %collective-permute-start.14 = (bf16[384,384]{1,0:T(8,128)(2,1)S(1)}, bf16[384,384]{1,0:T(8,128)(2,1)S(1)}, u32[]{:S(2)}, u32[]{:S(2)}) collective-permute-start(bf16[384,384]{1,0:T(8,128)(2,1)S(1)} %get-tuple-element.144), channel_id=1, source_target_pairs={{0,4},{1,5},{2,6},{3,7},{4,0},{5,1},{6,2},{7,3},{8,12},{9,13},{10,... | collective-permute-start | bytes 884744 | tf_op jit(solution)/shard_map/ppermute | solution.py:622
  55.8 0.3 collective-permute-start.15
  56.1 2.8 %shard_map.244 = (bf16[512,384]{1,0:T(8,128)(2,1)S(1)}, f32[512,384]{1,0:T(8,128)S(1)}, bf16[384,384]{1,0:T(8,128)(2,1)S(1)}, f32[16,384]{1,0:T(8,128)S(1)}, f32[2,1152]{1,0:T(2,128)S(1)}) custom-call(f32[2,128]{1,0:T(2,128)S(1)} %copy-done.7, bf16[512,384]{1,0:T(8,128)(2,1)S(1)} %get-tuple-element.111.cot, ...), custom_call_target="tpu_custom_call" | custom-call | bytes 11070000 | tf_op jit(solution)/shard_map/pallas_call | solution.py:65
  58.9 3.5 %shard_map.245.refs_7_.refs_3_ = bf16[256,1152]{1,0:T(8,128)(2,1)S(1)} custom-call(bf16[512,1152]{1,0:T(8,128)(2,1)S(1)} %get-tuple-element.133.projected, bf16[512,384]{1,0:T(8,128)(2,1)S(1)} %get-tuple-element.135.grad_mixed), custom_call_target="tpu_custom_call" | custom-call | bytes 12177000 | tf_op jit(solution)/shard_map/pallas_call | solution.py:65
  62.4 3.5 %shard_map.246.refs_8_.refs_4_ = bf16[256,1152]{1,0:T(8,128)(2,1)S(1)} custom-call(bf16[512,1152]{1,0:T(8,128)(2,1)S(1)} %get-tuple-element.133.projected, bf16[512,384]{1,0:T(8,128)(2,1)S(1)} %get-tuple-element.135.grad_mixed), custom_call_target="tpu_custom_call" | custom-call | bytes 12177000 | tf_op jit(solution)/shard_map/pallas_call | solution.py:65
  65.9 1.8 %shard_map.247 = (bf16[512,384]{1,0:T(8,128)(2,1)}, bf16[16,384]{1,0:T(8,128)(2,1)S(1)}, bf16[512,384]{1,0:T(8,128)(2,1)S(1)}) custom-call(bf16[512,384]{1,0:T(8,128)(2,1)S(1)} %bitcast.17, bf16[2,384]{1,0:T(2,128)(2,1)S(1)} %bitcast.21, f32[512,384]{1,0:T(8,128)S(1)} %get-tuple-element.130.refs_2_, bf16[384,1152]{1,0:T(8,128)(2,1)S(1)} %get-tuple-element.131.refs_3_, ...), custom_call_target="tpu_custom_call" | custom-call | bytes 7380000 | tf_op jit(solution)/shard_map/pallas_call | solution.py:65
  67.7 1.7 %collective-permute-done.14.refs_1_ = bf16[384,384]{1,0:T(8,128)(2,1)S(1)} collective-permute-done((bf16[384,384]{1,0:T(8,128)(2,1)S(1)}, bf16[384,384]{1,0:T(8,128)(2,1)S(1)}, u32[]{:S(2)}, u32[]{:S(2)}) %collective-permute-start.14) | collective-permute-done | bytes 294944 | tf_op jit(solution)/shard_map/ppermute | solution.py:622
  69.4 0.9 shard_map.249
  70.4 0.2 shard_map.250
  70.6 1.6 %collective-permute-start.20 = (bf16[192,384]{1,0:T(8,128)(2,1)S(1)}, bf16[192,384]{1,0:T(8,128)(2,1)S(1)}, u32[]{:S(2)}, u32[]{:S(2)}) collective-permute-start(bf16[192,384]{1,0:T(8,128)(2,1)S(1)} %get-tuple-element.157), channel_id=1, source_target_pairs={{0,8},{8,0},{16,24},{24,16},{1,9},{9,1},{17,25},{25,17},{2,10},{10... | collective-permute-start | bytes 442376 | tf_op jit(solution)/shard_map/ppermute | solution.py:622
  72.3 0.2 collective-permute-done.16.received
  72.5 0.1 shard_map.251
  72.6 1.3 %collective-permute-start.17 = (bf16[224,384]{1,0:T(8,128)(2,1)S(1)}, bf16[224,384]{1,0:T(8,128)(2,1)S(1)}, u32[]{:S(2)}, u32[]{:S(2)}) collective-permute-start(bf16[224,384]{1,0:T(8,128)(2,1)S(1)} %get-tuple-element.154), channel_id=1, source_target_pairs={{0,2},{1,3},{2,0},{3,1},{4,6},{5,7},{6,4},{7,5},{8,10},{9,11},{10,... | collective-permute-start | bytes 516104 | tf_op jit(solution)/shard_map/ppermute | solution.py:622
  73.9 0.8 collective-permute-start.18
  74.7 1.4 %collective-permute-start.19 = (bf16[224,384]{1,0:T(8,128)(2,1)S(1)}, bf16[224,384]{1,0:T(8,128)(2,1)S(1)}, u32[]{:S(2)}, u32[]{:S(2)}) collective-permute-start(bf16[224,384]{1,0:T(8,128)(2,1)S(1)} %get-tuple-element.156), channel_id=1, source_target_pairs={{0,6},{1,7},{2,4},{3,5},{4,2},{5,3},{6,0},{7,1},{8,14},{9,15},{10,... | collective-permute-start | bytes 516104 | tf_op jit(solution)/shard_map/ppermute | solution.py:622
  76.2 0.8 collective-permute-done.20.received
  77.0 2.7 %collective-permute-start.21 = (bf16[96,384]{1,0:T(8,128)(2,1)S(1)}, bf16[96,384]{1,0:T(8,128)(2,1)S(1)}, u32[]{:S(2)}, u32[]{:S(2)}) collective-permute-start(bf16[96,384]{1,0:T(8,128)(2,1)S(1)} %get-tuple-element.158), channel_id=1, source_target_pairs={{0,16},{8,24},{16,0},{24,8},{1,17},{9,25},{17,1},{25,9},{2,18},{10... | collective-permute-start | bytes 221192 | tf_op jit(solution)/shard_map/ppermute | solution.py:622
  79.7 1.7 %shard_map.248 = bf16[2,384]{1,0:T(2,128)(2,1)} custom-call(bf16[2,384]{1,0:T(2,128)(2,1)S(1)} %bitcast.22, bf16[16,384]{1,0:T(8,128)(2,1)S(1)} %get-tuple-element.137.mods, bf16[384,768]{1,0:T(8,128)(2,1)S(1)} %get-tuple-element.138.first, bf16[384,1536]{1,0:T(8,128)(2,1)S(1)} %get-tuple-element.139.second), custom_call_target="tpu_custom_call" | custom-call | bytes 7380000 | tf_op jit(solution)/shard_map/pallas_call | solution.py:65
  81.4 2.3 %collective-permute-done.21.second = bf16[96,384]{1,0:T(8,128)(2,1)S(1)} collective-permute-done((bf16[96,384]{1,0:T(8,128)(2,1)S(1)}, bf16[96,384]{1,0:T(8,128)(2,1)S(1)}, u32[]{:S(2)}, u32[]{:S(2)}) %collective-permute-start.21) | collective-permute-done | bytes 73760 | tf_op jit(solution)/shard_map/ppermute | solution.py:622
  83.9 1.6 %collective-permute-start.22 = (bf16[112,384]{1,0:T(8,128)(2,1)S(1)}, bf16[112,384]{1,0:T(8,128)(2,1)S(1)}, u32[]{:S(2)}, u32[]{:S(2)}) collective-permute-start(bf16[112,384]{1,0:T(8,128)(2,1)S(1)} %get-tuple-element.163), channel_id=1, source_target_pairs={{0,8},{8,0},{16,24},{24,16},{1,9},{9,1},{17,25},{25,17},{2,10},{10... | collective-permute-start | bytes 258056 | tf_op jit(solution)/shard_map/ppermute | solution.py:622
  85.5 2.6 %collective-permute-start.23 = (bf16[112,384]{1,0:T(8,128)(2,1)S(1)}, bf16[112,384]{1,0:T(8,128)(2,1)S(1)}, u32[]{:S(2)}, u32[]{:S(2)}) collective-permute-start(bf16[112,384]{1,0:T(8,128)(2,1)S(1)} %get-tuple-element.164), channel_id=1, source_target_pairs={{0,16},{8,24},{16,0},{24,8},{1,17},{9,25},{17,1},{25,9},{2,18},{10... | collective-permute-start | bytes 258056 | tf_op jit(solution)/shard_map/ppermute | solution.py:622
  88.1 0.2 collective-permute-start.24
  88.3 1.8 %collective-permute-start.26 = (bf16[96,384]{1,0:T(8,128)(2,1)S(1)}, bf16[96,384]{1,0:T(8,128)(2,1)S(1)}, u32[]{:S(2)}, u32[]{:S(2)}) collective-permute-start(bf16[96,384]{1,0:T(8,128)(2,1)S(1)} %shard_map.256.refs_0_), channel_id=1, source_target_pairs={{0,16},{8,24},{16,0},{24,8},{1,17},{9,25},{17,1},{25,9},{2,18},{10... | collective-permute-start | bytes 221192 | tf_op jit(solution)/shard_map/ppermute | solution.py:622
  90.1 6.1 %collective-permute-done.23.refs_2_ = bf16[112,384]{1,0:T(8,128)(2,1)S(1)} collective-permute-done((bf16[112,384]{1,0:T(8,128)(2,1)S(1)}, bf16[112,384]{1,0:T(8,128)(2,1)S(1)}, u32[]{:S(2)}, u32[]{:S(2)}) %collective-permute-start.23) | collective-permute-done | bytes 86048 | tf_op jit(solution)/shard_map/ppermute | solution.py:622
  96.3 2.2 %collective-permute-done.26.refs_1_ = bf16[96,384]{1,0:T(8,128)(2,1)S(1)} collective-permute-done((bf16[96,384]{1,0:T(8,128)(2,1)S(1)}, bf16[96,384]{1,0:T(8,128)(2,1)S(1)}, u32[]{:S(2)}, u32[]{:S(2)}) %collective-permute-start.26) | collective-permute-done | bytes 73760 | tf_op jit(solution)/shard_map/ppermute | solution.py:622
  98.7 2.5 %collective-permute-start.29 = (bf16[48,384]{1,0:T(8,128)(2,1)S(1)}, bf16[48,384]{1,0:T(8,128)(2,1)S(1)}, u32[]{:S(2)}, u32[]{:S(2)}) collective-permute-start(bf16[48,384]{1,0:T(8,128)(2,1)S(1)} %get-tuple-element.172.refs_2_), channel_id=1, source_target_pairs={{0,24},{8,16},{16,8},{24,0},{1,25},{9,17},{17,9},{25,1},{2,26},{10... | collective-permute-start | bytes 110600 | tf_op jit(solution)/shard_map/ppermute | solution.py:622
  101.2 0.9 collective-permute-start.28
  102.1 1.0 collective-permute-start.27
  103.1 1.9 %shard_map.255 = (f32[48,2304]{1,0:T(8,128)}, f32[1,288]{1,0:T(1,128)S(1)}, f32[1,96]{1,0:T(1,128)}, f32[1,48]{1,0:T(1,128)}, f32[1,192]{1,0:T(1,128)}, /*index=5*/f32[1,48]{1,0:T(1,128)}) custom-call(f32[112,384]{1,0:T(8,128)S(1)} %get-tuple-element.162.refs_0_, bf16[112,384]{1,0:T(8,128)(2,1)S(1)} %collective-permute-done.22.refs_1_, ...), custom_call_target="tpu_custom_call" | custom-call | bytes 7380000 | tf_op jit(solution)/shard_map/pallas_call | solution.py:65
  105.0 0.6 reduce
  105.6 1.0 collective-permute-done.29.refs_5_
  106.6 0.4 collective-permute-done.28.refs_4_
  107.0 1.0 shard_map.258
  (38 shorter events, 1.0 us)
Async XLA Ops:
  5.0 9.9 %collective-permute-start.5 = (bf16[256,384]{1,0:T(8,128)(2,1)}, bf16[256,384]{1,0:T(8,128)(2,1)S(1)}, u32[]{:S(2)}, u32[]{:S(2)}) collective-permute-start(bf16[256,384]{1,0:T(8,128)(2,1)} %get-tuple-element.100.refs_3_), channel_id=1, source_target_pairs={{0,6},{1,7},{2,4},{3,5},{4,2},{5,3},{6,0},{7,1},{8,14},{9,15},{10,... | collective-permute-start | bytes 589832 | tf_op jit(solution)/shard_map/ppermute | solution.py:622
  9.0 9.4 %collective-permute-start.3 = (bf16[256,384]{1,0:T(8,128)(2,1)}, bf16[256,384]{1,0:T(8,128)(2,1)S(1)}, u32[]{:S(2)}, u32[]{:S(2)}) collective-permute-start(bf16[256,384]{1,0:T(8,128)(2,1)} %get-tuple-element.100.refs_3_), channel_id=1, source_target_pairs={{0,4},{1,5},{2,6},{3,7},{4,0},{5,1},{6,2},{7,3},{8,12},{9,13},{10,... | collective-permute-start | bytes 589832 | tf_op jit(solution)/shard_map/ppermute | solution.py:622
  9.5 10.3 %collective-permute-start.1 = (bf16[256,384]{1,0:T(8,128)(2,1)}, bf16[256,384]{1,0:T(8,128)(2,1)S(1)}, u32[]{:S(2)}, u32[]{:S(2)}) collective-permute-start(bf16[256,384]{1,0:T(8,128)(2,1)} %get-tuple-element.100.refs_3_), channel_id=1, source_target_pairs={{0,2},{1,3},{2,0},{3,1},{4,6},{5,7},{6,4},{7,5},{8,10},{9,11},{10,... | collective-permute-start | bytes 589832 | tf_op jit(solution)/shard_map/ppermute | solution.py:622
  9.7 20.8 %collective-permute-start.7 = (bf16[624,384]{1,0:T(8,128)(2,1)}, bf16[624,384]{1,0:T(8,128)(2,1)S(1)}, u32[]{:S(2)}, u32[]{:S(2)}) collective-permute-start(bf16[624,384]{1,0:T(8,128)(2,1)} %get-tuple-element.107.refs_0_), channel_id=1, source_target_pairs={{0,2},{1,3},{2,0},{3,1},{4,6},{5,7},{6,4},{7,5},{8,10},{9,11},{10,... | collective-permute-start | bytes 1437704 | tf_op jit(solution)/shard_map/ppermute | solution.py:622
  11.5 27.4 %collective-permute-start.10 = (bf16[624,384]{1,0:T(8,128)(2,1)}, bf16[624,384]{1,0:T(8,128)(2,1)S(1)}, u32[]{:S(2)}, u32[]{:S(2)}) collective-permute-start(bf16[624,384]{1,0:T(8,128)(2,1)} %get-tuple-element.107.refs_0_), channel_id=1, source_target_pairs={{0,6},{1,7},{2,4},{3,5},{4,2},{5,3},{6,0},{7,1},{8,14},{9,15},{10,... | collective-permute-start | bytes 1437704 | tf_op jit(solution)/shard_map/ppermute | solution.py:622
  15.0 23.9 %collective-permute-start.9 = (bf16[624,384]{1,0:T(8,128)(2,1)}, bf16[624,384]{1,0:T(8,128)(2,1)S(1)}, u32[]{:S(2)}, u32[]{:S(2)}) collective-permute-start(bf16[624,384]{1,0:T(8,128)(2,1)} %get-tuple-element.107.refs_0_), channel_id=1, source_target_pairs={{0,4},{1,5},{2,6},{3,7},{4,0},{5,1},{6,2},{7,3},{8,12},{9,13},{10,... | collective-permute-start | bytes 1437704 | tf_op jit(solution)/shard_map/ppermute | solution.py:622
  18.4 1.7 %collective-permute-start = (bf16[256,384]{1,0:T(8,128)(2,1)}, bf16[256,384]{1,0:T(8,128)(2,1)S(1)}, u32[]{:S(2)}, u32[]{:S(2)}) collective-permute-start(bf16[256,384]{1,0:T(8,128)(2,1)} %get-tuple-element.100.refs_3_), channel_id=1, source_target_pairs={{0,1},{1,0},{2,3},{3,2},{4,5},{5,4},{6,7},{7,6},{8,9},{9,8},{10,11... | collective-permute-start | bytes 589832 | tf_op jit(solution)/shard_map/ppermute | solution.py:622
  19.8 1.4 %collective-permute-start.6 = (bf16[256,384]{1,0:T(8,128)(2,1)S(1)}, bf16[256,384]{1,0:T(8,128)(2,1)S(1)}, u32[]{:S(2)}, u32[]{:S(2)}) collective-permute-start(bf16[256,384]{1,0:T(8,128)(2,1)S(1)} %collective-permute-done.5.refs_9_), channel_id=1, source_target_pairs={{0,1},{1,0},{2,3},{3,2},{4,5},{5,4},{6,7},{7,6},{8,9},{9,8},{10,11... | collective-permute-start | bytes 589832 | tf_op jit(solution)/shard_map/ppermute | solution.py:622
  20.1 1.4 %collective-permute-start.4 = (bf16[256,384]{1,0:T(8,128)(2,1)S(1)}, bf16[256,384]{1,0:T(8,128)(2,1)S(1)}, u32[]{:S(2)}, u32[]{:S(2)}) collective-permute-start(bf16[256,384]{1,0:T(8,128)(2,1)S(1)} %collective-permute-done.3.refs_7_), channel_id=1, source_target_pairs={{0,1},{1,0},{2,3},{3,2},{4,5},{5,4},{6,7},{7,6},{8,9},{9,8},{10,11... | collective-permute-start | bytes 589832 | tf_op jit(solution)/shard_map/ppermute | solution.py:622
  21.2 1.4 %collective-permute-start.2 = (bf16[256,384]{1,0:T(8,128)(2,1)S(1)}, bf16[256,384]{1,0:T(8,128)(2,1)S(1)}, u32[]{:S(2)}, u32[]{:S(2)}) collective-permute-start(bf16[256,384]{1,0:T(8,128)(2,1)S(1)} %collective-permute-done.1.refs_5_), channel_id=1, source_target_pairs={{0,1},{1,0},{2,3},{3,2},{4,5},{5,4},{6,7},{7,6},{8,9},{9,8},{10,11... | collective-permute-start | bytes 589832 | tf_op jit(solution)/shard_map/ppermute | solution.py:622
  22.7 1.0 copy-start
  23.7 1.0 copy-start.3
  24.7 0.9 copy-start.4
  25.6 0.7 copy-start.5
  26.3 4.2 %copy-start.2 = (bf16[624,384]{1,0:T(8,128)(2,1)S(1)}, bf16[624,384]{1,0:T(8,128)(2,1)}, u32[]{:S(2)}) copy-start(bf16[624,384]{1,0:T(8,128)(2,1)} %get-tuple-element.107.refs_0_) | copy-start | bytes 1437700
  30.5 12.5 %copy-start.6 = (bf16[2,1,384]{2,0,1:T(2,128)(2,1)S(1)}, bf16[2,1,384]{2,0,1:T(2,128)(2,1)}, u32[]{:S(2)}) copy-start(bf16[2,1,384]{2,0,1:T(2,128)(2,1)} %param.15) | copy-start | bytes 4612
  30.5 12.4 %copy-start.7 = (f32[2,128]{1,0:T(2,128)S(1)}, f32[2,128]{1,0:T(2,128)}, u32[]{:S(2)}) copy-start(f32[2,128]{1,0:T(2,128)} %get-tuple-element.99.refs_0_.lives) | copy-start | bytes 3076
  39.0 2.6 %collective-permute-start.11 = (bf16[1248,384]{1,0:T(8,128)(2,1)S(1)}, bf16[1248,384]{1,0:T(8,128)(2,1)S(1)}, u32[]{:S(2)}, u32[]{:S(2)}) collective-permute-start(bf16[1248,384]{1,0:T(8,128)(2,1)S(1)} %shard_map.240.refs_8_), channel_id=1, source_target_pairs={{0,1},{1,0},{2,3},{3,2},{4,5},{5,4},{6,7},{7,6},{8,9},{9,8},{10,11... | collective-permute-start | bytes 2875400 | tf_op jit(solution)/shard_map/ppermute | solution.py:622
  39.1 3.9 %collective-permute-start.8 = (bf16[1248,384]{1,0:T(8,128)(2,1)S(1)}, bf16[1248,384]{1,0:T(8,128)(2,1)S(1)}, u32[]{:S(2)}, u32[]{:S(2)}) collective-permute-start(bf16[1248,384]{1,0:T(8,128)(2,1)S(1)} %shard_map.239.refs_6_), channel_id=1, source_target_pairs={{0,1},{1,0},{2,3},{3,2},{4,5},{5,4},{6,7},{7,6},{8,9},{9,8},{10,11... | collective-permute-start | bytes 2875400 | tf_op jit(solution)/shard_map/ppermute | solution.py:622
  49.3 2.9 %collective-permute-start.12 = (bf16[1536,384]{1,0:T(8,128)(2,1)S(1)}, bf16[1536,384]{1,0:T(8,128)(2,1)S(1)}, u32[]{:S(2)}, u32[]{:S(2)}) collective-permute-start(bf16[1536,384]{1,0:T(8,128)(2,1)S(1)} %get-tuple-element.119), channel_id=1, source_target_pairs={{0,1},{1,0},{2,3},{3,2},{4,5},{5,4},{6,7},{7,6},{8,9},{9,8},{10,11... | collective-permute-start | bytes 3538952 | tf_op jit(solution)/shard_map/ppermute | solution.py:622
  52.6 15.2 %collective-permute-start.13 = (bf16[384,384]{1,0:T(8,128)(2,1)S(1)}, bf16[384,384]{1,0:T(8,128)(2,1)S(1)}, u32[]{:S(2)}, u32[]{:S(2)}) collective-permute-start(bf16[384,384]{1,0:T(8,128)(2,1)S(1)} %get-tuple-element.143), channel_id=1, source_target_pairs={{0,2},{1,3},{2,0},{3,1},{4,6},{5,7},{6,4},{7,5},{8,10},{9,11},{10,... | collective-permute-start | bytes 884744 | tf_op jit(solution)/shard_map/ppermute | solution.py:622
  54.3 15.1 %collective-permute-start.14 = (bf16[384,384]{1,0:T(8,128)(2,1)S(1)}, bf16[384,384]{1,0:T(8,128)(2,1)S(1)}, u32[]{:S(2)}, u32[]{:S(2)}) collective-permute-start(bf16[384,384]{1,0:T(8,128)(2,1)S(1)} %get-tuple-element.144), channel_id=1, source_target_pairs={{0,4},{1,5},{2,6},{3,7},{4,0},{5,1},{6,2},{7,3},{8,12},{9,13},{10,... | collective-permute-start | bytes 884744 | tf_op jit(solution)/shard_map/ppermute | solution.py:622
  55.8 13.6 %collective-permute-start.15 = (bf16[384,384]{1,0:T(8,128)(2,1)S(1)}, bf16[384,384]{1,0:T(8,128)(2,1)S(1)}, u32[]{:S(2)}, u32[]{:S(2)}) collective-permute-start(bf16[384,384]{1,0:T(8,128)(2,1)S(1)} %get-tuple-element.145), channel_id=1, source_target_pairs={{0,6},{1,7},{2,4},{3,5},{4,2},{5,3},{6,0},{7,1},{8,14},{9,15},{10,... | collective-permute-start | bytes 884744 | tf_op jit(solution)/shard_map/ppermute | solution.py:622
  62.4 3.5 %copy-start.1 = (bf16[2,1,256,384]{3,2,1,0:T(8,128)(2,1)S(1)}, bf16[2,1,256,384]{3,2,1,0:T(8,128)(2,1)}, u32[]{:S(2)}) copy-start(bf16[2,1,256,384]{3,2,1,0:T(8,128)(2,1)} %param.14) | copy-start | bytes 1179652
  70.3 2.1 %collective-permute-start.16 = (bf16[832,384]{1,0:T(8,128)(2,1)S(1)}, bf16[832,384]{1,0:T(8,128)(2,1)S(1)}, u32[]{:S(2)}, u32[]{:S(2)}) collective-permute-start(bf16[832,384]{1,0:T(8,128)(2,1)S(1)} %get-tuple-element.148), channel_id=1, source_target_pairs={{0,1},{1,0},{2,3},{3,2},{4,5},{5,4},{6,7},{7,6},{8,9},{9,8},{10,11... | collective-permute-start | bytes 1916936 | tf_op jit(solution)/shard_map/ppermute | solution.py:622
  70.6 6.3 %collective-permute-start.20 = (bf16[192,384]{1,0:T(8,128)(2,1)S(1)}, bf16[192,384]{1,0:T(8,128)(2,1)S(1)}, u32[]{:S(2)}, u32[]{:S(2)}) collective-permute-start(bf16[192,384]{1,0:T(8,128)(2,1)S(1)} %get-tuple-element.157), channel_id=1, source_target_pairs={{0,8},{8,0},{16,24},{24,16},{1,9},{9,1},{17,25},{25,17},{2,10},{10... | collective-permute-start | bytes 442376 | tf_op jit(solution)/shard_map/ppermute | solution.py:622
  72.6 11.0 %collective-permute-start.17 = (bf16[224,384]{1,0:T(8,128)(2,1)S(1)}, bf16[224,384]{1,0:T(8,128)(2,1)S(1)}, u32[]{:S(2)}, u32[]{:S(2)}) collective-permute-start(bf16[224,384]{1,0:T(8,128)(2,1)S(1)} %get-tuple-element.154), channel_id=1, source_target_pairs={{0,2},{1,3},{2,0},{3,1},{4,6},{5,7},{6,4},{7,5},{8,10},{9,11},{10,... | collective-permute-start | bytes 516104 | tf_op jit(solution)/shard_map/ppermute | solution.py:622
  73.9 9.7 %collective-permute-start.18 = (bf16[224,384]{1,0:T(8,128)(2,1)S(1)}, bf16[224,384]{1,0:T(8,128)(2,1)S(1)}, u32[]{:S(2)}, u32[]{:S(2)}) collective-permute-start(bf16[224,384]{1,0:T(8,128)(2,1)S(1)} %get-tuple-element.155), channel_id=1, source_target_pairs={{0,4},{1,5},{2,6},{3,7},{4,0},{5,1},{6,2},{7,3},{8,12},{9,13},{10,... | collective-permute-start | bytes 516104 | tf_op jit(solution)/shard_map/ppermute | solution.py:622
  74.7 9.0 %collective-permute-start.19 = (bf16[224,384]{1,0:T(8,128)(2,1)S(1)}, bf16[224,384]{1,0:T(8,128)(2,1)S(1)}, u32[]{:S(2)}, u32[]{:S(2)}) collective-permute-start(bf16[224,384]{1,0:T(8,128)(2,1)S(1)} %get-tuple-element.156), channel_id=1, source_target_pairs={{0,6},{1,7},{2,4},{3,5},{4,2},{5,3},{6,0},{7,1},{8,14},{9,15},{10,... | collective-permute-start | bytes 516104 | tf_op jit(solution)/shard_map/ppermute | solution.py:622
  77.0 6.7 %collective-permute-start.21 = (bf16[96,384]{1,0:T(8,128)(2,1)S(1)}, bf16[96,384]{1,0:T(8,128)(2,1)S(1)}, u32[]{:S(2)}, u32[]{:S(2)}) collective-permute-start(bf16[96,384]{1,0:T(8,128)(2,1)S(1)} %get-tuple-element.158), channel_id=1, source_target_pairs={{0,16},{8,24},{16,0},{24,8},{1,17},{9,25},{17,1},{25,9},{2,18},{10... | collective-permute-start | bytes 221192 | tf_op jit(solution)/shard_map/ppermute | solution.py:622
  83.9 6.2 %collective-permute-start.22 = (bf16[112,384]{1,0:T(8,128)(2,1)S(1)}, bf16[112,384]{1,0:T(8,128)(2,1)S(1)}, u32[]{:S(2)}, u32[]{:S(2)}) collective-permute-start(bf16[112,384]{1,0:T(8,128)(2,1)S(1)} %get-tuple-element.163), channel_id=1, source_target_pairs={{0,8},{8,0},{16,24},{24,16},{1,9},{9,1},{17,25},{25,17},{2,10},{10... | collective-permute-start | bytes 258056 | tf_op jit(solution)/shard_map/ppermute | solution.py:622
  85.5 10.7 %collective-permute-start.23 = (bf16[112,384]{1,0:T(8,128)(2,1)S(1)}, bf16[112,384]{1,0:T(8,128)(2,1)S(1)}, u32[]{:S(2)}, u32[]{:S(2)}) collective-permute-start(bf16[112,384]{1,0:T(8,128)(2,1)S(1)} %get-tuple-element.164), channel_id=1, source_target_pairs={{0,16},{8,24},{16,0},{24,8},{1,17},{9,25},{17,1},{25,9},{2,18},{10... | collective-permute-start | bytes 258056 | tf_op jit(solution)/shard_map/ppermute | solution.py:622
  88.1 8.1 %collective-permute-start.24 = (bf16[112,384]{1,0:T(8,128)(2,1)S(1)}, bf16[112,384]{1,0:T(8,128)(2,1)S(1)}, u32[]{:S(2)}, u32[]{:S(2)}) collective-permute-start(bf16[112,384]{1,0:T(8,128)(2,1)S(1)} %get-tuple-element.165), channel_id=1, source_target_pairs={{0,24},{8,16},{16,8},{24,0},{1,25},{9,17},{17,9},{25,1},{2,26},{10... | collective-permute-start | bytes 258056 | tf_op jit(solution)/shard_map/ppermute | solution.py:622
  88.3 10.2 %collective-permute-start.26 = (bf16[96,384]{1,0:T(8,128)(2,1)S(1)}, bf16[96,384]{1,0:T(8,128)(2,1)S(1)}, u32[]{:S(2)}, u32[]{:S(2)}) collective-permute-start(bf16[96,384]{1,0:T(8,128)(2,1)S(1)} %shard_map.256.refs_0_), channel_id=1, source_target_pairs={{0,16},{8,24},{16,0},{24,8},{1,17},{9,25},{17,1},{25,9},{2,18},{10... | collective-permute-start | bytes 221192 | tf_op jit(solution)/shard_map/ppermute | solution.py:622
  96.3 6.8 %collective-permute-start.25 = (bf16[256,384]{1,0:T(8,128)(2,1)S(1)}, bf16[256,384]{1,0:T(8,128)(2,1)S(1)}, u32[]{:S(2)}, u32[]{:S(2)}) collective-permute-start(bf16[256,384]{1,0:T(8,128)(2,1)S(1)} %get-tuple-element.166.refs_4_), channel_id=1, source_target_pairs={{0,1},{1,0},{2,3},{3,2},{4,5},{5,4},{6,7},{7,6},{8,9},{9,8},{10,11... | collective-permute-start | bytes 589832 | tf_op jit(solution)/shard_map/ppermute | solution.py:622
  98.6 8.4 %collective-permute-start.30 = (bf16[192,384]{1,0:T(8,128)(2,1)S(1)}, bf16[192,384]{1,0:T(8,128)(2,1)S(1)}, u32[]{:S(2)}, u32[]{:S(2)}) collective-permute-start(bf16[192,384]{1,0:T(8,128)(2,1)S(1)} %shard_map.257.refs_0_), channel_id=1, source_target_pairs={{0,8},{8,0},{16,24},{24,16},{1,9},{9,1},{17,25},{25,17},{2,10},{10... | collective-permute-start | bytes 442376 | tf_op jit(solution)/shard_map/ppermute | solution.py:622
  98.7 7.9 %collective-permute-start.29 = (bf16[48,384]{1,0:T(8,128)(2,1)S(1)}, bf16[48,384]{1,0:T(8,128)(2,1)S(1)}, u32[]{:S(2)}, u32[]{:S(2)}) collective-permute-start(bf16[48,384]{1,0:T(8,128)(2,1)S(1)} %get-tuple-element.172.refs_2_), channel_id=1, source_target_pairs={{0,24},{8,16},{16,8},{24,0},{1,25},{9,17},{17,9},{25,1},{2,26},{10... | collective-permute-start | bytes 110600 | tf_op jit(solution)/shard_map/ppermute | solution.py:622
  101.2 5.8 %collective-permute-start.28 = (bf16[48,384]{1,0:T(8,128)(2,1)S(1)}, bf16[48,384]{1,0:T(8,128)(2,1)S(1)}, u32[]{:S(2)}, u32[]{:S(2)}) collective-permute-start(bf16[48,384]{1,0:T(8,128)(2,1)S(1)} %get-tuple-element.172.refs_2_), channel_id=1, source_target_pairs={{0,16},{8,24},{16,0},{24,8},{1,17},{9,25},{17,1},{25,9},{2,18},{10... | collective-permute-start | bytes 110600 | tf_op jit(solution)/shard_map/ppermute | solution.py:622
  102.1 4.9 %collective-permute-start.27 = (bf16[48,384]{1,0:T(8,128)(2,1)S(1)}, bf16[48,384]{1,0:T(8,128)(2,1)S(1)}, u32[]{:S(2)}, u32[]{:S(2)}) collective-permute-start(bf16[48,384]{1,0:T(8,128)(2,1)S(1)} %get-tuple-element.172.refs_2_), channel_id=1, source_target_pairs={{0,8},{8,0},{16,24},{24,16},{1,9},{9,1},{17,25},{25,17},{2,10},{10... | collective-permute-start | bytes 110600 | tf_op jit(solution)/shard_map/ppermute | solution.py:622

commit v5 on v4

--- a/solution.py
+++ b/solution.py
@@ -157,6 +157,11 @@
     for ref in refs[:-1]:
         out[at : at + ref.shape[0], :] = ref[...]
         at += ref.shape[0]
+
+
+def join_after(gate, *refs):
+    del gate
+    join(*refs)
 
 
 def views(plan, joined):
@@ -639,9 +644,8 @@
     joined = []
     count = len(chips) // 2
     for some in (chips[:count], chips[count:]):
-        some = [behind([v], gate, *joined[:1])[0] for v in some]
         shape = (sum(v.shape[0] for v in some), plan.d)
-        (mine,) = call(join, [(shape, BF)], some, micros=0.4)
+        (mine,) = call(join_after, [(shape, BF)], [gate] + some, micros=0.4)
         joined += [mine, swap(plan, mine, 1)]
     return joined
 

time: 108 us -> 107 us (level)
  waiting for transfers between devices: 34.5 us -> 33.4 us
    ppermute x31, waiting for transfers between devices: 34.5 us -> 33.4 us  [swap(): return lax.ppermute(value, axis, [(i, i ^ k) for i in range(size)])]
  transfers between devices with their start and end apart: 31 -> 31, of which waited for: 20 -> 19; matrix products, arithmetic and copies ran while one was open for 1% -> 1% of each run, Pallas kernels for 20% -> 21%
where the time goes in v5:
time: 107 us
  Pallas kernels  33.6 us (31%)
  waiting for transfers between devices  33.4 us (31%)
  starting transfers between devices  33.1 us (31%)
  local copies, waits for them, and re-layouts  3.62 us (3%)
  other arithmetic  2.01 us (2%)
    pallas_call x22, Pallas kernels, call(): pl.pallas_call(body, out_shape=[jax.ShapeDtypeStruct(shape, kind) for sha...  33.6 us
    ppermute x31, waiting for transfers between devices, swap(): return lax.ppermute(value, axis, [(i, i ^ k) for i in range(size)])  33.4 us
    ppermute x31, starting transfers between devices, swap(): return lax.ppermute(value, axis, [(i, i ^ k) for i in range(size)])  33.1 us
    unnamed x16, local copies, waits for them, and re-layouts  3.62 us
  transfers between devices with their start and end apart: 31, of which 19 were waited for; matrix products, arithmetic and copies ran while one was open for 1% of the time, Pallas kernels for 21%

profile of v5, /device:TPU:0, one launch (start us, length us, event | category | flops | bytes accessed | tf_op | source)
XLA Modules:
  0.0 106.6 jit_solution(10592919991181342565)
XLA Ops:
  0.6 1.4 %convert_add_fusion = f32[1024]{0:T(1024)} fusion(bf16[48]{0:T(256)(128)(2,1)} %param.27, bf16[192]{0:T(256)(128)(2,1)} %param.25, bf16[48]{0:T(256)(128)(2,1)} %param.23, bf16[96]{0:T(256)(128)(2,1)} %param.21, bf16[288]{0:T(512)(128)(2,1)} %param.19), kind=kLoop, calls=%fused_computation | loop fusion | flops 9216 | bytes 5440 | tf_op jit(solution)/shard_map/add | solution.py:817
  2.1 3.0 %shard_map.237 = (bf16[256,384]{1,0:T(8,128)(2,1)}, bf16[624,384]{1,0:T(8,128)(2,1)}, f32[2,128]{1,0:T(2,128)}) custom-call(bf16[48,2304]{1,0:T(8,128)(2,1)} %ada.1, bf16[48,1152]{1,0:T(8,128)(2,1)} %qkv.1, bf16[48,384]{1,0:T(8,128)(2,1)} %proj.1, bf16[48,1536]{1,0:T(8,128)(2,1)} %fc1.1, bf16[192,384]{1,0:T(8,128)(2,1)} %fc2.1, f32[1,1024]{1,0:T(1,128)} %bitcast.23, ...), custom_call_target="tpu_custom_call" | custom-call | bytes 3690000 | tf_op jit(solution)/shard_map/pallas_call | solution.py:65
  5.0 4.0 %collective-permute-start.5 = (bf16[256,384]{1,0:T(8,128)(2,1)}, bf16[256,384]{1,0:T(8,128)(2,1)S(1)}, u32[]{:S(2)}, u32[]{:S(2)}) collective-permute-start(bf16[256,384]{1,0:T(8,128)(2,1)} %get-tuple-element.96.refs_3_), channel_id=1, source_target_pairs={{0,6},{1,7},{2,4},{3,5},{4,2},{5,3},{6,0},{7,1},{8,14},{9,15},{10,... | collective-permute-start | bytes 589832 | tf_op jit(solution)/shard_map/ppermute | solution.py:627
  9.0 0.5 collective-permute-start.3
  9.5 0.1 collective-permute-start.1
  9.7 1.9 %collective-permute-start.7 = (bf16[624,384]{1,0:T(8,128)(2,1)}, bf16[624,384]{1,0:T(8,128)(2,1)S(1)}, u32[]{:S(2)}, u32[]{:S(2)}) collective-permute-start(bf16[624,384]{1,0:T(8,128)(2,1)} %get-tuple-element.102.refs_0_), channel_id=1, source_target_pairs={{0,2},{1,3},{2,0},{3,1},{4,6},{5,7},{6,4},{7,5},{8,10},{9,11},{10,... | collective-permute-start | bytes 1437704 | tf_op jit(solution)/shard_map/ppermute | solution.py:627
  11.5 1.5 %collective-permute-start.10 = (bf16[624,384]{1,0:T(8,128)(2,1)}, bf16[624,384]{1,0:T(8,128)(2,1)S(1)}, u32[]{:S(2)}, u32[]{:S(2)}) collective-permute-start(bf16[624,384]{1,0:T(8,128)(2,1)} %get-tuple-element.102.refs_0_), channel_id=1, source_target_pairs={{0,6},{1,7},{2,4},{3,5},{4,2},{5,3},{6,0},{7,1},{8,14},{9,15},{10,... | collective-permute-start | bytes 1437704 | tf_op jit(solution)/shard_map/ppermute | solution.py:627
  13.0 2.0 %collective-permute-done.5.refs_9_ = bf16[256,384]{1,0:T(8,128)(2,1)S(1)} collective-permute-done((bf16[256,384]{1,0:T(8,128)(2,1)}, bf16[256,384]{1,0:T(8,128)(2,1)S(1)}, u32[]{:S(2)}, u32[]{:S(2)}) %collective-permute-start.5) | collective-permute-done | bytes 196640 | tf_op jit(solution)/shard_map/ppermute | solution.py:627
  15.0 2.0 %collective-permute-start.9 = (bf16[624,384]{1,0:T(8,128)(2,1)}, bf16[624,384]{1,0:T(8,128)(2,1)S(1)}, u32[]{:S(2)}, u32[]{:S(2)}) collective-permute-start(bf16[624,384]{1,0:T(8,128)(2,1)} %get-tuple-element.102.refs_0_), channel_id=1, source_target_pairs={{0,4},{1,5},{2,6},{3,7},{4,0},{5,1},{6,2},{7,3},{8,12},{9,13},{10,... | collective-permute-start | bytes 1437704 | tf_op jit(solution)/shard_map/ppermute | solution.py:627
  17.0 1.4 %collective-permute-done.3.refs_7_ = bf16[256,384]{1,0:T(8,128)(2,1)S(1)} collective-permute-done((bf16[256,384]{1,0:T(8,128)(2,1)}, bf16[256,384]{1,0:T(8,128)(2,1)S(1)}, u32[]{:S(2)}, u32[]{:S(2)}) %collective-permute-start.3) | collective-permute-done | bytes 196640 | tf_op jit(solution)/shard_map/ppermute | solution.py:627
  18.4 1.3 %collective-permute-done.1.refs_5_ = bf16[256,384]{1,0:T(8,128)(2,1)S(1)} collective-permute-done((bf16[256,384]{1,0:T(8,128)(2,1)}, bf16[256,384]{1,0:T(8,128)(2,1)S(1)}, u32[]{:S(2)}, u32[]{:S(2)}) %collective-permute-start.1) | collective-permute-done | bytes 196640 | tf_op jit(solution)/shard_map/ppermute | solution.py:627
  19.8 0.3 collective-permute-done.refs_4_
  20.1 0.2 collective-permute-start.4
  20.3 0.9 collective-permute-done.6.refs_10_
  21.2 0.1 collective-permute-start.2
  21.4 0.2 collective-permute-done.4.refs_8_
  21.5 1.1 %collective-permute-done.2.refs_6_ = bf16[256,384]{1,0:T(8,128)(2,1)S(1)} collective-permute-done((bf16[256,384]{1,0:T(8,128)(2,1)S(1)}, bf16[256,384]{1,0:T(8,128)(2,1)S(1)}, u32[]{:S(2)}, u32[]{:S(2)}) %collective-permute-start.2) | collective-permute-done | bytes 196640 | tf_op jit(solution)/shard_map/ppermute | solution.py:627
  22.7 1.0 copy-done
  23.7 1.0 copy-done.3
  24.7 0.9 copy-done.4
  25.6 0.7 copy-done.5
  26.3 4.1 %shard_map.238 = (bf16[512,1152]{1,0:T(8,128)(2,1)S(1)}, bf16[512,384]{1,0:T(8,128)(2,1)S(1)}, f32[2,768]{1,0:T(2,128)S(1)}, f32[16,384]{1,0:T(8,128)S(1)}, bf16...) custom-call(bf16[512,384]{1,0:T(8,128)(2,1)S(1)} %bitcast.16, ...), custom_call_target="tpu_custom_call" | custom-call | bytes 14760000 | tf_op jit(solution)/shard_map/pallas_call | solution.py:65
  30.5 0.2 collective-permute-start.8
  30.7 8.2 %collective-permute-done.10.refs_1_ = bf16[624,384]{1,0:T(8,128)(2,1)S(1)} collective-permute-done((bf16[624,384]{1,0:T(8,128)(2,1)}, bf16[624,384]{1,0:T(8,128)(2,1)S(1)}, u32[]{:S(2)}, u32[]{:S(2)}) %collective-permute-start.10) | collective-permute-done | bytes 479264 | tf_op jit(solution)/shard_map/ppermute | solution.py:627
  39.1 2.5 %collective-permute-done.11.refs_9_ = bf16[1248,384]{1,0:T(8,128)(2,1)S(1)} collective-permute-done((bf16[1248,384]{1,0:T(8,128)(2,1)S(1)}, bf16[1248,384]{1,0:T(8,128)(2,1)S(1)}, u32[]{:S(2)}, u32[]{:S(2)}) %collective-permute-start.11) | collective-permute-done | bytes 958496 | tf_op jit(solution)/shard_map/ppermute | solution.py:627
  41.6 6.4 %shard_map.241 = (bf16[1536,384]{1,0:T(8,128)(2,1)S(1)}, bf16[1536,384]{1,0:T(8,128)(2,1)S(1)}, bf16[512,1536]{1,0:T(8,128)(2,1)S(1)}, bf16[512,1536]{1,0:T(8,12...) custom-call(f32[2,128]{1,0:T(2,128)S(1)} %copy-done.7, ...), custom_call_target="tpu_custom_call" | custom-call | bytes 36900000 | tf_op jit(solution)/shard_map/pallas_call | solution.py:65
  48.0 0.2 collective-permute-start.12
  48.2 2.0 %shard_map.242 = (bf16[512,384]{1,0:T(8,128)(2,1)}, f32[2,384]{1,0:T(2,128)S(1)}) custom-call(f32[2,128]{1,0:T(2,128)S(1)} %copy-done.7, bf16[512,384]{1,0:T(8,128)(2,1)S(1)} %get-tuple-element.103.cot, bf16[512,1536]{1,0:T(8,128)(2,1)S(1)} %get-tuple-element.104.act, bf16[1536,384]{1,0:T(8,128)(2,1)S(1)} %get-tuple-element.105.fc2, ...), custom_call_target="tpu_custom_call" | custom-call | bytes 5535000 | tf_op jit(solution)/shard_map/pallas_call | solution.py:65
  50.2 0.7 collective-permute-done.12.refs_1_
  50.9 0.3 shard_map.243
  51.2 1.7 %collective-permute-start.13 = (bf16[384,384]{1,0:T(8,128)(2,1)S(1)}, bf16[384,384]{1,0:T(8,128)(2,1)S(1)}, u32[]{:S(2)}, u32[]{:S(2)}) collective-permute-start(bf16[384,384]{1,0:T(8,128)(2,1)S(1)} %get-tuple-element.135), channel_id=1, source_target_pairs={{0,2},{1,3},{2,0},{3,1},{4,6},{5,7},{6,4},{7,5},{8,10},{9,11},{10,... | collective-permute-start | bytes 884744 | tf_op jit(solution)/shard_map/ppermute | solution.py:627
  53.0 1.5 %collective-permute-start.14 = (bf16[384,384]{1,0:T(8,128)(2,1)S(1)}, bf16[384,384]{1,0:T(8,128)(2,1)S(1)}, u32[]{:S(2)}, u32[]{:S(2)}) collective-permute-start(bf16[384,384]{1,0:T(8,128)(2,1)S(1)} %get-tuple-element.136), channel_id=1, source_target_pairs={{0,4},{1,5},{2,6},{3,7},{4,0},{5,1},{6,2},{7,3},{8,12},{9,13},{10,... | collective-permute-start | bytes 884744 | tf_op jit(solution)/shard_map/ppermute | solution.py:627
  54.5 0.3 collective-permute-start.15
  54.8 2.8 %shard_map.244 = (bf16[512,384]{1,0:T(8,128)(2,1)S(1)}, f32[512,384]{1,0:T(8,128)S(1)}, bf16[384,384]{1,0:T(8,128)(2,1)S(1)}, f32[16,384]{1,0:T(8,128)S(1)}, f32[2,1152]{1,0:T(2,128)S(1)}) custom-call(f32[2,128]{1,0:T(2,128)S(1)} %copy-done.7, bf16[512,384]{1,0:T(8,128)(2,1)S(1)} %get-tuple-element.103.cot, ...), custom_call_target="tpu_custom_call" | custom-call | bytes 11070000 | tf_op jit(solution)/shard_map/pallas_call | solution.py:65
  57.6 3.5 %shard_map.245.refs_7_.refs_3_ = bf16[256,1152]{1,0:T(8,128)(2,1)S(1)} custom-call(bf16[512,1152]{1,0:T(8,128)(2,1)S(1)} %get-tuple-element.125.projected, bf16[512,384]{1,0:T(8,128)(2,1)S(1)} %get-tuple-element.127.grad_mixed), custom_call_target="tpu_custom_call" | custom-call | bytes 12177000 | tf_op jit(solution)/shard_map/pallas_call | solution.py:65
  61.1 3.5 %shard_map.246.refs_8_.refs_4_ = bf16[256,1152]{1,0:T(8,128)(2,1)S(1)} custom-call(bf16[512,1152]{1,0:T(8,128)(2,1)S(1)} %get-tuple-element.125.projected, bf16[512,384]{1,0:T(8,128)(2,1)S(1)} %get-tuple-element.127.grad_mixed), custom_call_target="tpu_custom_call" | custom-call | bytes 12177000 | tf_op jit(solution)/shard_map/pallas_call | solution.py:65
  64.5 1.9 %shard_map.247 = (bf16[512,384]{1,0:T(8,128)(2,1)}, bf16[16,384]{1,0:T(8,128)(2,1)S(1)}, bf16[512,384]{1,0:T(8,128)(2,1)S(1)}) custom-call(bf16[512,384]{1,0:T(8,128)(2,1)S(1)} %bitcast.17, bf16[2,384]{1,0:T(2,128)(2,1)S(1)} %bitcast.21, f32[512,384]{1,0:T(8,128)S(1)} %get-tuple-element.122.refs_2_, bf16[384,1152]{1,0:T(8,128)(2,1)S(1)} %get-tuple-element.123.refs_3_, ...), custom_call_target="tpu_custom_call" | custom-call | bytes 7380000 | tf_op jit(solution)/shard_map/pallas_call | solution.py:65
  66.4 1.6 %collective-permute-done.14.refs_1_ = bf16[384,384]{1,0:T(8,128)(2,1)S(1)} collective-permute-done((bf16[384,384]{1,0:T(8,128)(2,1)S(1)}, bf16[384,384]{1,0:T(8,128)(2,1)S(1)}, u32[]{:S(2)}, u32[]{:S(2)}) %collective-permute-start.14) | collective-permute-done | bytes 294944 | tf_op jit(solution)/shard_map/ppermute | solution.py:627
  68.0 0.9 shard_map.249
  69.0 0.2 shard_map.250
  69.3 1.6 %collective-permute-start.20 = (bf16[192,384]{1,0:T(8,128)(2,1)S(1)}, bf16[192,384]{1,0:T(8,128)(2,1)S(1)}, u32[]{:S(2)}, u32[]{:S(2)}) collective-permute-start(bf16[192,384]{1,0:T(8,128)(2,1)S(1)} %get-tuple-element.149), channel_id=1, source_target_pairs={{0,8},{8,0},{16,24},{24,16},{1,9},{9,1},{17,25},{25,17},{2,10},{10... | collective-permute-start | bytes 442376 | tf_op jit(solution)/shard_map/ppermute | solution.py:627
  70.9 0.2 collective-permute-done.16.received
  71.1 0.1 shard_map.251
  71.2 1.3 %collective-permute-start.17 = (bf16[224,384]{1,0:T(8,128)(2,1)S(1)}, bf16[224,384]{1,0:T(8,128)(2,1)S(1)}, u32[]{:S(2)}, u32[]{:S(2)}) collective-permute-start(bf16[224,384]{1,0:T(8,128)(2,1)S(1)} %get-tuple-element.146), channel_id=1, source_target_pairs={{0,2},{1,3},{2,0},{3,1},{4,6},{5,7},{6,4},{7,5},{8,10},{9,11},{10,... | collective-permute-start | bytes 516104 | tf_op jit(solution)/shard_map/ppermute | solution.py:627
  72.5 0.8 collective-permute-start.18
  73.4 1.4 %collective-permute-start.19 = (bf16[224,384]{1,0:T(8,128)(2,1)S(1)}, bf16[224,384]{1,0:T(8,128)(2,1)S(1)}, u32[]{:S(2)}, u32[]{:S(2)}) collective-permute-start(bf16[224,384]{1,0:T(8,128)(2,1)S(1)} %get-tuple-element.148), channel_id=1, source_target_pairs={{0,6},{1,7},{2,4},{3,5},{4,2},{5,3},{6,0},{7,1},{8,14},{9,15},{10,... | collective-permute-start | bytes 516104 | tf_op jit(solution)/shard_map/ppermute | solution.py:627
  74.8 0.8 collective-permute-done.20.received
  75.6 2.7 %collective-permute-start.21 = (bf16[96,384]{1,0:T(8,128)(2,1)S(1)}, bf16[96,384]{1,0:T(8,128)(2,1)S(1)}, u32[]{:S(2)}, u32[]{:S(2)}) collective-permute-start(bf16[96,384]{1,0:T(8,128)(2,1)S(1)} %get-tuple-element.150), channel_id=1, source_target_pairs={{0,16},{8,24},{16,0},{24,8},{1,17},{9,25},{17,1},{25,9},{2,18},{10... | collective-permute-start | bytes 221192 | tf_op jit(solution)/shard_map/ppermute | solution.py:627
  78.3 1.7 %shard_map.248 = bf16[2,384]{1,0:T(2,128)(2,1)} custom-call(bf16[2,384]{1,0:T(2,128)(2,1)S(1)} %bitcast.22, bf16[16,384]{1,0:T(8,128)(2,1)S(1)} %get-tuple-element.129.mods, bf16[384,768]{1,0:T(8,128)(2,1)S(1)} %get-tuple-element.130.first, bf16[384,1536]{1,0:T(8,128)(2,1)S(1)} %get-tuple-element.131.second), custom_call_target="tpu_custom_call" | custom-call | bytes 7380000 | tf_op jit(solution)/shard_map/pallas_call | solution.py:65
  80.0 2.3 %collective-permute-done.21.second = bf16[96,384]{1,0:T(8,128)(2,1)S(1)} collective-permute-done((bf16[96,384]{1,0:T(8,128)(2,1)S(1)}, bf16[96,384]{1,0:T(8,128)(2,1)S(1)}, u32[]{:S(2)}, u32[]{:S(2)}) %collective-permute-start.21) | collective-permute-done | bytes 73760 | tf_op jit(solution)/shard_map/ppermute | solution.py:627
  82.5 1.6 %collective-permute-start.22 = (bf16[112,384]{1,0:T(8,128)(2,1)S(1)}, bf16[112,384]{1,0:T(8,128)(2,1)S(1)}, u32[]{:S(2)}, u32[]{:S(2)}) collective-permute-start(bf16[112,384]{1,0:T(8,128)(2,1)S(1)} %get-tuple-element.155), channel_id=1, source_target_pairs={{0,8},{8,0},{16,24},{24,16},{1,9},{9,1},{17,25},{25,17},{2,10},{10... | collective-permute-start | bytes 258056 | tf_op jit(solution)/shard_map/ppermute | solution.py:627
  84.1 2.6 %collective-permute-start.23 = (bf16[112,384]{1,0:T(8,128)(2,1)S(1)}, bf16[112,384]{1,0:T(8,128)(2,1)S(1)}, u32[]{:S(2)}, u32[]{:S(2)}) collective-permute-start(bf16[112,384]{1,0:T(8,128)(2,1)S(1)} %get-tuple-element.156), channel_id=1, source_target_pairs={{0,16},{8,24},{16,0},{24,8},{1,17},{9,25},{17,1},{25,9},{2,18},{10... | collective-permute-start | bytes 258056 | tf_op jit(solution)/shard_map/ppermute | solution.py:627
  86.7 0.2 collective-permute-start.24
  87.0 1.8 %collective-permute-start.26 = (bf16[96,384]{1,0:T(8,128)(2,1)S(1)}, bf16[96,384]{1,0:T(8,128)(2,1)S(1)}, u32[]{:S(2)}, u32[]{:S(2)}) collective-permute-start(bf16[96,384]{1,0:T(8,128)(2,1)S(1)} %shard_map.256.refs_0_), channel_id=1, source_target_pairs={{0,16},{8,24},{16,0},{24,8},{1,17},{9,25},{17,1},{25,9},{2,18},{10... | collective-permute-start | bytes 221192 | tf_op jit(solution)/shard_map/ppermute | solution.py:627
  88.7 6.1 %collective-permute-done.23.refs_2_ = bf16[112,384]{1,0:T(8,128)(2,1)S(1)} collective-permute-done((bf16[112,384]{1,0:T(8,128)(2,1)S(1)}, bf16[112,384]{1,0:T(8,128)(2,1)S(1)}, u32[]{:S(2)}, u32[]{:S(2)}) %collective-permute-start.23) | collective-permute-done | bytes 86048 | tf_op jit(solution)/shard_map/ppermute | solution.py:627
  95.0 2.2 %collective-permute-done.26.refs_1_ = bf16[96,384]{1,0:T(8,128)(2,1)S(1)} collective-permute-done((bf16[96,384]{1,0:T(8,128)(2,1)S(1)}, bf16[96,384]{1,0:T(8,128)(2,1)S(1)}, u32[]{:S(2)}, u32[]{:S(2)}) %collective-permute-start.26) | collective-permute-done | bytes 73760 | tf_op jit(solution)/shard_map/ppermute | solution.py:627
  97.3 2.5 %collective-permute-start.29 = (bf16[48,384]{1,0:T(8,128)(2,1)S(1)}, bf16[48,384]{1,0:T(8,128)(2,1)S(1)}, u32[]{:S(2)}, u32[]{:S(2)}) collective-permute-start(bf16[48,384]{1,0:T(8,128)(2,1)S(1)} %get-tuple-element.164.refs_2_), channel_id=1, source_target_pairs={{0,24},{8,16},{16,8},{24,0},{1,25},{9,17},{17,9},{25,1},{2,26},{10... | collective-permute-start | bytes 110600 | tf_op jit(solution)/shard_map/ppermute | solution.py:627
  99.8 0.9 collective-permute-start.28
  100.8 1.0 collective-permute-start.27
  101.7 1.9 %shard_map.255 = (f32[48,2304]{1,0:T(8,128)}, f32[1,288]{1,0:T(1,128)S(1)}, f32[1,96]{1,0:T(1,128)}, f32[1,48]{1,0:T(1,128)}, f32[1,192]{1,0:T(1,128)}, /*index=5*/f32[1,48]{1,0:T(1,128)}) custom-call(f32[112,384]{1,0:T(8,128)S(1)} %get-tuple-element.154.refs_0_, bf16[112,384]{1,0:T(8,128)(2,1)S(1)} %collective-permute-done.22.refs_1_, ...), custom_call_target="tpu_custom_call" | custom-call | bytes 7380000 | tf_op jit(solution)/shard_map/pallas_call | solution.py:65
  103.6 0.6 reduce
  104.2 1.0 collective-permute-done.29.refs_5_
  105.2 0.4 collective-permute-done.28.refs_4_
  105.6 1.0 shard_map.258
  (38 shorter events, 0.8 us)
Async XLA Ops:
  5.0 9.9 %collective-permute-start.5 = (bf16[256,384]{1,0:T(8,128)(2,1)}, bf16[256,384]{1,0:T(8,128)(2,1)S(1)}, u32[]{:S(2)}, u32[]{:S(2)}) collective-permute-start(bf16[256,384]{1,0:T(8,128)(2,1)} %get-tuple-element.96.refs_3_), channel_id=1, source_target_pairs={{0,6},{1,7},{2,4},{3,5},{4,2},{5,3},{6,0},{7,1},{8,14},{9,15},{10,... | collective-permute-start | bytes 589832 | tf_op jit(solution)/shard_map/ppermute | solution.py:627
  9.0 9.4 %collective-permute-start.3 = (bf16[256,384]{1,0:T(8,128)(2,1)}, bf16[256,384]{1,0:T(8,128)(2,1)S(1)}, u32[]{:S(2)}, u32[]{:S(2)}) collective-permute-start(bf16[256,384]{1,0:T(8,128)(2,1)} %get-tuple-element.96.refs_3_), channel_id=1, source_target_pairs={{0,4},{1,5},{2,6},{3,7},{4,0},{5,1},{6,2},{7,3},{8,12},{9,13},{10,... | collective-permute-start | bytes 589832 | tf_op jit(solution)/shard_map/ppermute | solution.py:627
  9.5 10.3 %collective-permute-start.1 = (bf16[256,384]{1,0:T(8,128)(2,1)}, bf16[256,384]{1,0:T(8,128)(2,1)S(1)}, u32[]{:S(2)}, u32[]{:S(2)}) collective-permute-start(bf16[256,384]{1,0:T(8,128)(2,1)} %get-tuple-element.96.refs_3_), channel_id=1, source_target_pairs={{0,2},{1,3},{2,0},{3,1},{4,6},{5,7},{6,4},{7,5},{8,10},{9,11},{10,... | collective-permute-start | bytes 589832 | tf_op jit(solution)/shard_map/ppermute | solution.py:627
  9.7 20.8 %collective-permute-start.7 = (bf16[624,384]{1,0:T(8,128)(2,1)}, bf16[624,384]{1,0:T(8,128)(2,1)S(1)}, u32[]{:S(2)}, u32[]{:S(2)}) collective-permute-start(bf16[624,384]{1,0:T(8,128)(2,1)} %get-tuple-element.102.refs_0_), channel_id=1, source_target_pairs={{0,2},{1,3},{2,0},{3,1},{4,6},{5,7},{6,4},{7,5},{8,10},{9,11},{10,... | collective-permute-start | bytes 1437704 | tf_op jit(solution)/shard_map/ppermute | solution.py:627
  11.5 27.4 %collective-permute-start.10 = (bf16[624,384]{1,0:T(8,128)(2,1)}, bf16[624,384]{1,0:T(8,128)(2,1)S(1)}, u32[]{:S(2)}, u32[]{:S(2)}) collective-permute-start(bf16[624,384]{1,0:T(8,128)(2,1)} %get-tuple-element.102.refs_0_), channel_id=1, source_target_pairs={{0,6},{1,7},{2,4},{3,5},{4,2},{5,3},{6,0},{7,1},{8,14},{9,15},{10,... | collective-permute-start | bytes 1437704 | tf_op jit(solution)/shard_map/ppermute | solution.py:627
  15.0 23.9 %collective-permute-start.9 = (bf16[624,384]{1,0:T(8,128)(2,1)}, bf16[624,384]{1,0:T(8,128)(2,1)S(1)}, u32[]{:S(2)}, u32[]{:S(2)}) collective-permute-start(bf16[624,384]{1,0:T(8,128)(2,1)} %get-tuple-element.102.refs_0_), channel_id=1, source_target_pairs={{0,4},{1,5},{2,6},{3,7},{4,0},{5,1},{6,2},{7,3},{8,12},{9,13},{10,... | collective-permute-start | bytes 1437704 | tf_op jit(solution)/shard_map/ppermute | solution.py:627
  18.4 1.7 %collective-permute-start = (bf16[256,384]{1,0:T(8,128)(2,1)}, bf16[256,384]{1,0:T(8,128)(2,1)S(1)}, u32[]{:S(2)}, u32[]{:S(2)}) collective-permute-start(bf16[256,384]{1,0:T(8,128)(2,1)} %get-tuple-element.96.refs_3_), channel_id=1, source_target_pairs={{0,1},{1,0},{2,3},{3,2},{4,5},{5,4},{6,7},{7,6},{8,9},{9,8},{10,11... | collective-permute-start | bytes 589832 | tf_op jit(solution)/shard_map/ppermute | solution.py:627
  19.8 1.4 %collective-permute-start.6 = (bf16[256,384]{1,0:T(8,128)(2,1)S(1)}, bf16[256,384]{1,0:T(8,128)(2,1)S(1)}, u32[]{:S(2)}, u32[]{:S(2)}) collective-permute-start(bf16[256,384]{1,0:T(8,128)(2,1)S(1)} %collective-permute-done.5.refs_9_), channel_id=1, source_target_pairs={{0,1},{1,0},{2,3},{3,2},{4,5},{5,4},{6,7},{7,6},{8,9},{9,8},{10,11... | collective-permute-start | bytes 589832 | tf_op jit(solution)/shard_map/ppermute | solution.py:627
  20.1 1.4 %collective-permute-start.4 = (bf16[256,384]{1,0:T(8,128)(2,1)S(1)}, bf16[256,384]{1,0:T(8,128)(2,1)S(1)}, u32[]{:S(2)}, u32[]{:S(2)}) collective-permute-start(bf16[256,384]{1,0:T(8,128)(2,1)S(1)} %collective-permute-done.3.refs_7_), channel_id=1, source_target_pairs={{0,1},{1,0},{2,3},{3,2},{4,5},{5,4},{6,7},{7,6},{8,9},{9,8},{10,11... | collective-permute-start | bytes 589832 | tf_op jit(solution)/shard_map/ppermute | solution.py:627
  21.2 1.4 %collective-permute-start.2 = (bf16[256,384]{1,0:T(8,128)(2,1)S(1)}, bf16[256,384]{1,0:T(8,128)(2,1)S(1)}, u32[]{:S(2)}, u32[]{:S(2)}) collective-permute-start(bf16[256,384]{1,0:T(8,128)(2,1)S(1)} %collective-permute-done.1.refs_5_), channel_id=1, source_target_pairs={{0,1},{1,0},{2,3},{3,2},{4,5},{5,4},{6,7},{7,6},{8,9},{9,8},{10,11... | collective-permute-start | bytes 589832 | tf_op jit(solution)/shard_map/ppermute | solution.py:627
  22.7 1.0 copy-start
  23.7 1.0 copy-start.3
  24.7 0.9 copy-start.4
  25.6 0.7 copy-start.5
  26.3 4.2 %copy-start.2 = (bf16[624,384]{1,0:T(8,128)(2,1)S(1)}, bf16[624,384]{1,0:T(8,128)(2,1)}, u32[]{:S(2)}) copy-start(bf16[624,384]{1,0:T(8,128)(2,1)} %get-tuple-element.102.refs_0_) | copy-start | bytes 1437700
  30.5 11.1 %copy-start.6 = (bf16[2,1,384]{2,0,1:T(2,128)(2,1)S(1)}, bf16[2,1,384]{2,0,1:T(2,128)(2,1)}, u32[]{:S(2)}) copy-start(bf16[2,1,384]{2,0,1:T(2,128)(2,1)} %param.15) | copy-start | bytes 4612
  30.5 11.1 %copy-start.7 = (f32[2,128]{1,0:T(2,128)S(1)}, f32[2,128]{1,0:T(2,128)}, u32[]{:S(2)}) copy-start(f32[2,128]{1,0:T(2,128)} %get-tuple-element.95.refs_0_.lives) | copy-start | bytes 3076
  30.5 8.5 %collective-permute-start.8 = (bf16[1248,384]{1,0:T(8,128)(2,1)S(1)}, bf16[1248,384]{1,0:T(8,128)(2,1)S(1)}, u32[]{:S(2)}, u32[]{:S(2)}) collective-permute-start(bf16[1248,384]{1,0:T(8,128)(2,1)S(1)} %shard_map.239.refs_6_), channel_id=1, source_target_pairs={{0,1},{1,0},{2,3},{3,2},{4,5},{5,4},{6,7},{7,6},{8,9},{9,8},{10,11... | collective-permute-start | bytes 2875400 | tf_op jit(solution)/shard_map/ppermute | solution.py:627
  39.0 2.6 %collective-permute-start.11 = (bf16[1248,384]{1,0:T(8,128)(2,1)S(1)}, bf16[1248,384]{1,0:T(8,128)(2,1)S(1)}, u32[]{:S(2)}, u32[]{:S(2)}) collective-permute-start(bf16[1248,384]{1,0:T(8,128)(2,1)S(1)} %shard_map.240.refs_8_), channel_id=1, source_target_pairs={{0,1},{1,0},{2,3},{3,2},{4,5},{5,4},{6,7},{7,6},{8,9},{9,8},{10,11... | collective-permute-start | bytes 2875400 | tf_op jit(solution)/shard_map/ppermute | solution.py:627
  48.0 2.9 %collective-permute-start.12 = (bf16[1536,384]{1,0:T(8,128)(2,1)S(1)}, bf16[1536,384]{1,0:T(8,128)(2,1)S(1)}, u32[]{:S(2)}, u32[]{:S(2)}) collective-permute-start(bf16[1536,384]{1,0:T(8,128)(2,1)S(1)} %get-tuple-element.111), channel_id=1, source_target_pairs={{0,1},{1,0},{2,3},{3,2},{4,5},{5,4},{6,7},{7,6},{8,9},{9,8},{10,11... | collective-permute-start | bytes 3538952 | tf_op jit(solution)/shard_map/ppermute | solution.py:627
  51.2 15.2 %collective-permute-start.13 = (bf16[384,384]{1,0:T(8,128)(2,1)S(1)}, bf16[384,384]{1,0:T(8,128)(2,1)S(1)}, u32[]{:S(2)}, u32[]{:S(2)}) collective-permute-start(bf16[384,384]{1,0:T(8,128)(2,1)S(1)} %get-tuple-element.135), channel_id=1, source_target_pairs={{0,2},{1,3},{2,0},{3,1},{4,6},{5,7},{6,4},{7,5},{8,10},{9,11},{10,... | collective-permute-start | bytes 884744 | tf_op jit(solution)/shard_map/ppermute | solution.py:627
  53.0 15.1 %collective-permute-start.14 = (bf16[384,384]{1,0:T(8,128)(2,1)S(1)}, bf16[384,384]{1,0:T(8,128)(2,1)S(1)}, u32[]{:S(2)}, u32[]{:S(2)}) collective-permute-start(bf16[384,384]{1,0:T(8,128)(2,1)S(1)} %get-tuple-element.136), channel_id=1, source_target_pairs={{0,4},{1,5},{2,6},{3,7},{4,0},{5,1},{6,2},{7,3},{8,12},{9,13},{10,... | collective-permute-start | bytes 884744 | tf_op jit(solution)/shard_map/ppermute | solution.py:627
  54.5 13.6 %collective-permute-start.15 = (bf16[384,384]{1,0:T(8,128)(2,1)S(1)}, bf16[384,384]{1,0:T(8,128)(2,1)S(1)}, u32[]{:S(2)}, u32[]{:S(2)}) collective-permute-start(bf16[384,384]{1,0:T(8,128)(2,1)S(1)} %get-tuple-element.137), channel_id=1, source_target_pairs={{0,6},{1,7},{2,4},{3,5},{4,2},{5,3},{6,0},{7,1},{8,14},{9,15},{10,... | collective-permute-start | bytes 884744 | tf_op jit(solution)/shard_map/ppermute | solution.py:627
  61.0 3.5 %copy-start.1 = (bf16[2,1,256,384]{3,2,1,0:T(8,128)(2,1)S(1)}, bf16[2,1,256,384]{3,2,1,0:T(8,128)(2,1)}, u32[]{:S(2)}) copy-start(bf16[2,1,256,384]{3,2,1,0:T(8,128)(2,1)} %param.14) | copy-start | bytes 1179652
  68.9 2.1 %collective-permute-start.16 = (bf16[832,384]{1,0:T(8,128)(2,1)S(1)}, bf16[832,384]{1,0:T(8,128)(2,1)S(1)}, u32[]{:S(2)}, u32[]{:S(2)}) collective-permute-start(bf16[832,384]{1,0:T(8,128)(2,1)S(1)} %get-tuple-element.140), channel_id=1, source_target_pairs={{0,1},{1,0},{2,3},{3,2},{4,5},{5,4},{6,7},{7,6},{8,9},{9,8},{10,11... | collective-permute-start | bytes 1916936 | tf_op jit(solution)/shard_map/ppermute | solution.py:627
  69.3 6.3 %collective-permute-start.20 = (bf16[192,384]{1,0:T(8,128)(2,1)S(1)}, bf16[192,384]{1,0:T(8,128)(2,1)S(1)}, u32[]{:S(2)}, u32[]{:S(2)}) collective-permute-start(bf16[192,384]{1,0:T(8,128)(2,1)S(1)} %get-tuple-element.149), channel_id=1, source_target_pairs={{0,8},{8,0},{16,24},{24,16},{1,9},{9,1},{17,25},{25,17},{2,10},{10... | collective-permute-start | bytes 442376 | tf_op jit(solution)/shard_map/ppermute | solution.py:627
  71.2 11.0 %collective-permute-start.17 = (bf16[224,384]{1,0:T(8,128)(2,1)S(1)}, bf16[224,384]{1,0:T(8,128)(2,1)S(1)}, u32[]{:S(2)}, u32[]{:S(2)}) collective-permute-start(bf16[224,384]{1,0:T(8,128)(2,1)S(1)} %get-tuple-element.146), channel_id=1, source_target_pairs={{0,2},{1,3},{2,0},{3,1},{4,6},{5,7},{6,4},{7,5},{8,10},{9,11},{10,... | collective-permute-start | bytes 516104 | tf_op jit(solution)/shard_map/ppermute | solution.py:627
  72.5 9.7 %collective-permute-start.18 = (bf16[224,384]{1,0:T(8,128)(2,1)S(1)}, bf16[224,384]{1,0:T(8,128)(2,1)S(1)}, u32[]{:S(2)}, u32[]{:S(2)}) collective-permute-start(bf16[224,384]{1,0:T(8,128)(2,1)S(1)} %get-tuple-element.147), channel_id=1, source_target_pairs={{0,4},{1,5},{2,6},{3,7},{4,0},{5,1},{6,2},{7,3},{8,12},{9,13},{10,... | collective-permute-start | bytes 516104 | tf_op jit(solution)/shard_map/ppermute | solution.py:627
  73.4 9.0 %collective-permute-start.19 = (bf16[224,384]{1,0:T(8,128)(2,1)S(1)}, bf16[224,384]{1,0:T(8,128)(2,1)S(1)}, u32[]{:S(2)}, u32[]{:S(2)}) collective-permute-start(bf16[224,384]{1,0:T(8,128)(2,1)S(1)} %get-tuple-element.148), channel_id=1, source_target_pairs={{0,6},{1,7},{2,4},{3,5},{4,2},{5,3},{6,0},{7,1},{8,14},{9,15},{10,... | collective-permute-start | bytes 516104 | tf_op jit(solution)/shard_map/ppermute | solution.py:627
  75.6 6.7 %collective-permute-start.21 = (bf16[96,384]{1,0:T(8,128)(2,1)S(1)}, bf16[96,384]{1,0:T(8,128)(2,1)S(1)}, u32[]{:S(2)}, u32[]{:S(2)}) collective-permute-start(bf16[96,384]{1,0:T(8,128)(2,1)S(1)} %get-tuple-element.150), channel_id=1, source_target_pairs={{0,16},{8,24},{16,0},{24,8},{1,17},{9,25},{17,1},{25,9},{2,18},{10... | collective-permute-start | bytes 221192 | tf_op jit(solution)/shard_map/ppermute | solution.py:627
  82.5 6.2 %collective-permute-start.22 = (bf16[112,384]{1,0:T(8,128)(2,1)S(1)}, bf16[112,384]{1,0:T(8,128)(2,1)S(1)}, u32[]{:S(2)}, u32[]{:S(2)}) collective-permute-start(bf16[112,384]{1,0:T(8,128)(2,1)S(1)} %get-tuple-element.155), channel_id=1, source_target_pairs={{0,8},{8,0},{16,24},{24,16},{1,9},{9,1},{17,25},{25,17},{2,10},{10... | collective-permute-start | bytes 258056 | tf_op jit(solution)/shard_map/ppermute | solution.py:627
  84.1 10.7 %collective-permute-start.23 = (bf16[112,384]{1,0:T(8,128)(2,1)S(1)}, bf16[112,384]{1,0:T(8,128)(2,1)S(1)}, u32[]{:S(2)}, u32[]{:S(2)}) collective-permute-start(bf16[112,384]{1,0:T(8,128)(2,1)S(1)} %get-tuple-element.156), channel_id=1, source_target_pairs={{0,16},{8,24},{16,0},{24,8},{1,17},{9,25},{17,1},{25,9},{2,18},{10... | collective-permute-start | bytes 258056 | tf_op jit(solution)/shard_map/ppermute | solution.py:627
  86.7 8.1 %collective-permute-start.24 = (bf16[112,384]{1,0:T(8,128)(2,1)S(1)}, bf16[112,384]{1,0:T(8,128)(2,1)S(1)}, u32[]{:S(2)}, u32[]{:S(2)}) collective-permute-start(bf16[112,384]{1,0:T(8,128)(2,1)S(1)} %get-tuple-element.157), channel_id=1, source_target_pairs={{0,24},{8,16},{16,8},{24,0},{1,25},{9,17},{17,9},{25,1},{2,26},{10... | collective-permute-start | bytes 258056 | tf_op jit(solution)/shard_map/ppermute | solution.py:627
  87.0 10.2 %collective-permute-start.26 = (bf16[96,384]{1,0:T(8,128)(2,1)S(1)}, bf16[96,384]{1,0:T(8,128)(2,1)S(1)}, u32[]{:S(2)}, u32[]{:S(2)}) collective-permute-start(bf16[96,384]{1,0:T(8,128)(2,1)S(1)} %shard_map.256.refs_0_), channel_id=1, source_target_pairs={{0,16},{8,24},{16,0},{24,8},{1,17},{9,25},{17,1},{25,9},{2,18},{10... | collective-permute-start | bytes 221192 | tf_op jit(solution)/shard_map/ppermute | solution.py:627
  94.9 6.8 %collective-permute-start.25 = (bf16[256,384]{1,0:T(8,128)(2,1)S(1)}, bf16[256,384]{1,0:T(8,128)(2,1)S(1)}, u32[]{:S(2)}, u32[]{:S(2)}) collective-permute-start(bf16[256,384]{1,0:T(8,128)(2,1)S(1)} %get-tuple-element.158.refs_4_), channel_id=1, source_target_pairs={{0,1},{1,0},{2,3},{3,2},{4,5},{5,4},{6,7},{7,6},{8,9},{9,8},{10,11... | collective-permute-start | bytes 589832 | tf_op jit(solution)/shard_map/ppermute | solution.py:627
  97.2 8.4 %collective-permute-start.30 = (bf16[192,384]{1,0:T(8,128)(2,1)S(1)}, bf16[192,384]{1,0:T(8,128)(2,1)S(1)}, u32[]{:S(2)}, u32[]{:S(2)}) collective-permute-start(bf16[192,384]{1,0:T(8,128)(2,1)S(1)} %shard_map.257.refs_0_), channel_id=1, source_target_pairs={{0,8},{8,0},{16,24},{24,16},{1,9},{9,1},{17,25},{25,17},{2,10},{10... | collective-permute-start | bytes 442376 | tf_op jit(solution)/shard_map/ppermute | solution.py:627
  97.3 7.9 %collective-permute-start.29 = (bf16[48,384]{1,0:T(8,128)(2,1)S(1)}, bf16[48,384]{1,0:T(8,128)(2,1)S(1)}, u32[]{:S(2)}, u32[]{:S(2)}) collective-permute-start(bf16[48,384]{1,0:T(8,128)(2,1)S(1)} %get-tuple-element.164.refs_2_), channel_id=1, source_target_pairs={{0,24},{8,16},{16,8},{24,0},{1,25},{9,17},{17,9},{25,1},{2,26},{10... | collective-permute-start | bytes 110600 | tf_op jit(solution)/shard_map/ppermute | solution.py:627
  99.8 5.8 %collective-permute-start.28 = (bf16[48,384]{1,0:T(8,128)(2,1)S(1)}, bf16[48,384]{1,0:T(8,128)(2,1)S(1)}, u32[]{:S(2)}, u32[]{:S(2)}) collective-permute-start(bf16[48,384]{1,0:T(8,128)(2,1)S(1)} %get-tuple-element.164.refs_2_), channel_id=1, source_target_pairs={{0,16},{8,24},{16,0},{24,8},{1,17},{9,25},{17,1},{25,9},{2,18},{10... | collective-permute-start | bytes 110600 | tf_op jit(solution)/shard_map/ppermute | solution.py:627
  100.8 4.9 %collective-permute-start.27 = (bf16[48,384]{1,0:T(8,128)(2,1)S(1)}, bf16[48,384]{1,0:T(8,128)(2,1)S(1)}, u32[]{:S(2)}, u32[]{:S(2)}) collective-permute-start(bf16[48,384]{1,0:T(8,128)(2,1)S(1)} %get-tuple-element.164.refs_2_), channel_id=1, source_target_pairs={{0,8},{8,0},{16,24},{24,16},{1,9},{9,1},{17,25},{25,17},{2,10},{10... | collective-permute-start | bytes 110600 | tf_op jit(solution)/shard_map/ppermute | solution.py:627

commit v6 on v5

--- a/solution.py
+++ b/solution.py
@@ -936,8 +936,6 @@
         [cond, mods, ada_first, ada_second],
         micros=2,
     )
-    if plan.direct:
-        parts = behind(parts, *mlp_pieces)
     last_chunk = call(
         functools.partial(attn_grads, plan),
         [((halves * (4 * r + 16), d), BF)] * sides,
@@ -948,7 +946,7 @@
             pltpu.VMEM((d, n), BF),
         ],
         room=5,
-        micros=1.5,
+        micros=0.1,
     )
     if plan.direct:
         layout = ((plan.ffb, r), (1, plan.ffb * r))

time: 107 us -> 116 us (1.084)
  waiting for transfers between devices: 33.4 us -> 42.2 us
    ppermute x31, waiting for transfers between devices: 33.4 us -> 42.2 us  [swap(): return lax.ppermute(value, axis, [(i, i ^ k) for i in range(size)])]
  transfers between devices with their start and end apart: 31 -> 31, of which waited for: 19 -> 19; matrix products, arithmetic and copies ran while one was open for 1% -> 1% of each run, Pallas kernels for 21% -> 9%
where the time goes in v6:
time: 116 us
  waiting for transfers between devices  42.2 us (36%)
  Pallas kernels  33.7 us (29%)
  starting transfers between devices  33.2 us (29%)
  local copies, waits for them, and re-layouts  3.62 us (3%)
  other arithmetic  2.01 us (2%)
    ppermute x31, waiting for transfers between devices, swap(): return lax.ppermute(value, axis, [(i, i ^ k) for i in range(size)])  42.2 us
    pallas_call x22, Pallas kernels, call(): pl.pallas_call(body, out_shape=[jax.ShapeDtypeStruct(shape, kind) for sha...  33.7 us
    ppermute x31, starting transfers between devices, swap(): return lax.ppermute(value, axis, [(i, i ^ k) for i in range(size)])  33.2 us
    unnamed x16, local copies, waits for them, and re-layouts  3.62 us
  transfers between devices with their start and end apart: 31, of which 19 were waited for; matrix products, arithmetic and copies ran while one was open for 1% of the time, Pallas kernels for 9%

profile of v6, /device:TPU:0, one launch (start us, length us, event | category | flops | bytes accessed | tf_op | source)
XLA Modules:
  0.0 115.6 jit_solution(6502592229367384676)
XLA Ops:
  0.6 1.4 %convert_add_fusion = f32[1024]{0:T(1024)} fusion(bf16[48]{0:T(256)(128)(2,1)} %param.27, bf16[192]{0:T(256)(128)(2,1)} %param.25, bf16[48]{0:T(256)(128)(2,1)} %param.23, bf16[96]{0:T(256)(128)(2,1)} %param.21, bf16[288]{0:T(512)(128)(2,1)} %param.19), kind=kLoop, calls=%fused_computation | loop fusion | flops 9216 | bytes 5440 | tf_op jit(solution)/shard_map/add | solution.py:817
  2.1 3.0 %shard_map.237 = (bf16[256,384]{1,0:T(8,128)(2,1)}, bf16[624,384]{1,0:T(8,128)(2,1)}, f32[2,128]{1,0:T(2,128)}) custom-call(bf16[48,2304]{1,0:T(8,128)(2,1)} %ada.1, bf16[48,1152]{1,0:T(8,128)(2,1)} %qkv.1, bf16[48,384]{1,0:T(8,128)(2,1)} %proj.1, bf16[48,1536]{1,0:T(8,128)(2,1)} %fc1.1, bf16[192,384]{1,0:T(8,128)(2,1)} %fc2.1, f32[1,1024]{1,0:T(1,128)} %bitcast.23, ...), custom_call_target="tpu_custom_call" | custom-call | bytes 3690000 | tf_op jit(solution)/shard_map/pallas_call | solution.py:65
  5.0 4.0 %collective-permute-start.5 = (bf16[256,384]{1,0:T(8,128)(2,1)}, bf16[256,384]{1,0:T(8,128)(2,1)S(1)}, u32[]{:S(2)}, u32[]{:S(2)}) collective-permute-start(bf16[256,384]{1,0:T(8,128)(2,1)} %get-tuple-element.94.refs_3_), channel_id=1, source_target_pairs={{0,6},{1,7},{2,4},{3,5},{4,2},{5,3},{6,0},{7,1},{8,14},{9,15},{10,... | collective-permute-start | bytes 589832 | tf_op jit(solution)/shard_map/ppermute | solution.py:627
  9.0 0.5 collective-permute-start.3
  9.7 1.9 %collective-permute-start.7 = (bf16[624,384]{1,0:T(8,128)(2,1)}, bf16[624,384]{1,0:T(8,128)(2,1)S(1)}, u32[]{:S(2)}, u32[]{:S(2)}) collective-permute-start(bf16[624,384]{1,0:T(8,128)(2,1)} %get-tuple-element.100.refs_0_), channel_id=1, source_target_pairs={{0,2},{1,3},{2,0},{3,1},{4,6},{5,7},{6,4},{7,5},{8,10},{9,11},{10,... | collective-permute-start | bytes 1437704 | tf_op jit(solution)/shard_map/ppermute | solution.py:627
  11.5 1.5 %collective-permute-start.10 = (bf16[624,384]{1,0:T(8,128)(2,1)}, bf16[624,384]{1,0:T(8,128)(2,1)S(1)}, u32[]{:S(2)}, u32[]{:S(2)}) collective-permute-start(bf16[624,384]{1,0:T(8,128)(2,1)} %get-tuple-element.100.refs_0_), channel_id=1, source_target_pairs={{0,6},{1,7},{2,4},{3,5},{4,2},{5,3},{6,0},{7,1},{8,14},{9,15},{10,... | collective-permute-start | bytes 1437704 | tf_op jit(solution)/shard_map/ppermute | solution.py:627
  13.0 2.0 %collective-permute-done.5.refs_9_ = bf16[256,384]{1,0:T(8,128)(2,1)S(1)} collective-permute-done((bf16[256,384]{1,0:T(8,128)(2,1)}, bf16[256,384]{1,0:T(8,128)(2,1)S(1)}, u32[]{:S(2)}, u32[]{:S(2)}) %collective-permute-start.5) | collective-permute-done | bytes 196640 | tf_op jit(solution)/shard_map/ppermute | solution.py:627
  15.0 2.0 %collective-permute-start.9 = (bf16[624,384]{1,0:T(8,128)(2,1)}, bf16[624,384]{1,0:T(8,128)(2,1)S(1)}, u32[]{:S(2)}, u32[]{:S(2)}) collective-permute-start(bf16[624,384]{1,0:T(8,128)(2,1)} %get-tuple-element.100.refs_0_), channel_id=1, source_target_pairs={{0,4},{1,5},{2,6},{3,7},{4,0},{5,1},{6,2},{7,3},{8,12},{9,13},{10,... | collective-permute-start | bytes 1437704 | tf_op jit(solution)/shard_map/ppermute | solution.py:627
  17.0 1.4 %collective-permute-done.3.refs_7_ = bf16[256,384]{1,0:T(8,128)(2,1)S(1)} collective-permute-done((bf16[256,384]{1,0:T(8,128)(2,1)}, bf16[256,384]{1,0:T(8,128)(2,1)S(1)}, u32[]{:S(2)}, u32[]{:S(2)}) %collective-permute-start.3) | collective-permute-done | bytes 196640 | tf_op jit(solution)/shard_map/ppermute | solution.py:627
  18.4 1.3 %collective-permute-done.1.refs_5_ = bf16[256,384]{1,0:T(8,128)(2,1)S(1)} collective-permute-done((bf16[256,384]{1,0:T(8,128)(2,1)}, bf16[256,384]{1,0:T(8,128)(2,1)S(1)}, u32[]{:S(2)}, u32[]{:S(2)}) %collective-permute-start.1) | collective-permute-done | bytes 196640 | tf_op jit(solution)/shard_map/ppermute | solution.py:627
  19.8 0.3 collective-permute-done.refs_4_
  20.1 0.2 collective-permute-start.4
  20.3 0.9 collective-permute-done.6.refs_10_
  21.4 0.2 collective-permute-done.4.refs_8_
  21.5 1.1 collective-permute-done.2.refs_6_
  22.7 1.0 copy-done
  23.7 1.0 copy-done.3
  24.7 0.9 copy-done.4
  25.6 0.7 copy-done.5
  26.3 4.1 %shard_map.238 = (bf16[512,1152]{1,0:T(8,128)(2,1)S(1)}, bf16[512,384]{1,0:T(8,128)(2,1)S(1)}, f32[2,768]{1,0:T(2,128)S(1)}, f32[16,384]{1,0:T(8,128)S(1)}, bf16...) custom-call(bf16[512,384]{1,0:T(8,128)(2,1)S(1)} %bitcast.16, ...), custom_call_target="tpu_custom_call" | custom-call | bytes 14760000 | tf_op jit(solution)/shard_map/pallas_call | solution.py:65
  30.5 0.2 collective-permute-start.8
  30.7 8.2 %collective-permute-done.10.refs_1_ = bf16[624,384]{1,0:T(8,128)(2,1)S(1)} collective-permute-done((bf16[624,384]{1,0:T(8,128)(2,1)}, bf16[624,384]{1,0:T(8,128)(2,1)S(1)}, u32[]{:S(2)}, u32[]{:S(2)}) %collective-permute-start.10) | collective-permute-done | bytes 479264 | tf_op jit(solution)/shard_map/ppermute | solution.py:627
  39.1 2.5 %collective-permute-done.11.refs_9_ = bf16[1248,384]{1,0:T(8,128)(2,1)S(1)} collective-permute-done((bf16[1248,384]{1,0:T(8,128)(2,1)S(1)}, bf16[1248,384]{1,0:T(8,128)(2,1)S(1)}, u32[]{:S(2)}, u32[]{:S(2)}) %collective-permute-start.11) | collective-permute-done | bytes 958496 | tf_op jit(solution)/shard_map/ppermute | solution.py:627
  41.6 6.4 %shard_map.241 = (bf16[1536,384]{1,0:T(8,128)(2,1)S(1)}, bf16[1536,384]{1,0:T(8,128)(2,1)S(1)}, bf16[512,1536]{1,0:T(8,128)(2,1)S(1)}, bf16[512,1536]{1,0:T(8,12...) custom-call(f32[2,128]{1,0:T(2,128)S(1)} %copy-done.7, ...), custom_call_target="tpu_custom_call" | custom-call | bytes 36900000 | tf_op jit(solution)/shard_map/pallas_call | solution.py:65
  48.0 0.2 collective-permute-start.12
  48.2 2.0 %shard_map.242 = (bf16[512,384]{1,0:T(8,128)(2,1)}, f32[2,384]{1,0:T(2,128)S(1)}) custom-call(f32[2,128]{1,0:T(2,128)S(1)} %copy-done.7, bf16[512,384]{1,0:T(8,128)(2,1)S(1)} %get-tuple-element.101.cot, bf16[512,1536]{1,0:T(8,128)(2,1)S(1)} %get-tuple-element.102.act, bf16[1536,384]{1,0:T(8,128)(2,1)S(1)} %get-tuple-element.103.fc2, ...), custom_call_target="tpu_custom_call" | custom-call | bytes 5535000 | tf_op jit(solution)/shard_map/pallas_call | solution.py:65
  50.2 0.7 collective-permute-done.12.refs_1_
  50.9 0.3 shard_map.243
  51.2 2.8 %shard_map.244 = (bf16[512,384]{1,0:T(8,128)(2,1)S(1)}, f32[512,384]{1,0:T(8,128)S(1)}, bf16[384,384]{1,0:T(8,128)(2,1)S(1)}, f32[16,384]{1,0:T(8,128)S(1)}, f32[2,1152]{1,0:T(2,128)S(1)}) custom-call(f32[2,128]{1,0:T(2,128)S(1)} %copy-done.7, bf16[512,384]{1,0:T(8,128)(2,1)S(1)} %get-tuple-element.101.cot, ...), custom_call_target="tpu_custom_call" | custom-call | bytes 11070000 | tf_op jit(solution)/shard_map/pallas_call | solution.py:65
  54.0 3.5 %shard_map.245.refs_7_.refs_3_ = bf16[256,1152]{1,0:T(8,128)(2,1)S(1)} custom-call(bf16[512,1152]{1,0:T(8,128)(2,1)S(1)} %get-tuple-element.123.projected, bf16[512,384]{1,0:T(8,128)(2,1)S(1)} %get-tuple-element.125.grad_mixed), custom_call_target="tpu_custom_call" | custom-call | bytes 12177000 | tf_op jit(solution)/shard_map/pallas_call | solution.py:65
  57.5 3.5 %shard_map.246.refs_8_.refs_4_ = bf16[256,1152]{1,0:T(8,128)(2,1)S(1)} custom-call(bf16[512,1152]{1,0:T(8,128)(2,1)S(1)} %get-tuple-element.123.projected, bf16[512,384]{1,0:T(8,128)(2,1)S(1)} %get-tuple-element.125.grad_mixed), custom_call_target="tpu_custom_call" | custom-call | bytes 12177000 | tf_op jit(solution)/shard_map/pallas_call | solution.py:65
  61.0 1.9 %shard_map.247 = (bf16[512,384]{1,0:T(8,128)(2,1)}, bf16[16,384]{1,0:T(8,128)(2,1)S(1)}, bf16[512,384]{1,0:T(8,128)(2,1)S(1)}) custom-call(bf16[512,384]{1,0:T(8,128)(2,1)S(1)} %bitcast.17, bf16[2,384]{1,0:T(2,128)(2,1)S(1)} %bitcast.21, f32[512,384]{1,0:T(8,128)S(1)} %get-tuple-element.120.refs_2_, bf16[384,1152]{1,0:T(8,128)(2,1)S(1)} %get-tuple-element.121.refs_3_, ...), custom_call_target="tpu_custom_call" | custom-call | bytes 7380000 | tf_op jit(solution)/shard_map/pallas_call | solution.py:65
  62.9 0.9 shard_map.249
  63.7 0.2 collective-permute-start.13
  63.9 1.7 %collective-permute-start.14 = (bf16[384,384]{1,0:T(8,128)(2,1)S(1)}, bf16[384,384]{1,0:T(8,128)(2,1)S(1)}, u32[]{:S(2)}, u32[]{:S(2)}) collective-permute-start(bf16[384,384]{1,0:T(8,128)(2,1)S(1)} %get-tuple-element.135), channel_id=1, source_target_pairs={{0,2},{1,3},{2,0},{3,1},{4,6},{5,7},{6,4},{7,5},{8,10},{9,11},{10,... | collective-permute-start | bytes 884744 | tf_op jit(solution)/shard_map/ppermute | solution.py:627
  65.6 1.5 %collective-permute-start.15 = (bf16[384,384]{1,0:T(8,128)(2,1)S(1)}, bf16[384,384]{1,0:T(8,128)(2,1)S(1)}, u32[]{:S(2)}, u32[]{:S(2)}) collective-permute-start(bf16[384,384]{1,0:T(8,128)(2,1)S(1)} %get-tuple-element.136), channel_id=1, source_target_pairs={{0,4},{1,5},{2,6},{3,7},{4,0},{5,1},{6,2},{7,3},{8,12},{9,13},{10,... | collective-permute-start | bytes 884744 | tf_op jit(solution)/shard_map/ppermute | solution.py:627
  67.2 0.3 collective-permute-start.16
  67.5 6.3 %collective-permute-done.14.refs_0_ = bf16[384,384]{1,0:T(8,128)(2,1)S(1)} collective-permute-done((bf16[384,384]{1,0:T(8,128)(2,1)S(1)}, bf16[384,384]{1,0:T(8,128)(2,1)S(1)}, u32[]{:S(2)}, u32[]{:S(2)}) %collective-permute-start.14) | collective-permute-done | bytes 294944 | tf_op jit(solution)/shard_map/ppermute | solution.py:627
  73.8 7.2 %collective-permute-done.15.refs_1_ = bf16[384,384]{1,0:T(8,128)(2,1)S(1)} collective-permute-done((bf16[384,384]{1,0:T(8,128)(2,1)S(1)}, bf16[384,384]{1,0:T(8,128)(2,1)S(1)}, u32[]{:S(2)}, u32[]{:S(2)}) %collective-permute-start.15) | collective-permute-done | bytes 294944 | tf_op jit(solution)/shard_map/ppermute | solution.py:627
  81.0 0.2 shard_map.250
  81.2 1.6 %collective-permute-start.20 = (bf16[192,384]{1,0:T(8,128)(2,1)S(1)}, bf16[192,384]{1,0:T(8,128)(2,1)S(1)}, u32[]{:S(2)}, u32[]{:S(2)}) collective-permute-start(bf16[192,384]{1,0:T(8,128)(2,1)S(1)} %get-tuple-element.145), channel_id=1, source_target_pairs={{0,8},{8,0},{16,24},{24,16},{1,9},{9,1},{17,25},{25,17},{2,10},{10... | collective-permute-start | bytes 442376 | tf_op jit(solution)/shard_map/ppermute | solution.py:627
  82.9 0.1 shard_map.251
  83.0 1.3 %collective-permute-start.17 = (bf16[224,384]{1,0:T(8,128)(2,1)S(1)}, bf16[224,384]{1,0:T(8,128)(2,1)S(1)}, u32[]{:S(2)}, u32[]{:S(2)}) collective-permute-start(bf16[224,384]{1,0:T(8,128)(2,1)S(1)} %get-tuple-element.142), channel_id=1, source_target_pairs={{0,2},{1,3},{2,0},{3,1},{4,6},{5,7},{6,4},{7,5},{8,10},{9,11},{10,... | collective-permute-start | bytes 516104 | tf_op jit(solution)/shard_map/ppermute | solution.py:627
  84.3 0.8 collective-permute-start.18
  85.1 1.5 %collective-permute-start.19 = (bf16[224,384]{1,0:T(8,128)(2,1)S(1)}, bf16[224,384]{1,0:T(8,128)(2,1)S(1)}, u32[]{:S(2)}, u32[]{:S(2)}) collective-permute-start(bf16[224,384]{1,0:T(8,128)(2,1)S(1)} %get-tuple-element.144), channel_id=1, source_target_pairs={{0,6},{1,7},{2,4},{3,5},{4,2},{5,3},{6,0},{7,1},{8,14},{9,15},{10,... | collective-permute-start | bytes 516104 | tf_op jit(solution)/shard_map/ppermute | solution.py:627
  86.6 2.6 %collective-permute-start.21 = (bf16[96,384]{1,0:T(8,128)(2,1)S(1)}, bf16[96,384]{1,0:T(8,128)(2,1)S(1)}, u32[]{:S(2)}, u32[]{:S(2)}) collective-permute-start(bf16[96,384]{1,0:T(8,128)(2,1)S(1)} %get-tuple-element.146), channel_id=1, source_target_pairs={{0,16},{8,24},{16,0},{24,8},{1,17},{9,25},{17,1},{25,9},{2,18},{10... | collective-permute-start | bytes 221192 | tf_op jit(solution)/shard_map/ppermute | solution.py:627
  89.3 1.7 %shard_map.248 = bf16[2,384]{1,0:T(2,128)(2,1)} custom-call(bf16[2,384]{1,0:T(2,128)(2,1)S(1)} %bitcast.22, bf16[16,384]{1,0:T(8,128)(2,1)S(1)} %get-tuple-element.127.mods, bf16[384,768]{1,0:T(8,128)(2,1)S(1)} %get-tuple-element.128.first, bf16[384,1536]{1,0:T(8,128)(2,1)S(1)} %get-tuple-element.129.second), custom_call_target="tpu_custom_call" | custom-call | bytes 7380000 | tf_op jit(solution)/shard_map/pallas_call | solution.py:65
  91.0 1.0 collective-permute-done.21.second
  91.9 1.4 %collective-permute-done.18.refs_1_ = bf16[224,384]{1,0:T(8,128)(2,1)S(1)} collective-permute-done((bf16[224,384]{1,0:T(8,128)(2,1)S(1)}, bf16[224,384]{1,0:T(8,128)(2,1)S(1)}, u32[]{:S(2)}, u32[]{:S(2)}) %collective-permute-start.18) | collective-permute-done | bytes 172064 | tf_op jit(solution)/shard_map/ppermute | solution.py:627
  93.4 0.5 collective-permute-start.22
  93.9 3.1 %collective-permute-start.23 = (bf16[112,384]{1,0:T(8,128)(2,1)S(1)}, bf16[112,384]{1,0:T(8,128)(2,1)S(1)}, u32[]{:S(2)}, u32[]{:S(2)}) collective-permute-start(bf16[112,384]{1,0:T(8,128)(2,1)S(1)} %get-tuple-element.152), channel_id=1, source_target_pairs={{0,16},{8,24},{16,0},{24,8},{1,17},{9,25},{17,1},{25,9},{2,18},{10... | collective-permute-start | bytes 258056 | tf_op jit(solution)/shard_map/ppermute | solution.py:627
  96.9 0.9 collective-permute-start.24
  97.9 1.8 %collective-permute-start.26 = (bf16[96,384]{1,0:T(8,128)(2,1)S(1)}, bf16[96,384]{1,0:T(8,128)(2,1)S(1)}, u32[]{:S(2)}, u32[]{:S(2)}) collective-permute-start(bf16[96,384]{1,0:T(8,128)(2,1)S(1)} %shard_map.256.refs_0_), channel_id=1, source_target_pairs={{0,16},{8,24},{16,0},{24,8},{1,17},{9,25},{17,1},{25,9},{2,18},{10... | collective-permute-start | bytes 221192 | tf_op jit(solution)/shard_map/ppermute | solution.py:627
  99.7 2.8 %collective-permute-done.23.refs_2_ = bf16[112,384]{1,0:T(8,128)(2,1)S(1)} collective-permute-done((bf16[112,384]{1,0:T(8,128)(2,1)S(1)}, bf16[112,384]{1,0:T(8,128)(2,1)S(1)}, u32[]{:S(2)}, u32[]{:S(2)}) %collective-permute-start.23) | collective-permute-done | bytes 86048 | tf_op jit(solution)/shard_map/ppermute | solution.py:627
  102.4 0.9 collective-permute-done.24.refs_3_
  103.5 2.6 %collective-permute-done.26.refs_1_ = bf16[96,384]{1,0:T(8,128)(2,1)S(1)} collective-permute-done((bf16[96,384]{1,0:T(8,128)(2,1)S(1)}, bf16[96,384]{1,0:T(8,128)(2,1)S(1)}, u32[]{:S(2)}, u32[]{:S(2)}) %collective-permute-start.26) | collective-permute-done | bytes 73760 | tf_op jit(solution)/shard_map/ppermute | solution.py:627
  106.2 2.6 %collective-permute-start.29 = (bf16[48,384]{1,0:T(8,128)(2,1)S(1)}, bf16[48,384]{1,0:T(8,128)(2,1)S(1)}, u32[]{:S(2)}, u32[]{:S(2)}) collective-permute-start(bf16[48,384]{1,0:T(8,128)(2,1)S(1)} %get-tuple-element.160.refs_2_), channel_id=1, source_target_pairs={{0,24},{8,16},{16,8},{24,0},{1,25},{9,17},{17,9},{25,1},{2,26},{10... | collective-permute-start | bytes 110600 | tf_op jit(solution)/shard_map/ppermute | solution.py:627
  108.8 0.8 collective-permute-start.28
  109.6 1.0 collective-permute-start.27
  110.6 1.9 %shard_map.255 = (f32[48,2304]{1,0:T(8,128)}, f32[1,288]{1,0:T(1,128)S(1)}, f32[1,96]{1,0:T(1,128)}, f32[1,48]{1,0:T(1,128)}, f32[1,192]{1,0:T(1,128)}, /*index=5*/f32[1,48]{1,0:T(1,128)}) custom-call(f32[112,384]{1,0:T(8,128)S(1)} %get-tuple-element.150.refs_0_, bf16[112,384]{1,0:T(8,128)(2,1)S(1)} %collective-permute-done.22.refs_1_, ...), custom_call_target="tpu_custom_call" | custom-call | bytes 7380000 | tf_op jit(solution)/shard_map/pallas_call | solution.py:65
  112.5 0.6 reduce
  113.1 1.1 collective-permute-done.29.refs_5_
  114.2 0.4 collective-permute-done.28.refs_4_
  114.6 1.0 shard_map.258
  (38 shorter events, 1.0 us)
Async XLA Ops:
  5.0 9.9 %collective-permute-start.5 = (bf16[256,384]{1,0:T(8,128)(2,1)}, bf16[256,384]{1,0:T(8,128)(2,1)S(1)}, u32[]{:S(2)}, u32[]{:S(2)}) collective-permute-start(bf16[256,384]{1,0:T(8,128)(2,1)} %get-tuple-element.94.refs_3_), channel_id=1, source_target_pairs={{0,6},{1,7},{2,4},{3,5},{4,2},{5,3},{6,0},{7,1},{8,14},{9,15},{10,... | collective-permute-start | bytes 589832 | tf_op jit(solution)/shard_map/ppermute | solution.py:627
  9.0 9.4 %collective-permute-start.3 = (bf16[256,384]{1,0:T(8,128)(2,1)}, bf16[256,384]{1,0:T(8,128)(2,1)S(1)}, u32[]{:S(2)}, u32[]{:S(2)}) collective-permute-start(bf16[256,384]{1,0:T(8,128)(2,1)} %get-tuple-element.94.refs_3_), channel_id=1, source_target_pairs={{0,4},{1,5},{2,6},{3,7},{4,0},{5,1},{6,2},{7,3},{8,12},{9,13},{10,... | collective-permute-start | bytes 589832 | tf_op jit(solution)/shard_map/ppermute | solution.py:627
  9.5 10.3 %collective-permute-start.1 = (bf16[256,384]{1,0:T(8,128)(2,1)}, bf16[256,384]{1,0:T(8,128)(2,1)S(1)}, u32[]{:S(2)}, u32[]{:S(2)}) collective-permute-start(bf16[256,384]{1,0:T(8,128)(2,1)} %get-tuple-element.94.refs_3_), channel_id=1, source_target_pairs={{0,2},{1,3},{2,0},{3,1},{4,6},{5,7},{6,4},{7,5},{8,10},{9,11},{10,... | collective-permute-start | bytes 589832 | tf_op jit(solution)/shard_map/ppermute | solution.py:627
  9.7 20.8 %collective-permute-start.7 = (bf16[624,384]{1,0:T(8,128)(2,1)}, bf16[624,384]{1,0:T(8,128)(2,1)S(1)}, u32[]{:S(2)}, u32[]{:S(2)}) collective-permute-start(bf16[624,384]{1,0:T(8,128)(2,1)} %get-tuple-element.100.refs_0_), channel_id=1, source_target_pairs={{0,2},{1,3},{2,0},{3,1},{4,6},{5,7},{6,4},{7,5},{8,10},{9,11},{10,... | collective-permute-start | bytes 1437704 | tf_op jit(solution)/shard_map/ppermute | solution.py:627
  11.5 27.4 %collective-permute-start.10 = (bf16[624,384]{1,0:T(8,128)(2,1)}, bf16[624,384]{1,0:T(8,128)(2,1)S(1)}, u32[]{:S(2)}, u32[]{:S(2)}) collective-permute-start(bf16[624,384]{1,0:T(8,128)(2,1)} %get-tuple-element.100.refs_0_), channel_id=1, source_target_pairs={{0,6},{1,7},{2,4},{3,5},{4,2},{5,3},{6,0},{7,1},{8,14},{9,15},{10,... | collective-permute-start | bytes 1437704 | tf_op jit(solution)/shard_map/ppermute | solution.py:627
  15.0 23.9 %collective-permute-start.9 = (bf16[624,384]{1,0:T(8,128)(2,1)}, bf16[624,384]{1,0:T(8,128)(2,1)S(1)}, u32[]{:S(2)}, u32[]{:S(2)}) collective-permute-start(bf16[624,384]{1,0:T(8,128)(2,1)} %get-tuple-element.100.refs_0_), channel_id=1, source_target_pairs={{0,4},{1,5},{2,6},{3,7},{4,0},{5,1},{6,2},{7,3},{8,12},{9,13},{10,... | collective-permute-start | bytes 1437704 | tf_op jit(solution)/shard_map/ppermute | solution.py:627
  18.4 1.7 %collective-permute-start = (bf16[256,384]{1,0:T(8,128)(2,1)}, bf16[256,384]{1,0:T(8,128)(2,1)S(1)}, u32[]{:S(2)}, u32[]{:S(2)}) collective-permute-start(bf16[256,384]{1,0:T(8,128)(2,1)} %get-tuple-element.94.refs_3_), channel_id=1, source_target_pairs={{0,1},{1,0},{2,3},{3,2},{4,5},{5,4},{6,7},{7,6},{8,9},{9,8},{10,11... | collective-permute-start | bytes 589832 | tf_op jit(solution)/shard_map/ppermute | solution.py:627
  19.8 1.4 %collective-permute-start.6 = (bf16[256,384]{1,0:T(8,128)(2,1)S(1)}, bf16[256,384]{1,0:T(8,128)(2,1)S(1)}, u32[]{:S(2)}, u32[]{:S(2)}) collective-permute-start(bf16[256,384]{1,0:T(8,128)(2,1)S(1)} %collective-permute-done.5.refs_9_), channel_id=1, source_target_pairs={{0,1},{1,0},{2,3},{3,2},{4,5},{5,4},{6,7},{7,6},{8,9},{9,8},{10,11... | collective-permute-start | bytes 589832 | tf_op jit(solution)/shard_map/ppermute | solution.py:627
  20.1 1.4 %collective-permute-start.4 = (bf16[256,384]{1,0:T(8,128)(2,1)S(1)}, bf16[256,384]{1,0:T(8,128)(2,1)S(1)}, u32[]{:S(2)}, u32[]{:S(2)}) collective-permute-start(bf16[256,384]{1,0:T(8,128)(2,1)S(1)} %collective-permute-done.3.refs_7_), channel_id=1, source_target_pairs={{0,1},{1,0},{2,3},{3,2},{4,5},{5,4},{6,7},{7,6},{8,9},{9,8},{10,11... | collective-permute-start | bytes 589832 | tf_op jit(solution)/shard_map/ppermute | solution.py:627
  21.2 1.4 %collective-permute-start.2 = (bf16[256,384]{1,0:T(8,128)(2,1)S(1)}, bf16[256,384]{1,0:T(8,128)(2,1)S(1)}, u32[]{:S(2)}, u32[]{:S(2)}) collective-permute-start(bf16[256,384]{1,0:T(8,128)(2,1)S(1)} %collective-permute-done.1.refs_5_), channel_id=1, source_target_pairs={{0,1},{1,0},{2,3},{3,2},{4,5},{5,4},{6,7},{7,6},{8,9},{9,8},{10,11... | collective-permute-start | bytes 589832 | tf_op jit(solution)/shard_map/ppermute | solution.py:627
  22.7 1.0 copy-start
  23.7 1.0 copy-start.3
  24.7 0.9 copy-start.4
  25.6 0.7 copy-start.5
  26.3 4.2 %copy-start.2 = (bf16[624,384]{1,0:T(8,128)(2,1)S(1)}, bf16[624,384]{1,0:T(8,128)(2,1)}, u32[]{:S(2)}) copy-start(bf16[624,384]{1,0:T(8,128)(2,1)} %get-tuple-element.100.refs_0_) | copy-start | bytes 1437700
  30.5 11.1 %copy-start.6 = (bf16[2,1,384]{2,0,1:T(2,128)(2,1)S(1)}, bf16[2,1,384]{2,0,1:T(2,128)(2,1)}, u32[]{:S(2)}) copy-start(bf16[2,1,384]{2,0,1:T(2,128)(2,1)} %param.15) | copy-start | bytes 4612
  30.5 11.1 %copy-start.7 = (f32[2,128]{1,0:T(2,128)S(1)}, f32[2,128]{1,0:T(2,128)}, u32[]{:S(2)}) copy-start(f32[2,128]{1,0:T(2,128)} %get-tuple-element.93.refs_0_.lives) | copy-start | bytes 3076
  30.5 8.5 %collective-permute-start.8 = (bf16[1248,384]{1,0:T(8,128)(2,1)S(1)}, bf16[1248,384]{1,0:T(8,128)(2,1)S(1)}, u32[]{:S(2)}, u32[]{:S(2)}) collective-permute-start(bf16[1248,384]{1,0:T(8,128)(2,1)S(1)} %shard_map.239.refs_6_), channel_id=1, source_target_pairs={{0,1},{1,0},{2,3},{3,2},{4,5},{5,4},{6,7},{7,6},{8,9},{9,8},{10,11... | collective-permute-start | bytes 2875400 | tf_op jit(solution)/shard_map/ppermute | solution.py:627
  39.0 2.6 %collective-permute-start.11 = (bf16[1248,384]{1,0:T(8,128)(2,1)S(1)}, bf16[1248,384]{1,0:T(8,128)(2,1)S(1)}, u32[]{:S(2)}, u32[]{:S(2)}) collective-permute-start(bf16[1248,384]{1,0:T(8,128)(2,1)S(1)} %shard_map.240.refs_8_), channel_id=1, source_target_pairs={{0,1},{1,0},{2,3},{3,2},{4,5},{5,4},{6,7},{7,6},{8,9},{9,8},{10,11... | collective-permute-start | bytes 2875400 | tf_op jit(solution)/shard_map/ppermute | solution.py:627
  48.0 2.9 %collective-permute-start.12 = (bf16[1536,384]{1,0:T(8,128)(2,1)S(1)}, bf16[1536,384]{1,0:T(8,128)(2,1)S(1)}, u32[]{:S(2)}, u32[]{:S(2)}) collective-permute-start(bf16[1536,384]{1,0:T(8,128)(2,1)S(1)} %get-tuple-element.109), channel_id=1, source_target_pairs={{0,1},{1,0},{2,3},{3,2},{4,5},{5,4},{6,7},{7,6},{8,9},{9,8},{10,11... | collective-permute-start | bytes 3538952 | tf_op jit(solution)/shard_map/ppermute | solution.py:627
  57.5 3.5 %copy-start.1 = (bf16[2,1,256,384]{3,2,1,0:T(8,128)(2,1)S(1)}, bf16[2,1,256,384]{3,2,1,0:T(8,128)(2,1)}, u32[]{:S(2)}) copy-start(bf16[2,1,256,384]{3,2,1,0:T(8,128)(2,1)} %param.14) | copy-start | bytes 1179652
  63.7 19.1 %collective-permute-start.13 = (bf16[832,384]{1,0:T(8,128)(2,1)S(1)}, bf16[832,384]{1,0:T(8,128)(2,1)S(1)}, u32[]{:S(2)}, u32[]{:S(2)}) collective-permute-start(bf16[832,384]{1,0:T(8,128)(2,1)S(1)} %get-tuple-element.133), channel_id=1, source_target_pairs={{0,1},{1,0},{2,3},{3,2},{4,5},{5,4},{6,7},{7,6},{8,9},{9,8},{10,11... | collective-permute-start | bytes 1916936 | tf_op jit(solution)/shard_map/ppermute | solution.py:627
  63.9 9.9 %collective-permute-start.14 = (bf16[384,384]{1,0:T(8,128)(2,1)S(1)}, bf16[384,384]{1,0:T(8,128)(2,1)S(1)}, u32[]{:S(2)}, u32[]{:S(2)}) collective-permute-start(bf16[384,384]{1,0:T(8,128)(2,1)S(1)} %get-tuple-element.135), channel_id=1, source_target_pairs={{0,2},{1,3},{2,0},{3,1},{4,6},{5,7},{6,4},{7,5},{8,10},{9,11},{10,... | collective-permute-start | bytes 884744 | tf_op jit(solution)/shard_map/ppermute | solution.py:627
  65.6 15.3 %collective-permute-start.15 = (bf16[384,384]{1,0:T(8,128)(2,1)S(1)}, bf16[384,384]{1,0:T(8,128)(2,1)S(1)}, u32[]{:S(2)}, u32[]{:S(2)}) collective-permute-start(bf16[384,384]{1,0:T(8,128)(2,1)S(1)} %get-tuple-element.136), channel_id=1, source_target_pairs={{0,4},{1,5},{2,6},{3,7},{4,0},{5,1},{6,2},{7,3},{8,12},{9,13},{10,... | collective-permute-start | bytes 884744 | tf_op jit(solution)/shard_map/ppermute | solution.py:627
  67.2 13.8 %collective-permute-start.16 = (bf16[384,384]{1,0:T(8,128)(2,1)S(1)}, bf16[384,384]{1,0:T(8,128)(2,1)S(1)}, u32[]{:S(2)}, u32[]{:S(2)}) collective-permute-start(bf16[384,384]{1,0:T(8,128)(2,1)S(1)} %get-tuple-element.137), channel_id=1, source_target_pairs={{0,6},{1,7},{2,4},{3,5},{4,2},{5,3},{6,0},{7,1},{8,14},{9,15},{10,... | collective-permute-start | bytes 884744 | tf_op jit(solution)/shard_map/ppermute | solution.py:627
  81.2 5.4 %collective-permute-start.20 = (bf16[192,384]{1,0:T(8,128)(2,1)S(1)}, bf16[192,384]{1,0:T(8,128)(2,1)S(1)}, u32[]{:S(2)}, u32[]{:S(2)}) collective-permute-start(bf16[192,384]{1,0:T(8,128)(2,1)S(1)} %get-tuple-element.145), channel_id=1, source_target_pairs={{0,8},{8,0},{16,24},{24,16},{1,9},{9,1},{17,25},{25,17},{2,10},{10... | collective-permute-start | bytes 442376 | tf_op jit(solution)/shard_map/ppermute | solution.py:627
  83.0 8.9 %collective-permute-start.17 = (bf16[224,384]{1,0:T(8,128)(2,1)S(1)}, bf16[224,384]{1,0:T(8,128)(2,1)S(1)}, u32[]{:S(2)}, u32[]{:S(2)}) collective-permute-start(bf16[224,384]{1,0:T(8,128)(2,1)S(1)} %get-tuple-element.142), channel_id=1, source_target_pairs={{0,2},{1,3},{2,0},{3,1},{4,6},{5,7},{6,4},{7,5},{8,10},{9,11},{10,... | collective-permute-start | bytes 516104 | tf_op jit(solution)/shard_map/ppermute | solution.py:627
  84.3 9.0 %collective-permute-start.18 = (bf16[224,384]{1,0:T(8,128)(2,1)S(1)}, bf16[224,384]{1,0:T(8,128)(2,1)S(1)}, u32[]{:S(2)}, u32[]{:S(2)}) collective-permute-start(bf16[224,384]{1,0:T(8,128)(2,1)S(1)} %get-tuple-element.143), channel_id=1, source_target_pairs={{0,4},{1,5},{2,6},{3,7},{4,0},{5,1},{6,2},{7,3},{8,12},{9,13},{10,... | collective-permute-start | bytes 516104 | tf_op jit(solution)/shard_map/ppermute | solution.py:627
  85.1 8.2 %collective-permute-start.19 = (bf16[224,384]{1,0:T(8,128)(2,1)S(1)}, bf16[224,384]{1,0:T(8,128)(2,1)S(1)}, u32[]{:S(2)}, u32[]{:S(2)}) collective-permute-start(bf16[224,384]{1,0:T(8,128)(2,1)S(1)} %get-tuple-element.144), channel_id=1, source_target_pairs={{0,6},{1,7},{2,4},{3,5},{4,2},{5,3},{6,0},{7,1},{8,14},{9,15},{10,... | collective-permute-start | bytes 516104 | tf_op jit(solution)/shard_map/ppermute | solution.py:627
  86.6 5.3 %collective-permute-start.21 = (bf16[96,384]{1,0:T(8,128)(2,1)S(1)}, bf16[96,384]{1,0:T(8,128)(2,1)S(1)}, u32[]{:S(2)}, u32[]{:S(2)}) collective-permute-start(bf16[96,384]{1,0:T(8,128)(2,1)S(1)} %get-tuple-element.146), channel_id=1, source_target_pairs={{0,16},{8,24},{16,0},{24,8},{1,17},{9,25},{17,1},{25,9},{2,18},{10... | collective-permute-start | bytes 221192 | tf_op jit(solution)/shard_map/ppermute | solution.py:627
  93.4 6.2 %collective-permute-start.22 = (bf16[112,384]{1,0:T(8,128)(2,1)S(1)}, bf16[112,384]{1,0:T(8,128)(2,1)S(1)}, u32[]{:S(2)}, u32[]{:S(2)}) collective-permute-start(bf16[112,384]{1,0:T(8,128)(2,1)S(1)} %get-tuple-element.151), channel_id=1, source_target_pairs={{0,8},{8,0},{16,24},{24,16},{1,9},{9,1},{17,25},{25,17},{2,10},{10... | collective-permute-start | bytes 258056 | tf_op jit(solution)/shard_map/ppermute | solution.py:627
  93.9 8.5 %collective-permute-start.23 = (bf16[112,384]{1,0:T(8,128)(2,1)S(1)}, bf16[112,384]{1,0:T(8,128)(2,1)S(1)}, u32[]{:S(2)}, u32[]{:S(2)}) collective-permute-start(bf16[112,384]{1,0:T(8,128)(2,1)S(1)} %get-tuple-element.152), channel_id=1, source_target_pairs={{0,16},{8,24},{16,0},{24,8},{1,17},{9,25},{17,1},{25,9},{2,18},{10... | collective-permute-start | bytes 258056 | tf_op jit(solution)/shard_map/ppermute | solution.py:627
  96.9 6.4 %collective-permute-start.24 = (bf16[112,384]{1,0:T(8,128)(2,1)S(1)}, bf16[112,384]{1,0:T(8,128)(2,1)S(1)}, u32[]{:S(2)}, u32[]{:S(2)}) collective-permute-start(bf16[112,384]{1,0:T(8,128)(2,1)S(1)} %get-tuple-element.153), channel_id=1, source_target_pairs={{0,24},{8,16},{16,8},{24,0},{1,25},{9,17},{17,9},{25,1},{2,26},{10... | collective-permute-start | bytes 258056 | tf_op jit(solution)/shard_map/ppermute | solution.py:627
  97.9 8.2 %collective-permute-start.26 = (bf16[96,384]{1,0:T(8,128)(2,1)S(1)}, bf16[96,384]{1,0:T(8,128)(2,1)S(1)}, u32[]{:S(2)}, u32[]{:S(2)}) collective-permute-start(bf16[96,384]{1,0:T(8,128)(2,1)S(1)} %shard_map.256.refs_0_), channel_id=1, source_target_pairs={{0,16},{8,24},{16,0},{24,8},{1,17},{9,25},{17,1},{25,9},{2,18},{10... | collective-permute-start | bytes 221192 | tf_op jit(solution)/shard_map/ppermute | solution.py:627
  103.4 7.2 %collective-permute-start.25 = (bf16[256,384]{1,0:T(8,128)(2,1)S(1)}, bf16[256,384]{1,0:T(8,128)(2,1)S(1)}, u32[]{:S(2)}, u32[]{:S(2)}) collective-permute-start(bf16[256,384]{1,0:T(8,128)(2,1)S(1)} %get-tuple-element.154.refs_4_), channel_id=1, source_target_pairs={{0,1},{1,0},{2,3},{3,2},{4,5},{5,4},{6,7},{7,6},{8,9},{9,8},{10,11... | collective-permute-start | bytes 589832 | tf_op jit(solution)/shard_map/ppermute | solution.py:627
  106.1 8.5 %collective-permute-start.30 = (bf16[192,384]{1,0:T(8,128)(2,1)S(1)}, bf16[192,384]{1,0:T(8,128)(2,1)S(1)}, u32[]{:S(2)}, u32[]{:S(2)}) collective-permute-start(bf16[192,384]{1,0:T(8,128)(2,1)S(1)} %shard_map.257.refs_0_), channel_id=1, source_target_pairs={{0,8},{8,0},{16,24},{24,16},{1,9},{9,1},{17,25},{25,17},{2,10},{10... | collective-permute-start | bytes 442376 | tf_op jit(solution)/shard_map/ppermute | solution.py:627
  106.2 8.0 %collective-permute-start.29 = (bf16[48,384]{1,0:T(8,128)(2,1)S(1)}, bf16[48,384]{1,0:T(8,128)(2,1)S(1)}, u32[]{:S(2)}, u32[]{:S(2)}) collective-permute-start(bf16[48,384]{1,0:T(8,128)(2,1)S(1)} %get-tuple-element.160.refs_2_), channel_id=1, source_target_pairs={{0,24},{8,16},{16,8},{24,0},{1,25},{9,17},{17,9},{25,1},{2,26},{10... | collective-permute-start | bytes 110600 | tf_op jit(solution)/shard_map/ppermute | solution.py:627
  108.8 5.8 %collective-permute-start.28 = (bf16[48,384]{1,0:T(8,128)(2,1)S(1)}, bf16[48,384]{1,0:T(8,128)(2,1)S(1)}, u32[]{:S(2)}, u32[]{:S(2)}) collective-permute-start(bf16[48,384]{1,0:T(8,128)(2,1)S(1)} %get-tuple-element.160.refs_2_), channel_id=1, source_target_pairs={{0,16},{8,24},{16,0},{24,8},{1,17},{9,25},{17,1},{25,9},{2,18},{10... | collective-permute-start | bytes 110600 | tf_op jit(solution)/shard_map/ppermute | solution.py:627
  109.6 4.9 %collective-permute-start.27 = (bf16[48,384]{1,0:T(8,128)(2,1)S(1)}, bf16[48,384]{1,0:T(8,128)(2,1)S(1)}, u32[]{:S(2)}, u32[]{:S(2)}) collective-permute-start(bf16[48,384]{1,0:T(8,128)(2,1)S(1)} %get-tuple-element.160.refs_2_), channel_id=1, source_target_pairs={{0,8},{8,0},{16,24},{24,16},{1,9},{9,1},{17,25},{25,17},{2,10},{10... | collective-permute-start | bytes 110600 | tf_op jit(solution)/shard_map/ppermute | solution.py:627
